TPU v7x, 256 devices: a whole 4x4x8 slice. The times are simulated.
256 devices in a mesh: dp: 64 (over z, x, core), proto: 4 (over y).
Axes of the slice: x: 4, y: 4, z: 8, core: 2. Of those that a mesh axis runs over, the one named last changes fastest.
Arguments:
- teacher_feats: bfloat16 [64, 256, 256], P('dp'), may hold values from -32 to 32
- student_feats: bfloat16 [64, 256, 256], P('dp'), may hold values from -48 to 48
- prototypes: bfloat16 [32768, 256], P('proto'), may hold values from -0.45 to 0.45
- patch_mask: int32 [64, 256], P('dp'), may hold values from 0 to 1, as said below
Outputs:
- loss: float32 [], replicated
- student_grad: float32 [64, 256, 256], P('dp')
- proto_grad: float32 [4, 8192, 256], P('proto', 'dp')
Inputs may be any that keep to these rules, and one draw needn't show every extreme that they name: `patch_mask`: each image masks between 64 and 128 of its patches; at least one image masks exactly 128.
All inputs are finite; a program needn't handle non-finite values.
Results may differ from a plain program's by a relative error of at most 0.0065.
Values may be sent and summed in bfloat16 or wider, within the bound.
No kernel may reach another device: no remote copies, remote signals or barrier semaphores. Data moves between devices by JAX's collectives and lax.ppermute only.
A program may use at most 128 MiB of HBM per device.

v0:
```python
import jax
import jax.numpy as jnp
from jax import lax
from jax.sharding import PartitionSpec as P

BALANCING_PASSES = 3
LOSS_SCALE = 16384


teacher_temp = 0.07
student_temp = 0.1


def local(teacher_feats, student_feats, prototypes, patch_mask):
    images, patches, feat_width = teacher_feats.shape
    n_data = lax.axis_size("dp")
    all_images = images * n_data
    counts = jnp.sum(patch_mask, axis=1)
    count_float = counts.astype(jnp.float32)
    teach_rows = teacher_feats.reshape(-1, feat_width)
    student_rows = student_feats.reshape(-1, feat_width)
    live_grid = patch_mask.astype(jnp.float32)
    live_rows = live_grid.reshape(-1)
    weight_rows = (live_grid / count_float[:, None]).reshape(-1)
    teach_logits = (
        jnp.dot(teach_rows, prototypes.T, preferred_element_type=jnp.float32) / teacher_temp
    )
    student_logits = (
        jnp.dot(student_rows, prototypes.T, preferred_element_type=jnp.float32) / student_temp
    )
    teach_local = jnp.max(teach_logits, axis=1)
    student_local = jnp.max(student_logits, axis=1)
    teach_peak, student_peak = lax.pmax((teach_local, student_local), "proto")
    shifted_total = jnp.sum(jnp.exp(student_logits - student_peak[:, None]), axis=1)
    student_total = lax.psum(shifted_total, "proto")
    teach_exp = jnp.exp(teach_logits - teach_peak[:, None])
    row_scale = live_rows
    column_scale = jnp.zeros((prototypes.shape[0],), jnp.float32)
    for balancing_pass_index in range(BALANCING_PASSES):
        column_part = jnp.dot(row_scale, teach_exp, precision=lax.Precision.HIGHEST)
        column_scale = 1.0 / lax.psum(column_part, "dp")
        row_part = jnp.dot(teach_exp, column_scale, precision=lax.Precision.HIGHEST)
        row_scale = live_rows / lax.psum(row_part, "proto")
    target = teach_exp * row_scale[:, None] * column_scale[None, :]
    log_prob = student_logits - (student_peak + jnp.log(student_total))[:, None]
    loss_part = -jnp.sum(weight_rows * jnp.sum(target * log_prob, axis=1)) / all_images
    loss_value = lax.psum(loss_part, ("dp", "proto"))
    grad_coef = weight_rows * (LOSS_SCALE / (all_images * student_temp))
    grad_logits = (grad_coef[:, None] * (jnp.exp(log_prob) - target)).astype(jnp.bfloat16)
    row_grads = lax.psum(
        jnp.dot(grad_logits, prototypes, preferred_element_type=jnp.float32), "proto"
    )
    student_grad = row_grads.reshape(images, patches, feat_width)
    proto_grad = lax.psum_scatter(
        jnp.dot(grad_logits.T, student_rows, preferred_element_type=jnp.float32),
        "dp",
        scatter_dimension=0,
        tiled=True,
    )
    return (loss_value, student_grad, proto_grad[None])


def solution(mesh):
    return jax.shard_map(
        local,
        mesh=mesh,
        in_specs=(P("dp", None, None), P("dp", None, None), P("proto", None), P("dp", None)),
        out_specs=(P(), P("dp", None, None), P("proto", "dp", None)),
        check_vma=False,
    )
```

profile of v0, /device:TPU:1, one launch (start us, length us, event | category | flops | bytes accessed | tf_op | source)
XLA Modules:
  0.0 1029.8 jit_solution(9785363351665570312)
XLA Ops:
  8.0 0.0 copy-start
  8.0 0.0 all-reduce.4.cloned.1.call-start
  8.1 1.4 fusion.12
  10.1 0.0 copy-start.2
  10.1 0.8 broadcast_divide_fusion.3
  11.0 7.0 fusion.14
  17.9 4.5 fusion.13
  22.4 9.5 all-reduce.1
  32.0 8.6 fusion.4
  40.6 248.6 %psum.63 = f32[8192]{0:T(1024)S(1)} all-reduce(f32[8192]{0:T(1024)S(1)} %bitcast.46), channel_id=1, replica_groups=mesh['dp'=64,'proto'=4] {'dp'}, use_global_device_ids=true, to_apply=%region_3.0 | all-reduce | flops 8192 | bytes 65536 | tf_op jit(solution)/shard_map/psum | solution.py:41
  289.2 9.4 fusion.11
  298.6 6.2 psum.64
  304.8 8.2 fusion.10
  313.0 247.9 %psum.65 = f32[8192]{0:T(1024)S(1)} all-reduce(f32[8192]{0:T(1024)S(1)} %bitcast.43), channel_id=1, replica_groups=mesh['dp'=64,'proto'=4] {'dp'}, use_global_device_ids=true, to_apply=%region_5.0 | all-reduce | flops 8192 | bytes 65536 | tf_op jit(solution)/shard_map/psum | solution.py:41
  560.9 9.4 fusion.9
  570.3 7.9 psum.66
  578.2 8.2 fusion.8
  586.4 248.2 %psum.67 = f32[8192]{0:T(1024)S(1)} all-reduce(f32[8192]{0:T(1024)S(1)} %bitcast.45), channel_id=1, replica_groups=mesh['dp'=64,'proto'=4] {'dp'}, use_global_device_ids=true, to_apply=%region_7.0 | all-reduce | flops 8192 | bytes 65536 | tf_op jit(solution)/shard_map/psum | solution.py:41
  834.6 9.4 fusion.7
  843.9 4.7 exponential_reduce_fusion
  848.6 6.3 all-reduce
  854.9 8.1 multiply_convert_fusion
  863.0 2.0 copy-done.1
  865.0 1.9 convolution_bitcast_fusion
  866.9 0.0 all-reduce.4.cloned.1.call-update
  866.9 0.0 reduce-scatter.2.cloned.1.call-start
  867.0 6.7 fusion
  873.7 0.0 reduce-scatter.2.cloned.1.call-update
  873.8 0.6 multiply_reduce_fusion.1
  875.0 79.9 %psum.70 = f32[]{:T(128)} all-reduce(f32[]{:T(128)S(6)} %div.53), channel_id=1, replica_groups=mesh['dp'=64,'proto'=4] {'dp','proto'}, use_global_device_ids=true, to_apply=%region_15.0 | all-reduce | flops 1 | bytes 8 | tf_op jit(solution)/shard_map/psum | solution.py:47
  954.9 65.8 %reduce-scatter.2.cloned.1.call-done = f32[128,256]{1,0:T(8,128)} async-done(((f32[8192,256]{1,0:T(8,128)}), f32[128,256]{1,0:T(8,128)}) %reduce-scatter.2.cloned.1.call-update) | async-done | bytes 131088 | tf_op jit(solution)/shard_map/reduce_scatter | solution.py:54
  1020.7 1.7 copy.8
  (16 shorter events, 0.1 us)
Async XLA Ops:
  8.0 9.9 copy-start
  8.0 946.9 %all-reduce.4.cloned.1.call-start = ((), (), s32[]{:S(2)}) async-start(), calls=%async_computation.1 | async-start | bytes 524288 | tf_op jit(solution)/shard_map/psum | solution.py:50
  10.1 7.8 copy-start.2
  17.9 14.1 %copy-start.4 = (s32[1,256]{1,0:T(1,128)S(1)}, s32[1,256]{1,0:T(1,128)}, u32[]{:S(2)}) copy-start(s32[1,256]{1,0:T(1,128)} %param.7) | copy-start | bytes 3076
  854.9 10.1 copy-start.3
  863.0 2.0 copy-start.1
  866.9 153.8 %reduce-scatter.2.cloned.1.call-start = ((), (), s32[]{:S(2)}) async-start(), calls=%async_computation.2 | async-start | bytes 8519680 | tf_op jit(solution)/shard_map/reduce_scatter | solution.py:54
Sparse Core Ops, SparseCore 0:
  867.1 45.4 all-reduce.3
Sparse Core Ops, SparseCore 1:
  873.8 146.8 reduce-scatter.1
where the time goes:
time: 1030 us
  blocking collectives  854 us (83%)
  matrix products  73.3 us (7%)
  waiting for transfers between devices  65.8 us (6%)
  between operations  16.8 us (2%)
  other arithmetic  15.6 us (2%)
    psum x3, blocking collectives, local(): column_scale = 1.0 / lax.psum(column_part, 'dp')  745 us
    psum x1, blocking collectives, local(): loss_value = lax.psum(loss_part, ('dp', 'proto'))  79.9 us
    reduce_scatter x1, waiting for transfers between devices, local(): lax.psum_scatter(jnp.dot(grad_logits.T, student_rows, preferred_element_t...  65.8 us
    dot_general x3, matrix products, local(): row_part = jnp.dot(teach_exp, column_scale, precision=lax.Precision.HIGHEST)  28.1 us
    dot_general x3, matrix products, local(): column_part = jnp.dot(row_scale, teach_exp, precision=lax.Precision.HIGHEST)  25 us
  transfers between devices with their start and end apart: 2, of which 1 were waited for; matrix products, arithmetic and copies ran while one was open for 1% of the time, Pallas kernels for 0%

commit v1 on v0

v1 whole, which is shorter than its diff:
```python
import functools

import jax
import jax.numpy as jnp
from jax import lax
from jax.experimental import pallas as pl
from jax.experimental.pallas import tpu as pltpu
from jax.sharding import Mesh, PartitionSpec as P

BALANCING_PASSES = 3
LOSS_SCALE = 16384
TEACHER_INV = 1.0 / 0.07
STUDENT_INV = 1.0 / 0.1
IMAGES = 64
LIVE = 128
NT = (((1,), (1,)), ((), ()))
NN = (((1,), (0,)), ((), ()))
TN = (((0,), (0,)), ((), ()))
f32 = jnp.float32
bf16 = jnp.bfloat16


def dot(a, b, dims):
    return lax.dot_general(a, b, dims, preferred_element_type=f32)


def to_lanes(v):
    return jnp.concatenate([v[i : i + 1, :] for i in range(8)], axis=1)


def to_tile(v):
    return jnp.concatenate([v[:, 128 * i : 128 * (i + 1)] for i in range(8)], axis=0)


def split3(v):
    hi = v.astype(bf16).astype(f32)
    mid = (v - hi).astype(bf16).astype(f32)
    lo = (v - hi - mid).astype(bf16).astype(f32)
    return jnp.concatenate([hi, mid, lo, jnp.zeros((13, v.shape[1]), f32)], axis=0).astype(bf16)


def selection(mask):
    patches = mask.shape[1]
    maskf = mask.astype(f32)
    before = lax.broadcasted_iota(jnp.int32, (patches, patches), 0)
    after = lax.broadcasted_iota(jnp.int32, (patches, patches), 1)
    tri = jnp.where(before <= after, 1.0, 0.0).astype(bf16)
    rank = dot(jnp.broadcast_to(maskf, (16, patches)).astype(bf16), tri, NN)[0:1, :]
    slot = lax.broadcasted_iota(jnp.int32, (LIVE, patches), 0).astype(f32)
    hit = jnp.where(rank - 1.0 == slot, 1.0, 0.0) * maskf
    return hit


def pack_kernel(mask_ref, teach_ref, student_ref, out_ref):
    pick = selection(mask_ref[...]).astype(bf16)
    out_ref[0] = dot(pick, teach_ref[...], NN).astype(bf16)
    out_ref[1] = dot(pick, student_ref[...], NN).astype(bf16)


def peak_kernel(mask_ref, rows_ref, proto_ref, out_ref, peak_ref):
    step = pl.program_id(0)
    logits = dot(proto_ref[...], rows_ref[0], NT)
    top = jnp.max(logits, axis=0, keepdims=True)

    @pl.when(step == 0)
    def _():
        peak_ref[...] = top

    @pl.when(step > 0)
    def _():
        peak_ref[...] = jnp.maximum(peak_ref[...], top)

    @pl.when(step == pl.num_programs(0) - 1)
    def _():
        count = jnp.sum(mask_ref[...].astype(f32), axis=1, keepdims=True)
        tile = jnp.concatenate(
            [peak_ref[...] * TEACHER_INV, jnp.broadcast_to(count, (1, LIVE)), jnp.zeros((6, LIVE), f32)], axis=0
        )
        out_ref[...] = jnp.broadcast_to(tile[None], out_ref.shape)


def expo_kernel(me_ref, recv_ref, a_ref, b_ref, c_ref, d_ref, proto_ref, et_ref, srows_ref, stat_ref, pay_ref, trows):
    for k, piece in enumerate((a_ref, b_ref, c_ref, d_ref)):
        start = pl.multiple_of(((me_ref[0] - k) & 3) * 256, 256)
        for core in range(2):
            trows[pl.ds(start + core * 128, 128), :] = piece[core, 0]
            srows_ref[pl.ds(start + core * 128, 128), :] = piece[core, 1]
    peaks, counts = [], []
    for x in range(4):
        for core in range(2):
            at = [(x * 4 + y) * 2 + core for y in range(4)]
            top = recv_ref[at[0], 0:1, :]
            for i in at[1:]:
                top = jnp.maximum(top, recv_ref[i, 0:1, :])
            peaks.append(top)
            counts.append(recv_ref[at[0], 1:2, :])
    peak = jnp.concatenate(peaks, axis=1)
    count = jnp.concatenate(counts, axis=0)
    slot = lax.broadcasted_iota(jnp.int32, (8, 128), 1).astype(f32)
    live = jnp.where(slot < count, 1.0, 0.0)
    stat_ref[0] = live
    stat_ref[1] = live / count
    live_rows = jnp.broadcast_to(to_lanes(live), (16, 1024)).astype(bf16)
    sums = []
    for j in range(8):
        logits = dot(proto_ref[128 * j : 128 * (j + 1), :], trows[...], NT)
        block = jnp.exp(logits * TEACHER_INV - peak).astype(bf16)
        et_ref[128 * j : 128 * (j + 1), :] = block
        sums.append(dot(live_rows, block, NT)[0:1, :])
    tile = jnp.concatenate(sums, axis=0)
    pay_ref[...] = jnp.broadcast_to(tile[None], pay_ref.shape)


def col_kernel(recv_ref, et_ref, *refs):
    extra, (pay_ref, col_ref) = refs[:-2], refs[-2:]
    col = 1.0 / jnp.sum(recv_ref[...], axis=0)
    col_ref[...] = col
    lhs = split3(to_lanes(col))
    out = jnp.sum(dot(lhs, et_ref[...], NN), axis=0, keepdims=True)
    pay_ref[:, 0:8, :] = jnp.broadcast_to(to_tile(out)[None], (pay_ref.shape[0], 8, 128))
    for ref in extra:
        pay_ref[:, 8:, :] = jnp.broadcast_to(ref[...][None], (pay_ref.shape[0],) + ref.shape)


def last_col_kernel(recv_ref, et_ref, w_ref, pay_ref, col_ref):
    col = 1.0 / jnp.sum(recv_ref[...], axis=0)
    col_ref[...] = col
    lhs = split3(to_lanes(col))
    out = jnp.sum(dot(lhs, et_ref[...], NN), axis=0, keepdims=True)
    pay_ref[:, 0:8, :] = jnp.broadcast_to(to_tile(out)[None], (pay_ref.shape[0], 8, 128))
    out = jnp.sum(dot(lhs, w_ref[...], NN), axis=0, keepdims=True)
    pay_ref[:, 8:16, :] = jnp.broadcast_to(to_tile(out)[None], (pay_ref.shape[0], 8, 128))


def row_kernel(recv_ref, stat_ref, et_ref, pay_ref):
    row = stat_ref[0] / jnp.sum(recv_ref[:, 0:8, :], axis=0)
    lhs = split3(to_lanes(row))
    out = jnp.sum(dot(lhs, et_ref[...], NT), axis=0, keepdims=True)
    pay_ref[...] = jnp.broadcast_to(to_tile(out)[None], pay_ref.shape)


def student_sum_kernel(srows_ref, proto_ref, out_ref, logit_ref):
    top = None
    for j in range(8):
        logits = dot(proto_ref[128 * j : 128 * (j + 1), :], srows_ref[...], NT) * STUDENT_INV
        logit_ref[128 * j : 128 * (j + 1), :] = logits
        now = jnp.max(logits, axis=0, keepdims=True)
        top = now if top is None else jnp.maximum(top, now)
    total = jnp.zeros((1, 1024), f32)
    for j in range(8):
        total += jnp.sum(jnp.exp(logit_ref[128 * j : 128 * (j + 1), :] - top), axis=0, keepdims=True)
    out_ref[0:8, :] = to_tile(top)
    out_ref[8:16, :] = to_tile(total)


def student_prob_kernel(recv_ref, srows_ref, proto_ref, et_ref, prob_ref, w_ref):
    tops = recv_ref[:, 8:16, :]
    top = jnp.max(tops, axis=0)
    total = jnp.sum(recv_ref[:, 16:24, :] * jnp.exp(tops - top[None]), axis=0)
    norm = to_lanes(top + jnp.log(total))
    for j in range(8):
        at = slice(128 * j, 128 * (j + 1))
        log_prob = dot(proto_ref[at, :], srows_ref[...], NT) * STUDENT_INV - norm
        prob_ref[at, :] = jnp.exp(log_prob)
        w_ref[at, :] = (et_ref[at, :].astype(f32) * log_prob).astype(bf16)


def grad_kernel(recv_ref, stat_ref, col_ref, et_ref, prob_ref, srows_ref, proto_ref, pout_ref, sout_ref, grad_ref):
    sums = jnp.sum(recv_ref[...], axis=0)
    row = stat_ref[0] / sums[0:8]
    weight = stat_ref[1]
    loss = -jnp.sum(jnp.sum(weight * row * sums[8:16], axis=1, keepdims=True), axis=0, keepdims=True) / IMAGES
    hi = loss.astype(bf16).astype(f32)
    mid = (loss - hi).astype(bf16).astype(f32)
    lo = loss - hi - mid
    which = lax.broadcasted_iota(jnp.int32, (16, 256), 0)
    tail = jnp.where(which == 0, hi, jnp.where(which == 1, mid, jnp.where(which == 2, lo, 0.0))).astype(bf16)
    coef = weight * (LOSS_SCALE / (IMAGES * 0.1))
    coef_rows = to_lanes(coef)
    scale_rows = to_lanes(coef * row)
    for j in range(8):
        at = slice(128 * j, 128 * (j + 1))
        col = jnp.broadcast_to(col_ref[j : j + 1, :], (128, 128)).T
        col = jnp.concatenate([col] * 8, axis=1)
        grad = (prob_ref[at, :] * coef_rows - et_ref[at, :].astype(f32) * col * scale_rows).astype(bf16)
        grad_ref[at, :] = grad
        pout_ref[j, 0:128, :] = dot(grad, srows_ref[...], NN).astype(bf16)
        pout_ref[j, 128:144, :] = tail
    for i in range(8):
        sout_ref[i] = dot(grad_ref[:, 128 * i : 128 * (i + 1)], proto_ref[...], TN).astype(bf16)


def add_kernel(recv_ref, out_ref):
    out_ref[...] = jnp.sum(recv_ref[...].astype(f32), axis=0)


def end_kernel(mask_ref, recv_ref, a_ref, b_ref, c_ref, d_ref, student_ref, proto_ref, loss_ref):
    pick = selection(mask_ref[...]).astype(bf16)
    rows = (a_ref[...] + c_ref[...]) + (b_ref[...] + d_ref[...])
    hi = rows.astype(bf16)
    rest = rows - hi.astype(f32)
    mid = rest.astype(bf16)
    lo = (rest - mid.astype(f32)).astype(bf16)
    student_ref[...] = dot(pick, hi, TN) + dot(pick, mid, TN) + dot(pick, lo, TN)
    total = jnp.sum(recv_ref[...].astype(f32), axis=0)
    proto_ref[...] = total[0:128, :]
    loss_ref[...] = total[128:129, 0:128] + total[129:130, 0:128] + total[130:131, 0:128]


VM = pl.BlockSpec(memory_space=pltpu.VMEM)


def call(kernel, out, *args, scratch=(), limit=32, cost=None):
    out = [jax.ShapeDtypeStruct(s, d) for s, d in out]
    return pl.pallas_call(
        kernel,
        out_shape=out,
        in_specs=[VM] * len(args),
        out_specs=[VM] * len(out),
        scratch_shapes=list(scratch),
        compiler_params=pltpu.CompilerParams(vmem_limit_bytes=limit << 20),
        cost_estimate=cost and pl.CostEstimate(flops=cost, bytes_accessed=1 << 20, transcendentals=1 << 20),
    )(*args)


def a2a(v, axes):
    return lax.all_to_all(v, axes, 0, 0, tiled=True)


def shift(v, axis, n, k):
    return lax.ppermute(v, axis, [(i, (i + k) % n) for i in range(n)])


PLANE = ("x", "y", "c")


def local(teacher_feats, student_feats, prototypes, patch_mask):
    x, c = lax.axis_index("x"), lax.axis_index("c")
    (own,) = call(pack_kernel, [((2, LIVE, 256), bf16)], patch_mask, teacher_feats[0], student_feats[0])
    mine = lax.dynamic_index_in_dim(prototypes.reshape(8, 8, 128, 256), x * 2 + c, 1, keepdims=False)
    mine = mine.reshape(1024, 256)

    other = shift(own, "c", 2, 1)
    pair = jnp.where(c == 0, jnp.stack([own, other]), jnp.stack([other, own]))
    parts = [pair] + [shift(pair, "x", 4, k) for k in (1, 2, 3)]

    peak_pay = pl.pallas_call(
        peak_kernel,
        grid=(8,),
        out_shape=jax.ShapeDtypeStruct((32, 8, 128), f32),
        in_specs=[
            pl.BlockSpec((1, 256), lambda i: (0, 0)),
            pl.BlockSpec((1, LIVE, 256), lambda i: (0, 0, 0)),
            pl.BlockSpec((1024, 256), lambda i: (i, 0)),
        ],
        out_specs=pl.BlockSpec((32, 8, 128), lambda i: (0, 0, 0)),
        scratch_shapes=[pltpu.VMEM((1, LIVE), f32)],
        compiler_params=pltpu.CompilerParams(vmem_limit_bytes=16 << 20),
    )(patch_mask, own, prototypes)
    peak_recv = a2a(peak_pay, PLANE)

    et, srows, stat, pay = pl.pallas_call(
        expo_kernel,
        out_shape=[
            jax.ShapeDtypeStruct((1024, 1024), bf16),
            jax.ShapeDtypeStruct((1024, 256), bf16),
            jax.ShapeDtypeStruct((2, 8, 128), f32),
            jax.ShapeDtypeStruct((8, 8, 128), f32),
        ],
        in_specs=[pl.BlockSpec(memory_space=pltpu.SMEM)] + [VM] * 6,
        out_specs=[VM] * 4,
        scratch_shapes=[pltpu.VMEM((1024, 256), bf16)],
        compiler_params=pltpu.CompilerParams(vmem_limit_bytes=32 << 20),
    )(x.astype(jnp.int32)[None], peak_recv, *parts, mine)

    (student_sum,) = call(
        student_sum_kernel, [((16, 128), f32)], srows, mine,
        scratch=[pltpu.VMEM((1024, 1024), f32)], cost=1 << 29,
    )

    recv = a2a(pay, "z")
    pay, _ = call(col_kernel, [((32, 24, 128), f32), ((8, 128), f32)], recv, et, student_sum)
    recv = a2a(pay, PLANE)
    prob, w = call(
        student_prob_kernel, [((1024, 1024), f32), ((1024, 1024), bf16)], recv, srows, mine, et, cost=1 << 29
    )
    (pay,) = call(row_kernel, [((8, 8, 128), f32)], recv, stat, et)
    for _ in range(BALANCING_PASSES - 2):
        recv = a2a(pay, "z")
        pay, _ = call(col_kernel, [((32, 8, 128), f32), ((8, 128), f32)], recv, et)
        recv = a2a(pay, PLANE)
        (pay,) = call(row_kernel, [((8, 8, 128), f32)], recv, stat, et)
    recv = a2a(pay, "z")
    pay, col = call(last_col_kernel, [((32, 16, 128), f32), ((8, 128), f32)], recv, et, w)
    recv = a2a(pay, PLANE)

    proto_part, student_part = call(
        grad_kernel, [((8, 144, 256), bf16), ((8, 128, 256), bf16)], recv, stat, col, et, prob, srows, mine,
        scratch=[pltpu.VMEM((1024, 1024), bf16)],
    )
    (student_rows,) = call(add_kernel, [((128, 256), f32)], a2a(student_part, ("x", "c")))
    student_rows = [student_rows] + [shift(student_rows, "y", 4, k) for k in (1, 2, 3)]
    proto_recv = a2a(proto_part, "z")
    student, proto, loss = call(
        end_kernel, [((256, 256), f32), ((128, 256), f32), ((1, 128), f32)], patch_mask, proto_recv, *student_rows
    )
    return loss[0, 0], student[None], proto[None]


def solution(mesh):
    fine = Mesh(mesh.devices.reshape(8, 4, 2, 4), ("z", "x", "c", "y"))
    dp = ("z", "x", "c")
    return jax.shard_map(
        local,
        mesh=fine,
        in_specs=(P(dp, None, None), P(dp, None, None), P("y", None), P(dp, None)),
        out_specs=(P(), P(dp, None, None), P("y", dp, None)),
        check_vma=False,
    )
```

time: 1030 us -> 161 us (0.16)
  blocking collectives: 854 us -> 62.5 us
  matrix products: 73.3 us -> 0 us
  waiting for transfers between devices: 65.8 us -> 31 us
  starting transfers between devices: 0.08 us -> 30.9 us
  Pallas kernels: 0 us -> 17.6 us
  between operations: 16.8 us -> 0.78 us
  other arithmetic: 15.6 us -> 0.03 us
  local copies, waits for them, and re-layouts: 3.66 us -> 17.8 us
    psum x7 -> x0, blocking collectives: 845 us -> none  [the longest x3 745 us: local(): column_scale = 1.0 / lax.psum(column_part, 'dp')]
    dot_general x10 -> x0, matrix products: 73.3 us -> none  [the longest x3 28.1 us: local(): row_part = jnp.dot(teach_exp, column_scale, precision=lax.Precision.HIGHEST)]
    reduce_scatter x1 -> x0, waiting for transfers between devices: 65.8 us -> none  [local(): lax.psum_scatter(jnp.dot(grad_logits.T, student_rows, preferred_element_t...]
    all_to_all x0 -> x5, blocking collectives: none -> 62.5 us  [a2a(): return lax.all_to_all(v, axes, 0, 0, tiled=True)]
    all_to_all x0 -> x4, starting transfers between devices: none -> 23.5 us  [a2a(): return lax.all_to_all(v, axes, 0, 0, tiled=True)]
    all_to_all x0 -> x4, waiting for transfers between devices: none -> 22.4 us  [a2a(): return lax.all_to_all(v, axes, 0, 0, tiled=True)]
    pallas_call x0 -> x13, Pallas kernels: none -> 17.6 us  [the longest x11 11.9 us: call(): pl.pallas_call(kernel, out_shape=out, in_specs=[VM] * len(args), out_spec...]
    unnamed x11 -> x38, local copies, waits for them, and re-layouts: 3.66 us -> 16.7 us
  transfers between devices with their start and end apart: 2 -> 11, of which waited for: 1 -> 8; matrix products, arithmetic and copies ran while one was open for 1% -> 1% of each run, Pallas kernels for 0% -> 4%
where the time goes in v1:
time: 161 us; the launch traced here: 160 us
  blocking collectives  62.5 us (39%)
  waiting for transfers between devices  31 us (19%)
  starting transfers between devices  30.9 us (19%)
  local copies, waits for them, and re-layouts  17.8 us (11%)
  Pallas kernels  17.6 us (11%)
    all_to_all x5, blocking collectives, a2a(): return lax.all_to_all(v, axes, 0, 0, tiled=True)  62.5 us
    all_to_all x4, starting transfers between devices, a2a(): return lax.all_to_all(v, axes, 0, 0, tiled=True)  23.5 us
    all_to_all x4, waiting for transfers between devices, a2a(): return lax.all_to_all(v, axes, 0, 0, tiled=True)  22.4 us
    unnamed x38, local copies, waits for them, and re-layouts  16.7 us
    pallas_call x11, Pallas kernels, call(): pl.pallas_call(kernel, out_shape=out, in_specs=[VM] * len(args), out_spec...  11.9 us
    ppermute x7, waiting for transfers between devices, shift(): return lax.ppermute(v, axis, [(i, (i + k) % n) for i in range(n)])  8.59 us
    ppermute x7, starting transfers between devices, shift(): return lax.ppermute(v, axis, [(i, (i + k) % n) for i in range(n)])  7.32 us
    pallas_call x1, Pallas kernels, local(): pl.pallas_call(peak_kernel, grid=(8,), out_shape=jax.ShapeDtypeStruct((32...  3.3 us
  transfers between devices with their start and end apart: 11, of which 8 were waited for; matrix products, arithmetic and copies ran while one was open for 1% of the time, Pallas kernels for 4%

profile of v1, /device:TPU:1, one launch (start us, length us, event | category | flops | bytes accessed | tf_op | source)
XLA Modules:
  0.0 160.4 jit_solution(8511098433877126945)
XLA Ops:
  3.5 3.3 %collective-permute-start = (bf16[2,128,256]{2,1,0:T(8,128)(2,1)S(1)}, bf16[2,128,256]{2,1,0:T(8,128)(2,1)S(1)}, u32[]{:S(2)}, u32[]{:S(2)}) collective-permute-start(bf16[2,128,256]{2,1,0:T(8,128)(2,1)S(1)} %shard_map.67.rows_ref), channel_id=1, source_target_pairs={{0,4},{4,0},{1,5},{5,1},{2,6},{6,2},{3,7},{7,3},{8,12},{12,8},{9,1... | collective-permute-start | bytes 393224 | tf_op jit(solution)/shard_map/ppermute | solution.py:231
  6.8 1.0 collective-permute-done
  9.7 2.2 %copy-done = bf16[8192,256]{1,0:T(8,128)(2,1)S(1)} copy-done((bf16[8192,256]{1,0:T(8,128)(2,1)S(1)}, bf16[8192,256]{1,0:T(8,128)(2,1)}, u32[]{:S(2)}) %copy-start) | copy-done | bytes 4194328
  12.6 3.3 %shard_map.68 = f32[32,8,128]{2,1,0:T(8,128)} custom-call(s32[1,256]{1,0:T(1,128)S(1)} %copy-done.17, bf16[2,128,256]{2,1,0:T(8,128)(2,1)S(1)} %shard_map.67.rows_ref, bf16[8192,256]{1,0:T(8,128)(2,1)S(1)} %copy-done), custom_call_target="tpu_custom_call" | custom-call | tf_op jit(solution)/shard_map/pallas_call | solution.py:247
  15.9 7.6 %all-to-all-start = ((f32[32,8,128]{2,1,0:T(8,128)}), f32[32,8,128]{2,1,0:T(8,128)S(1)}, u32[]{:S(2)}, u32[]{:S(2)}) async-start(f32[32,8,128]{2,1,0:T(8,128)} %shard_map.68), calls=%async_computation | async-start | bytes 262144 | tf_op jit(solution)/shard_map/all_to_all | solution.py:227
  23.5 1.1 constant_dynamic-slice_fusion
  24.6 6.6 %all-to-all-done.recv_ref = f32[32,8,128]{2,1,0:T(8,128)S(1)} async-done(((f32[32,8,128]{2,1,0:T(8,128)}), f32[32,8,128]{2,1,0:T(8,128)S(1)}, u32[]{:S(2)}, u32[]{:S(2)}) %all-to-all-start) | async-done | bytes 131104 | tf_op jit(solution)/shard_map/all_to_all | solution.py:227
  36.2 2.4 %shard_map.69 = (bf16[1024,1024]{1,0:T(8,128)(2,1)S(1)}, bf16[1024,256]{1,0:T(8,128)(2,1)S(1)}, f32[2,8,128]{2,1,0:T(8,128)S(1)}, f32[8,8,128]{2,1,0:T(8,128)S(1)}) custom-call(s32[1]{0:T(128)} %bitcast.me_ref, f32[32,8,128]{2,1,0:T(8,128)S(1)} %all-to-all-done.recv_ref, bf16[2,2,128,256]{3,2,1,0:T(8,128)(2,1)S(1)} %maximum_select_fusion.a_ref, ...), custom_call_target="tpu_custom_call" | custom-call | tf_op jit(solution)/shard_map/pallas_call | solution.py:262
  39.2 8.2 %all-to-all-start.1 = ((f32[8,8,128]{2,1,0:T(8,128)}), f32[8,8,128]{2,1,0:T(8,128)S(1)}, u32[]{:S(2)}, u32[]{:S(2)}) async-start(f32[8,8,128]{2,1,0:T(8,128)} %copy-done.15), calls=%async_computation.1 | async-start | bytes 65536 | tf_op jit(solution)/shard_map/all_to_all | solution.py:227
  47.4 2.2 %shard_map.70.refs_0_ = f32[16,128]{1,0:T(8,128)S(1)} custom-call(bf16[1024,256]{1,0:T(8,128)(2,1)S(1)} %get-tuple-element.20.srows_ref, bf16[1024,256]{1,0:T(8,128)(2,1)S(1)} %bitcast.14), custom_call_target="tpu_custom_call" | custom-call | flops 536870912 | bytes 1048576 | tf_op jit(solution)/shard_map/pallas_call | solution.py:215
  49.7 4.8 %all-to-all-done.1.recv_ref = f32[8,8,128]{2,1,0:T(8,128)S(1)} async-done(((f32[8,8,128]{2,1,0:T(8,128)}), f32[8,8,128]{2,1,0:T(8,128)S(1)}, u32[]{:S(2)}, u32[]{:S(2)}) %all-to-all-start.1) | async-done | bytes 32800 | tf_op jit(solution)/shard_map/all_to_all | solution.py:227
  55.3 15.2 %all_to_all.45.recv_ref = f32[32,24,128]{2,1,0:T(8,128)S(1)} all-to-all(f32[32,24,128]{2,1,0:T(8,128)S(1)} %get-tuple-element.21), channel_id=1, replica_groups=mesh['z'=8,'x'=4,'c'=2,'y'=4] {'x','y','c'}, dimensions={0} | all-to-all | bytes 786432 | tf_op jit(solution)/shard_map/all_to_all | solution.py:227
  71.1 9.3 %all_to_all.46.recv_ref = f32[8,8,128]{2,1,0:T(8,128)S(1)} all-to-all(f32[8,8,128]{2,1,0:T(8,128)S(1)} %shard_map.72), channel_id=1, replica_groups=mesh['z'=8,'x'=4,'c'=2,'y'=4] {'z'}, dimensions={0} | all-to-all | bytes 65536 | tf_op jit(solution)/shard_map/all_to_all | solution.py:227
  81.2 12.2 %all_to_all.47.recv_ref = f32[32,8,128]{2,1,0:T(8,128)S(1)} all-to-all(f32[32,8,128]{2,1,0:T(8,128)S(1)} %get-tuple-element.23), channel_id=1, replica_groups=mesh['z'=8,'x'=4,'c'=2,'y'=4] {'x','y','c'}, dimensions={0} | all-to-all | bytes 262144 | tf_op jit(solution)/shard_map/all_to_all | solution.py:227
  94.7 4.0 %all-to-all-start.5 = ((f32[8,8,128]{2,1,0:T(8,128)}), f32[8,8,128]{2,1,0:T(8,128)}, u32[]{:S(2)}, u32[]{:S(2)}) async-start(f32[8,8,128]{2,1,0:T(8,128)} %copy-done.12), calls=%async_computation.5 | async-start | bytes 65536 | tf_op jit(solution)/shard_map/all_to_all | solution.py:227
  98.7 1.6 shard_map.75
  100.3 2.0 %copy-done.1 = f32[1024,1024]{1,0:T(8,128)} copy-done((f32[1024,1024]{1,0:T(8,128)}, f32[1024,1024]{1,0:T(8,128)S(1)}, u32[]{:S(2)}) %copy-start.1) | copy-done | bytes 4194328
  102.3 1.4 copy-done.3
  103.6 1.9 %all-to-all-done.5.recv_ref = f32[8,8,128]{2,1,0:T(8,128)} async-done(((f32[8,8,128]{2,1,0:T(8,128)}), f32[8,8,128]{2,1,0:T(8,128)}, u32[]{:S(2)}, u32[]{:S(2)}) %all-to-all-start.5) | async-done | bytes 32800 | tf_op jit(solution)/shard_map/all_to_all | solution.py:227
  105.5 1.7 %copy-done.4 = bf16[1024,1024]{1,0:T(8,128)(2,1)S(1)} copy-done((bf16[1024,1024]{1,0:T(8,128)(2,1)S(1)}, bf16[1024,1024]{1,0:T(8,128)(2,1)}, u32[]{:S(2)}) %copy-start.4) | copy-done | bytes 2097176
  107.3 1.6 shard_map.76
  108.9 13.9 %all_to_all.48.recv_ref = f32[32,16,128]{2,1,0:T(8,128)S(1)} all-to-all(f32[32,16,128]{2,1,0:T(8,128)S(1)} %get-tuple-element.25), channel_id=1, replica_groups=mesh['z'=8,'x'=4,'c'=2,'y'=4] {'x','y','c'}, dimensions={0} | all-to-all | bytes 524288 | tf_op jit(solution)/shard_map/all_to_all | solution.py:227
  122.8 1.8 %shard_map.77 = (bf16[8,144,256]{2,1,0:T(8,128)(2,1)S(1)}, bf16[8,128,256]{2,1,0:T(8,128)(2,1)S(1)}) custom-call(f32[32,16,128]{2,1,0:T(8,128)S(1)} %all_to_all.48.recv_ref, f32[2,8,128]{2,1,0:T(8,128)S(1)} %get-tuple-element.22.stat_ref, f32[8,128]{1,0:T(8,128)S(1)} %get-tuple-element.26.col_ref, bf16[1024,1024]{1,0:T(8,128)(2,1)S(1)} %get-tuple-element.19.et_ref, ...), custom_call_target="tpu_custom_call" | custom-call | tf_op jit(solution)/shard_map/pallas_call | solution.py:215
  124.6 12.0 %all_to_all.49.recv_ref = bf16[8,128,256]{2,1,0:T(8,128)(2,1)S(1)} all-to-all(bf16[8,128,256]{2,1,0:T(8,128)(2,1)S(1)} %get-tuple-element.29), channel_id=1, replica_groups=mesh['z'=8,'x'=4,'c'=2,'y'=4] {'x','c'}, dimensions={0} | all-to-all | bytes 1048576 | tf_op jit(solution)/shard_map/all_to_all | solution.py:227
  136.6 3.8 %all-to-all-start.7 = ((bf16[8,144,256]{2,1,0:T(8,128)(2,1)}), bf16[8,144,256]{2,1,0:T(8,128)(2,1)S(1)}, u32[]{:S(2)}, u32[]{:S(2)}) async-start(bf16[8,144,256]{2,1,0:T(8,128)(2,1)} %copy-done.5), calls=%async_computation.7 | async-start | bytes 1179648 | tf_op jit(solution)/shard_map/all_to_all | solution.py:227
  140.4 1.1 collective-permute-start.6
  141.5 1.0 collective-permute-start.5
  142.5 1.9 %collective-permute-done.6.d_ref = f32[128,256]{1,0:T(8,128)S(1)} collective-permute-done((f32[128,256]{1,0:T(8,128)S(1)}, f32[128,256]{1,0:T(8,128)S(1)}, u32[]{:S(2)}, u32[]{:S(2)}) %collective-permute-start.6) | collective-permute-done | bytes 131104 | tf_op jit(solution)/shard_map/ppermute | solution.py:231
  144.3 2.6 %collective-permute-done.5.c_ref = f32[128,256]{1,0:T(8,128)S(1)} collective-permute-done((f32[128,256]{1,0:T(8,128)S(1)}, f32[128,256]{1,0:T(8,128)S(1)}, u32[]{:S(2)}, u32[]{:S(2)}) %collective-permute-start.5) | collective-permute-done | bytes 131104 | tf_op jit(solution)/shard_map/ppermute | solution.py:231
  146.9 3.2 %collective-permute-done.4.b_ref = f32[128,256]{1,0:T(8,128)S(1)} collective-permute-done((f32[128,256]{1,0:T(8,128)S(1)}, f32[128,256]{1,0:T(8,128)S(1)}, u32[]{:S(2)}, u32[]{:S(2)}) %collective-permute-start.4) | collective-permute-done | bytes 131104 | tf_op jit(solution)/shard_map/ppermute | solution.py:231
  150.1 9.1 %all-to-all-done.7.recv_ref = bf16[8,144,256]{2,1,0:T(8,128)(2,1)S(1)} async-done(((bf16[8,144,256]{2,1,0:T(8,128)(2,1)}), bf16[8,144,256]{2,1,0:T(8,128)(2,1)S(1)}, u32[]{:S(2)}, u32[]{:S(2)}) %all-to-all-start.7) | async-done | bytes 589856 | tf_op jit(solution)/shard_map/all_to_all | solution.py:227
  159.2 1.2 shard_map.79
  (48 shorter events, 14.8 us)
Async XLA Ops:
  0.6 0.9 copy-start.13
  1.5 0.9 copy-start.14
  2.4 0.7 copy-start.16
  3.5 4.3 %collective-permute-start = (bf16[2,128,256]{2,1,0:T(8,128)(2,1)S(1)}, bf16[2,128,256]{2,1,0:T(8,128)(2,1)S(1)}, u32[]{:S(2)}, u32[]{:S(2)}) collective-permute-start(bf16[2,128,256]{2,1,0:T(8,128)(2,1)S(1)} %shard_map.67.rows_ref), channel_id=1, source_target_pairs={{0,4},{4,0},{1,5},{5,1},{2,6},{6,2},{3,7},{7,3},{8,12},{12,8},{9,1... | collective-permute-start | bytes 393224 | tf_op jit(solution)/shard_map/ppermute | solution.py:231
  7.8 23.4 %collective-permute-start.3 = (bf16[2,2,128,256]{3,2,1,0:T(8,128)(2,1)S(1)}, bf16[2,2,128,256]{3,2,1,0:T(8,128)(2,1)S(1)}, u32[]{:S(2)}, u32[]{:S(2)}) collective-permute-start(bf16[2,2,128,256]{3,2,1,0:T(8,128)(2,1)S(1)} %maximum_select_fusion.a_ref), channel_id=1, source_target_pairs={{0,24},{8,0},{16,8},{24,16},{1,25},{9,1},{17,9},{25,17},{2,26},{10... | collective-permute-start | bytes 786440 | tf_op jit(solution)/shard_map/ppermute | solution.py:231
  8.6 23.3 %collective-permute-start.2 = (bf16[2,2,128,256]{3,2,1,0:T(8,128)(2,1)S(1)}, bf16[2,2,128,256]{3,2,1,0:T(8,128)(2,1)S(1)}, u32[]{:S(2)}, u32[]{:S(2)}) collective-permute-start(bf16[2,2,128,256]{3,2,1,0:T(8,128)(2,1)S(1)} %maximum_select_fusion.a_ref), channel_id=1, source_target_pairs={{0,16},{8,24},{16,0},{24,8},{1,17},{9,25},{17,1},{25,9},{2,18},{10... | collective-permute-start | bytes 786440 | tf_op jit(solution)/shard_map/ppermute | solution.py:231
  9.1 23.5 %collective-permute-start.1 = (bf16[2,2,128,256]{3,2,1,0:T(8,128)(2,1)S(1)}, bf16[2,2,128,256]{3,2,1,0:T(8,128)(2,1)S(1)}, u32[]{:S(2)}, u32[]{:S(2)}) collective-permute-start(bf16[2,2,128,256]{3,2,1,0:T(8,128)(2,1)S(1)} %maximum_select_fusion.a_ref), channel_id=1, source_target_pairs={{0,8},{8,16},{16,24},{24,0},{1,9},{9,17},{17,25},{25,1},{2,10},{10... | collective-permute-start | bytes 786440 | tf_op jit(solution)/shard_map/ppermute | solution.py:231
  9.7 2.2 %copy-start = (bf16[8192,256]{1,0:T(8,128)(2,1)S(1)}, bf16[8192,256]{1,0:T(8,128)(2,1)}, u32[]{:S(2)}) copy-start(bf16[8192,256]{1,0:T(8,128)(2,1)} %proto_ref.1) | copy-start | bytes 12582916
  11.9 0.7 copy-start.17
  15.9 15.3 %all-to-all-start = ((f32[32,8,128]{2,1,0:T(8,128)}), f32[32,8,128]{2,1,0:T(8,128)S(1)}, u32[]{:S(2)}, u32[]{:S(2)}) async-start(f32[32,8,128]{2,1,0:T(8,128)} %shard_map.68), calls=%async_computation | async-start | bytes 262144 | tf_op jit(solution)/shard_map/all_to_all | solution.py:227
  31.2 0.7 copy-start.6
  31.9 0.7 copy-start.8
  32.7 0.7 copy-start.10
  33.4 0.9 copy-start.7
  34.3 0.9 copy-start.9
  35.3 0.9 copy-start.11
  38.6 0.6 copy-start.15
  39.2 15.2 %all-to-all-start.1 = ((f32[8,8,128]{2,1,0:T(8,128)}), f32[8,8,128]{2,1,0:T(8,128)S(1)}, u32[]{:S(2)}, u32[]{:S(2)}) async-start(f32[8,8,128]{2,1,0:T(8,128)} %copy-done.15), calls=%async_computation.1 | async-start | bytes 65536 | tf_op jit(solution)/shard_map/all_to_all | solution.py:227
  94.1 0.6 copy-start.12
  94.7 10.8 %all-to-all-start.5 = ((f32[8,8,128]{2,1,0:T(8,128)}), f32[8,8,128]{2,1,0:T(8,128)}, u32[]{:S(2)}, u32[]{:S(2)}) async-start(f32[8,8,128]{2,1,0:T(8,128)} %copy-done.12), calls=%async_computation.5 | async-start | bytes 65536 | tf_op jit(solution)/shard_map/all_to_all | solution.py:227
  100.3 2.0 %copy-start.1 = (f32[1024,1024]{1,0:T(8,128)}, f32[1024,1024]{1,0:T(8,128)S(1)}, u32[]{:S(2)}) copy-start(f32[1024,1024]{1,0:T(8,128)S(1)} %get-tuple-element.27.prob_ref) | copy-start | bytes 12582916
  102.3 1.4 copy-start.3
  105.5 17.2 %copy-start.2 = (f32[1024,1024]{1,0:T(8,128)S(1)}, f32[1024,1024]{1,0:T(8,128)}, u32[]{:S(2)}) copy-start(f32[1024,1024]{1,0:T(8,128)} %copy-done.1) | copy-start | bytes 12582916
  105.5 1.7 %copy-start.4 = (bf16[1024,1024]{1,0:T(8,128)(2,1)S(1)}, bf16[1024,1024]{1,0:T(8,128)(2,1)}, u32[]{:S(2)}) copy-start(bf16[1024,1024]{1,0:T(8,128)(2,1)} %copy-done.3) | copy-start | bytes 6291460
  122.8 36.4 %copy-start.18 = (s32[1,256]{1,0:T(1,128)S(1)}, s32[1,256]{1,0:T(1,128)}, u32[]{:S(2)}) copy-start(s32[1,256]{1,0:T(1,128)} %mask_ref.5) | copy-start | bytes 3076
  124.6 12.0 %copy-start.5 = (bf16[8,144,256]{2,1,0:T(8,128)(2,1)}, bf16[8,144,256]{2,1,0:T(8,128)(2,1)S(1)}, u32[]{:S(2)}) copy-start(bf16[8,144,256]{2,1,0:T(8,128)(2,1)S(1)} %get-tuple-element.28) | copy-start | bytes 1769476
  136.6 22.6 %all-to-all-start.7 = ((bf16[8,144,256]{2,1,0:T(8,128)(2,1)}), bf16[8,144,256]{2,1,0:T(8,128)(2,1)S(1)}, u32[]{:S(2)}, u32[]{:S(2)}) async-start(bf16[8,144,256]{2,1,0:T(8,128)(2,1)} %copy-done.5), calls=%async_computation.7 | async-start | bytes 1179648 | tf_op jit(solution)/shard_map/all_to_all | solution.py:227
  140.4 3.9 %collective-permute-start.6 = (f32[128,256]{1,0:T(8,128)S(1)}, f32[128,256]{1,0:T(8,128)S(1)}, u32[]{:S(2)}, u32[]{:S(2)}) collective-permute-start(f32[128,256]{1,0:T(8,128)S(1)} %shard_map.78.a_ref), channel_id=1, source_target_pairs={{0,3},{1,0},{2,1},{3,2},{4,7},{5,4},{6,5},{7,6},{8,11},{9,8},{10,9... | collective-permute-start | bytes 393224 | tf_op jit(solution)/shard_map/ppermute | solution.py:231
  141.5 5.4 %collective-permute-start.5 = (f32[128,256]{1,0:T(8,128)S(1)}, f32[128,256]{1,0:T(8,128)S(1)}, u32[]{:S(2)}, u32[]{:S(2)}) collective-permute-start(f32[128,256]{1,0:T(8,128)S(1)} %shard_map.78.a_ref), channel_id=1, source_target_pairs={{0,2},{1,3},{2,0},{3,1},{4,6},{5,7},{6,4},{7,5},{8,10},{9,11},{10,... | collective-permute-start | bytes 393224 | tf_op jit(solution)/shard_map/ppermute | solution.py:231
  142.5 7.6 %collective-permute-start.4 = (f32[128,256]{1,0:T(8,128)S(1)}, f32[128,256]{1,0:T(8,128)S(1)}, u32[]{:S(2)}, u32[]{:S(2)}) collective-permute-start(f32[128,256]{1,0:T(8,128)S(1)} %shard_map.78.a_ref), channel_id=1, source_target_pairs={{0,1},{1,2},{2,3},{3,0},{4,5},{5,6},{6,7},{7,4},{8,9},{9,10},{10,1... | collective-permute-start | bytes 393224 | tf_op jit(solution)/shard_map/ppermute | solution.py:231

commit v2 on v1

--- a/solution.py
+++ b/solution.py
@@ -1,5 +1,3 @@
-import functools
-
 import jax
 import jax.numpy as jnp
 from jax import lax
@@ -51,40 +49,60 @@
     return hit
 
 
-def pack_kernel(mask_ref, teach_ref, student_ref, out_ref):
+def pack_kernel(mask_hbm, teach_hbm, student_hbm, out_ref, mask_ref, teach_ref, student_ref, sems):
+    copies = [
+        pltpu.make_async_copy(src, dst, sems.at[i])
+        for i, (src, dst) in enumerate(((mask_hbm, mask_ref), (teach_hbm, teach_ref), (student_hbm, student_ref)))
+    ]
+    for copy in copies:
+        copy.start()
+    copies[0].wait()
     pick = selection(mask_ref[...]).astype(bf16)
-    out_ref[0] = dot(pick, teach_ref[...], NN).astype(bf16)
-    out_ref[1] = dot(pick, student_ref[...], NN).astype(bf16)
-
-
-def peak_kernel(mask_ref, rows_ref, proto_ref, out_ref, peak_ref):
-    step = pl.program_id(0)
-    logits = dot(proto_ref[...], rows_ref[0], NT)
-    top = jnp.max(logits, axis=0, keepdims=True)
-
-    @pl.when(step == 0)
-    def _():
-        peak_ref[...] = top
-
-    @pl.when(step > 0)
-    def _():
-        peak_ref[...] = jnp.maximum(peak_ref[...], top)
-
-    @pl.when(step == pl.num_programs(0) - 1)
-    def _():
-        count = jnp.sum(mask_ref[...].astype(f32), axis=1, keepdims=True)
-        tile = jnp.concatenate(
-            [peak_ref[...] * TEACHER_INV, jnp.broadcast_to(count, (1, LIVE)), jnp.zeros((6, LIVE), f32)], axis=0
-        )
-        out_ref[...] = jnp.broadcast_to(tile[None], out_ref.shape)
-
-
-def expo_kernel(me_ref, recv_ref, a_ref, b_ref, c_ref, d_ref, proto_ref, et_ref, srows_ref, stat_ref, pay_ref, trows):
-    for k, piece in enumerate((a_ref, b_ref, c_ref, d_ref)):
-        start = pl.multiple_of(((me_ref[0] - k) & 3) * 256, 256)
+    copies[1].wait()
+    out_ref[0] = dot(pick, teach_ref[0], NN).astype(bf16)
+    copies[2].wait()
+    out_ref[1] = dot(pick, student_ref[0], NN).astype(bf16)
+
+
+def peak_kernel(mask_hbm, rows_hbm, proto_hbm, out_ref, mine_ref, mask_ref, rows_ref, proto_ref, sems):
+    chunks = 8
+    tall = proto_ref.shape[0] // chunks
+    first = [
+        pltpu.make_async_copy(rows_hbm.at[0], rows_ref, sems.at[chunks]),
+        pltpu.make_async_copy(mask_hbm, mask_ref, sems.at[chunks + 1]),
+    ]
+    copies = [
+        pltpu.make_async_copy(proto_hbm.at[pl.ds(i * tall, tall)], proto_ref.at[pl.ds(i * tall, tall)], sems.at[i])
+        for i in range(chunks)
+    ]
+    for copy in first + copies:
+        copy.start()
+    for copy in first:
+        copy.wait()
+    image = lax.axis_index("x") * 2 + lax.axis_index("c")
+    count = jnp.sum(mask_ref[...].astype(f32), axis=1, keepdims=True)
+    peak = None
+    for i in range(chunks):
+        copies[i].wait()
+        mine_ref[128 * i : 128 * (i + 1), :] = proto_ref[pl.ds(pl.multiple_of(i * tall + image * 128, 128), 128), :]
+        logits = dot(proto_ref[i * tall : (i + 1) * tall, :], rows_ref[...], NT)
+        top = jnp.max(logits, axis=0, keepdims=True)
+        peak = top if peak is None else jnp.maximum(peak, top)
+    tile = jnp.concatenate([peak * TEACHER_INV, jnp.broadcast_to(count, (1, LIVE)), jnp.zeros((6, LIVE), f32)], axis=0)
+    out_ref[...] = jnp.broadcast_to(tile[None], out_ref.shape)
+
+
+def expo_kernel(recv_ref, a_hbm, b_hbm, c_hbm, d_hbm, mine_ref, et_ref, srows_ref, stat_ref, pay_ref, trows, sems):
+    x = lax.axis_index("x")
+    tcopies, scopies = [], []
+    for k, piece in enumerate((a_hbm, b_hbm, c_hbm, d_hbm)):
+        start = pl.multiple_of(((x + 4 - k) & 3) * 256, 256)
         for core in range(2):
-            trows[pl.ds(start + core * 128, 128), :] = piece[core, 0]
-            srows_ref[pl.ds(start + core * 128, 128), :] = piece[core, 1]
+            at = pl.ds(start + core * 128, 128)
+            tcopies.append(pltpu.make_async_copy(piece.at[core, 0], trows.at[at], sems.at[k * 4 + core]))
+            scopies.append(pltpu.make_async_copy(piece.at[core, 1], srows_ref.at[at], sems.at[k * 4 + 2 + core]))
+    for copy in tcopies + scopies:
+        copy.start()
     peaks, counts = [], []
     for x in range(4):
         for core in range(2):
@@ -100,15 +118,20 @@
     live = jnp.where(slot < count, 1.0, 0.0)
     stat_ref[0] = live
     stat_ref[1] = live / count
+    stat_ref[2] = jnp.concatenate(peaks, axis=0)
     live_rows = jnp.broadcast_to(to_lanes(live), (16, 1024)).astype(bf16)
     sums = []
-    for j in range(8):
-        logits = dot(proto_ref[128 * j : 128 * (j + 1), :], trows[...], NT)
+    for copy in tcopies:
+        copy.wait()
+    for j in range(8):
+        logits = dot(mine_ref[128 * j : 128 * (j + 1), :], trows[...], NT)
         block = jnp.exp(logits * TEACHER_INV - peak).astype(bf16)
         et_ref[128 * j : 128 * (j + 1), :] = block
         sums.append(dot(live_rows, block, NT)[0:1, :])
     tile = jnp.concatenate(sums, axis=0)
     pay_ref[...] = jnp.broadcast_to(tile[None], pay_ref.shape)
+    for copy in scopies:
+        copy.wait()
 
 
 def col_kernel(recv_ref, et_ref, *refs):
@@ -130,6 +153,7 @@
     pay_ref[:, 0:8, :] = jnp.broadcast_to(to_tile(out)[None], (pay_ref.shape[0], 8, 128))
     out = jnp.sum(dot(lhs, w_ref[...], NN), axis=0, keepdims=True)
     pay_ref[:, 8:16, :] = jnp.broadcast_to(to_tile(out)[None], (pay_ref.shape[0], 8, 128))
+    pay_ref[:, 16:24, :] = jnp.broadcast_to(col[None], (pay_ref.shape[0], 8, 128))
 
 
 def row_kernel(recv_ref, stat_ref, et_ref, pay_ref):
@@ -153,11 +177,12 @@
     out_ref[8:16, :] = to_tile(total)
 
 
-def student_prob_kernel(recv_ref, srows_ref, proto_ref, et_ref, prob_ref, w_ref):
+def student_prob_kernel(recv_ref, srows_ref, proto_ref, et_ref, prob_ref, w_ref, norm_ref):
     tops = recv_ref[:, 8:16, :]
     top = jnp.max(tops, axis=0)
     total = jnp.sum(recv_ref[:, 16:24, :] * jnp.exp(tops - top[None]), axis=0)
-    norm = to_lanes(top + jnp.log(total))
+    norm_ref[...] = top + jnp.log(total)
+    norm = to_lanes(norm_ref[...])
     for j in range(8):
         at = slice(128 * j, 128 * (j + 1))
         log_prob = dot(proto_ref[at, :], srows_ref[...], NT) * STUDENT_INV - norm
@@ -165,8 +190,8 @@
         w_ref[at, :] = (et_ref[at, :].astype(f32) * log_prob).astype(bf16)
 
 
-def grad_kernel(recv_ref, stat_ref, col_ref, et_ref, prob_ref, srows_ref, proto_ref, pout_ref, sout_ref, grad_ref):
-    sums = jnp.sum(recv_ref[...], axis=0)
+def grad_kernel(recv_ref, stat_ref, col_ref, et_ref, prob_ref, srows_ref, pout_ref, scale_ref):
+    sums = jnp.sum(recv_ref[:, 0:16, :], axis=0)
     row = stat_ref[0] / sums[0:8]
     weight = stat_ref[1]
     loss = -jnp.sum(jnp.sum(weight * row * sums[8:16], axis=1, keepdims=True), axis=0, keepdims=True) / IMAGES
@@ -176,6 +201,8 @@
     which = lax.broadcasted_iota(jnp.int32, (16, 256), 0)
     tail = jnp.where(which == 0, hi, jnp.where(which == 1, mid, jnp.where(which == 2, lo, 0.0))).astype(bf16)
     coef = weight * (LOSS_SCALE / (IMAGES * 0.1))
+    scale_ref[0] = coef
+    scale_ref[1] = coef * row
     coef_rows = to_lanes(coef)
     scale_rows = to_lanes(coef * row)
     for j in range(8):
@@ -183,15 +210,38 @@
         col = jnp.broadcast_to(col_ref[j : j + 1, :], (128, 128)).T
         col = jnp.concatenate([col] * 8, axis=1)
         grad = (prob_ref[at, :] * coef_rows - et_ref[at, :].astype(f32) * col * scale_rows).astype(bf16)
-        grad_ref[at, :] = grad
         pout_ref[j, 0:128, :] = dot(grad, srows_ref[...], NN).astype(bf16)
         pout_ref[j, 128:144, :] = tail
-    for i in range(8):
-        sout_ref[i] = dot(grad_ref[:, 128 * i : 128 * (i + 1)], proto_ref[...], TN).astype(bf16)
-
-
-def add_kernel(recv_ref, out_ref):
-    out_ref[...] = jnp.sum(recv_ref[...].astype(f32), axis=0)
+
+
+def own_kernel(recv_ref, scale_ref, stat_ref, norm_ref, rows_ref, proto_ref, out_ref):
+    step = pl.program_id(0)
+    y = lax.axis_index("y")
+    image = lax.axis_index("x") * 2 + lax.axis_index("c")
+
+    def column(row):
+        return jnp.concatenate([jnp.broadcast_to(row, (LIVE, 128)).T] * 8, axis=1)
+
+    peak = column(stat_ref[2, pl.ds(image, 1), :])
+    norm = column(norm_ref[pl.ds(image, 1), :])
+    coef = column(scale_ref[0, pl.ds(image, 1), :])
+    scale = column(scale_ref[1, pl.ds(image, 1), :])
+    col = jnp.concatenate(
+        [recv_ref[(x * 4 + y) * 2 + c, pl.ds(16 + step, 1), :] for x in range(4) for c in range(2)], axis=1
+    )
+    logits = dot(rows_ref[...].reshape(2 * LIVE, 256), proto_ref[...], NT)
+    teach = jnp.exp(logits[0:LIVE] * TEACHER_INV - peak).astype(bf16).astype(f32)
+    prob = jnp.exp(logits[LIVE:] * STUDENT_INV - norm)
+    grad = (prob * coef - teach * col * scale).astype(bf16)
+    part = dot(grad, proto_ref[...], NN)
+
+    @pl.when(step == 0)
+    def _():
+        out_ref[...] = part
+
+    @pl.when(step > 0)
+    def _():
+        out_ref[...] += part
 
 
 def end_kernel(mask_ref, recv_ref, a_ref, b_ref, c_ref, d_ref, student_ref, proto_ref, loss_ref):
@@ -210,7 +260,7 @@
 VM = pl.BlockSpec(memory_space=pltpu.VMEM)
 
 
-def call(kernel, out, *args, scratch=(), limit=32, cost=None):
+def call(kernel, out, *args, scratch=(), limit=8, cost=None):
     out = [jax.ShapeDtypeStruct(s, d) for s, d in out]
     return pl.pallas_call(
         kernel,
@@ -232,30 +282,41 @@
 
 
 PLANE = ("x", "y", "c")
+HBM = pl.BlockSpec(memory_space=pl.ANY)
 
 
 def local(teacher_feats, student_feats, prototypes, patch_mask):
-    x, c = lax.axis_index("x"), lax.axis_index("c")
-    (own,) = call(pack_kernel, [((2, LIVE, 256), bf16)], patch_mask, teacher_feats[0], student_feats[0])
-    mine = lax.dynamic_index_in_dim(prototypes.reshape(8, 8, 128, 256), x * 2 + c, 1, keepdims=False)
-    mine = mine.reshape(1024, 256)
+    c = lax.axis_index("c")
+    own = pl.pallas_call(
+        pack_kernel,
+        out_shape=jax.ShapeDtypeStruct((2, LIVE, 256), bf16),
+        in_specs=[HBM] * 3,
+        out_specs=VM,
+        scratch_shapes=[
+            pltpu.VMEM((1, 256), jnp.int32),
+            pltpu.VMEM((1, 256, 256), bf16),
+            pltpu.VMEM((1, 256, 256), bf16),
+            pltpu.SemaphoreType.DMA((3,)),
+        ],
+        compiler_params=pltpu.CompilerParams(vmem_limit_bytes=60 << 20),
+    )(patch_mask, teacher_feats, student_feats)
 
     other = shift(own, "c", 2, 1)
     pair = jnp.where(c == 0, jnp.stack([own, other]), jnp.stack([other, own]))
     parts = [pair] + [shift(pair, "x", 4, k) for k in (1, 2, 3)]
 
-    peak_pay = pl.pallas_call(
+    peak_pay, mine = pl.pallas_call(
         peak_kernel,
-        grid=(8,),
-        out_shape=jax.ShapeDtypeStruct((32, 8, 128), f32),
-        in_specs=[
-            pl.BlockSpec((1, 256), lambda i: (0, 0)),
-            pl.BlockSpec((1, LIVE, 256), lambda i: (0, 0, 0)),
-            pl.BlockSpec((1024, 256), lambda i: (i, 0)),
+        out_shape=[jax.ShapeDtypeStruct((32, 8, 128), f32), jax.ShapeDtypeStruct((1024, 256), bf16)],
+        in_specs=[HBM] * 3,
+        out_specs=[VM] * 2,
+        scratch_shapes=[
+            pltpu.VMEM((1, 256), jnp.int32),
+            pltpu.VMEM((LIVE, 256), bf16),
+            pltpu.VMEM((8192, 256), bf16),
+            pltpu.SemaphoreType.DMA((10,)),
         ],
-        out_specs=pl.BlockSpec((32, 8, 128), lambda i: (0, 0, 0)),
-        scratch_shapes=[pltpu.VMEM((1, LIVE), f32)],
-        compiler_params=pltpu.CompilerParams(vmem_limit_bytes=16 << 20),
+        compiler_params=pltpu.CompilerParams(vmem_limit_bytes=60 << 20),
     )(patch_mask, own, prototypes)
     peak_recv = a2a(peak_pay, PLANE)
 
@@ -264,25 +325,26 @@
         out_shape=[
             jax.ShapeDtypeStruct((1024, 1024), bf16),
             jax.ShapeDtypeStruct((1024, 256), bf16),
-            jax.ShapeDtypeStruct((2, 8, 128), f32),
+            jax.ShapeDtypeStruct((3, 8, 128), f32),
             jax.ShapeDtypeStruct((8, 8, 128), f32),
         ],
-        in_specs=[pl.BlockSpec(memory_space=pltpu.SMEM)] + [VM] * 6,
+        in_specs=[VM] + [HBM] * 4 + [VM],
         out_specs=[VM] * 4,
-        scratch_shapes=[pltpu.VMEM((1024, 256), bf16)],
-        compiler_params=pltpu.CompilerParams(vmem_limit_bytes=32 << 20),
-    )(x.astype(jnp.int32)[None], peak_recv, *parts, mine)
+        scratch_shapes=[pltpu.VMEM((1024, 256), bf16), pltpu.SemaphoreType.DMA((16,))],
+        compiler_params=pltpu.CompilerParams(vmem_limit_bytes=16 << 20),
+    )(peak_recv, *parts, mine)
 
     (student_sum,) = call(
         student_sum_kernel, [((16, 128), f32)], srows, mine,
-        scratch=[pltpu.VMEM((1024, 1024), f32)], cost=1 << 29,
+        scratch=[pltpu.VMEM((1024, 1024), f32)], cost=1 << 29, limit=16,
     )
 
     recv = a2a(pay, "z")
     pay, _ = call(col_kernel, [((32, 24, 128), f32), ((8, 128), f32)], recv, et, student_sum)
     recv = a2a(pay, PLANE)
-    prob, w = call(
-        student_prob_kernel, [((1024, 1024), f32), ((1024, 1024), bf16)], recv, srows, mine, et, cost=1 << 29
+    prob, w, norm = call(
+        student_prob_kernel, [((1024, 1024), f32), ((1024, 1024), bf16), ((8, 128), f32)], recv, srows, mine, et,
+        cost=1 << 29, limit=24,
     )
     (pay,) = call(row_kernel, [((8, 8, 128), f32)], recv, stat, et)
     for _ in range(BALANCING_PASSES - 2):
@@ -291,18 +353,33 @@
         recv = a2a(pay, PLANE)
         (pay,) = call(row_kernel, [((8, 8, 128), f32)], recv, stat, et)
     recv = a2a(pay, "z")
-    pay, col = call(last_col_kernel, [((32, 16, 128), f32), ((8, 128), f32)], recv, et, w)
+    pay, col = call(last_col_kernel, [((32, 24, 128), f32), ((8, 128), f32)], recv, et, w)
     recv = a2a(pay, PLANE)
 
-    proto_part, student_part = call(
-        grad_kernel, [((8, 144, 256), bf16), ((8, 128, 256), bf16)], recv, stat, col, et, prob, srows, mine,
-        scratch=[pltpu.VMEM((1024, 1024), bf16)],
-    )
-    (student_rows,) = call(add_kernel, [((128, 256), f32)], a2a(student_part, ("x", "c")))
+    proto_part, scale = call(
+        grad_kernel, [((8, 144, 256), bf16), ((2, 8, 128), f32)], recv, stat, col, et, prob, srows, limit=24
+    )
+    proto_recv = a2a(proto_part, "z")
+    student_rows = pl.pallas_call(
+        own_kernel,
+        grid=(8,),
+        out_shape=jax.ShapeDtypeStruct((LIVE, 256), f32),
+        in_specs=[
+            pl.BlockSpec((32, 24, 128), lambda i: (0, 0, 0)),
+            pl.BlockSpec((2, 8, 128), lambda i: (0, 0, 0)),
+            pl.BlockSpec((3, 8, 128), lambda i: (0, 0, 0)),
+            pl.BlockSpec((8, 128), lambda i: (0, 0)),
+            pl.BlockSpec((2, LIVE, 256), lambda i: (0, 0, 0)),
+            pl.BlockSpec((1024, 256), lambda i: (i, 0)),
+        ],
+        out_specs=pl.BlockSpec((LIVE, 256), lambda i: (0, 0)),
+        compiler_params=pltpu.CompilerParams(vmem_limit_bytes=24 << 20),
+        cost_estimate=pl.CostEstimate(flops=1 << 31, bytes_accessed=4 << 20, transcendentals=2 << 20),
+    )(recv, scale, stat, norm, own, prototypes)
     student_rows = [student_rows] + [shift(student_rows, "y", 4, k) for k in (1, 2, 3)]
-    proto_recv = a2a(proto_part, "z")
     student, proto, loss = call(
-        end_kernel, [((256, 256), f32), ((128, 256), f32), ((1, 128), f32)], patch_mask, proto_recv, *student_rows
+        end_kernel, [((256, 256), f32), ((128, 256), f32), ((1, 128), f32)], patch_mask, proto_recv, *student_rows,
+        limit=16,
     )
     return loss[0, 0], student[None], proto[None]
 

time: 161 us -> 147 us (0.913)
  waiting for transfers between devices: 31 us -> 16.4 us
  Pallas kernels: 17.6 us -> 27.1 us
  local copies, waits for them, and re-layouts: 17.8 us -> 10.8 us
  starting transfers between devices: 30.9 us -> 25.3 us
  blocking collectives: 62.5 us -> 65.4 us
    all_to_all x4 -> x3, waiting for transfers between devices: 22.4 us -> 8.64 us  [a2a(): return lax.all_to_all(v, axes, 0, 0, tiled=True)]
    pallas_call x1 -> x3, Pallas kernels: 3.3 us -> 12 us  [the longest x1 5.36 us: local(): pl.pallas_call(peak_kernel, out_shape=[jax.ShapeDtypeStruct((32, 8, 128),...]
    all_to_all x4 -> x3, starting transfers between devices: 23.5 us -> 16.1 us  [a2a(): return lax.all_to_all(v, axes, 0, 0, tiled=True)]
    unnamed x38 -> x24, local copies, waits for them, and re-layouts: 16.7 us -> 10.8 us
    all_to_all x5, blocking collectives: 62.5 us -> 65.4 us  [a2a(): return lax.all_to_all(v, axes, 0, 0, tiled=True)]
    pallas_call x1, Pallas kernels: 2.38 us -> 4.49 us  [local(): pl.pallas_call(expo_kernel, out_shape=[jax.ShapeDtypeStruct((1024, 1024),...]
    ppermute x7, starting transfers between devices: 7.32 us -> 9.24 us  [shift(): return lax.ppermute(v, axis, [(i, (i + k) % n) for i in range(n)])]
    pallas_call x11 -> x9, Pallas kernels: 11.9 us -> 10.6 us  [call(): pl.pallas_call(kernel, out_shape=out, in_specs=[VM] * len(args), out_spec...]
  transfers between devices with their start and end apart: 11 -> 10, of which waited for: 8 -> 7; matrix products, arithmetic and copies ran while one was open for 1% -> 0% of each run, Pallas kernels for 4% -> 9%
where the time goes in v2:
time: 147 us
  blocking collectives  65.4 us (44%)
  Pallas kernels  27.1 us (18%)
  starting transfers between devices  25.3 us (17%)
  waiting for transfers between devices  16.4 us (11%)
  local copies, waits for them, and re-layouts  10.8 us (7%)
    all_to_all x5, blocking collectives, a2a(): return lax.all_to_all(v, axes, 0, 0, tiled=True)  65.4 us
    all_to_all x3, starting transfers between devices, a2a(): return lax.all_to_all(v, axes, 0, 0, tiled=True)  16.1 us
    unnamed x24, local copies, waits for them, and re-layouts  10.8 us
    pallas_call x9, Pallas kernels, call(): pl.pallas_call(kernel, out_shape=out, in_specs=[VM] * len(args), out_spec...  10.6 us
    ppermute x7, starting transfers between devices, shift(): return lax.ppermute(v, axis, [(i, (i + k) % n) for i in range(n)])  9.24 us
    all_to_all x3, waiting for transfers between devices, a2a(): return lax.all_to_all(v, axes, 0, 0, tiled=True)  8.64 us
    ppermute x7, waiting for transfers between devices, shift(): return lax.ppermute(v, axis, [(i, (i + k) % n) for i in range(n)])  7.79 us
    pallas_call x1, Pallas kernels, local(): pl.pallas_call(peak_kernel, out_shape=[jax.ShapeDtypeStruct((32, 8, 128),...  5.36 us
  transfers between devices with their start and end apart: 10, of which 7 were waited for; matrix products, arithmetic and copies ran while one was open for 0% of the time, Pallas kernels for 9%

profile of v2, /device:TPU:1, one launch (start us, length us, event | category | flops | bytes accessed | tf_op | source)
XLA Modules:
  0.0 146.8 jit_solution(11508645648815797582)
XLA Ops:
  0.6 1.9 %shard_map.67.rows_hbm.rows_ref = bf16[2,128,256]{2,1,0:T(8,128)(2,1)} custom-call(s32[1,256]{1,0:T(1,128)} %mask_ref.1, bf16[1,256,256]{2,1,0:T(8,128)(2,1)} %teach_hbm.1, bf16[1,256,256]{2,1,0:T(8,128)(2,1)} %student_hbm.1), custom_call_target="tpu_custom_call" | custom-call | tf_op jit(solution)/shard_map/pallas_call | solution.py:290
  2.6 3.3 %collective-permute-start = (bf16[2,128,256]{2,1,0:T(8,128)(2,1)}, bf16[2,128,256]{2,1,0:T(8,128)(2,1)S(1)}, u32[]{:S(2)}, u32[]{:S(2)}) collective-permute-start(bf16[2,128,256]{2,1,0:T(8,128)(2,1)} %shard_map.67.rows_hbm.rows_ref), channel_id=1, source_target_pairs={{0,4},{4,0},{1,5},{5,1},{2,6},{6,2},{3,7},{7,3},{8,12},{12,8},{9,1... | collective-permute-start | bytes 393224 | tf_op jit(solution)/shard_map/ppermute | solution.py:281
  5.9 1.2 collective-permute-done
  8.2 1.9 %collective-permute-start.2 = (bf16[2,2,128,256]{3,2,1,0:T(8,128)(2,1)S(1)}, bf16[2,2,128,256]{3,2,1,0:T(8,128)(2,1)S(1)}, u32[]{:S(2)}, u32[]{:S(2)}) collective-permute-start(bf16[2,2,128,256]{3,2,1,0:T(8,128)(2,1)S(1)} %maximum_select_fusion.a_hbm), channel_id=1, source_target_pairs={{0,16},{8,24},{16,0},{24,8},{1,17},{9,25},{17,1},{25,9},{2,18},{10... | collective-permute-start | bytes 786440 | tf_op jit(solution)/shard_map/ppermute | solution.py:281
  10.1 1.2 collective-permute-start.3
  11.3 5.4 %shard_map.68 = (f32[32,8,128]{2,1,0:T(8,128)}, bf16[1024,256]{1,0:T(8,128)(2,1)}) custom-call(s32[1,256]{1,0:T(1,128)} %mask_ref.1, bf16[2,128,256]{2,1,0:T(8,128)(2,1)} %shard_map.67.rows_hbm.rows_ref, bf16[8192,256]{1,0:T(8,128)(2,1)} %proto_ref.1), custom_call_target="tpu_custom_call" | custom-call | tf_op jit(solution)/shard_map/pallas_call | solution.py:308
  16.7 13.6 %all_to_all.40.recv_ref = f32[32,8,128]{2,1,0:T(8,128)S(1)} all-to-all(f32[32,8,128]{2,1,0:T(8,128)} %get-tuple-element.21), channel_id=1, replica_groups=mesh['z'=8,'x'=4,'c'=2,'y'=4] {'x','y','c'}, dimensions={0} | all-to-all | bytes 262144 | tf_op jit(solution)/shard_map/all_to_all | solution.py:277
  30.2 1.0 copy-done.3
  31.3 4.5 %shard_map.69 = (bf16[1024,1024]{1,0:T(8,128)(2,1)S(1)}, bf16[1024,256]{1,0:T(8,128)(2,1)S(1)}, f32[3,8,128]{2,1,0:T(8,128)S(1)}, f32[8,8,128]{2,1,0:T(8,128)}) custom-call(f32[32,8,128]{2,1,0:T(8,128)S(1)} %all_to_all.40.recv_ref, bf16[2,2,128,256]{3,2,1,0:T(8,128)(2,1)S(1)} %maximum_select_fusion.a_hbm, ...), custom_call_target="tpu_custom_call" | custom-call | tf_op jit(solution)/shard_map/pallas_call | solution.py:323
  35.8 8.2 %all-to-all-start.1 = ((f32[8,8,128]{2,1,0:T(8,128)}), f32[8,8,128]{2,1,0:T(8,128)S(1)}, u32[]{:S(2)}, u32[]{:S(2)}) async-start(f32[8,8,128]{2,1,0:T(8,128)} %get-tuple-element.23), calls=%async_computation.1 | async-start | bytes 65536 | tf_op jit(solution)/shard_map/all_to_all | solution.py:277
  44.0 1.0 copy-done.4
  45.0 2.2 %shard_map.70.refs_0_ = f32[16,128]{1,0:T(8,128)S(1)} custom-call(bf16[1024,256]{1,0:T(8,128)(2,1)S(1)} %get-tuple-element.25.srows_ref, bf16[1024,256]{1,0:T(8,128)(2,1)S(1)} %copy-done.4), custom_call_target="tpu_custom_call" | custom-call | flops 536870912 | bytes 1048576 | tf_op jit(solution)/shard_map/pallas_call | solution.py:265
  47.2 3.7 %all-to-all-done.1.recv_ref = f32[8,8,128]{2,1,0:T(8,128)S(1)} async-done(((f32[8,8,128]{2,1,0:T(8,128)}), f32[8,8,128]{2,1,0:T(8,128)S(1)}, u32[]{:S(2)}, u32[]{:S(2)}) %all-to-all-start.1) | async-done | bytes 32800 | tf_op jit(solution)/shard_map/all_to_all | solution.py:277
  51.8 15.3 %all_to_all.41.recv_ref = f32[32,24,128]{2,1,0:T(8,128)S(1)} all-to-all(f32[32,24,128]{2,1,0:T(8,128)S(1)} %get-tuple-element.26), channel_id=1, replica_groups=mesh['z'=8,'x'=4,'c'=2,'y'=4] {'x','y','c'}, dimensions={0} | all-to-all | bytes 786432 | tf_op jit(solution)/shard_map/all_to_all | solution.py:277
  67.8 9.3 %all_to_all.42.recv_ref = f32[8,8,128]{2,1,0:T(8,128)S(1)} all-to-all(f32[8,8,128]{2,1,0:T(8,128)S(1)} %shard_map.72), channel_id=1, replica_groups=mesh['z'=8,'x'=4,'c'=2,'y'=4] {'z'}, dimensions={0} | all-to-all | bytes 65536 | tf_op jit(solution)/shard_map/all_to_all | solution.py:277
  77.9 12.2 %all_to_all.43.recv_ref = f32[32,8,128]{2,1,0:T(8,128)S(1)} all-to-all(f32[32,8,128]{2,1,0:T(8,128)S(1)} %get-tuple-element.28), channel_id=1, replica_groups=mesh['z'=8,'x'=4,'c'=2,'y'=4] {'x','y','c'}, dimensions={0} | all-to-all | bytes 262144 | tf_op jit(solution)/shard_map/all_to_all | solution.py:277
  91.4 4.1 %all-to-all-start.5 = ((f32[8,8,128]{2,1,0:T(8,128)}), f32[8,8,128]{2,1,0:T(8,128)}, u32[]{:S(2)}, u32[]{:S(2)}) async-start(f32[8,8,128]{2,1,0:T(8,128)} %copy-done.10), calls=%async_computation.5 | async-start | bytes 65536 | tf_op jit(solution)/shard_map/all_to_all | solution.py:277
  95.5 1.6 %shard_map.75 = (f32[1024,1024]{1,0:T(8,128)S(1)}, bf16[1024,1024]{1,0:T(8,128)(2,1)S(1)}, f32[8,128]{1,0:T(8,128)S(1)}) custom-call(f32[32,24,128]{2,1,0:T(8,128)S(1)} %all_to_all.41.recv_ref, bf16[1024,256]{1,0:T(8,128)(2,1)S(1)} %get-tuple-element.25.srows_ref, bf16[1024,256]{1,0:T(8,128)(2,1)S(1)} %copy-done.5, ...), custom_call_target="tpu_custom_call" | custom-call | flops 536870912 | bytes 1048576 | tf_op jit(solution)/shard_map/pallas_call | solution.py:265
  97.1 2.0 %copy-done = f32[1024,1024]{1,0:T(8,128)} copy-done((f32[1024,1024]{1,0:T(8,128)}, f32[1024,1024]{1,0:T(8,128)S(1)}, u32[]{:S(2)}) %copy-start) | copy-done | bytes 4194328
  99.1 1.4 copy-done.6
  100.5 1.7 %all-to-all-done.5.recv_ref = f32[8,8,128]{2,1,0:T(8,128)} async-done(((f32[8,8,128]{2,1,0:T(8,128)}), f32[8,8,128]{2,1,0:T(8,128)}, u32[]{:S(2)}, u32[]{:S(2)}) %all-to-all-start.5) | async-done | bytes 32800 | tf_op jit(solution)/shard_map/all_to_all | solution.py:277
  102.2 1.7 %copy-done.7 = bf16[1024,1024]{1,0:T(8,128)(2,1)S(1)} copy-done((bf16[1024,1024]{1,0:T(8,128)(2,1)S(1)}, bf16[1024,1024]{1,0:T(8,128)(2,1)}, u32[]{:S(2)}) %copy-start.7) | copy-done | bytes 2097176
  103.9 1.6 %shard_map.76 = (f32[32,24,128]{2,1,0:T(8,128)S(1)}, f32[8,128]{1,0:T(8,128)S(1)}) custom-call(f32[8,8,128]{2,1,0:T(8,128)} %all-to-all-done.5.recv_ref, bf16[1024,1024]{1,0:T(8,128)(2,1)S(1)} %get-tuple-element.24.et_ref, bf16[1024,1024]{1,0:T(8,128)(2,1)S(1)} %copy-done.7), custom_call_target="tpu_custom_call" | custom-call | tf_op jit(solution)/shard_map/pallas_call | solution.py:265
  105.5 15.0 %all_to_all.44.recv_ref = f32[32,24,128]{2,1,0:T(8,128)S(1)} all-to-all(f32[32,24,128]{2,1,0:T(8,128)S(1)} %get-tuple-element.30), channel_id=1, replica_groups=mesh['z'=8,'x'=4,'c'=2,'y'=4] {'x','y','c'}, dimensions={0} | all-to-all | bytes 786432 | tf_op jit(solution)/shard_map/all_to_all | solution.py:277
  122.4 3.7 %all-to-all-start.7 = ((bf16[8,144,256]{2,1,0:T(8,128)(2,1)}), bf16[8,144,256]{2,1,0:T(8,128)(2,1)S(1)}, u32[]{:S(2)}, u32[]{:S(2)}) async-start(bf16[8,144,256]{2,1,0:T(8,128)(2,1)} %copy-done.9), calls=%async_computation.7 | async-start | bytes 1179648 | tf_op jit(solution)/shard_map/all_to_all | solution.py:277
  126.1 2.2 %copy-done.2 = bf16[8192,256]{1,0:T(8,128)(2,1)S(1)} copy-done((bf16[8192,256]{1,0:T(8,128)(2,1)S(1)}, bf16[8192,256]{1,0:T(8,128)(2,1)}, u32[]{:S(2)}) %copy-start.2) | copy-done | bytes 4194328
  128.3 4.7 %shard_map.78.a_ref = f32[128,256]{1,0:T(8,128)S(1)} custom-call(f32[32,24,128]{2,1,0:T(8,128)S(1)} %all_to_all.44.recv_ref, f32[2,8,128]{2,1,0:T(8,128)S(1)} %get-tuple-element.34.scale_ref, f32[3,8,128]{2,1,0:T(8,128)S(1)} %get-tuple-element.27.stat_ref, f32[8,128]{1,0:T(8,128)S(1)} %get-tuple-element.35.norm_ref, bf16[2,128,256]{2,1,0:T(8,128)(2,1)S(1)} %copy-done.8, ...), custom_call_target="tpu_custom_call" | custom-call | flops 2147483648 | bytes 4194304 | tf_op jit(solution)/shard_map/pallas_call | solution.py:363
  133.3 2.0 %collective-permute-start.5 = (f32[128,256]{1,0:T(8,128)S(1)}, f32[128,256]{1,0:T(8,128)S(1)}, u32[]{:S(2)}, u32[]{:S(2)}) collective-permute-start(f32[128,256]{1,0:T(8,128)S(1)} %shard_map.78.a_ref), channel_id=1, source_target_pairs={{0,2},{1,3},{2,0},{3,1},{4,6},{5,7},{6,4},{7,5},{8,10},{9,11},{10,... | collective-permute-start | bytes 393224 | tf_op jit(solution)/shard_map/ppermute | solution.py:281
  135.8 4.0 %collective-permute-done.4.b_ref = f32[128,256]{1,0:T(8,128)S(1)} collective-permute-done((f32[128,256]{1,0:T(8,128)S(1)}, f32[128,256]{1,0:T(8,128)S(1)}, u32[]{:S(2)}, u32[]{:S(2)}) %collective-permute-start.4) | collective-permute-done | bytes 131104 | tf_op jit(solution)/shard_map/ppermute | solution.py:281
  139.8 1.7 %collective-permute-done.5.c_ref = f32[128,256]{1,0:T(8,128)S(1)} collective-permute-done((f32[128,256]{1,0:T(8,128)S(1)}, f32[128,256]{1,0:T(8,128)S(1)}, u32[]{:S(2)}, u32[]{:S(2)}) %collective-permute-start.5) | collective-permute-done | bytes 131104 | tf_op jit(solution)/shard_map/ppermute | solution.py:281
  142.4 3.2 %all-to-all-done.7.recv_ref = bf16[8,144,256]{2,1,0:T(8,128)(2,1)S(1)} async-done(((bf16[8,144,256]{2,1,0:T(8,128)(2,1)}), bf16[8,144,256]{2,1,0:T(8,128)(2,1)S(1)}, u32[]{:S(2)}, u32[]{:S(2)}) %all-to-all-start.7) | async-done | bytes 589856 | tf_op jit(solution)/shard_map/all_to_all | solution.py:277
  145.6 1.2 shard_map.79
  (31 shorter events, 8.1 us)
Async XLA Ops:
  2.6 4.5 %collective-permute-start = (bf16[2,128,256]{2,1,0:T(8,128)(2,1)}, bf16[2,128,256]{2,1,0:T(8,128)(2,1)S(1)}, u32[]{:S(2)}, u32[]{:S(2)}) collective-permute-start(bf16[2,128,256]{2,1,0:T(8,128)(2,1)} %shard_map.67.rows_hbm.rows_ref), channel_id=1, source_target_pairs={{0,4},{4,0},{1,5},{5,1},{2,6},{6,2},{3,7},{7,3},{8,12},{12,8},{9,1... | collective-permute-start | bytes 393224 | tf_op jit(solution)/shard_map/ppermute | solution.py:281
  8.1 22.1 %collective-permute-start.1 = (bf16[2,2,128,256]{3,2,1,0:T(8,128)(2,1)S(1)}, bf16[2,2,128,256]{3,2,1,0:T(8,128)(2,1)S(1)}, u32[]{:S(2)}, u32[]{:S(2)}) collective-permute-start(bf16[2,2,128,256]{3,2,1,0:T(8,128)(2,1)S(1)} %maximum_select_fusion.a_hbm), channel_id=1, source_target_pairs={{0,8},{8,16},{16,24},{24,0},{1,9},{9,17},{17,25},{25,1},{2,10},{10... | collective-permute-start | bytes 786440 | tf_op jit(solution)/shard_map/ppermute | solution.py:281
  8.2 22.0 %collective-permute-start.2 = (bf16[2,2,128,256]{3,2,1,0:T(8,128)(2,1)S(1)}, bf16[2,2,128,256]{3,2,1,0:T(8,128)(2,1)S(1)}, u32[]{:S(2)}, u32[]{:S(2)}) collective-permute-start(bf16[2,2,128,256]{3,2,1,0:T(8,128)(2,1)S(1)} %maximum_select_fusion.a_hbm), channel_id=1, source_target_pairs={{0,16},{8,24},{16,0},{24,8},{1,17},{9,25},{17,1},{25,9},{2,18},{10... | collective-permute-start | bytes 786440 | tf_op jit(solution)/shard_map/ppermute | solution.py:281
  10.1 20.1 %collective-permute-start.3 = (bf16[2,2,128,256]{3,2,1,0:T(8,128)(2,1)S(1)}, bf16[2,2,128,256]{3,2,1,0:T(8,128)(2,1)S(1)}, u32[]{:S(2)}, u32[]{:S(2)}) collective-permute-start(bf16[2,2,128,256]{3,2,1,0:T(8,128)(2,1)S(1)} %maximum_select_fusion.a_hbm), channel_id=1, source_target_pairs={{0,24},{8,0},{16,8},{24,16},{1,25},{9,1},{17,9},{25,17},{2,26},{10... | collective-permute-start | bytes 786440 | tf_op jit(solution)/shard_map/ppermute | solution.py:281
  30.2 1.0 copy-start.3
  35.8 15.2 %all-to-all-start.1 = ((f32[8,8,128]{2,1,0:T(8,128)}), f32[8,8,128]{2,1,0:T(8,128)S(1)}, u32[]{:S(2)}, u32[]{:S(2)}) async-start(f32[8,8,128]{2,1,0:T(8,128)} %get-tuple-element.23), calls=%async_computation.1 | async-start | bytes 65536 | tf_op jit(solution)/shard_map/all_to_all | solution.py:277
  44.0 1.0 copy-start.4
  51.8 43.7 %copy-start.5 = (bf16[1024,256]{1,0:T(8,128)(2,1)S(1)}, bf16[1024,256]{1,0:T(8,128)(2,1)}, u32[]{:S(2)}) copy-start(bf16[1024,256]{1,0:T(8,128)(2,1)} %get-tuple-element.22.mine_ref.proto_ref) | copy-start | bytes 1572868
  90.8 0.6 copy-start.10
  91.4 10.8 %all-to-all-start.5 = ((f32[8,8,128]{2,1,0:T(8,128)}), f32[8,8,128]{2,1,0:T(8,128)}, u32[]{:S(2)}, u32[]{:S(2)}) async-start(f32[8,8,128]{2,1,0:T(8,128)} %copy-done.10), calls=%async_computation.5 | async-start | bytes 65536 | tf_op jit(solution)/shard_map/all_to_all | solution.py:277
  97.1 2.0 %copy-start = (f32[1024,1024]{1,0:T(8,128)}, f32[1024,1024]{1,0:T(8,128)S(1)}, u32[]{:S(2)}) copy-start(f32[1024,1024]{1,0:T(8,128)S(1)} %get-tuple-element.32.prob_ref) | copy-start | bytes 12582916
  99.1 1.4 copy-start.6
  102.2 18.4 %copy-start.1 = (f32[1024,1024]{1,0:T(8,128)S(1)}, f32[1024,1024]{1,0:T(8,128)}, u32[]{:S(2)}) copy-start(f32[1024,1024]{1,0:T(8,128)} %copy-done) | copy-start | bytes 12582916
  102.2 1.7 %copy-start.7 = (bf16[1024,1024]{1,0:T(8,128)(2,1)S(1)}, bf16[1024,1024]{1,0:T(8,128)(2,1)}, u32[]{:S(2)}) copy-start(bf16[1024,1024]{1,0:T(8,128)(2,1)} %copy-done.6) | copy-start | bytes 6291460
  120.6 5.5 %copy-start.8 = (bf16[2,128,256]{2,1,0:T(8,128)(2,1)S(1)}, bf16[2,128,256]{2,1,0:T(8,128)(2,1)}, u32[]{:S(2)}) copy-start(bf16[2,128,256]{2,1,0:T(8,128)(2,1)} %shard_map.67.rows_hbm.rows_ref) | copy-start | bytes 393220
  121.6 0.8 copy-start.9
  122.4 23.2 %all-to-all-start.7 = ((bf16[8,144,256]{2,1,0:T(8,128)(2,1)}), bf16[8,144,256]{2,1,0:T(8,128)(2,1)S(1)}, u32[]{:S(2)}, u32[]{:S(2)}) async-start(bf16[8,144,256]{2,1,0:T(8,128)(2,1)} %copy-done.9), calls=%async_computation.7 | async-start | bytes 1179648 | tf_op jit(solution)/shard_map/all_to_all | solution.py:277
  126.1 19.4 %copy-start.11 = (s32[1,256]{1,0:T(1,128)S(1)}, s32[1,256]{1,0:T(1,128)}, u32[]{:S(2)}) copy-start(s32[1,256]{1,0:T(1,128)} %mask_ref.1) | copy-start | bytes 3076
  126.1 2.2 %copy-start.2 = (bf16[8192,256]{1,0:T(8,128)(2,1)S(1)}, bf16[8192,256]{1,0:T(8,128)(2,1)}, u32[]{:S(2)}) copy-start(bf16[8192,256]{1,0:T(8,128)(2,1)} %proto_ref.1) | copy-start | bytes 12582916
  133.0 6.8 %collective-permute-start.4 = (f32[128,256]{1,0:T(8,128)S(1)}, f32[128,256]{1,0:T(8,128)S(1)}, u32[]{:S(2)}, u32[]{:S(2)}) collective-permute-start(f32[128,256]{1,0:T(8,128)S(1)} %shard_map.78.a_ref), channel_id=1, source_target_pairs={{0,1},{1,2},{2,3},{3,0},{4,5},{5,6},{6,7},{7,4},{8,9},{9,10},{10,1... | collective-permute-start | bytes 393224 | tf_op jit(solution)/shard_map/ppermute | solution.py:281
  133.3 8.3 %collective-permute-start.5 = (f32[128,256]{1,0:T(8,128)S(1)}, f32[128,256]{1,0:T(8,128)S(1)}, u32[]{:S(2)}, u32[]{:S(2)}) collective-permute-start(f32[128,256]{1,0:T(8,128)S(1)} %shard_map.78.a_ref), channel_id=1, source_target_pairs={{0,2},{1,3},{2,0},{3,1},{4,6},{5,7},{6,4},{7,5},{8,10},{9,11},{10,... | collective-permute-start | bytes 393224 | tf_op jit(solution)/shard_map/ppermute | solution.py:281
  135.3 7.1 %collective-permute-start.6 = (f32[128,256]{1,0:T(8,128)S(1)}, f32[128,256]{1,0:T(8,128)S(1)}, u32[]{:S(2)}, u32[]{:S(2)}) collective-permute-start(f32[128,256]{1,0:T(8,128)S(1)} %shard_map.78.a_ref), channel_id=1, source_target_pairs={{0,3},{1,0},{2,1},{3,2},{4,7},{5,4},{6,5},{7,6},{8,11},{9,8},{10,9... | collective-permute-start | bytes 393224 | tf_op jit(solution)/shard_map/ppermute | solution.py:281

commit v3 on v2

v3 whole, which is shorter than its diff:
```python
import jax
import jax.numpy as jnp
from jax import lax
from jax.experimental import pallas as pl
from jax.experimental.pallas import tpu as pltpu
from jax.sharding import Mesh, PartitionSpec as P

BALANCING_PASSES = 3
LOSS_SCALE = 16384
TEACHER_INV = 1.0 / 0.07
STUDENT_INV = 1.0 / 0.1
IMAGES = 64
LIVE = 128
NT = (((1,), (1,)), ((), ()))
NN = (((1,), (0,)), ((), ()))
TN = (((0,), (0,)), ((), ()))
f32 = jnp.float32
bf16 = jnp.bfloat16


def dot(a, b, dims):
    return lax.dot_general(a, b, dims, preferred_element_type=f32)


def to_lanes(v):
    return jnp.concatenate([v[i : i + 1, :] for i in range(8)], axis=1)


def to_tile(v):
    return jnp.concatenate([v[:, 128 * i : 128 * (i + 1)] for i in range(8)], axis=0)


def split3(v):
    hi = v.astype(bf16).astype(f32)
    mid = (v - hi).astype(bf16).astype(f32)
    lo = (v - hi - mid).astype(bf16).astype(f32)
    return jnp.concatenate([hi, mid, lo, jnp.zeros((13, v.shape[1]), f32)], axis=0).astype(bf16)


def selection(mask):
    patches = mask.shape[1]
    maskf = mask.astype(f32)
    before = lax.broadcasted_iota(jnp.int32, (patches, patches), 0)
    after = lax.broadcasted_iota(jnp.int32, (patches, patches), 1)
    tri = jnp.where(before <= after, 1.0, 0.0).astype(bf16)
    rank = dot(jnp.broadcast_to(maskf, (16, patches)).astype(bf16), tri, NN)[0:1, :]
    slot = lax.broadcasted_iota(jnp.int32, (LIVE, patches), 0).astype(f32)
    hit = jnp.where(rank - 1.0 == slot, 1.0, 0.0) * maskf
    return hit


def head_kernel(
    mask_hbm, teach_hbm, student_hbm, proto_hbm, own_ref, out_ref, mine_ref, mask_ref, teach_ref, student_ref, proto_ref, sems
):
    chunks = 8
    tall = proto_ref.shape[0] // chunks
    small = ((mask_hbm, mask_ref), (teach_hbm, teach_ref), (student_hbm, student_ref))
    first = [pltpu.make_async_copy(src, dst, sems.at[chunks + i]) for i, (src, dst) in enumerate(small)]
    copies = [
        pltpu.make_async_copy(proto_hbm.at[pl.ds(i * tall, tall)], proto_ref.at[pl.ds(i * tall, tall)], sems.at[i])
        for i in range(chunks)
    ]
    for copy in first + copies:
        copy.start()
    image = lax.axis_index("x") * 2 + lax.axis_index("c")
    first[0].wait()
    pick = selection(mask_ref[...]).astype(bf16)
    count = jnp.sum(mask_ref[...].astype(f32), axis=1, keepdims=True)
    first[1].wait()
    own_ref[0] = dot(pick, teach_ref[0], NN).astype(bf16)
    first[2].wait()
    own_ref[1] = dot(pick, student_ref[0], NN).astype(bf16)
    rows = own_ref[0]
    peak = None
    for i in range(chunks):
        copies[i].wait()
        mine_ref[128 * i : 128 * (i + 1), :] = proto_ref[pl.ds(pl.multiple_of(i * tall + image * 128, 128), 128), :]
        logits = dot(proto_ref[i * tall : (i + 1) * tall, :], rows, NT)
        top = jnp.max(logits, axis=0, keepdims=True)
        peak = top if peak is None else jnp.maximum(peak, top)
    tile = jnp.concatenate([peak * TEACHER_INV, jnp.broadcast_to(count, (1, LIVE)), jnp.zeros((6, LIVE), f32)], axis=0)
    out_ref[...] = jnp.broadcast_to(tile[None], out_ref.shape)


def expo_kernel(recv_ref, a_hbm, b_hbm, c_hbm, d_hbm, mine_ref, et_ref, srows_ref, stat_ref, pay_ref, trows, sems):
    x = lax.axis_index("x")
    tcopies, scopies = [], []
    for k, piece in enumerate((a_hbm, b_hbm, c_hbm, d_hbm)):
        start = pl.multiple_of(((x + 4 - k) & 3) * 256, 256)
        for core in range(2):
            at = pl.ds(start + core * 128, 128)
            tcopies.append(pltpu.make_async_copy(piece.at[core, 0], trows.at[at], sems.at[k * 4 + core]))
            scopies.append(pltpu.make_async_copy(piece.at[core, 1], srows_ref.at[at], sems.at[k * 4 + 2 + core]))
    for copy in tcopies + scopies:
        copy.start()
    peaks, counts = [], []
    for x in range(4):
        for core in range(2):
            at = [(x * 4 + y) * 2 + core for y in range(4)]
            top = recv_ref[at[0], 0:1, :]
            for i in at[1:]:
                top = jnp.maximum(top, recv_ref[i, 0:1, :])
            peaks.append(top)
            counts.append(recv_ref[at[0], 1:2, :])
    peak = jnp.concatenate(peaks, axis=1)
    count = jnp.concatenate(counts, axis=0)
    slot = lax.broadcasted_iota(jnp.int32, (8, 128), 1).astype(f32)
    live = jnp.where(slot < count, 1.0, 0.0)
    stat_ref[0] = live
    stat_ref[1] = live / count
    stat_ref[2] = jnp.concatenate(peaks, axis=0)
    live_rows = jnp.broadcast_to(to_lanes(live), (16, 1024)).astype(bf16)
    total = jnp.zeros((16, 1024), f32)
    for copy in tcopies:
        copy.wait()
    for r in range(4):
        at = slice(256 * r, 256 * (r + 1))
        logits = dot(mine_ref[...], trows[at, :], NT)
        block = jnp.exp(logits * TEACHER_INV - peak[:, at]).astype(bf16)
        et_ref[:, at] = block
        total += dot(live_rows[:, at], block, NT)
    pay_ref[...] = jnp.broadcast_to(to_tile(total[0:1])[None], pay_ref.shape)
    for copy in scopies:
        copy.wait()


def col_kernel(recv_ref, et_ref, extra_ref, pay_ref):
    col = 1.0 / jnp.sum(recv_ref[...], axis=0)
    out = jnp.sum(dot(split3(to_lanes(col)), et_ref[...], NN), axis=0, keepdims=True)
    pay_ref[:, 0:8, :] = jnp.broadcast_to(to_tile(out)[None], (pay_ref.shape[0], 8, 128))
    if pay_ref.shape[1] > 8:
        pay_ref[:, 8:, :] = jnp.broadcast_to(extra_ref[...][None], (pay_ref.shape[0], 8, 128))


def last_col_kernel(recv_ref, et_ref, w_ref, pay_ref, col_ref):
    col = 1.0 / jnp.sum(recv_ref[...], axis=0)
    col_ref[...] = col
    lhs = split3(to_lanes(col))
    out = to_tile(jnp.sum(dot(lhs, et_ref[...], NN), axis=0, keepdims=True))
    hi = out.astype(bf16).astype(f32)
    sums = jnp.concatenate([hi, out - hi], axis=0).astype(bf16)
    out = to_tile(jnp.sum(dot(lhs, w_ref[...], NN), axis=0, keepdims=True))
    rest = jnp.concatenate([out, col], axis=0).astype(bf16)
    pay_ref[:, 0:16, :] = jnp.broadcast_to(sums[None], (pay_ref.shape[0], 16, 128))
    pay_ref[:, 16:32, :] = jnp.broadcast_to(rest[None], (pay_ref.shape[0], 16, 128))


def row_kernel(recv_ref, stat_ref, et_ref, pay_ref):
    row = stat_ref[0] / jnp.sum(recv_ref[:, 0:8, :], axis=0)
    lhs = split3(to_lanes(row))
    out = jnp.sum(dot(lhs, et_ref[...], NT), axis=0, keepdims=True)
    pay_ref[...] = jnp.broadcast_to(to_tile(out)[None], pay_ref.shape)


def student_sum_kernel(srows_ref, mine_ref, out_ref):
    parts = []
    for r in range(4):
        logits = dot(mine_ref[...], srows_ref[256 * r : 256 * (r + 1), :], NT) * STUDENT_INV
        top = jnp.max(logits, axis=0, keepdims=True)
        parts.append(top + jnp.log(jnp.sum(jnp.exp(logits - top), axis=0, keepdims=True)))
    out_ref[...] = to_tile(jnp.concatenate(parts, axis=1))


def student_prob_kernel(recv_ref, srows_ref, mine_ref, et_ref, prob_hbm, w_hbm, norm_ref, prob_ref, w_ref, sems):
    parts = recv_ref[:, 8:16, :]
    top = jnp.max(parts, axis=0)
    norm_ref[...] = top + jnp.log(jnp.sum(jnp.exp(parts - top[None]), axis=0))
    norm = to_lanes(norm_ref[...])
    copies = []
    for r in range(4):
        at = slice(256 * r, 256 * (r + 1))
        log_prob = dot(mine_ref[...], srows_ref[at, :], NT) * STUDENT_INV - norm[:, at]
        prob_ref[:, at] = jnp.exp(log_prob)
        w_ref[:, at] = (et_ref[:, at].astype(f32) * log_prob).astype(bf16)
        at = (pl.ds(0, 1024), pl.ds(256 * r, 256))
        copies.append(pltpu.make_async_copy(prob_ref.at[at], prob_hbm.at[at], sems.at[r]))
        copies.append(pltpu.make_async_copy(w_ref.at[at], w_hbm.at[at], sems.at[4 + r]))
        copies[-2].start()
        copies[-1].start()
    for copy in copies:
        copy.wait()


def grad_kernel(recv_ref, stat_ref, col_ref, et_ref, prob_ref, srows_ref, pout_ref, scale_ref):
    sums = jnp.sum(recv_ref[:, 0:16, :].astype(f32), axis=0)
    entropy = jnp.sum(recv_ref[:, 16:32, :].astype(f32), axis=0)[0:8]
    row = stat_ref[0] / (sums[0:8] + sums[8:16])
    weight = stat_ref[1]
    loss = -jnp.sum(jnp.sum(weight * row * entropy, axis=1, keepdims=True), axis=0, keepdims=True) / IMAGES
    hi = loss.astype(bf16).astype(f32)
    mid = (loss - hi).astype(bf16).astype(f32)
    lo = loss - hi - mid
    which = lax.broadcasted_iota(jnp.int32, (16, 256), 0)
    tail = jnp.where(which == 0, hi, jnp.where(which == 1, mid, jnp.where(which == 2, lo, 0.0))).astype(bf16)
    coef = weight * (LOSS_SCALE / (IMAGES * 0.1))
    scale_ref[0] = coef
    scale_ref[1] = coef * row
    coef_rows = to_lanes(coef)
    scale_rows = to_lanes(coef * row)
    for j in range(4):
        at = slice(256 * j, 256 * (j + 1))
        col = jnp.concatenate([jnp.broadcast_to(col_ref[i : i + 1, :], (128, 128)).T for i in (2 * j, 2 * j + 1)], axis=0)
        col = jnp.concatenate([col] * 8, axis=1)
        grad = (prob_ref[at, :] * coef_rows - et_ref[at, :].astype(f32) * col * scale_rows).astype(bf16)
        part = dot(grad, srows_ref[...], NN).astype(bf16)
        for i in (0, 1):
            pout_ref[2 * j + i, 0:128, :] = part[128 * i : 128 * (i + 1)]
            pout_ref[2 * j + i, 128:144, :] = tail


def own_kernel(recv_ref, scale_ref, stat_ref, norm_ref, rows_hbm, proto_hbm, out_ref, rows_ref, proto_ref, sems):
    chunks = 8
    tall = proto_ref.shape[0] // chunks
    rows_copy = pltpu.make_async_copy(rows_hbm, rows_ref, sems.at[chunks])
    copies = [
        pltpu.make_async_copy(proto_hbm.at[pl.ds(i * tall, tall)], proto_ref.at[pl.ds(i * tall, tall)], sems.at[i])
        for i in range(chunks)
    ]
    for copy in [rows_copy] + copies:
        copy.start()
    y = lax.axis_index("y")
    image = lax.axis_index("x") * 2 + lax.axis_index("c")

    def column(row):
        return jnp.concatenate([jnp.broadcast_to(row, (LIVE, 128)).T] * 8, axis=1)

    peak = column(stat_ref[2, pl.ds(image, 1), :])
    norm = column(norm_ref[pl.ds(image, 1), :])
    coef = column(scale_ref[0, pl.ds(image, 1), :])
    scale = column(scale_ref[1, pl.ds(image, 1), :])
    cols = [recv_ref[(x * 4 + y) * 2 + c, 16:32, :].astype(f32) for x in range(4) for c in range(2)]
    rows_copy.wait()
    rows = rows_ref[...].reshape(2 * LIVE, 256)
    total = jnp.zeros((LIVE, 256), f32)
    for i in range(chunks):
        col = jnp.concatenate([v[8 + i : 9 + i, :] for v in cols], axis=1)
        copies[i].wait()
        block = proto_ref[i * tall : (i + 1) * tall, :]
        logits = dot(rows, block, NT)
        teach = jnp.exp(logits[0:LIVE] * TEACHER_INV - peak).astype(bf16).astype(f32)
        prob = jnp.exp(logits[LIVE:] * STUDENT_INV - norm)
        grad = (prob * coef - teach * (col * scale)).astype(bf16)
        total += dot(grad, block, NN)
    out_ref[...] = total


def end_kernel(mask_ref, recv_ref, a_ref, b_ref, c_ref, d_ref, student_ref, proto_ref, loss_ref):
    pick = selection(mask_ref[...]).astype(bf16)
    rows = (a_ref[...] + c_ref[...]) + (b_ref[...] + d_ref[...])
    hi = rows.astype(bf16)
    rest = rows - hi.astype(f32)
    mid = rest.astype(bf16)
    lo = (rest - mid.astype(f32)).astype(bf16)
    student_ref[...] = dot(pick, hi, TN) + dot(pick, mid, TN) + dot(pick, lo, TN)
    total = jnp.sum(recv_ref[...].astype(f32), axis=0)
    proto_ref[...] = total[0:128, :]
    loss_ref[...] = total[128:129, 0:128] + total[129:130, 0:128] + total[130:131, 0:128]


VM = pl.BlockSpec(memory_space=pltpu.VMEM)


def call(kernel, out, *args, scratch=(), limit=8, cost=None):
    out = [jax.ShapeDtypeStruct(s, d) for s, d in out]
    return pl.pallas_call(
        kernel,
        out_shape=out,
        in_specs=[VM] * len(args),
        out_specs=[VM] * len(out),
        scratch_shapes=list(scratch),
        compiler_params=pltpu.CompilerParams(vmem_limit_bytes=limit << 20),
        cost_estimate=cost and pl.CostEstimate(flops=cost, bytes_accessed=1 << 20, transcendentals=1 << 20),
    )(*args)


def in_hbm(v):
    return pltpu.with_memory_space_constraint(v, pltpu.HBM)


def a2a(v, axes):
    return lax.all_to_all(v, axes, 0, 0, tiled=True)


def shift(v, axis, n, k):
    return lax.ppermute(v, axis, [(i, (i + k) % n) for i in range(n)])


PLANE = ("x", "y", "c")
HBM = pl.BlockSpec(memory_space=pl.ANY)


def local(teacher_feats, student_feats, prototypes, patch_mask):
    c = lax.axis_index("c")
    own, peak_pay, mine = pl.pallas_call(
        head_kernel,
        out_shape=[
            jax.ShapeDtypeStruct((2, LIVE, 256), bf16),
            jax.ShapeDtypeStruct((32, 8, 128), f32),
            jax.ShapeDtypeStruct((1024, 256), bf16),
        ],
        in_specs=[pl.BlockSpec(memory_space=pltpu.HBM)] * 4,
        out_specs=[VM] * 3,
        scratch_shapes=[
            pltpu.VMEM((1, 256), jnp.int32),
            pltpu.VMEM((1, 256, 256), bf16),
            pltpu.VMEM((1, 256, 256), bf16),
            pltpu.VMEM((8192, 256), bf16),
            pltpu.SemaphoreType.DMA((11,)),
        ],
        compiler_params=pltpu.CompilerParams(vmem_limit_bytes=32 << 20),
    )(*(in_hbm(v) for v in (patch_mask, teacher_feats, student_feats, prototypes)))

    other = shift(own, "c", 2, 1)
    pair = jnp.where(c == 0, jnp.stack([own, other]), jnp.stack([other, own]))
    parts = [pair] + [shift(pair, "x", 4, k) for k in (1, 2, 3)]

    peak_recv = a2a(peak_pay, PLANE)

    et, srows, stat, pay = pl.pallas_call(
        expo_kernel,
        out_shape=[
            jax.ShapeDtypeStruct((1024, 1024), bf16),
            jax.ShapeDtypeStruct((1024, 256), bf16),
            jax.ShapeDtypeStruct((3, 8, 128), f32),
            jax.ShapeDtypeStruct((8, 8, 128), f32),
        ],
        in_specs=[VM] + [HBM] * 4 + [VM],
        out_specs=[VM] * 4,
        scratch_shapes=[pltpu.VMEM((1024, 256), bf16), pltpu.SemaphoreType.DMA((16,))],
        compiler_params=pltpu.CompilerParams(vmem_limit_bytes=16 << 20),
    )(peak_recv, *parts, mine)

    (student_sum,) = call(student_sum_kernel, [((8, 128), f32)], srows, mine, cost=1 << 29, limit=16)

    recv = a2a(pay, "z")
    (pay,) = call(col_kernel, [((32, 16, 128), f32)], recv, et, student_sum)
    recv = a2a(pay, PLANE)
    prob, w, norm = pl.pallas_call(
        student_prob_kernel,
        out_shape=[
            pltpu.HBM((1024, 1024), f32),
            pltpu.HBM((1024, 1024), bf16),
            jax.ShapeDtypeStruct((8, 128), f32),
        ],
        in_specs=[VM] * 4,
        out_specs=[pl.BlockSpec(memory_space=pltpu.HBM)] * 2 + [VM],
        scratch_shapes=[
            pltpu.VMEM((1024, 1024), f32),
            pltpu.VMEM((1024, 1024), bf16),
            pltpu.SemaphoreType.DMA((8,)),
        ],
        compiler_params=pltpu.CompilerParams(vmem_limit_bytes=24 << 20),
        cost_estimate=pl.CostEstimate(flops=1 << 29, bytes_accessed=8 << 20, transcendentals=1 << 20),
    )(recv, srows, mine, et)
    (pay,) = call(row_kernel, [((8, 8, 128), f32)], recv, stat, et)
    for _ in range(BALANCING_PASSES - 2):
        recv = a2a(pay, "z")
        (pay,) = call(col_kernel, [((32, 8, 128), f32)], recv, et, norm)
        recv = a2a(pay, PLANE)
        (pay,) = call(row_kernel, [((8, 8, 128), f32)], recv, stat, et)
    recv = a2a(pay, "z")
    pay, col = call(last_col_kernel, [((32, 32, 128), bf16), ((8, 128), f32)], recv, et, w)
    recv = a2a(pay, PLANE)

    proto_part, scale = call(
        grad_kernel, [((8, 144, 256), bf16), ((2, 8, 128), f32)], recv, stat, col, et, prob, srows, limit=24
    )
    proto_recv = a2a(proto_part, "z")
    student_rows = pl.pallas_call(
        own_kernel,
        out_shape=jax.ShapeDtypeStruct((LIVE, 256), f32),
        in_specs=[VM] * 4 + [pl.BlockSpec(memory_space=pltpu.HBM)] * 2,
        out_specs=VM,
        scratch_shapes=[
            pltpu.VMEM((2, LIVE, 256), bf16),
            pltpu.VMEM((8192, 256), bf16),
            pltpu.SemaphoreType.DMA((9,)),
        ],
        compiler_params=pltpu.CompilerParams(vmem_limit_bytes=24 << 20),
        cost_estimate=pl.CostEstimate(flops=1 << 31, bytes_accessed=4 << 20, transcendentals=2 << 20),
    )(recv, scale, stat, norm, in_hbm(own), in_hbm(prototypes))
    student_rows = [student_rows] + [shift(student_rows, "y", 4, k) for k in (1, 2, 3)]
    student, proto, loss = call(
        end_kernel, [((256, 256), f32), ((128, 256), f32), ((1, 128), f32)], patch_mask, proto_recv, *student_rows,
        limit=16,
    )
    return loss[0, 0], student[None], proto[None]


def solution(mesh):
    fine = Mesh(mesh.devices.reshape(8, 4, 2, 4), ("z", "x", "c", "y"))
    dp = ("z", "x", "c")
    return jax.shard_map(
        local,
        mesh=fine,
        in_specs=(P(dp, None, None), P(dp, None, None), P("y", None), P(dp, None)),
        out_specs=(P(), P(dp, None, None), P("y", dp, None)),
        check_vma=False,
    )
```

time: 147 us -> 138 us (0.939)
  local copies, waits for them, and re-layouts: 10.8 us -> 0.02 us
  waiting for transfers between devices: 16.4 us -> 21.1 us
  Pallas kernels: 27.1 us -> 25.3 us
    unnamed x24 -> x8, local copies, waits for them, and re-layouts: 10.8 us -> 0.02 us
    all_to_all x3, waiting for transfers between devices: 8.64 us -> 13.6 us  [a2a(): return lax.all_to_all(v, axes, 0, 0, tiled=True)]
    pallas_call x9 -> x8, Pallas kernels: 10.6 us -> 8.01 us  [call(): pl.pallas_call(kernel, out_shape=out, in_specs=[VM] * len(args), out_spec...]
  transfers between devices with their start and end apart: 10 -> 10, of which waited for: 7 -> 7; matrix products, arithmetic and copies ran while one was open for 0% -> 0% of each run, Pallas kernels for 9% -> 7%
where the time goes in v3:
time: 138 us
  blocking collectives  65.9 us (48%)
  Pallas kernels  25.3 us (18%)
  starting transfers between devices  24.3 us (18%)
  waiting for transfers between devices  21.1 us (15%)
    all_to_all x5, blocking collectives, a2a(): return lax.all_to_all(v, axes, 0, 0, tiled=True)  65.9 us
    all_to_all x3, starting transfers between devices, a2a(): return lax.all_to_all(v, axes, 0, 0, tiled=True)  15.1 us
    all_to_all x3, waiting for transfers between devices, a2a(): return lax.all_to_all(v, axes, 0, 0, tiled=True)  13.6 us
    ppermute x7, starting transfers between devices, shift(): return lax.ppermute(v, axis, [(i, (i + k) % n) for i in range(n)])  9.26 us
    pallas_call x8, Pallas kernels, call(): pl.pallas_call(kernel, out_shape=out, in_specs=[VM] * len(args), out_spec...  8.01 us
    ppermute x7, waiting for transfers between devices, shift(): return lax.ppermute(v, axis, [(i, (i + k) % n) for i in range(n)])  7.53 us
    pallas_call x1, Pallas kernels, local(): pl.pallas_call(own_kernel, out_shape=jax.ShapeDtypeStruct((LIVE, 256), f3...  5.18 us
    pallas_call x1, Pallas kernels, local(): pl.pallas_call(head_kernel, out_shape=[jax.ShapeDtypeStruct((2, LIVE, 256...  4.81 us
  transfers between devices with their start and end apart: 10, of which 7 were waited for; matrix products, arithmetic and copies ran while one was open for 0% of the time, Pallas kernels for 7%

profile of v3, /device:TPU:1, one launch (start us, length us, event | category | flops | bytes accessed | tf_op | source)
XLA Modules:
  0.0 137.5 jit_solution(4723219420779315221)
XLA Ops:
  0.6 4.8 %shard_map.67 = (bf16[2,128,256]{2,1,0:T(8,128)(2,1)S(1)}, f32[32,8,128]{2,1,0:T(8,128)S(1)}, bf16[1024,256]{1,0:T(8,128)(2,1)S(1)}) custom-call(s32[1,256]{1,0:T(1,128)} %mask_ref.1, bf16[1,256,256]{2,1,0:T(8,128)(2,1)} %teach_hbm.1, bf16[1,256,256]{2,1,0:T(8,128)(2,1)} %student_hbm.1, bf16[8192,256]{1,0:T(8,128)(2,1)} %proto_hbm.3), custom_call_target="tpu_custom_call" | custom-call | tf_op jit(solution)/shard_map/pallas_call | solution.py:294
  5.5 3.3 %collective-permute-start = (bf16[2,128,256]{2,1,0:T(8,128)(2,1)S(1)}, bf16[2,128,256]{2,1,0:T(8,128)(2,1)S(1)}, u32[]{:S(2)}, u32[]{:S(2)}) collective-permute-start(bf16[2,128,256]{2,1,0:T(8,128)(2,1)S(1)} %get-tuple-element.21.rows_hbm), channel_id=1, source_target_pairs={{0,4},{4,0},{1,5},{5,1},{2,6},{6,2},{3,7},{7,3},{8,12},{12,8},{9,1... | collective-permute-start | bytes 393224 | tf_op jit(solution)/shard_map/ppermute | solution.py:285
  8.8 1.0 collective-permute-done
  9.9 1.9 %collective-permute-start.2 = (bf16[2,2,128,256]{3,2,1,0:T(8,128)(2,1)S(1)}, bf16[2,2,128,256]{3,2,1,0:T(8,128)(2,1)S(1)}, u32[]{:S(2)}, u32[]{:S(2)}) collective-permute-start(bf16[2,2,128,256]{3,2,1,0:T(8,128)(2,1)S(1)} %maximum_select_fusion.a_hbm), channel_id=1, source_target_pairs={{0,16},{8,24},{16,0},{24,8},{1,17},{9,25},{17,1},{25,9},{2,18},{10... | collective-permute-start | bytes 786440 | tf_op jit(solution)/shard_map/ppermute | solution.py:285
  11.8 1.2 collective-permute-start.3
  13.0 15.2 %all_to_all.40.recv_ref = f32[32,8,128]{2,1,0:T(8,128)S(1)} all-to-all(f32[32,8,128]{2,1,0:T(8,128)S(1)} %get-tuple-element.20), channel_id=1, replica_groups=mesh['z'=8,'x'=4,'c'=2,'y'=4] {'x','y','c'}, dimensions={0} | all-to-all | bytes 262144 | tf_op jit(solution)/shard_map/all_to_all | solution.py:281
  28.2 3.8 %shard_map.68 = (bf16[1024,1024]{1,0:T(8,128)(2,1)S(1)}, bf16[1024,256]{1,0:T(8,128)(2,1)S(1)}, f32[3,8,128]{2,1,0:T(8,128)S(1)}, f32[8,8,128]{2,1,0:T(8,128)}) custom-call(f32[32,8,128]{2,1,0:T(8,128)S(1)} %all_to_all.40.recv_ref, bf16[2,2,128,256]{3,2,1,0:T(8,128)(2,1)S(1)} %maximum_select_fusion.a_hbm, ...), custom_call_target="tpu_custom_call" | custom-call | tf_op jit(solution)/shard_map/pallas_call | solution.py:319
  32.0 8.2 %all-to-all-start.1 = ((f32[8,8,128]{2,1,0:T(8,128)}), f32[8,8,128]{2,1,0:T(8,128)S(1)}, u32[]{:S(2)}, u32[]{:S(2)}) async-start(f32[8,8,128]{2,1,0:T(8,128)} %get-tuple-element.23), calls=%async_computation.1 | async-start | bytes 65536 | tf_op jit(solution)/shard_map/all_to_all | solution.py:281
  40.2 1.4 %shard_map.69.extra_ref = f32[8,128]{1,0:T(8,128)S(1)} custom-call(bf16[1024,256]{1,0:T(8,128)(2,1)S(1)} %get-tuple-element.25.srows_ref, bf16[1024,256]{1,0:T(8,128)(2,1)S(1)} %get-tuple-element.22.mine_ref), custom_call_target="tpu_custom_call" | custom-call | flops 536870912 | bytes 1048576 | tf_op jit(solution)/shard_map/pallas_call | solution.py:265
  41.7 5.4 %all-to-all-done.1.recv_ref = f32[8,8,128]{2,1,0:T(8,128)S(1)} async-done(((f32[8,8,128]{2,1,0:T(8,128)}), f32[8,8,128]{2,1,0:T(8,128)S(1)}, u32[]{:S(2)}, u32[]{:S(2)}) %all-to-all-start.1) | async-done | bytes 32800 | tf_op jit(solution)/shard_map/all_to_all | solution.py:281
  47.1 0.4 shard_map.70
  47.5 15.2 %all_to_all.41.recv_ref = f32[32,16,128]{2,1,0:T(8,128)S(1)} all-to-all(f32[32,16,128]{2,1,0:T(8,128)S(1)} %shard_map.70), channel_id=1, replica_groups=mesh['z'=8,'x'=4,'c'=2,'y'=4] {'x','y','c'}, dimensions={0} | all-to-all | bytes 524288 | tf_op jit(solution)/shard_map/all_to_all | solution.py:281
  62.7 1.3 shard_map.71
  63.9 3.3 %all-to-all-start.3 = ((f32[8,8,128]{2,1,0:T(8,128)}), f32[8,8,128]{2,1,0:T(8,128)S(1)}, u32[]{:S(2)}, u32[]{:S(2)}) async-start(f32[8,8,128]{2,1,0:T(8,128)} %shard_map.71), calls=%async_computation.3 | async-start | bytes 65536 | tf_op jit(solution)/shard_map/all_to_all | solution.py:281
  67.3 3.4 %shard_map.72 = (f32[1024,1024]{1,0:T(8,128)}, bf16[1024,1024]{1,0:T(8,128)(2,1)}, f32[8,128]{1,0:T(8,128)S(1)}) custom-call(f32[32,16,128]{2,1,0:T(8,128)S(1)} %all_to_all.41.recv_ref, bf16[1024,256]{1,0:T(8,128)(2,1)S(1)} %get-tuple-element.25.srows_ref, bf16[1024,256]{1,0:T(8,128)(2,1)S(1)} %get-tuple-element.22.mine_ref, ...), custom_call_target="tpu_custom_call" | custom-call | flops 536870912 | bytes 8388608 | tf_op jit(solution)/shard_map/pallas_call | solution.py:338
  70.7 3.3 %all-to-all-done.3.recv_ref = f32[8,8,128]{2,1,0:T(8,128)S(1)} async-done(((f32[8,8,128]{2,1,0:T(8,128)}), f32[8,8,128]{2,1,0:T(8,128)S(1)}, u32[]{:S(2)}, u32[]{:S(2)}) %all-to-all-start.3) | async-done | bytes 32800 | tf_op jit(solution)/shard_map/all_to_all | solution.py:281
  74.1 0.4 shard_map.73
  74.5 12.6 %all_to_all.42.recv_ref = f32[32,8,128]{2,1,0:T(8,128)S(1)} all-to-all(f32[32,8,128]{2,1,0:T(8,128)S(1)} %shard_map.73), channel_id=1, replica_groups=mesh['z'=8,'x'=4,'c'=2,'y'=4] {'x','y','c'}, dimensions={0} | all-to-all | bytes 262144 | tf_op jit(solution)/shard_map/all_to_all | solution.py:281
  87.1 0.7 shard_map.74
  87.8 9.2 %all_to_all.43.recv_ref = f32[8,8,128]{2,1,0:T(8,128)S(1)} all-to-all(f32[8,8,128]{2,1,0:T(8,128)S(1)} %shard_map.74), channel_id=1, replica_groups=mesh['z'=8,'x'=4,'c'=2,'y'=4] {'z'}, dimensions={0} | all-to-all | bytes 65536 | tf_op jit(solution)/shard_map/all_to_all | solution.py:281
  97.0 0.7 shard_map.75
  97.7 13.8 %all_to_all.44.recv_ref = bf16[32,32,128]{2,1,0:T(8,128)(2,1)S(1)} all-to-all(bf16[32,32,128]{2,1,0:T(8,128)(2,1)S(1)} %get-tuple-element.29), channel_id=1, replica_groups=mesh['z'=8,'x'=4,'c'=2,'y'=4] {'x','y','c'}, dimensions={0} | all-to-all | bytes 524288 | tf_op jit(solution)/shard_map/all_to_all | solution.py:281
  111.5 1.9 %shard_map.76 = (bf16[8,144,256]{2,1,0:T(8,128)(2,1)}, f32[2,8,128]{2,1,0:T(8,128)S(1)}) custom-call(bf16[32,32,128]{2,1,0:T(8,128)(2,1)S(1)} %all_to_all.44.recv_ref, f32[3,8,128]{2,1,0:T(8,128)S(1)} %get-tuple-element.26.stat_ref, f32[8,128]{1,0:T(8,128)S(1)} %get-tuple-element.30.col_ref, bf16[1024,1024]{1,0:T(8,128)(2,1)S(1)} %get-tuple-element.24.et_ref, ...), custom_call_target="tpu_custom_call" | custom-call | tf_op jit(solution)/shard_map/pallas_call | solution.py:265
  113.4 3.5 %all-to-all-start.7 = ((bf16[8,144,256]{2,1,0:T(8,128)(2,1)}), bf16[8,144,256]{2,1,0:T(8,128)(2,1)S(1)}, u32[]{:S(2)}, u32[]{:S(2)}) async-start(bf16[8,144,256]{2,1,0:T(8,128)(2,1)} %get-tuple-element.32), calls=%async_computation.7 | async-start | bytes 1179648 | tf_op jit(solution)/shard_map/all_to_all | solution.py:281
  117.0 5.2 %shard_map.77.a_ref = f32[128,256]{1,0:T(8,128)S(1)} custom-call(bf16[32,32,128]{2,1,0:T(8,128)(2,1)S(1)} %all_to_all.44.recv_ref, f32[2,8,128]{2,1,0:T(8,128)S(1)} %get-tuple-element.33.scale_ref, f32[3,8,128]{2,1,0:T(8,128)S(1)} %get-tuple-element.26.stat_ref, f32[8,128]{1,0:T(8,128)S(1)} %get-tuple-element.27.extra_ref.norm_ref, ...), custom_call_target="tpu_custom_call" | custom-call | flops 2147483648 | bytes 4194304 | tf_op jit(solution)/shard_map/pallas_call | solution.py:369
  122.4 1.9 %collective-permute-start.5 = (f32[128,256]{1,0:T(8,128)S(1)}, f32[128,256]{1,0:T(8,128)S(1)}, u32[]{:S(2)}, u32[]{:S(2)}) collective-permute-start(f32[128,256]{1,0:T(8,128)S(1)} %shard_map.77.a_ref), channel_id=1, source_target_pairs={{0,2},{1,3},{2,0},{3,1},{4,6},{5,7},{6,4},{7,5},{8,10},{9,11},{10,... | collective-permute-start | bytes 393224 | tf_op jit(solution)/shard_map/ppermute | solution.py:285
  124.4 0.6 collective-permute-start.6
  124.9 3.7 %collective-permute-done.4.b_ref = f32[128,256]{1,0:T(8,128)S(1)} collective-permute-done((f32[128,256]{1,0:T(8,128)S(1)}, f32[128,256]{1,0:T(8,128)S(1)}, u32[]{:S(2)}, u32[]{:S(2)}) %collective-permute-start.4) | collective-permute-done | bytes 131104 | tf_op jit(solution)/shard_map/ppermute | solution.py:285
  128.7 2.2 %collective-permute-done.5.c_ref = f32[128,256]{1,0:T(8,128)S(1)} collective-permute-done((f32[128,256]{1,0:T(8,128)S(1)}, f32[128,256]{1,0:T(8,128)S(1)}, u32[]{:S(2)}, u32[]{:S(2)}) %collective-permute-start.5) | collective-permute-done | bytes 131104 | tf_op jit(solution)/shard_map/ppermute | solution.py:285
  130.9 0.6 collective-permute-done.6.d_ref
  131.5 4.8 %all-to-all-done.7.recv_ref = bf16[8,144,256]{2,1,0:T(8,128)(2,1)S(1)} async-done(((bf16[8,144,256]{2,1,0:T(8,128)(2,1)}), bf16[8,144,256]{2,1,0:T(8,128)(2,1)S(1)}, u32[]{:S(2)}, u32[]{:S(2)}) %all-to-all-start.7) | async-done | bytes 589856 | tf_op jit(solution)/shard_map/all_to_all | solution.py:281
  136.3 1.2 shard_map.78
  (14 shorter events, 0.4 us)
Async XLA Ops:
  5.5 22.7 %copy-start.2 = (bf16[2,128,256]{2,1,0:T(8,128)(2,1)}, bf16[2,128,256]{2,1,0:T(8,128)(2,1)S(1)}, u32[]{:S(2)}) copy-start(bf16[2,128,256]{2,1,0:T(8,128)(2,1)S(1)} %get-tuple-element.21.rows_hbm) | copy-start | bytes 393220
  5.5 4.3 %collective-permute-start = (bf16[2,128,256]{2,1,0:T(8,128)(2,1)S(1)}, bf16[2,128,256]{2,1,0:T(8,128)(2,1)S(1)}, u32[]{:S(2)}, u32[]{:S(2)}) collective-permute-start(bf16[2,128,256]{2,1,0:T(8,128)(2,1)S(1)} %get-tuple-element.21.rows_hbm), channel_id=1, source_target_pairs={{0,4},{4,0},{1,5},{5,1},{2,6},{6,2},{3,7},{7,3},{8,12},{12,8},{9,1... | collective-permute-start | bytes 393224 | tf_op jit(solution)/shard_map/ppermute | solution.py:285
  9.8 18.3 %collective-permute-start.1 = (bf16[2,2,128,256]{3,2,1,0:T(8,128)(2,1)S(1)}, bf16[2,2,128,256]{3,2,1,0:T(8,128)(2,1)S(1)}, u32[]{:S(2)}, u32[]{:S(2)}) collective-permute-start(bf16[2,2,128,256]{3,2,1,0:T(8,128)(2,1)S(1)} %maximum_select_fusion.a_hbm), channel_id=1, source_target_pairs={{0,8},{8,16},{16,24},{24,0},{1,9},{9,17},{17,25},{25,1},{2,10},{10... | collective-permute-start | bytes 786440 | tf_op jit(solution)/shard_map/ppermute | solution.py:285
  9.9 18.2 %collective-permute-start.2 = (bf16[2,2,128,256]{3,2,1,0:T(8,128)(2,1)S(1)}, bf16[2,2,128,256]{3,2,1,0:T(8,128)(2,1)S(1)}, u32[]{:S(2)}, u32[]{:S(2)}) collective-permute-start(bf16[2,2,128,256]{3,2,1,0:T(8,128)(2,1)S(1)} %maximum_select_fusion.a_hbm), channel_id=1, source_target_pairs={{0,16},{8,24},{16,0},{24,8},{1,17},{9,25},{17,1},{25,9},{2,18},{10... | collective-permute-start | bytes 786440 | tf_op jit(solution)/shard_map/ppermute | solution.py:285
  11.8 16.3 %collective-permute-start.3 = (bf16[2,2,128,256]{3,2,1,0:T(8,128)(2,1)S(1)}, bf16[2,2,128,256]{3,2,1,0:T(8,128)(2,1)S(1)}, u32[]{:S(2)}, u32[]{:S(2)}) collective-permute-start(bf16[2,2,128,256]{3,2,1,0:T(8,128)(2,1)S(1)} %maximum_select_fusion.a_hbm), channel_id=1, source_target_pairs={{0,24},{8,0},{16,8},{24,16},{1,25},{9,1},{17,9},{25,17},{2,26},{10... | collective-permute-start | bytes 786440 | tf_op jit(solution)/shard_map/ppermute | solution.py:285
  32.0 15.1 %all-to-all-start.1 = ((f32[8,8,128]{2,1,0:T(8,128)}), f32[8,8,128]{2,1,0:T(8,128)S(1)}, u32[]{:S(2)}, u32[]{:S(2)}) async-start(f32[8,8,128]{2,1,0:T(8,128)} %get-tuple-element.23), calls=%async_computation.1 | async-start | bytes 65536 | tf_op jit(solution)/shard_map/all_to_all | solution.py:281
  63.9 10.1 %all-to-all-start.3 = ((f32[8,8,128]{2,1,0:T(8,128)}), f32[8,8,128]{2,1,0:T(8,128)S(1)}, u32[]{:S(2)}, u32[]{:S(2)}) async-start(f32[8,8,128]{2,1,0:T(8,128)} %shard_map.71), calls=%async_computation.3 | async-start | bytes 65536 | tf_op jit(solution)/shard_map/all_to_all | solution.py:281
  74.1 22.9 %copy-start.1 = (bf16[1024,1024]{1,0:T(8,128)(2,1)S(1)}, bf16[1024,1024]{1,0:T(8,128)(2,1)}, u32[]{:S(2)}) copy-start(bf16[1024,1024]{1,0:T(8,128)(2,1)} %get-tuple-element.28.w_ref) | copy-start | bytes 6291460
  74.5 37.0 %copy-start = (f32[1024,1024]{1,0:T(8,128)S(1)}, f32[1024,1024]{1,0:T(8,128)}, u32[]{:S(2)}) copy-start(f32[1024,1024]{1,0:T(8,128)} %get-tuple-element.31.prob_ref) | copy-start | bytes 12582916
  113.4 22.9 %all-to-all-start.7 = ((bf16[8,144,256]{2,1,0:T(8,128)(2,1)}), bf16[8,144,256]{2,1,0:T(8,128)(2,1)S(1)}, u32[]{:S(2)}, u32[]{:S(2)}) async-start(bf16[8,144,256]{2,1,0:T(8,128)(2,1)} %get-tuple-element.32), calls=%async_computation.7 | async-start | bytes 1179648 | tf_op jit(solution)/shard_map/all_to_all | solution.py:281
  116.9 19.4 %copy-start.3 = (s32[1,256]{1,0:T(1,128)S(1)}, s32[1,256]{1,0:T(1,128)}, u32[]{:S(2)}) copy-start(s32[1,256]{1,0:T(1,128)} %mask_ref.1) | copy-start | bytes 3076
  122.1 6.5 %collective-permute-start.4 = (f32[128,256]{1,0:T(8,128)S(1)}, f32[128,256]{1,0:T(8,128)S(1)}, u32[]{:S(2)}, u32[]{:S(2)}) collective-permute-start(f32[128,256]{1,0:T(8,128)S(1)} %shard_map.77.a_ref), channel_id=1, source_target_pairs={{0,1},{1,2},{2,3},{3,0},{4,5},{5,6},{6,7},{7,4},{8,9},{9,10},{10,1... | collective-permute-start | bytes 393224 | tf_op jit(solution)/shard_map/ppermute | solution.py:285
  122.4 8.4 %collective-permute-start.5 = (f32[128,256]{1,0:T(8,128)S(1)}, f32[128,256]{1,0:T(8,128)S(1)}, u32[]{:S(2)}, u32[]{:S(2)}) collective-permute-start(f32[128,256]{1,0:T(8,128)S(1)} %shard_map.77.a_ref), channel_id=1, source_target_pairs={{0,2},{1,3},{2,0},{3,1},{4,6},{5,7},{6,4},{7,5},{8,10},{9,11},{10,... | collective-permute-start | bytes 393224 | tf_op jit(solution)/shard_map/ppermute | solution.py:285
  124.4 7.1 %collective-permute-start.6 = (f32[128,256]{1,0:T(8,128)S(1)}, f32[128,256]{1,0:T(8,128)S(1)}, u32[]{:S(2)}, u32[]{:S(2)}) collective-permute-start(f32[128,256]{1,0:T(8,128)S(1)} %shard_map.77.a_ref), channel_id=1, source_target_pairs={{0,3},{1,0},{2,1},{3,2},{4,7},{5,4},{6,5},{7,6},{8,11},{9,8},{10,9... | collective-permute-start | bytes 393224 | tf_op jit(solution)/shard_map/ppermute | solution.py:285

commit v4 on v3

--- a/solution.py
+++ b/solution.py
@@ -52,7 +52,7 @@
 def head_kernel(
     mask_hbm, teach_hbm, student_hbm, proto_hbm, own_ref, out_ref, mine_ref, mask_ref, teach_ref, student_ref, proto_ref, sems
 ):
-    chunks = 8
+    chunks = 4
     tall = proto_ref.shape[0] // chunks
     small = ((mask_hbm, mask_ref), (teach_hbm, teach_ref), (student_hbm, student_ref))
     first = [pltpu.make_async_copy(src, dst, sems.at[chunks + i]) for i, (src, dst) in enumerate(small)]
@@ -74,25 +74,18 @@
     peak = None
     for i in range(chunks):
         copies[i].wait()
-        mine_ref[128 * i : 128 * (i + 1), :] = proto_ref[pl.ds(pl.multiple_of(i * tall + image * 128, 128), 128), :]
-        logits = dot(proto_ref[i * tall : (i + 1) * tall, :], rows, NT)
-        top = jnp.max(logits, axis=0, keepdims=True)
+        for j in (2 * i, 2 * i + 1):
+            mine_ref[128 * j : 128 * (j + 1), :] = proto_ref[pl.ds(pl.multiple_of(j * 1024 + image * 128, 128), 128), :]
+        half = tall // 2
+        low = dot(proto_ref[i * tall : i * tall + half, :], rows, NT)
+        high = dot(proto_ref[i * tall + half : (i + 1) * tall, :], rows, NT)
+        top = jnp.max(jnp.maximum(low, high), axis=0, keepdims=True)
         peak = top if peak is None else jnp.maximum(peak, top)
     tile = jnp.concatenate([peak * TEACHER_INV, jnp.broadcast_to(count, (1, LIVE)), jnp.zeros((6, LIVE), f32)], axis=0)
     out_ref[...] = jnp.broadcast_to(tile[None], out_ref.shape)
 
 
-def expo_kernel(recv_ref, a_hbm, b_hbm, c_hbm, d_hbm, mine_ref, et_ref, srows_ref, stat_ref, pay_ref, trows, sems):
-    x = lax.axis_index("x")
-    tcopies, scopies = [], []
-    for k, piece in enumerate((a_hbm, b_hbm, c_hbm, d_hbm)):
-        start = pl.multiple_of(((x + 4 - k) & 3) * 256, 256)
-        for core in range(2):
-            at = pl.ds(start + core * 128, 128)
-            tcopies.append(pltpu.make_async_copy(piece.at[core, 0], trows.at[at], sems.at[k * 4 + core]))
-            scopies.append(pltpu.make_async_copy(piece.at[core, 1], srows_ref.at[at], sems.at[k * 4 + 2 + core]))
-    for copy in tcopies + scopies:
-        copy.start()
+def expo_kernel(recv_ref, a_ref, b_ref, c_ref, d_ref, mine_ref, et_ref, srows_ref, stat_ref, pay_ref, peak_ref, live_ref):
     peaks, counts = [], []
     for x in range(4):
         for core in range(2):
@@ -102,26 +95,27 @@
                 top = jnp.maximum(top, recv_ref[i, 0:1, :])
             peaks.append(top)
             counts.append(recv_ref[at[0], 1:2, :])
-    peak = jnp.concatenate(peaks, axis=1)
     count = jnp.concatenate(counts, axis=0)
     slot = lax.broadcasted_iota(jnp.int32, (8, 128), 1).astype(f32)
     live = jnp.where(slot < count, 1.0, 0.0)
     stat_ref[0] = live
     stat_ref[1] = live / count
     stat_ref[2] = jnp.concatenate(peaks, axis=0)
-    live_rows = jnp.broadcast_to(to_lanes(live), (16, 1024)).astype(bf16)
+    for x in range(4):
+        peak_ref[x : x + 1, :] = jnp.concatenate(peaks[2 * x : 2 * x + 2], axis=1)
+        live_ref[x : x + 1, :] = jnp.concatenate([live[2 * x : 2 * x + 1], live[2 * x + 1 : 2 * x + 2]], axis=1)
     total = jnp.zeros((16, 1024), f32)
-    for copy in tcopies:
-        copy.wait()
-    for r in range(4):
-        at = slice(256 * r, 256 * (r + 1))
-        logits = dot(mine_ref[...], trows[at, :], NT)
-        block = jnp.exp(logits * TEACHER_INV - peak[:, at]).astype(bf16)
-        et_ref[:, at] = block
-        total += dot(live_rows[:, at], block, NT)
+    for k, piece in enumerate((a_ref, b_ref, c_ref, d_ref)):
+        x = (lax.axis_index("x") + 4 - k) & 3
+        start = pl.multiple_of(x * 256, 256)
+        rows = jnp.concatenate([piece[0, 0], piece[1, 0]], axis=0)
+        logits = dot(mine_ref[...], rows, NT)
+        block = jnp.exp(logits * TEACHER_INV - peak_ref[pl.ds(x, 1), :]).astype(bf16)
+        et_ref[:, pl.ds(start, 256)] = block
+        total += dot(jnp.broadcast_to(live_ref[pl.ds(x, 1), :], (16, 256)).astype(bf16), block, NT)
+        for core in range(2):
+            srows_ref[pl.ds(pl.multiple_of(start + core * 128, 128), 128), :] = piece[core, 1]
     pay_ref[...] = jnp.broadcast_to(to_tile(total[0:1])[None], pay_ref.shape)
-    for copy in scopies:
-        copy.wait()
 
 
 def col_kernel(recv_ref, et_ref, extra_ref, pay_ref):
@@ -190,7 +184,7 @@
     hi = loss.astype(bf16).astype(f32)
     mid = (loss - hi).astype(bf16).astype(f32)
     lo = loss - hi - mid
-    which = lax.broadcasted_iota(jnp.int32, (16, 256), 0)
+    which = lax.broadcasted_iota(jnp.int32, (8, 256), 0)
     tail = jnp.where(which == 0, hi, jnp.where(which == 1, mid, jnp.where(which == 2, lo, 0.0))).astype(bf16)
     coef = weight * (LOSS_SCALE / (IMAGES * 0.1))
     scale_ref[0] = coef
@@ -205,11 +199,19 @@
         part = dot(grad, srows_ref[...], NN).astype(bf16)
         for i in (0, 1):
             pout_ref[2 * j + i, 0:128, :] = part[128 * i : 128 * (i + 1)]
-            pout_ref[2 * j + i, 128:144, :] = tail
+            pout_ref[2 * j + i, 128:136, :] = tail
+
+
+def column(row, wide):
+    return jnp.concatenate([jnp.broadcast_to(row, (128, 128)).T] * (wide // 128), axis=1)
+
+
+def own_image():
+    return pl.ds(lax.axis_index("x") * 2 + lax.axis_index("c"), 1)
 
 
 def own_kernel(recv_ref, scale_ref, stat_ref, norm_ref, rows_hbm, proto_hbm, out_ref, rows_ref, proto_ref, sems):
-    chunks = 8
+    chunks = 4
     tall = proto_ref.shape[0] // chunks
     rows_copy = pltpu.make_async_copy(rows_hbm, rows_ref, sems.at[chunks])
     copies = [
@@ -219,34 +221,31 @@
     for copy in [rows_copy] + copies:
         copy.start()
     y = lax.axis_index("y")
-    image = lax.axis_index("x") * 2 + lax.axis_index("c")
-
-    def column(row):
-        return jnp.concatenate([jnp.broadcast_to(row, (LIVE, 128)).T] * 8, axis=1)
-
-    peak = column(stat_ref[2, pl.ds(image, 1), :])
-    norm = column(norm_ref[pl.ds(image, 1), :])
-    coef = column(scale_ref[0, pl.ds(image, 1), :])
-    scale = column(scale_ref[1, pl.ds(image, 1), :])
+    peak = column(stat_ref[2, own_image(), :], 1024)
+    norm = column(norm_ref[own_image(), :], 1024)
+    coef = column(scale_ref[0, own_image(), :], 1024)
+    scale = column(scale_ref[1, own_image(), :], 1024)
     cols = [recv_ref[(x * 4 + y) * 2 + c, 16:32, :].astype(f32) for x in range(4) for c in range(2)]
     rows_copy.wait()
     rows = rows_ref[...].reshape(2 * LIVE, 256)
     total = jnp.zeros((LIVE, 256), f32)
-    for i in range(chunks):
+    for i in range(8):
+        if i % 2 == 0:
+            copies[i // 2].wait()
         col = jnp.concatenate([v[8 + i : 9 + i, :] for v in cols], axis=1)
-        copies[i].wait()
-        block = proto_ref[i * tall : (i + 1) * tall, :]
+        block = proto_ref[1024 * i : 1024 * (i + 1), :]
         logits = dot(rows, block, NT)
         teach = jnp.exp(logits[0:LIVE] * TEACHER_INV - peak).astype(bf16).astype(f32)
         prob = jnp.exp(logits[LIVE:] * STUDENT_INV - norm)
         grad = (prob * coef - teach * (col * scale)).astype(bf16)
         total += dot(grad, block, NN)
-    out_ref[...] = total
+    out_ref[...] = total.astype(bf16)
 
 
 def end_kernel(mask_ref, recv_ref, a_ref, b_ref, c_ref, d_ref, student_ref, proto_ref, loss_ref):
     pick = selection(mask_ref[...]).astype(bf16)
-    rows = (a_ref[...] + c_ref[...]) + (b_ref[...] + d_ref[...])
+    parts = [ref[...].astype(f32) for ref in (a_ref, b_ref, c_ref, d_ref)]
+    rows = (parts[0] + parts[2]) + (parts[1] + parts[3])
     hi = rows.astype(bf16)
     rest = rows - hi.astype(f32)
     mid = rest.astype(bf16)
@@ -298,14 +297,14 @@
             jax.ShapeDtypeStruct((32, 8, 128), f32),
             jax.ShapeDtypeStruct((1024, 256), bf16),
         ],
-        in_specs=[pl.BlockSpec(memory_space=pltpu.HBM)] * 4,
+        in_specs=[HBM] * 4,
         out_specs=[VM] * 3,
         scratch_shapes=[
             pltpu.VMEM((1, 256), jnp.int32),
             pltpu.VMEM((1, 256, 256), bf16),
             pltpu.VMEM((1, 256, 256), bf16),
             pltpu.VMEM((8192, 256), bf16),
-            pltpu.SemaphoreType.DMA((11,)),
+            pltpu.SemaphoreType.DMA((7,)),
         ],
         compiler_params=pltpu.CompilerParams(vmem_limit_bytes=32 << 20),
     )(*(in_hbm(v) for v in (patch_mask, teacher_feats, student_feats, prototypes)))
@@ -316,19 +315,11 @@
 
     peak_recv = a2a(peak_pay, PLANE)
 
-    et, srows, stat, pay = pl.pallas_call(
+    et, srows, stat, pay = call(
         expo_kernel,
-        out_shape=[
-            jax.ShapeDtypeStruct((1024, 1024), bf16),
-            jax.ShapeDtypeStruct((1024, 256), bf16),
-            jax.ShapeDtypeStruct((3, 8, 128), f32),
-            jax.ShapeDtypeStruct((8, 8, 128), f32),
-        ],
-        in_specs=[VM] + [HBM] * 4 + [VM],
-        out_specs=[VM] * 4,
-        scratch_shapes=[pltpu.VMEM((1024, 256), bf16), pltpu.SemaphoreType.DMA((16,))],
-        compiler_params=pltpu.CompilerParams(vmem_limit_bytes=16 << 20),
-    )(peak_recv, *parts, mine)
+        [((1024, 1024), bf16), ((1024, 256), bf16), ((3, 8, 128), f32), ((8, 8, 128), f32)],
+        peak_recv, *parts, mine, limit=16, scratch=[pltpu.VMEM((8, 256), f32)] * 2,
+    )
 
     (student_sum,) = call(student_sum_kernel, [((8, 128), f32)], srows, mine, cost=1 << 29, limit=16)
 
@@ -363,18 +354,18 @@
     recv = a2a(pay, PLANE)
 
     proto_part, scale = call(
-        grad_kernel, [((8, 144, 256), bf16), ((2, 8, 128), f32)], recv, stat, col, et, prob, srows, limit=24
+        grad_kernel, [((8, 136, 256), bf16), ((2, 8, 128), f32)], recv, stat, col, et, prob, srows, limit=24
     )
     proto_recv = a2a(proto_part, "z")
     student_rows = pl.pallas_call(
         own_kernel,
-        out_shape=jax.ShapeDtypeStruct((LIVE, 256), f32),
-        in_specs=[VM] * 4 + [pl.BlockSpec(memory_space=pltpu.HBM)] * 2,
+        out_shape=jax.ShapeDtypeStruct((LIVE, 256), bf16),
+        in_specs=[VM] * 4 + [HBM] * 2,
         out_specs=VM,
         scratch_shapes=[
             pltpu.VMEM((2, LIVE, 256), bf16),
             pltpu.VMEM((8192, 256), bf16),
-            pltpu.SemaphoreType.DMA((9,)),
+            pltpu.SemaphoreType.DMA((5,)),
         ],
         compiler_params=pltpu.CompilerParams(vmem_limit_bytes=24 << 20),
         cost_estimate=pl.CostEstimate(flops=1 << 31, bytes_accessed=4 << 20, transcendentals=2 << 20),

time: 138 us -> 134 us (0.971)
  Pallas kernels: 25.3 us -> 21.5 us
    pallas_call x2 -> x1, Pallas kernels: 9.03 us -> 4.42 us  [local(): pl.pallas_call(own_kernel, out_shape=jax.ShapeDtypeStruct((LIVE, 256), bf...]
    all_to_all x3, waiting for transfers between devices: 13.6 us -> 16.6 us  [a2a(): return lax.all_to_all(v, axes, 0, 0, tiled=True)]
    ppermute x7, waiting for transfers between devices: 7.53 us -> 4.67 us  [shift(): return lax.ppermute(v, axis, [(i, (i + k) % n) for i in range(n)])]
    pallas_call x8 -> x9, Pallas kernels: 8.01 us -> 10.4 us  [call(): pl.pallas_call(kernel, out_shape=out, in_specs=[VM] * len(args), out_spec...]
    pallas_call x1, Pallas kernels: 4.81 us -> 3.26 us  [local(): pl.pallas_call(head_kernel, out_shape=[jax.ShapeDtypeStruct((2, LIVE, 256...]
where the time goes in v4:
time: 134 us
  blocking collectives  65.8 us (49%)
  starting transfers between devices  24.3 us (18%)
  Pallas kernels  21.5 us (16%)
  waiting for transfers between devices  21.3 us (16%)
    all_to_all x5, blocking collectives, a2a(): return lax.all_to_all(v, axes, 0, 0, tiled=True)  65.8 us
    all_to_all x3, waiting for transfers between devices, a2a(): return lax.all_to_all(v, axes, 0, 0, tiled=True)  16.6 us
    all_to_all x3, starting transfers between devices, a2a(): return lax.all_to_all(v, axes, 0, 0, tiled=True)  15.1 us
    pallas_call x9, Pallas kernels, call(): pl.pallas_call(kernel, out_shape=out, in_specs=[VM] * len(args), out_spec...  10.4 us
    ppermute x7, starting transfers between devices, shift(): return lax.ppermute(v, axis, [(i, (i + k) % n) for i in range(n)])  9.26 us
    ppermute x7, waiting for transfers between devices, shift(): return lax.ppermute(v, axis, [(i, (i + k) % n) for i in range(n)])  4.67 us
    pallas_call x1, Pallas kernels, local(): pl.pallas_call(own_kernel, out_shape=jax.ShapeDtypeStruct((LIVE, 256), bf...  4.42 us
    pallas_call x1, Pallas kernels, local(): pl.pallas_call(student_prob_kernel, out_shape=[pltpu.HBM((1024, 1024), f3...  3.45 us
  transfers between devices with their start and end apart: 10, of which 7 were waited for; matrix products, arithmetic and copies ran while one was open for 0% of the time, Pallas kernels for 7%

profile of v4, /device:TPU:1, one launch (start us, length us, event | category | flops | bytes accessed | tf_op | source)
XLA Modules:
  0.0 133.7 jit_solution(14730112216232657965)
XLA Ops:
  0.6 3.3 %shard_map.67 = (bf16[2,128,256]{2,1,0:T(8,128)(2,1)S(1)}, f32[32,8,128]{2,1,0:T(8,128)S(1)}, bf16[1024,256]{1,0:T(8,128)(2,1)S(1)}) custom-call(s32[1,256]{1,0:T(1,128)} %mask_ref.1, bf16[1,256,256]{2,1,0:T(8,128)(2,1)} %teach_hbm.1, bf16[1,256,256]{2,1,0:T(8,128)(2,1)} %student_hbm.1, bf16[8192,256]{1,0:T(8,128)(2,1)} %proto_hbm.3), custom_call_target="tpu_custom_call" | custom-call | tf_op jit(solution)/shard_map/pallas_call | solution.py:293
  3.9 3.3 %collective-permute-start = (bf16[2,128,256]{2,1,0:T(8,128)(2,1)S(1)}, bf16[2,128,256]{2,1,0:T(8,128)(2,1)S(1)}, u32[]{:S(2)}, u32[]{:S(2)}) collective-permute-start(bf16[2,128,256]{2,1,0:T(8,128)(2,1)S(1)} %get-tuple-element.21.rows_hbm), channel_id=1, source_target_pairs={{0,4},{4,0},{1,5},{5,1},{2,6},{6,2},{3,7},{7,3},{8,12},{12,8},{9,1... | collective-permute-start | bytes 393224 | tf_op jit(solution)/shard_map/ppermute | solution.py:284
  7.2 1.0 collective-permute-done
  8.3 1.9 %collective-permute-start.2 = (bf16[2,2,128,256]{3,2,1,0:T(8,128)(2,1)S(1)}, bf16[2,2,128,256]{3,2,1,0:T(8,128)(2,1)S(1)}, u32[]{:S(2)}, u32[]{:S(2)}) collective-permute-start(bf16[2,2,128,256]{3,2,1,0:T(8,128)(2,1)S(1)} %maximum_select_fusion.a_ref), channel_id=1, source_target_pairs={{0,16},{8,24},{16,0},{24,8},{1,17},{9,25},{17,1},{25,9},{2,18},{10... | collective-permute-start | bytes 786440 | tf_op jit(solution)/shard_map/ppermute | solution.py:284
  10.2 1.2 collective-permute-start.3
  11.4 15.2 %all_to_all.40.recv_ref = f32[32,8,128]{2,1,0:T(8,128)S(1)} all-to-all(f32[32,8,128]{2,1,0:T(8,128)S(1)} %get-tuple-element.20), channel_id=1, replica_groups=mesh['z'=8,'x'=4,'c'=2,'y'=4] {'x','y','c'}, dimensions={0} | all-to-all | bytes 262144 | tf_op jit(solution)/shard_map/all_to_all | solution.py:280
  26.6 2.4 %shard_map.68 = (bf16[1024,1024]{1,0:T(8,128)(2,1)S(1)}, bf16[1024,256]{1,0:T(8,128)(2,1)S(1)}, f32[3,8,128]{2,1,0:T(8,128)S(1)}, f32[8,8,128]{2,1,0:T(8,128)}) custom-call(f32[32,8,128]{2,1,0:T(8,128)S(1)} %all_to_all.40.recv_ref, bf16[2,2,128,256]{3,2,1,0:T(8,128)(2,1)S(1)} %maximum_select_fusion.a_ref, ...), custom_call_target="tpu_custom_call" | custom-call | tf_op jit(solution)/shard_map/pallas_call | solution.py:264
  29.0 8.2 %all-to-all-start.1 = ((f32[8,8,128]{2,1,0:T(8,128)}), f32[8,8,128]{2,1,0:T(8,128)S(1)}, u32[]{:S(2)}, u32[]{:S(2)}) async-start(f32[8,8,128]{2,1,0:T(8,128)} %get-tuple-element.23), calls=%async_computation.1 | async-start | bytes 65536 | tf_op jit(solution)/shard_map/all_to_all | solution.py:280
  37.1 1.4 %shard_map.69.extra_ref = f32[8,128]{1,0:T(8,128)S(1)} custom-call(bf16[1024,256]{1,0:T(8,128)(2,1)S(1)} %get-tuple-element.25.srows_ref, bf16[1024,256]{1,0:T(8,128)(2,1)S(1)} %get-tuple-element.22.mine_ref), custom_call_target="tpu_custom_call" | custom-call | flops 536870912 | bytes 1048576 | tf_op jit(solution)/shard_map/pallas_call | solution.py:264
  38.6 5.5 %all-to-all-done.1.recv_ref = f32[8,8,128]{2,1,0:T(8,128)S(1)} async-done(((f32[8,8,128]{2,1,0:T(8,128)}), f32[8,8,128]{2,1,0:T(8,128)S(1)}, u32[]{:S(2)}, u32[]{:S(2)}) %all-to-all-start.1) | async-done | bytes 32800 | tf_op jit(solution)/shard_map/all_to_all | solution.py:280
  44.1 0.4 shard_map.70
  44.5 15.0 %all_to_all.41.recv_ref = f32[32,16,128]{2,1,0:T(8,128)S(1)} all-to-all(f32[32,16,128]{2,1,0:T(8,128)S(1)} %shard_map.70), channel_id=1, replica_groups=mesh['z'=8,'x'=4,'c'=2,'y'=4] {'x','y','c'}, dimensions={0} | all-to-all | bytes 524288 | tf_op jit(solution)/shard_map/all_to_all | solution.py:280
  59.6 1.3 shard_map.71
  60.9 3.3 %all-to-all-start.3 = ((f32[8,8,128]{2,1,0:T(8,128)}), f32[8,8,128]{2,1,0:T(8,128)S(1)}, u32[]{:S(2)}, u32[]{:S(2)}) async-start(f32[8,8,128]{2,1,0:T(8,128)} %shard_map.71), calls=%async_computation.3 | async-start | bytes 65536 | tf_op jit(solution)/shard_map/all_to_all | solution.py:280
  64.2 3.4 %shard_map.72 = (f32[1024,1024]{1,0:T(8,128)}, bf16[1024,1024]{1,0:T(8,128)(2,1)}, f32[8,128]{1,0:T(8,128)S(1)}) custom-call(f32[32,16,128]{2,1,0:T(8,128)S(1)} %all_to_all.41.recv_ref, bf16[1024,256]{1,0:T(8,128)(2,1)S(1)} %get-tuple-element.25.srows_ref, bf16[1024,256]{1,0:T(8,128)(2,1)S(1)} %get-tuple-element.22.mine_ref, ...), custom_call_target="tpu_custom_call" | custom-call | flops 536870912 | bytes 8388608 | tf_op jit(solution)/shard_map/pallas_call | solution.py:329
  67.7 3.3 %all-to-all-done.3.recv_ref = f32[8,8,128]{2,1,0:T(8,128)S(1)} async-done(((f32[8,8,128]{2,1,0:T(8,128)}), f32[8,8,128]{2,1,0:T(8,128)S(1)}, u32[]{:S(2)}, u32[]{:S(2)}) %all-to-all-start.3) | async-done | bytes 32800 | tf_op jit(solution)/shard_map/all_to_all | solution.py:280
  71.0 0.4 shard_map.73
  71.4 12.6 %all_to_all.42.recv_ref = f32[32,8,128]{2,1,0:T(8,128)S(1)} all-to-all(f32[32,8,128]{2,1,0:T(8,128)S(1)} %shard_map.73), channel_id=1, replica_groups=mesh['z'=8,'x'=4,'c'=2,'y'=4] {'x','y','c'}, dimensions={0} | all-to-all | bytes 262144 | tf_op jit(solution)/shard_map/all_to_all | solution.py:280
  84.0 0.7 shard_map.74
  84.7 9.2 %all_to_all.43.recv_ref = f32[8,8,128]{2,1,0:T(8,128)S(1)} all-to-all(f32[8,8,128]{2,1,0:T(8,128)S(1)} %shard_map.74), channel_id=1, replica_groups=mesh['z'=8,'x'=4,'c'=2,'y'=4] {'z'}, dimensions={0} | all-to-all | bytes 65536 | tf_op jit(solution)/shard_map/all_to_all | solution.py:280
  93.9 0.7 shard_map.75
  94.6 13.8 %all_to_all.44.recv_ref = bf16[32,32,128]{2,1,0:T(8,128)(2,1)S(1)} all-to-all(bf16[32,32,128]{2,1,0:T(8,128)(2,1)S(1)} %get-tuple-element.29), channel_id=1, replica_groups=mesh['z'=8,'x'=4,'c'=2,'y'=4] {'x','y','c'}, dimensions={0} | all-to-all | bytes 524288 | tf_op jit(solution)/shard_map/all_to_all | solution.py:280
  108.4 1.9 %shard_map.76 = (bf16[8,136,256]{2,1,0:T(8,128)(2,1)}, f32[2,8,128]{2,1,0:T(8,128)S(1)}) custom-call(bf16[32,32,128]{2,1,0:T(8,128)(2,1)S(1)} %all_to_all.44.recv_ref, f32[3,8,128]{2,1,0:T(8,128)S(1)} %get-tuple-element.26.stat_ref, f32[8,128]{1,0:T(8,128)S(1)} %get-tuple-element.30.col_ref, bf16[1024,1024]{1,0:T(8,128)(2,1)S(1)} %get-tuple-element.24.et_ref, ...), custom_call_target="tpu_custom_call" | custom-call | tf_op jit(solution)/shard_map/pallas_call | solution.py:264
  110.3 3.5 %all-to-all-start.7 = ((bf16[8,136,256]{2,1,0:T(8,128)(2,1)}), bf16[8,136,256]{2,1,0:T(8,128)(2,1)S(1)}, u32[]{:S(2)}, u32[]{:S(2)}) async-start(bf16[8,136,256]{2,1,0:T(8,128)(2,1)} %get-tuple-element.32), calls=%async_computation.7 | async-start | bytes 1114112 | tf_op jit(solution)/shard_map/all_to_all | solution.py:280
  113.9 4.4 %shard_map.77.a_ref = bf16[128,256]{1,0:T(8,128)(2,1)S(1)} custom-call(bf16[32,32,128]{2,1,0:T(8,128)(2,1)S(1)} %all_to_all.44.recv_ref, f32[2,8,128]{2,1,0:T(8,128)S(1)} %get-tuple-element.33.scale_ref, f32[3,8,128]{2,1,0:T(8,128)S(1)} %get-tuple-element.26.stat_ref, f32[8,128]{1,0:T(8,128)S(1)} %get-tuple-element.27.extra_ref.norm_ref, ...), custom_call_target="tpu_custom_call" | custom-call | flops 2147483648 | bytes 4194304 | tf_op jit(solution)/shard_map/pallas_call | solution.py:360
  118.6 1.9 %collective-permute-start.5 = (bf16[128,256]{1,0:T(8,128)(2,1)S(1)}, bf16[128,256]{1,0:T(8,128)(2,1)S(1)}, u32[]{:S(2)}, u32[]{:S(2)}) collective-permute-start(bf16[128,256]{1,0:T(8,128)(2,1)S(1)} %shard_map.77.a_ref), channel_id=1, source_target_pairs={{0,2},{1,3},{2,0},{3,1},{4,6},{5,7},{6,4},{7,5},{8,10},{9,11},{10,... | collective-permute-start | bytes 196616 | tf_op jit(solution)/shard_map/ppermute | solution.py:284
  120.5 0.6 collective-permute-start.6
  121.1 2.4 %collective-permute-done.4.b_ref = bf16[128,256]{1,0:T(8,128)(2,1)S(1)} collective-permute-done((bf16[128,256]{1,0:T(8,128)(2,1)S(1)}, bf16[128,256]{1,0:T(8,128)(2,1)S(1)}, u32[]{:S(2)}, u32[]{:S(2)}) %collective-permute-start.4) | collective-permute-done | bytes 65568 | tf_op jit(solution)/shard_map/ppermute | solution.py:284
  123.5 0.7 collective-permute-done.5.c_ref
  124.2 0.5 collective-permute-done.6.d_ref
  124.7 7.8 %all-to-all-done.7.recv_ref = bf16[8,136,256]{2,1,0:T(8,128)(2,1)S(1)} async-done(((bf16[8,136,256]{2,1,0:T(8,128)(2,1)}), bf16[8,136,256]{2,1,0:T(8,128)(2,1)S(1)}, u32[]{:S(2)}, u32[]{:S(2)}) %all-to-all-start.7) | async-done | bytes 557088 | tf_op jit(solution)/shard_map/all_to_all | solution.py:280
  132.5 1.2 shard_map.78
  (14 shorter events, 0.4 us)
Async XLA Ops:
  3.9 22.7 %copy-start.2 = (bf16[2,128,256]{2,1,0:T(8,128)(2,1)}, bf16[2,128,256]{2,1,0:T(8,128)(2,1)S(1)}, u32[]{:S(2)}) copy-start(bf16[2,128,256]{2,1,0:T(8,128)(2,1)S(1)} %get-tuple-element.21.rows_hbm) | copy-start | bytes 393220
  3.9 4.3 %collective-permute-start = (bf16[2,128,256]{2,1,0:T(8,128)(2,1)S(1)}, bf16[2,128,256]{2,1,0:T(8,128)(2,1)S(1)}, u32[]{:S(2)}, u32[]{:S(2)}) collective-permute-start(bf16[2,128,256]{2,1,0:T(8,128)(2,1)S(1)} %get-tuple-element.21.rows_hbm), channel_id=1, source_target_pairs={{0,4},{4,0},{1,5},{5,1},{2,6},{6,2},{3,7},{7,3},{8,12},{12,8},{9,1... | collective-permute-start | bytes 393224 | tf_op jit(solution)/shard_map/ppermute | solution.py:284
  8.2 18.3 %collective-permute-start.1 = (bf16[2,2,128,256]{3,2,1,0:T(8,128)(2,1)S(1)}, bf16[2,2,128,256]{3,2,1,0:T(8,128)(2,1)S(1)}, u32[]{:S(2)}, u32[]{:S(2)}) collective-permute-start(bf16[2,2,128,256]{3,2,1,0:T(8,128)(2,1)S(1)} %maximum_select_fusion.a_ref), channel_id=1, source_target_pairs={{0,8},{8,16},{16,24},{24,0},{1,9},{9,17},{17,25},{25,1},{2,10},{10... | collective-permute-start | bytes 786440 | tf_op jit(solution)/shard_map/ppermute | solution.py:284
  8.3 18.2 %collective-permute-start.2 = (bf16[2,2,128,256]{3,2,1,0:T(8,128)(2,1)S(1)}, bf16[2,2,128,256]{3,2,1,0:T(8,128)(2,1)S(1)}, u32[]{:S(2)}, u32[]{:S(2)}) collective-permute-start(bf16[2,2,128,256]{3,2,1,0:T(8,128)(2,1)S(1)} %maximum_select_fusion.a_ref), channel_id=1, source_target_pairs={{0,16},{8,24},{16,0},{24,8},{1,17},{9,25},{17,1},{25,9},{2,18},{10... | collective-permute-start | bytes 786440 | tf_op jit(solution)/shard_map/ppermute | solution.py:284
  10.2 16.4 %collective-permute-start.3 = (bf16[2,2,128,256]{3,2,1,0:T(8,128)(2,1)S(1)}, bf16[2,2,128,256]{3,2,1,0:T(8,128)(2,1)S(1)}, u32[]{:S(2)}, u32[]{:S(2)}) collective-permute-start(bf16[2,2,128,256]{3,2,1,0:T(8,128)(2,1)S(1)} %maximum_select_fusion.a_ref), channel_id=1, source_target_pairs={{0,24},{8,0},{16,8},{24,16},{1,25},{9,1},{17,9},{25,17},{2,26},{10... | collective-permute-start | bytes 786440 | tf_op jit(solution)/shard_map/ppermute | solution.py:284
  29.0 15.2 %all-to-all-start.1 = ((f32[8,8,128]{2,1,0:T(8,128)}), f32[8,8,128]{2,1,0:T(8,128)S(1)}, u32[]{:S(2)}, u32[]{:S(2)}) async-start(f32[8,8,128]{2,1,0:T(8,128)} %get-tuple-element.23), calls=%async_computation.1 | async-start | bytes 65536 | tf_op jit(solution)/shard_map/all_to_all | solution.py:280
  60.9 10.1 %all-to-all-start.3 = ((f32[8,8,128]{2,1,0:T(8,128)}), f32[8,8,128]{2,1,0:T(8,128)S(1)}, u32[]{:S(2)}, u32[]{:S(2)}) async-start(f32[8,8,128]{2,1,0:T(8,128)} %shard_map.71), calls=%async_computation.3 | async-start | bytes 65536 | tf_op jit(solution)/shard_map/all_to_all | solution.py:280
  71.0 22.9 %copy-start.1 = (bf16[1024,1024]{1,0:T(8,128)(2,1)S(1)}, bf16[1024,1024]{1,0:T(8,128)(2,1)}, u32[]{:S(2)}) copy-start(bf16[1024,1024]{1,0:T(8,128)(2,1)} %get-tuple-element.28.w_ref) | copy-start | bytes 6291460
  71.4 37.0 %copy-start = (f32[1024,1024]{1,0:T(8,128)S(1)}, f32[1024,1024]{1,0:T(8,128)}, u32[]{:S(2)}) copy-start(f32[1024,1024]{1,0:T(8,128)} %get-tuple-element.31.prob_ref) | copy-start | bytes 12582916
  110.3 22.2 %all-to-all-start.7 = ((bf16[8,136,256]{2,1,0:T(8,128)(2,1)}), bf16[8,136,256]{2,1,0:T(8,128)(2,1)S(1)}, u32[]{:S(2)}, u32[]{:S(2)}) async-start(bf16[8,136,256]{2,1,0:T(8,128)(2,1)} %get-tuple-element.32), calls=%async_computation.7 | async-start | bytes 1114112 | tf_op jit(solution)/shard_map/all_to_all | solution.py:280
  113.9 18.7 %copy-start.3 = (s32[1,256]{1,0:T(1,128)S(1)}, s32[1,256]{1,0:T(1,128)}, u32[]{:S(2)}) copy-start(s32[1,256]{1,0:T(1,128)} %mask_ref.1) | copy-start | bytes 3076
  118.3 5.2 %collective-permute-start.4 = (bf16[128,256]{1,0:T(8,128)(2,1)S(1)}, bf16[128,256]{1,0:T(8,128)(2,1)S(1)}, u32[]{:S(2)}, u32[]{:S(2)}) collective-permute-start(bf16[128,256]{1,0:T(8,128)(2,1)S(1)} %shard_map.77.a_ref), channel_id=1, source_target_pairs={{0,1},{1,2},{2,3},{3,0},{4,5},{5,6},{6,7},{7,4},{8,9},{9,10},{10,1... | collective-permute-start | bytes 196616 | tf_op jit(solution)/shard_map/ppermute | solution.py:284
  118.6 5.6 %collective-permute-start.5 = (bf16[128,256]{1,0:T(8,128)(2,1)S(1)}, bf16[128,256]{1,0:T(8,128)(2,1)S(1)}, u32[]{:S(2)}, u32[]{:S(2)}) collective-permute-start(bf16[128,256]{1,0:T(8,128)(2,1)S(1)} %shard_map.77.a_ref), channel_id=1, source_target_pairs={{0,2},{1,3},{2,0},{3,1},{4,6},{5,7},{6,4},{7,5},{8,10},{9,11},{10,... | collective-permute-start | bytes 196616 | tf_op jit(solution)/shard_map/ppermute | solution.py:284
  120.5 4.2 %collective-permute-start.6 = (bf16[128,256]{1,0:T(8,128)(2,1)S(1)}, bf16[128,256]{1,0:T(8,128)(2,1)S(1)}, u32[]{:S(2)}, u32[]{:S(2)}) collective-permute-start(bf16[128,256]{1,0:T(8,128)(2,1)S(1)} %shard_map.77.a_ref), channel_id=1, source_target_pairs={{0,3},{1,0},{2,1},{3,2},{4,7},{5,4},{6,5},{7,6},{8,11},{9,8},{10,9... | collective-permute-start | bytes 196616 | tf_op jit(solution)/shard_map/ppermute | solution.py:284

commit v5 on v4

--- a/solution.py
+++ b/solution.py
@@ -30,11 +30,14 @@
     return jnp.concatenate([v[:, 128 * i : 128 * (i + 1)] for i in range(8)], axis=0)
 
 
-def split3(v):
+def thirds(v):
     hi = v.astype(bf16).astype(f32)
     mid = (v - hi).astype(bf16).astype(f32)
-    lo = (v - hi - mid).astype(bf16).astype(f32)
-    return jnp.concatenate([hi, mid, lo, jnp.zeros((13, v.shape[1]), f32)], axis=0).astype(bf16)
+    return [hi, mid, (v - hi - mid).astype(bf16).astype(f32)]
+
+
+def split3(v):
+    return jnp.concatenate(thirds(v) + [jnp.zeros((13, v.shape[1]), f32)], axis=0).astype(bf16)
 
 
 def selection(mask):
@@ -70,31 +73,41 @@
     own_ref[0] = dot(pick, teach_ref[0], NN).astype(bf16)
     first[2].wait()
     own_ref[1] = dot(pick, student_ref[0], NN).astype(bf16)
-    rows = own_ref[0]
-    peak = None
+    rows = own_ref[...].reshape(2 * LIVE, 256)
+    peak = top = total = None
     for i in range(chunks):
         copies[i].wait()
         for j in (2 * i, 2 * i + 1):
             mine_ref[128 * j : 128 * (j + 1), :] = proto_ref[pl.ds(pl.multiple_of(j * 1024 + image * 128, 128), 128), :]
-        half = tall // 2
-        low = dot(proto_ref[i * tall : i * tall + half, :], rows, NT)
-        high = dot(proto_ref[i * tall + half : (i + 1) * tall, :], rows, NT)
-        top = jnp.max(jnp.maximum(low, high), axis=0, keepdims=True)
-        peak = top if peak is None else jnp.maximum(peak, top)
-    tile = jnp.concatenate([peak * TEACHER_INV, jnp.broadcast_to(count, (1, LIVE)), jnp.zeros((6, LIVE), f32)], axis=0)
-    out_ref[...] = jnp.broadcast_to(tile[None], out_ref.shape)
+            logits = dot(proto_ref[1024 * j : 1024 * (j + 1), :], rows, NT)
+            teach = jnp.max(logits[:, :LIVE], axis=0, keepdims=True)
+            student = logits[:, LIVE:] * STUDENT_INV
+            now = jnp.max(student, axis=0, keepdims=True)
+            part = jnp.sum(jnp.exp(student - now), axis=0, keepdims=True)
+            if peak is None:
+                peak, top, total = teach, now, part
+            else:
+                peak, both = jnp.maximum(peak, teach), jnp.maximum(top, now)
+                total = total * jnp.exp(top - both) + part * jnp.exp(now - both)
+                top = both
+    tile = jnp.concatenate(
+        thirds(peak * TEACHER_INV)
+        + [jnp.broadcast_to(count, (1, LIVE))]
+        + thirds(top + jnp.log(total))
+        + [jnp.zeros((1, LIVE), f32)],
+        axis=0,
+    )
+    out_ref[...] = jnp.broadcast_to(tile[None].astype(bf16), out_ref.shape)
 
 
 def expo_kernel(recv_ref, a_ref, b_ref, c_ref, d_ref, mine_ref, et_ref, srows_ref, stat_ref, pay_ref, peak_ref, live_ref):
     peaks, counts = [], []
     for x in range(4):
         for core in range(2):
-            at = [(x * 4 + y) * 2 + core for y in range(4)]
-            top = recv_ref[at[0], 0:1, :]
-            for i in at[1:]:
-                top = jnp.maximum(top, recv_ref[i, 0:1, :])
-            peaks.append(top)
-            counts.append(recv_ref[at[0], 1:2, :])
+            got = [recv_ref[(x * 4 + y) * 2 + core].astype(f32) for y in range(4)]
+            tops = [v[0:1] + v[1:2] + v[2:3] for v in got]
+            peaks.append(jnp.maximum(jnp.maximum(tops[0], tops[1]), jnp.maximum(tops[2], tops[3])))
+            counts.append(got[0][3:4])
     count = jnp.concatenate(counts, axis=0)
     slot = lax.broadcasted_iota(jnp.int32, (8, 128), 1).astype(f32)
     live = jnp.where(slot < count, 1.0, 0.0)
@@ -118,12 +131,14 @@
     pay_ref[...] = jnp.broadcast_to(to_tile(total[0:1])[None], pay_ref.shape)
 
 
-def col_kernel(recv_ref, et_ref, extra_ref, pay_ref):
+def spread(tile, ref):
+    ref[...] = jnp.broadcast_to(tile[None].astype(ref.dtype), ref.shape)
+
+
+def col_kernel(recv_ref, et_ref, *refs):
     col = 1.0 / jnp.sum(recv_ref[...], axis=0)
     out = jnp.sum(dot(split3(to_lanes(col)), et_ref[...], NN), axis=0, keepdims=True)
-    pay_ref[:, 0:8, :] = jnp.broadcast_to(to_tile(out)[None], (pay_ref.shape[0], 8, 128))
-    if pay_ref.shape[1] > 8:
-        pay_ref[:, 8:, :] = jnp.broadcast_to(extra_ref[...][None], (pay_ref.shape[0], 8, 128))
+    spread(to_tile(out), refs[-1])
 
 
 def last_col_kernel(recv_ref, et_ref, w_ref, pay_ref, col_ref):
@@ -131,34 +146,23 @@
     col_ref[...] = col
     lhs = split3(to_lanes(col))
     out = to_tile(jnp.sum(dot(lhs, et_ref[...], NN), axis=0, keepdims=True))
-    hi = out.astype(bf16).astype(f32)
-    sums = jnp.concatenate([hi, out - hi], axis=0).astype(bf16)
-    out = to_tile(jnp.sum(dot(lhs, w_ref[...], NN), axis=0, keepdims=True))
-    rest = jnp.concatenate([out, col], axis=0).astype(bf16)
-    pay_ref[:, 0:16, :] = jnp.broadcast_to(sums[None], (pay_ref.shape[0], 16, 128))
-    pay_ref[:, 16:32, :] = jnp.broadcast_to(rest[None], (pay_ref.shape[0], 16, 128))
+    entropy = to_tile(jnp.sum(dot(lhs, w_ref[...], NN), axis=0, keepdims=True))
+    spread(jnp.concatenate([out, entropy, col], axis=0), pay_ref)
 
 
 def row_kernel(recv_ref, stat_ref, et_ref, pay_ref):
-    row = stat_ref[0] / jnp.sum(recv_ref[:, 0:8, :], axis=0)
-    lhs = split3(to_lanes(row))
-    out = jnp.sum(dot(lhs, et_ref[...], NT), axis=0, keepdims=True)
-    pay_ref[...] = jnp.broadcast_to(to_tile(out)[None], pay_ref.shape)
-
-
-def student_sum_kernel(srows_ref, mine_ref, out_ref):
-    parts = []
-    for r in range(4):
-        logits = dot(mine_ref[...], srows_ref[256 * r : 256 * (r + 1), :], NT) * STUDENT_INV
-        top = jnp.max(logits, axis=0, keepdims=True)
-        parts.append(top + jnp.log(jnp.sum(jnp.exp(logits - top), axis=0, keepdims=True)))
-    out_ref[...] = to_tile(jnp.concatenate(parts, axis=1))
+    row = stat_ref[0] / jnp.sum(recv_ref[...].astype(f32), axis=0)
+    out = jnp.sum(dot(split3(to_lanes(row)), et_ref[...], NT), axis=0, keepdims=True)
+    spread(to_tile(out), pay_ref)
 
 
 def student_prob_kernel(recv_ref, srows_ref, mine_ref, et_ref, prob_hbm, w_hbm, norm_ref, prob_ref, w_ref, sems):
-    parts = recv_ref[:, 8:16, :]
-    top = jnp.max(parts, axis=0)
-    norm_ref[...] = top + jnp.log(jnp.sum(jnp.exp(parts - top[None]), axis=0))
+    for image in range(8):
+        got = [recv_ref[(image // 2 * 4 + y) * 2 + image % 2].astype(f32) for y in range(4)]
+        parts = [v[4:5] + v[5:6] + v[6:7] for v in got]
+        top = jnp.maximum(jnp.maximum(parts[0], parts[1]), jnp.maximum(parts[2], parts[3]))
+        total = sum(jnp.exp(v - top) for v in parts)
+        norm_ref[image : image + 1, :] = top + jnp.log(total)
     norm = to_lanes(norm_ref[...])
     copies = []
     for r in range(4):
@@ -175,22 +179,23 @@
         copy.wait()
 
 
-def grad_kernel(recv_ref, stat_ref, col_ref, et_ref, prob_ref, srows_ref, pout_ref, scale_ref):
-    sums = jnp.sum(recv_ref[:, 0:16, :].astype(f32), axis=0)
-    entropy = jnp.sum(recv_ref[:, 16:32, :].astype(f32), axis=0)[0:8]
-    row = stat_ref[0] / (sums[0:8] + sums[8:16])
+def grad_kernel(recv_ref, stat_ref, col_ref, et_ref, prob_ref, srows_ref, pout_hbm, scale_ref, pout_ref, sems):
+    sums = jnp.sum(recv_ref[...].astype(f32), axis=0)
+    entropy = sums[8:16]
+    row = stat_ref[0] / sums[0:8]
     weight = stat_ref[1]
     loss = -jnp.sum(jnp.sum(weight * row * entropy, axis=1, keepdims=True), axis=0, keepdims=True) / IMAGES
     hi = loss.astype(bf16).astype(f32)
     mid = (loss - hi).astype(bf16).astype(f32)
     lo = loss - hi - mid
-    which = lax.broadcasted_iota(jnp.int32, (8, 256), 0)
+    which = lax.broadcasted_iota(jnp.int32, (8, 128), 0)
     tail = jnp.where(which == 0, hi, jnp.where(which == 1, mid, jnp.where(which == 2, lo, 0.0))).astype(bf16)
     coef = weight * (LOSS_SCALE / (IMAGES * 0.1))
     scale_ref[0] = coef
     scale_ref[1] = coef * row
     coef_rows = to_lanes(coef)
     scale_rows = to_lanes(coef * row)
+    copies = []
     for j in range(4):
         at = slice(256 * j, 256 * (j + 1))
         col = jnp.concatenate([jnp.broadcast_to(col_ref[i : i + 1, :], (128, 128)).T for i in (2 * j, 2 * j + 1)], axis=0)
@@ -198,8 +203,14 @@
         grad = (prob_ref[at, :] * coef_rows - et_ref[at, :].astype(f32) * col * scale_rows).astype(bf16)
         part = dot(grad, srows_ref[...], NN).astype(bf16)
         for i in (0, 1):
-            pout_ref[2 * j + i, 0:128, :] = part[128 * i : 128 * (i + 1)]
-            pout_ref[2 * j + i, 128:136, :] = tail
+            pout_ref[2 * j + i, 0:128, :] = part[128 * i : 128 * (i + 1), 0:128]
+            pout_ref[2 * j + i, 128:256, :] = part[128 * i : 128 * (i + 1), 128:256]
+            pout_ref[2 * j + i, 256:264, :] = tail
+        at = pl.ds(2 * j, 2)
+        copies.append(pltpu.make_async_copy(pout_ref.at[at], pout_hbm.at[at], sems.at[j]))
+        copies[-1].start()
+    for copy in copies:
+        copy.wait()
 
 
 def column(row, wide):
@@ -225,14 +236,14 @@
     norm = column(norm_ref[own_image(), :], 1024)
     coef = column(scale_ref[0, own_image(), :], 1024)
     scale = column(scale_ref[1, own_image(), :], 1024)
-    cols = [recv_ref[(x * 4 + y) * 2 + c, 16:32, :].astype(f32) for x in range(4) for c in range(2)]
+    cols = [recv_ref[(x * 4 + y) * 2 + c].astype(f32)[16:24] for x in range(4) for c in range(2)]
     rows_copy.wait()
     rows = rows_ref[...].reshape(2 * LIVE, 256)
     total = jnp.zeros((LIVE, 256), f32)
     for i in range(8):
         if i % 2 == 0:
             copies[i // 2].wait()
-        col = jnp.concatenate([v[8 + i : 9 + i, :] for v in cols], axis=1)
+        col = jnp.concatenate([v[i : i + 1, :] for v in cols], axis=1)
         block = proto_ref[1024 * i : 1024 * (i + 1), :]
         logits = dot(rows, block, NT)
         teach = jnp.exp(logits[0:LIVE] * TEACHER_INV - peak).astype(bf16).astype(f32)
@@ -252,8 +263,9 @@
     lo = (rest - mid.astype(f32)).astype(bf16)
     student_ref[...] = dot(pick, hi, TN) + dot(pick, mid, TN) + dot(pick, lo, TN)
     total = jnp.sum(recv_ref[...].astype(f32), axis=0)
-    proto_ref[...] = total[0:128, :]
-    loss_ref[...] = total[128:129, 0:128] + total[129:130, 0:128] + total[130:131, 0:128]
+    proto_ref[:, 0:128] = total[0:128]
+    proto_ref[:, 128:256] = total[128:256]
+    loss_ref[...] = total[256:257] + total[257:258] + total[258:259]
 
 
 VM = pl.BlockSpec(memory_space=pltpu.VMEM)
@@ -294,7 +306,7 @@
         head_kernel,
         out_shape=[
             jax.ShapeDtypeStruct((2, LIVE, 256), bf16),
-            jax.ShapeDtypeStruct((32, 8, 128), f32),
+            jax.ShapeDtypeStruct((32, 8, 128), bf16),
             jax.ShapeDtypeStruct((1024, 256), bf16),
         ],
         in_specs=[HBM] * 4,
@@ -321,10 +333,8 @@
         peak_recv, *parts, mine, limit=16, scratch=[pltpu.VMEM((8, 256), f32)] * 2,
     )
 
-    (student_sum,) = call(student_sum_kernel, [((8, 128), f32)], srows, mine, cost=1 << 29, limit=16)
-
     recv = a2a(pay, "z")
-    (pay,) = call(col_kernel, [((32, 16, 128), f32)], recv, et, student_sum)
+    (pay,) = call(col_kernel, [((32, 8, 128), bf16)], recv, et)
     recv = a2a(pay, PLANE)
     prob, w, norm = pl.pallas_call(
         student_prob_kernel,
@@ -342,20 +352,25 @@
         ],
         compiler_params=pltpu.CompilerParams(vmem_limit_bytes=24 << 20),
         cost_estimate=pl.CostEstimate(flops=1 << 29, bytes_accessed=8 << 20, transcendentals=1 << 20),
-    )(recv, srows, mine, et)
+    )(peak_recv, srows, mine, et)
     (pay,) = call(row_kernel, [((8, 8, 128), f32)], recv, stat, et)
     for _ in range(BALANCING_PASSES - 2):
         recv = a2a(pay, "z")
-        (pay,) = call(col_kernel, [((32, 8, 128), f32)], recv, et, norm)
+        (pay,) = call(col_kernel, [((32, 8, 128), bf16)], recv, et, norm)
         recv = a2a(pay, PLANE)
         (pay,) = call(row_kernel, [((8, 8, 128), f32)], recv, stat, et)
     recv = a2a(pay, "z")
-    pay, col = call(last_col_kernel, [((32, 32, 128), bf16), ((8, 128), f32)], recv, et, w)
+    pay, col = call(last_col_kernel, [((32, 24, 128), bf16), ((8, 128), f32)], recv, et, w)
     recv = a2a(pay, PLANE)
 
-    proto_part, scale = call(
-        grad_kernel, [((8, 136, 256), bf16), ((2, 8, 128), f32)], recv, stat, col, et, prob, srows, limit=24
-    )
+    proto_part, scale = pl.pallas_call(
+        grad_kernel,
+        out_shape=[pltpu.HBM((8, 264, 128), bf16), jax.ShapeDtypeStruct((2, 8, 128), f32)],
+        in_specs=[VM] * 6,
+        out_specs=[pl.BlockSpec(memory_space=pltpu.HBM), VM],
+        scratch_shapes=[pltpu.VMEM((8, 264, 128), bf16), pltpu.SemaphoreType.DMA((4,))],
+        compiler_params=pltpu.CompilerParams(vmem_limit_bytes=24 << 20),
+    )(recv, stat, col, et, prob, srows)
     proto_recv = a2a(proto_part, "z")
     student_rows = pl.pallas_call(
         own_kernel,

time: 134 us -> 131 us (0.978)
  blocking collectives: 65.8 us -> 79 us
  starting transfers between devices: 24.3 us -> 14.3 us
  waiting for transfers between devices: 21.3 us -> 16 us
    all_to_all x5 -> x6, blocking collectives: 65.8 us -> 79 us  [a2a(): return lax.all_to_all(v, axes, 0, 0, tiled=True)]
    all_to_all x3 -> x2, starting transfers between devices: 15.1 us -> 6.89 us  [a2a(): return lax.all_to_all(v, axes, 0, 0, tiled=True)]
    all_to_all x3 -> x2, waiting for transfers between devices: 16.6 us -> 9.9 us  [a2a(): return lax.all_to_all(v, axes, 0, 0, tiled=True)]
    pallas_call x9 -> x7, Pallas kernels: 10.4 us -> 6.4 us  [call(): pl.pallas_call(kernel, out_shape=out, in_specs=[VM] * len(args), out_spec...]
    ppermute x7, starting transfers between devices: 9.26 us -> 7.37 us  [shift(): return lax.ppermute(v, axis, [(i, (i + k) % n) for i in range(n)])]
    pallas_call x0 -> x1, Pallas kernels: none -> 1.79 us  [local(): pl.pallas_call(grad_kernel, out_shape=[pltpu.HBM((8, 264, 128), bf16), ja...]
    ppermute x7, waiting for transfers between devices: 4.67 us -> 6.14 us  [shift(): return lax.ppermute(v, axis, [(i, (i + k) % n) for i in range(n)])]
  transfers between devices with their start and end apart: 10 -> 9, of which waited for: 7 -> 6; matrix products, arithmetic and copies ran while one was open for 0% -> 0% of each run, Pallas kernels for 7% -> 6%
where the time goes in v5:
time: 131 us
  blocking collectives  79 us (60%)
  Pallas kernels  20.5 us (16%)
  waiting for transfers between devices  16 us (12%)
  starting transfers between devices  14.3 us (11%)
    all_to_all x6, blocking collectives, a2a(): return lax.all_to_all(v, axes, 0, 0, tiled=True)  79 us
    all_to_all x2, waiting for transfers between devices, a2a(): return lax.all_to_all(v, axes, 0, 0, tiled=True)  9.9 us
    ppermute x7, starting transfers between devices, shift(): return lax.ppermute(v, axis, [(i, (i + k) % n) for i in range(n)])  7.37 us
    all_to_all x2, starting transfers between devices, a2a(): return lax.all_to_all(v, axes, 0, 0, tiled=True)  6.89 us
    pallas_call x7, Pallas kernels, call(): pl.pallas_call(kernel, out_shape=out, in_specs=[VM] * len(args), out_spec...  6.4 us
    ppermute x7, waiting for transfers between devices, shift(): return lax.ppermute(v, axis, [(i, (i + k) % n) for i in range(n)])  6.14 us
    pallas_call x1, Pallas kernels, local(): pl.pallas_call(own_kernel, out_shape=jax.ShapeDtypeStruct((LIVE, 256), bf...  4.43 us
    pallas_call x1, Pallas kernels, local(): pl.pallas_call(head_kernel, out_shape=[jax.ShapeDtypeStruct((2, LIVE, 256...  4.36 us
  transfers between devices with their start and end apart: 9, of which 6 were waited for; matrix products, arithmetic and copies ran while one was open for 0% of the time, Pallas kernels for 6%

profile of v5, /device:TPU:1, one launch (start us, length us, event | category | flops | bytes accessed | tf_op | source)
XLA Modules:
  0.0 130.5 jit_solution(15466257306143450484)
XLA Ops:
  0.6 4.4 %shard_map.67 = (bf16[2,128,256]{2,1,0:T(8,128)(2,1)S(1)}, bf16[32,8,128]{2,1,0:T(8,128)(2,1)S(1)}, bf16[1024,256]{1,0:T(8,128)(2,1)S(1)}) custom-call(s32[1,256]{1,0:T(1,128)} %mask_ref.1, bf16[1,256,256]{2,1,0:T(8,128)(2,1)} %teach_hbm.1, bf16[1,256,256]{2,1,0:T(8,128)(2,1)} %student_hbm.1, bf16[8192,256]{1,0:T(8,128)(2,1)} %proto_hbm.3), custom_call_target="tpu_custom_call" | custom-call | tf_op jit(solution)/shard_map/pallas_call | solution.py:305
  5.0 3.3 %collective-permute-start = (bf16[2,128,256]{2,1,0:T(8,128)(2,1)S(1)}, bf16[2,128,256]{2,1,0:T(8,128)(2,1)S(1)}, u32[]{:S(2)}, u32[]{:S(2)}) collective-permute-start(bf16[2,128,256]{2,1,0:T(8,128)(2,1)S(1)} %get-tuple-element.21.rows_hbm), channel_id=1, source_target_pairs={{0,4},{4,0},{1,5},{5,1},{2,6},{6,2},{3,7},{7,3},{8,12},{12,8},{9,1... | collective-permute-start | bytes 393224 | tf_op jit(solution)/shard_map/ppermute | solution.py:296
  8.3 1.0 collective-permute-done
  9.3 0.8 collective-permute-start.3
  10.2 0.5 collective-permute-start.2
  10.7 0.6 collective-permute-start.1
  11.3 17.5 %all_to_all.40.recv_ref = bf16[32,8,128]{2,1,0:T(8,128)(2,1)S(1)} all-to-all(bf16[32,8,128]{2,1,0:T(8,128)(2,1)S(1)} %get-tuple-element.20), channel_id=1, replica_groups=mesh['z'=8,'x'=4,'c'=2,'y'=4] {'x','y','c'}, dimensions={0} | all-to-all | bytes 131072 | tf_op jit(solution)/shard_map/all_to_all | solution.py:292
  28.8 1.7 %shard_map.68 = (bf16[1024,1024]{1,0:T(8,128)(2,1)S(1)}, bf16[1024,256]{1,0:T(8,128)(2,1)S(1)}, f32[3,8,128]{2,1,0:T(8,128)S(1)}, f32[8,8,128]{2,1,0:T(8,128)S(1)}) custom-call(bf16[32,8,128]{2,1,0:T(8,128)(2,1)S(1)} %all_to_all.40.recv_ref, bf16[2,2,128,256]{3,2,1,0:T(8,128)(2,1)S(1)} %maximum_select_fusion.a_ref, ...), custom_call_target="tpu_custom_call" | custom-call | tf_op jit(solution)/shard_map/pallas_call | solution.py:276
  30.6 14.9 %all_to_all.41.recv_ref = f32[8,8,128]{2,1,0:T(8,128)S(1)} all-to-all(f32[8,8,128]{2,1,0:T(8,128)S(1)} %get-tuple-element.23), channel_id=1, replica_groups=mesh['z'=8,'x'=4,'c'=2,'y'=4] {'z'}, dimensions={0} | all-to-all | bytes 65536 | tf_op jit(solution)/shard_map/all_to_all | solution.py:292
  45.4 0.4 shard_map.69
  45.8 12.0 %all_to_all.42.recv_ref = bf16[32,8,128]{2,1,0:T(8,128)(2,1)S(1)} all-to-all(bf16[32,8,128]{2,1,0:T(8,128)(2,1)S(1)} %shard_map.69), channel_id=1, replica_groups=mesh['z'=8,'x'=4,'c'=2,'y'=4] {'x','y','c'}, dimensions={0} | all-to-all | bytes 131072 | tf_op jit(solution)/shard_map/all_to_all | solution.py:292
  57.8 1.3 shard_map.70
  59.1 3.3 %all-to-all-start.3 = ((f32[8,8,128]{2,1,0:T(8,128)}), f32[8,8,128]{2,1,0:T(8,128)S(1)}, u32[]{:S(2)}, u32[]{:S(2)}) async-start(f32[8,8,128]{2,1,0:T(8,128)} %shard_map.70), calls=%async_computation.3 | async-start | bytes 65536 | tf_op jit(solution)/shard_map/all_to_all | solution.py:292
  62.4 3.5 %shard_map.71 = (f32[1024,1024]{1,0:T(8,128)}, bf16[1024,1024]{1,0:T(8,128)(2,1)}, f32[8,128]{1,0:T(8,128)S(1)}) custom-call(bf16[32,8,128]{2,1,0:T(8,128)(2,1)S(1)} %all_to_all.40.recv_ref, bf16[1024,256]{1,0:T(8,128)(2,1)S(1)} %get-tuple-element.26.srows_ref, bf16[1024,256]{1,0:T(8,128)(2,1)S(1)} %get-tuple-element.22.mine_ref, ...), custom_call_target="tpu_custom_call" | custom-call | flops 536870912 | bytes 8388608 | tf_op jit(solution)/shard_map/pallas_call | solution.py:339
  65.9 3.3 %all-to-all-done.3.recv_ref = f32[8,8,128]{2,1,0:T(8,128)S(1)} async-done(((f32[8,8,128]{2,1,0:T(8,128)}), f32[8,8,128]{2,1,0:T(8,128)S(1)}, u32[]{:S(2)}, u32[]{:S(2)}) %all-to-all-start.3) | async-done | bytes 32800 | tf_op jit(solution)/shard_map/all_to_all | solution.py:292
  69.2 0.4 shard_map.72
  69.6 12.3 %all_to_all.43.recv_ref = bf16[32,8,128]{2,1,0:T(8,128)(2,1)S(1)} all-to-all(bf16[32,8,128]{2,1,0:T(8,128)(2,1)S(1)} %shard_map.72), channel_id=1, replica_groups=mesh['z'=8,'x'=4,'c'=2,'y'=4] {'x','y','c'}, dimensions={0} | all-to-all | bytes 131072 | tf_op jit(solution)/shard_map/all_to_all | solution.py:292
  81.9 0.7 shard_map.73
  82.6 9.2 %all_to_all.44.recv_ref = f32[8,8,128]{2,1,0:T(8,128)S(1)} all-to-all(f32[8,8,128]{2,1,0:T(8,128)S(1)} %shard_map.73), channel_id=1, replica_groups=mesh['z'=8,'x'=4,'c'=2,'y'=4] {'z'}, dimensions={0} | all-to-all | bytes 65536 | tf_op jit(solution)/shard_map/all_to_all | solution.py:292
  91.8 0.7 shard_map.74
  92.5 13.1 %all_to_all.45.recv_ref = bf16[32,24,128]{2,1,0:T(8,128)(2,1)S(1)} all-to-all(bf16[32,24,128]{2,1,0:T(8,128)(2,1)S(1)} %get-tuple-element.29), channel_id=1, replica_groups=mesh['z'=8,'x'=4,'c'=2,'y'=4] {'x','y','c'}, dimensions={0} | all-to-all | bytes 393216 | tf_op jit(solution)/shard_map/all_to_all | solution.py:292
  105.6 1.8 %shard_map.75 = (bf16[8,264,128]{2,1,0:T(8,128)(2,1)}, f32[2,8,128]{2,1,0:T(8,128)S(1)}) custom-call(bf16[32,24,128]{2,1,0:T(8,128)(2,1)S(1)} %all_to_all.45.recv_ref, f32[3,8,128]{2,1,0:T(8,128)S(1)} %get-tuple-element.25.stat_ref, f32[8,128]{1,0:T(8,128)S(1)} %get-tuple-element.30.col_ref, bf16[1024,1024]{1,0:T(8,128)(2,1)S(1)} %get-tuple-element.24.et_ref, ...), custom_call_target="tpu_custom_call" | custom-call | tf_op jit(solution)/shard_map/pallas_call | solution.py:366
  107.4 3.5 %all-to-all-start.7 = ((bf16[8,264,128]{2,1,0:T(8,128)(2,1)}), bf16[8,264,128]{2,1,0:T(8,128)(2,1)S(1)}, u32[]{:S(2)}, u32[]{:S(2)}) async-start(bf16[8,264,128]{2,1,0:T(8,128)(2,1)} %get-tuple-element.32), calls=%async_computation.7 | async-start | bytes 1081344 | tf_op jit(solution)/shard_map/all_to_all | solution.py:292
  111.0 0.0 copy-start.3
  111.0 4.4 %shard_map.76.a_ref = bf16[128,256]{1,0:T(8,128)(2,1)S(1)} custom-call(bf16[32,24,128]{2,1,0:T(8,128)(2,1)S(1)} %all_to_all.45.recv_ref, f32[2,8,128]{2,1,0:T(8,128)S(1)} %get-tuple-element.33.scale_ref, f32[3,8,128]{2,1,0:T(8,128)S(1)} %get-tuple-element.25.stat_ref, f32[8,128]{1,0:T(8,128)S(1)} %get-tuple-element.27.refs_0_.norm_ref, ...), custom_call_target="tpu_custom_call" | custom-call | flops 2147483648 | bytes 4194304 | tf_op jit(solution)/shard_map/pallas_call | solution.py:375
  115.4 1.0 collective-permute-start.6
  116.5 1.1 collective-permute-start.5
  117.6 1.4 %collective-permute-done.6.d_ref = bf16[128,256]{1,0:T(8,128)(2,1)S(1)} collective-permute-done((bf16[128,256]{1,0:T(8,128)(2,1)S(1)}, bf16[128,256]{1,0:T(8,128)(2,1)S(1)}, u32[]{:S(2)}, u32[]{:S(2)}) %collective-permute-start.6) | collective-permute-done | bytes 65568 | tf_op jit(solution)/shard_map/ppermute | solution.py:296
  118.9 2.3 %collective-permute-done.5.c_ref = bf16[128,256]{1,0:T(8,128)(2,1)S(1)} collective-permute-done((bf16[128,256]{1,0:T(8,128)(2,1)S(1)}, bf16[128,256]{1,0:T(8,128)(2,1)S(1)}, u32[]{:S(2)}, u32[]{:S(2)}) %collective-permute-start.5) | collective-permute-done | bytes 65568 | tf_op jit(solution)/shard_map/ppermute | solution.py:296
  121.2 1.5 %collective-permute-done.4.b_ref = bf16[128,256]{1,0:T(8,128)(2,1)S(1)} collective-permute-done((bf16[128,256]{1,0:T(8,128)(2,1)S(1)}, bf16[128,256]{1,0:T(8,128)(2,1)S(1)}, u32[]{:S(2)}, u32[]{:S(2)}) %collective-permute-start.4) | collective-permute-done | bytes 65568 | tf_op jit(solution)/shard_map/ppermute | solution.py:296
  122.7 6.6 %all-to-all-done.7.recv_ref = bf16[8,264,128]{2,1,0:T(8,128)(2,1)S(1)} async-done(((bf16[8,264,128]{2,1,0:T(8,128)(2,1)}), bf16[8,264,128]{2,1,0:T(8,128)(2,1)S(1)}, u32[]{:S(2)}, u32[]{:S(2)}) %all-to-all-start.7) | async-done | bytes 540704 | tf_op jit(solution)/shard_map/all_to_all | solution.py:292
  129.3 1.2 shard_map.77
  (12 shorter events, 0.1 us)
Async XLA Ops:
  5.0 60.9 %copy-start.2 = (bf16[2,128,256]{2,1,0:T(8,128)(2,1)}, bf16[2,128,256]{2,1,0:T(8,128)(2,1)S(1)}, u32[]{:S(2)}) copy-start(bf16[2,128,256]{2,1,0:T(8,128)(2,1)S(1)} %get-tuple-element.21.rows_hbm) | copy-start | bytes 393220
  5.0 4.3 %collective-permute-start = (bf16[2,128,256]{2,1,0:T(8,128)(2,1)S(1)}, bf16[2,128,256]{2,1,0:T(8,128)(2,1)S(1)}, u32[]{:S(2)}, u32[]{:S(2)}) collective-permute-start(bf16[2,128,256]{2,1,0:T(8,128)(2,1)S(1)} %get-tuple-element.21.rows_hbm), channel_id=1, source_target_pairs={{0,4},{4,0},{1,5},{5,1},{2,6},{6,2},{3,7},{7,3},{8,12},{12,8},{9,1... | collective-permute-start | bytes 393224 | tf_op jit(solution)/shard_map/ppermute | solution.py:296
  9.3 19.5 %collective-permute-start.3 = (bf16[2,2,128,256]{3,2,1,0:T(8,128)(2,1)S(1)}, bf16[2,2,128,256]{3,2,1,0:T(8,128)(2,1)S(1)}, u32[]{:S(2)}, u32[]{:S(2)}) collective-permute-start(bf16[2,2,128,256]{3,2,1,0:T(8,128)(2,1)S(1)} %maximum_select_fusion.a_ref), channel_id=1, source_target_pairs={{0,24},{8,0},{16,8},{24,16},{1,25},{9,1},{17,9},{25,17},{2,26},{10... | collective-permute-start | bytes 786440 | tf_op jit(solution)/shard_map/ppermute | solution.py:296
  10.2 18.7 %collective-permute-start.2 = (bf16[2,2,128,256]{3,2,1,0:T(8,128)(2,1)S(1)}, bf16[2,2,128,256]{3,2,1,0:T(8,128)(2,1)S(1)}, u32[]{:S(2)}, u32[]{:S(2)}) collective-permute-start(bf16[2,2,128,256]{3,2,1,0:T(8,128)(2,1)S(1)} %maximum_select_fusion.a_ref), channel_id=1, source_target_pairs={{0,16},{8,24},{16,0},{24,8},{1,17},{9,25},{17,1},{25,9},{2,18},{10... | collective-permute-start | bytes 786440 | tf_op jit(solution)/shard_map/ppermute | solution.py:296
  10.7 18.1 %collective-permute-start.1 = (bf16[2,2,128,256]{3,2,1,0:T(8,128)(2,1)S(1)}, bf16[2,2,128,256]{3,2,1,0:T(8,128)(2,1)S(1)}, u32[]{:S(2)}, u32[]{:S(2)}) collective-permute-start(bf16[2,2,128,256]{3,2,1,0:T(8,128)(2,1)S(1)} %maximum_select_fusion.a_ref), channel_id=1, source_target_pairs={{0,8},{8,16},{16,24},{24,0},{1,9},{9,17},{17,25},{25,1},{2,10},{10... | collective-permute-start | bytes 786440 | tf_op jit(solution)/shard_map/ppermute | solution.py:296
  59.1 10.1 %all-to-all-start.3 = ((f32[8,8,128]{2,1,0:T(8,128)}), f32[8,8,128]{2,1,0:T(8,128)S(1)}, u32[]{:S(2)}, u32[]{:S(2)}) async-start(f32[8,8,128]{2,1,0:T(8,128)} %shard_map.70), calls=%async_computation.3 | async-start | bytes 65536 | tf_op jit(solution)/shard_map/all_to_all | solution.py:292
  69.2 22.6 %copy-start.1 = (bf16[1024,1024]{1,0:T(8,128)(2,1)S(1)}, bf16[1024,1024]{1,0:T(8,128)(2,1)}, u32[]{:S(2)}) copy-start(bf16[1024,1024]{1,0:T(8,128)(2,1)} %get-tuple-element.28.w_ref) | copy-start | bytes 6291460
  69.2 36.4 %copy-start = (f32[1024,1024]{1,0:T(8,128)S(1)}, f32[1024,1024]{1,0:T(8,128)}, u32[]{:S(2)}) copy-start(f32[1024,1024]{1,0:T(8,128)} %get-tuple-element.31.prob_ref) | copy-start | bytes 12582916
  107.4 21.8 %all-to-all-start.7 = ((bf16[8,264,128]{2,1,0:T(8,128)(2,1)}), bf16[8,264,128]{2,1,0:T(8,128)(2,1)S(1)}, u32[]{:S(2)}, u32[]{:S(2)}) async-start(bf16[8,264,128]{2,1,0:T(8,128)(2,1)} %get-tuple-element.32), calls=%async_computation.7 | async-start | bytes 1081344 | tf_op jit(solution)/shard_map/all_to_all | solution.py:292
  111.0 18.3 %copy-start.3 = (s32[1,256]{1,0:T(1,128)S(1)}, s32[1,256]{1,0:T(1,128)}, u32[]{:S(2)}) copy-start(s32[1,256]{1,0:T(1,128)} %mask_ref.1) | copy-start | bytes 3076
  115.4 3.5 %collective-permute-start.6 = (bf16[128,256]{1,0:T(8,128)(2,1)S(1)}, bf16[128,256]{1,0:T(8,128)(2,1)S(1)}, u32[]{:S(2)}, u32[]{:S(2)}) collective-permute-start(bf16[128,256]{1,0:T(8,128)(2,1)S(1)} %shard_map.76.a_ref), channel_id=1, source_target_pairs={{0,3},{1,0},{2,1},{3,2},{4,7},{5,4},{6,5},{7,6},{8,11},{9,8},{10,9... | collective-permute-start | bytes 196616 | tf_op jit(solution)/shard_map/ppermute | solution.py:296
  116.5 4.8 %collective-permute-start.5 = (bf16[128,256]{1,0:T(8,128)(2,1)S(1)}, bf16[128,256]{1,0:T(8,128)(2,1)S(1)}, u32[]{:S(2)}, u32[]{:S(2)}) collective-permute-start(bf16[128,256]{1,0:T(8,128)(2,1)S(1)} %shard_map.76.a_ref), channel_id=1, source_target_pairs={{0,2},{1,3},{2,0},{3,1},{4,6},{5,7},{6,4},{7,5},{8,10},{9,11},{10,... | collective-permute-start | bytes 196616 | tf_op jit(solution)/shard_map/ppermute | solution.py:296
  117.5 5.1 %collective-permute-start.4 = (bf16[128,256]{1,0:T(8,128)(2,1)S(1)}, bf16[128,256]{1,0:T(8,128)(2,1)S(1)}, u32[]{:S(2)}, u32[]{:S(2)}) collective-permute-start(bf16[128,256]{1,0:T(8,128)(2,1)S(1)} %shard_map.76.a_ref), channel_id=1, source_target_pairs={{0,1},{1,2},{2,3},{3,0},{4,5},{5,6},{6,7},{7,4},{8,9},{9,10},{10,1... | collective-permute-start | bytes 196616 | tf_op jit(solution)/shard_map/ppermute | solution.py:296

commit v6 on v5

--- a/solution.py
+++ b/solution.py
@@ -10,6 +10,7 @@
 TEACHER_INV = 1.0 / 0.07
 STUDENT_INV = 1.0 / 0.1
 IMAGES = 64
+GRAD_FACTOR = LOSS_SCALE / (IMAGES * 0.1)
 LIVE = 128
 NT = (((1,), (1,)), ((), ()))
 NN = (((1,), (0,)), ((), ()))
@@ -55,7 +56,7 @@
 def head_kernel(
     mask_hbm, teach_hbm, student_hbm, proto_hbm, own_ref, out_ref, mine_ref, mask_ref, teach_ref, student_ref, proto_ref, sems
 ):
-    chunks = 4
+    chunks = 2
     tall = proto_ref.shape[0] // chunks
     small = ((mask_hbm, mask_ref), (teach_hbm, teach_ref), (student_hbm, student_ref))
     first = [pltpu.make_async_copy(src, dst, sems.at[chunks + i]) for i, (src, dst) in enumerate(small)]
@@ -75,21 +76,24 @@
     own_ref[1] = dot(pick, student_ref[0], NN).astype(bf16)
     rows = own_ref[...].reshape(2 * LIVE, 256)
     peak = top = total = None
-    for i in range(chunks):
-        copies[i].wait()
-        for j in (2 * i, 2 * i + 1):
-            mine_ref[128 * j : 128 * (j + 1), :] = proto_ref[pl.ds(pl.multiple_of(j * 1024 + image * 128, 128), 128), :]
-            logits = dot(proto_ref[1024 * j : 1024 * (j + 1), :], rows, NT)
-            teach = jnp.max(logits[:, :LIVE], axis=0, keepdims=True)
-            student = logits[:, LIVE:] * STUDENT_INV
-            now = jnp.max(student, axis=0, keepdims=True)
-            part = jnp.sum(jnp.exp(student - now), axis=0, keepdims=True)
-            if peak is None:
-                peak, top, total = teach, now, part
-            else:
-                peak, both = jnp.maximum(peak, teach), jnp.maximum(top, now)
-                total = total * jnp.exp(top - both) + part * jnp.exp(now - both)
-                top = both
+    for i in range(0, 8192, 512):
+        if i % tall == 0:
+            copies[i // tall].wait()
+        if i % 1024 == 0:
+            at = pl.multiple_of(i + image * 128, 128)
+            mine_ref[i // 8 : i // 8 + 128, :] = proto_ref[pl.ds(at, 128), :]
+        low = dot(proto_ref[i : i + 256, :], rows, NT)
+        high = dot(proto_ref[i + 256 : i + 512, :], rows, NT)
+        teach = jnp.max(jnp.maximum(low[:, :LIVE], high[:, :LIVE]), axis=0, keepdims=True)
+        student = jnp.concatenate([low[:, LIVE:], high[:, LIVE:]], axis=0) * STUDENT_INV
+        now = jnp.max(student, axis=0, keepdims=True)
+        part = jnp.sum(jnp.exp(student - now), axis=0, keepdims=True)
+        if peak is None:
+            peak, top, total = teach, now, part
+        else:
+            peak, both = jnp.maximum(peak, teach), jnp.maximum(top, now)
+            total = total * jnp.exp(top - both) + part * jnp.exp(now - both)
+            top = both
     tile = jnp.concatenate(
         thirds(peak * TEACHER_INV)
         + [jnp.broadcast_to(count, (1, LIVE))]
@@ -98,6 +102,10 @@
         axis=0,
     )
     out_ref[...] = jnp.broadcast_to(tile[None].astype(bf16), out_ref.shape)
+
+
+def spread(tile, ref):
+    ref[...] = jnp.broadcast_to(tile[None].astype(ref.dtype), ref.shape)
 
 
 def expo_kernel(recv_ref, a_ref, b_ref, c_ref, d_ref, mine_ref, et_ref, srows_ref, stat_ref, pay_ref, peak_ref, live_ref):
@@ -128,21 +136,17 @@
         total += dot(jnp.broadcast_to(live_ref[pl.ds(x, 1), :], (16, 256)).astype(bf16), block, NT)
         for core in range(2):
             srows_ref[pl.ds(pl.multiple_of(start + core * 128, 128), 128), :] = piece[core, 1]
-    pay_ref[...] = jnp.broadcast_to(to_tile(total[0:1])[None], pay_ref.shape)
-
-
-def spread(tile, ref):
-    ref[...] = jnp.broadcast_to(tile[None].astype(ref.dtype), ref.shape)
+    spread(to_tile(total[0:1]), pay_ref)
 
 
 def col_kernel(recv_ref, et_ref, *refs):
-    col = 1.0 / jnp.sum(recv_ref[...], axis=0)
+    col = 1.0 / jnp.sum(recv_ref[...].astype(f32), axis=0)
     out = jnp.sum(dot(split3(to_lanes(col)), et_ref[...], NN), axis=0, keepdims=True)
     spread(to_tile(out), refs[-1])
 
 
 def last_col_kernel(recv_ref, et_ref, w_ref, pay_ref, col_ref):
-    col = 1.0 / jnp.sum(recv_ref[...], axis=0)
+    col = 1.0 / jnp.sum(recv_ref[...].astype(f32), axis=0)
     col_ref[...] = col
     lhs = split3(to_lanes(col))
     out = to_tile(jnp.sum(dot(lhs, et_ref[...], NN), axis=0, keepdims=True))
@@ -156,7 +160,7 @@
     spread(to_tile(out), pay_ref)
 
 
-def student_prob_kernel(recv_ref, srows_ref, mine_ref, et_ref, prob_hbm, w_hbm, norm_ref, prob_ref, w_ref, sems):
+def student_prob_kernel(recv_ref, stat_ref, srows_ref, mine_ref, et_ref, prob_hbm, w_hbm, norm_ref, prob_ref, w_ref, sems):
     for image in range(8):
         got = [recv_ref[(image // 2 * 4 + y) * 2 + image % 2].astype(f32) for y in range(4)]
         parts = [v[4:5] + v[5:6] + v[6:7] for v in got]
@@ -164,17 +168,19 @@
         total = sum(jnp.exp(v - top) for v in parts)
         norm_ref[image : image + 1, :] = top + jnp.log(total)
     norm = to_lanes(norm_ref[...])
+    coef = to_lanes(stat_ref[1]) * GRAD_FACTOR
     copies = []
     for r in range(4):
         at = slice(256 * r, 256 * (r + 1))
         log_prob = dot(mine_ref[...], srows_ref[at, :], NT) * STUDENT_INV - norm[:, at]
-        prob_ref[:, at] = jnp.exp(log_prob)
+        prob_ref[:, at] = jnp.exp(log_prob) * coef[:, at]
         w_ref[:, at] = (et_ref[:, at].astype(f32) * log_prob).astype(bf16)
-        at = (pl.ds(0, 1024), pl.ds(256 * r, 256))
-        copies.append(pltpu.make_async_copy(prob_ref.at[at], prob_hbm.at[at], sems.at[r]))
-        copies.append(pltpu.make_async_copy(w_ref.at[at], w_hbm.at[at], sems.at[4 + r]))
-        copies[-2].start()
-        copies[-1].start()
+        if r % 2:
+            at = (pl.ds(0, 1024), pl.ds(256 * (r - 1), 512))
+            copies.append(pltpu.make_async_copy(prob_ref.at[at], prob_hbm.at[at], sems.at[r - 1]))
+            copies.append(pltpu.make_async_copy(w_ref.at[at], w_hbm.at[at], sems.at[r]))
+            copies[-2].start()
+            copies[-1].start()
     for copy in copies:
         copy.wait()
 
@@ -190,25 +196,25 @@
     lo = loss - hi - mid
     which = lax.broadcasted_iota(jnp.int32, (8, 128), 0)
     tail = jnp.where(which == 0, hi, jnp.where(which == 1, mid, jnp.where(which == 2, lo, 0.0))).astype(bf16)
-    coef = weight * (LOSS_SCALE / (IMAGES * 0.1))
+    coef = weight * GRAD_FACTOR
     scale_ref[0] = coef
     scale_ref[1] = coef * row
-    coef_rows = to_lanes(coef)
     scale_rows = to_lanes(coef * row)
     copies = []
     for j in range(4):
         at = slice(256 * j, 256 * (j + 1))
         col = jnp.concatenate([jnp.broadcast_to(col_ref[i : i + 1, :], (128, 128)).T for i in (2 * j, 2 * j + 1)], axis=0)
         col = jnp.concatenate([col] * 8, axis=1)
-        grad = (prob_ref[at, :] * coef_rows - et_ref[at, :].astype(f32) * col * scale_rows).astype(bf16)
+        grad = (prob_ref[at, :] - et_ref[at, :].astype(f32) * col * scale_rows).astype(bf16)
         part = dot(grad, srows_ref[...], NN).astype(bf16)
         for i in (0, 1):
             pout_ref[2 * j + i, 0:128, :] = part[128 * i : 128 * (i + 1), 0:128]
             pout_ref[2 * j + i, 128:256, :] = part[128 * i : 128 * (i + 1), 128:256]
             pout_ref[2 * j + i, 256:264, :] = tail
-        at = pl.ds(2 * j, 2)
-        copies.append(pltpu.make_async_copy(pout_ref.at[at], pout_hbm.at[at], sems.at[j]))
-        copies[-1].start()
+        if j % 2:
+            at = pl.ds(2 * j - 2, 4)
+            copies.append(pltpu.make_async_copy(pout_ref.at[at], pout_hbm.at[at], sems.at[j // 2]))
+            copies[-1].start()
     for copy in copies:
         copy.wait()
 
@@ -222,7 +228,7 @@
 
 
 def own_kernel(recv_ref, scale_ref, stat_ref, norm_ref, rows_hbm, proto_hbm, out_ref, rows_ref, proto_ref, sems):
-    chunks = 4
+    chunks = 2
     tall = proto_ref.shape[0] // chunks
     rows_copy = pltpu.make_async_copy(rows_hbm, rows_ref, sems.at[chunks])
     copies = [
@@ -241,8 +247,8 @@
     rows = rows_ref[...].reshape(2 * LIVE, 256)
     total = jnp.zeros((LIVE, 256), f32)
     for i in range(8):
-        if i % 2 == 0:
-            copies[i // 2].wait()
+        if i % 4 == 0:
+            copies[i // 4].wait()
         col = jnp.concatenate([v[i : i + 1, :] for v in cols], axis=1)
         block = proto_ref[1024 * i : 1024 * (i + 1), :]
         logits = dot(rows, block, NT)
@@ -253,15 +259,14 @@
     out_ref[...] = total.astype(bf16)
 
 
-def end_kernel(mask_ref, recv_ref, a_ref, b_ref, c_ref, d_ref, student_ref, proto_ref, loss_ref):
+def place_kernel(mask_ref, a_ref, b_ref, c_ref, d_ref, student_ref):
     pick = selection(mask_ref[...]).astype(bf16)
     parts = [ref[...].astype(f32) for ref in (a_ref, b_ref, c_ref, d_ref)]
     rows = (parts[0] + parts[2]) + (parts[1] + parts[3])
-    hi = rows.astype(bf16)
-    rest = rows - hi.astype(f32)
-    mid = rest.astype(bf16)
-    lo = (rest - mid.astype(f32)).astype(bf16)
-    student_ref[...] = dot(pick, hi, TN) + dot(pick, mid, TN) + dot(pick, lo, TN)
+    student_ref[...] = sum(dot(pick, part.astype(bf16), TN) for part in thirds(rows))
+
+
+def end_kernel(recv_ref, proto_ref, loss_ref):
     total = jnp.sum(recv_ref[...].astype(f32), axis=0)
     proto_ref[:, 0:128] = total[0:128]
     proto_ref[:, 128:256] = total[128:256]
@@ -316,7 +321,7 @@
             pltpu.VMEM((1, 256, 256), bf16),
             pltpu.VMEM((1, 256, 256), bf16),
             pltpu.VMEM((8192, 256), bf16),
-            pltpu.SemaphoreType.DMA((7,)),
+            pltpu.SemaphoreType.DMA((5,)),
         ],
         compiler_params=pltpu.CompilerParams(vmem_limit_bytes=32 << 20),
     )(*(in_hbm(v) for v in (patch_mask, teacher_feats, student_feats, prototypes)))
@@ -329,7 +334,7 @@
 
     et, srows, stat, pay = call(
         expo_kernel,
-        [((1024, 1024), bf16), ((1024, 256), bf16), ((3, 8, 128), f32), ((8, 8, 128), f32)],
+        [((1024, 1024), bf16), ((1024, 256), bf16), ((3, 8, 128), f32), ((8, 8, 128), bf16)],
         peak_recv, *parts, mine, limit=16, scratch=[pltpu.VMEM((8, 256), f32)] * 2,
     )
 
@@ -343,22 +348,22 @@
             pltpu.HBM((1024, 1024), bf16),
             jax.ShapeDtypeStruct((8, 128), f32),
         ],
-        in_specs=[VM] * 4,
+        in_specs=[VM] * 5,
         out_specs=[pl.BlockSpec(memory_space=pltpu.HBM)] * 2 + [VM],
         scratch_shapes=[
             pltpu.VMEM((1024, 1024), f32),
             pltpu.VMEM((1024, 1024), bf16),
-            pltpu.SemaphoreType.DMA((8,)),
+            pltpu.SemaphoreType.DMA((4,)),
         ],
         compiler_params=pltpu.CompilerParams(vmem_limit_bytes=24 << 20),
         cost_estimate=pl.CostEstimate(flops=1 << 29, bytes_accessed=8 << 20, transcendentals=1 << 20),
-    )(peak_recv, srows, mine, et)
-    (pay,) = call(row_kernel, [((8, 8, 128), f32)], recv, stat, et)
+    )(peak_recv, stat, srows, mine, et)
+    (pay,) = call(row_kernel, [((8, 8, 128), bf16)], recv, stat, et)
     for _ in range(BALANCING_PASSES - 2):
         recv = a2a(pay, "z")
         (pay,) = call(col_kernel, [((32, 8, 128), bf16)], recv, et, norm)
         recv = a2a(pay, PLANE)
-        (pay,) = call(row_kernel, [((8, 8, 128), f32)], recv, stat, et)
+        (pay,) = call(row_kernel, [((8, 8, 128), bf16)], recv, stat, et)
     recv = a2a(pay, "z")
     pay, col = call(last_col_kernel, [((32, 24, 128), bf16), ((8, 128), f32)], recv, et, w)
     recv = a2a(pay, PLANE)
@@ -368,7 +373,7 @@
         out_shape=[pltpu.HBM((8, 264, 128), bf16), jax.ShapeDtypeStruct((2, 8, 128), f32)],
         in_specs=[VM] * 6,
         out_specs=[pl.BlockSpec(memory_space=pltpu.HBM), VM],
-        scratch_shapes=[pltpu.VMEM((8, 264, 128), bf16), pltpu.SemaphoreType.DMA((4,))],
+        scratch_shapes=[pltpu.VMEM((8, 264, 128), bf16), pltpu.SemaphoreType.DMA((2,))],
         compiler_params=pltpu.CompilerParams(vmem_limit_bytes=24 << 20),
     )(recv, stat, col, et, prob, srows)
     proto_recv = a2a(proto_part, "z")
@@ -380,16 +385,14 @@
         scratch_shapes=[
             pltpu.VMEM((2, LIVE, 256), bf16),
             pltpu.VMEM((8192, 256), bf16),
-            pltpu.SemaphoreType.DMA((5,)),
+            pltpu.SemaphoreType.DMA((3,)),
         ],
         compiler_params=pltpu.CompilerParams(vmem_limit_bytes=24 << 20),
         cost_estimate=pl.CostEstimate(flops=1 << 31, bytes_accessed=4 << 20, transcendentals=2 << 20),
     )(recv, scale, stat, norm, in_hbm(own), in_hbm(prototypes))
     student_rows = [student_rows] + [shift(student_rows, "y", 4, k) for k in (1, 2, 3)]
-    student, proto, loss = call(
-        end_kernel, [((256, 256), f32), ((128, 256), f32), ((1, 128), f32)], patch_mask, proto_recv, *student_rows,
-        limit=16,
-    )
+    (student,) = call(place_kernel, [((256, 256), f32)], patch_mask, *student_rows, limit=16)
+    proto, loss = call(end_kernel, [((128, 256), f32), ((1, 128), f32)], proto_recv, limit=16)
     return loss[0, 0], student[None], proto[None]
 
 

time: 131 us -> 129 us (0.985)
    all_to_all x2, waiting for transfers between devices: 9.9 us -> 8.55 us  [a2a(): return lax.all_to_all(v, axes, 0, 0, tiled=True)]
    pallas_call x7 -> x8, Pallas kernels: 6.4 us -> 7.05 us  [call(): pl.pallas_call(kernel, out_shape=out, in_specs=[VM] * len(args), out_spec...]
  transfers between devices with their start and end apart: 9 -> 9, of which waited for: 6 -> 6; matrix products, arithmetic and copies ran while one was open for 0% -> 0% of each run, Pallas kernels for 6% -> 7%
where the time goes in v6:
time: 129 us
  blocking collectives  78.7 us (61%)
  Pallas kernels  20.2 us (16%)
  waiting for transfers between devices  14.7 us (11%)
  starting transfers between devices  14.3 us (11%)
    all_to_all x6, blocking collectives, a2a(): return lax.all_to_all(v, axes, 0, 0, tiled=True)  78.7 us
    all_to_all x2, waiting for transfers between devices, a2a(): return lax.all_to_all(v, axes, 0, 0, tiled=True)  8.55 us
    ppermute x7, starting transfers between devices, shift(): return lax.ppermute(v, axis, [(i, (i + k) % n) for i in range(n)])  7.38 us
    pallas_call x8, Pallas kernels, call(): pl.pallas_call(kernel, out_shape=out, in_specs=[VM] * len(args), out_spec...  7.05 us
    all_to_all x2, starting transfers between devices, a2a(): return lax.all_to_all(v, axes, 0, 0, tiled=True)  6.88 us
    ppermute x7, waiting for transfers between devices, shift(): return lax.ppermute(v, axis, [(i, (i + k) % n) for i in range(n)])  6.15 us
    pallas_call x1, Pallas kernels, local(): pl.pallas_call(own_kernel, out_shape=jax.ShapeDtypeStruct((LIVE, 256), bf...  4.35 us
    pallas_call x1, Pallas kernels, local(): pl.pallas_call(head_kernel, out_shape=[jax.ShapeDtypeStruct((2, LIVE, 256...  3.65 us
  transfers between devices with their start and end apart: 9, of which 6 were waited for; matrix products, arithmetic and copies ran while one was open for 0% of the time, Pallas kernels for 7%

profile of v6, /device:TPU:1, one launch (start us, length us, event | category | flops | bytes accessed | tf_op | source)
XLA Modules:
  0.0 128.6 jit_solution(15032478613989703726)
XLA Ops:
  0.6 3.7 %shard_map.67 = (bf16[2,128,256]{2,1,0:T(8,128)(2,1)S(1)}, bf16[32,8,128]{2,1,0:T(8,128)(2,1)S(1)}, bf16[1024,256]{1,0:T(8,128)(2,1)S(1)}) custom-call(s32[1,256]{1,0:T(1,128)} %mask_ref.1, bf16[1,256,256]{2,1,0:T(8,128)(2,1)} %teach_hbm.1, bf16[1,256,256]{2,1,0:T(8,128)(2,1)} %student_hbm.1, bf16[8192,256]{1,0:T(8,128)(2,1)} %proto_hbm.3), custom_call_target="tpu_custom_call" | custom-call | tf_op jit(solution)/shard_map/pallas_call | solution.py:310
  4.3 3.3 %collective-permute-start = (bf16[2,128,256]{2,1,0:T(8,128)(2,1)S(1)}, bf16[2,128,256]{2,1,0:T(8,128)(2,1)S(1)}, u32[]{:S(2)}, u32[]{:S(2)}) collective-permute-start(bf16[2,128,256]{2,1,0:T(8,128)(2,1)S(1)} %get-tuple-element.20.rows_hbm), channel_id=1, source_target_pairs={{0,4},{4,0},{1,5},{5,1},{2,6},{6,2},{3,7},{7,3},{8,12},{12,8},{9,1... | collective-permute-start | bytes 393224 | tf_op jit(solution)/shard_map/ppermute | solution.py:301
  7.6 1.0 collective-permute-done
  8.6 0.8 collective-permute-start.3
  9.5 0.5 collective-permute-start.2
  10.0 0.6 collective-permute-start.1
  10.6 17.5 %all_to_all.40.recv_ref = bf16[32,8,128]{2,1,0:T(8,128)(2,1)S(1)} all-to-all(bf16[32,8,128]{2,1,0:T(8,128)(2,1)S(1)} %get-tuple-element.19), channel_id=1, replica_groups=mesh['z'=8,'x'=4,'c'=2,'y'=4] {'x','y','c'}, dimensions={0} | all-to-all | bytes 131072 | tf_op jit(solution)/shard_map/all_to_all | solution.py:297
  28.1 1.7 %shard_map.68 = (bf16[1024,1024]{1,0:T(8,128)(2,1)S(1)}, bf16[1024,256]{1,0:T(8,128)(2,1)S(1)}, f32[3,8,128]{2,1,0:T(8,128)S(1)}, bf16[8,8,128]{2,1,0:T(8,128)(2,1)S(1)}) custom-call(bf16[32,8,128]{2,1,0:T(8,128)(2,1)S(1)} %all_to_all.40.recv_ref, bf16[2,2,128,256]{3,2,1,0:T(8,128)(2,1)S(1)} %maximum_select_fusion.a_ref, ...), custom_call_target="tpu_custom_call" | custom-call | tf_op jit(solution)/shard_map/pallas_call | solution.py:281
  29.9 14.6 %all_to_all.41.recv_ref = bf16[8,8,128]{2,1,0:T(8,128)(2,1)S(1)} all-to-all(bf16[8,8,128]{2,1,0:T(8,128)(2,1)S(1)} %get-tuple-element.22), channel_id=1, replica_groups=mesh['z'=8,'x'=4,'c'=2,'y'=4] {'z'}, dimensions={0} | all-to-all | bytes 32768 | tf_op jit(solution)/shard_map/all_to_all | solution.py:297
  44.5 0.4 shard_map.69
  44.9 12.0 %all_to_all.42.recv_ref = bf16[32,8,128]{2,1,0:T(8,128)(2,1)S(1)} all-to-all(bf16[32,8,128]{2,1,0:T(8,128)(2,1)S(1)} %shard_map.69), channel_id=1, replica_groups=mesh['z'=8,'x'=4,'c'=2,'y'=4] {'x','y','c'}, dimensions={0} | all-to-all | bytes 131072 | tf_op jit(solution)/shard_map/all_to_all | solution.py:297
  56.8 1.3 shard_map.70
  58.1 3.3 %all-to-all-start.3 = ((bf16[8,8,128]{2,1,0:T(8,128)(2,1)}), bf16[8,8,128]{2,1,0:T(8,128)(2,1)S(1)}, u32[]{:S(2)}, u32[]{:S(2)}) async-start(bf16[8,8,128]{2,1,0:T(8,128)(2,1)} %shard_map.70), calls=%async_computation.3 | async-start | bytes 32768 | tf_op jit(solution)/shard_map/all_to_all | solution.py:297
  61.5 3.5 %shard_map.71 = (f32[1024,1024]{1,0:T(8,128)}, bf16[1024,1024]{1,0:T(8,128)(2,1)}, f32[8,128]{1,0:T(8,128)S(1)}) custom-call(bf16[32,8,128]{2,1,0:T(8,128)(2,1)S(1)} %all_to_all.40.recv_ref, f32[3,8,128]{2,1,0:T(8,128)S(1)} %get-tuple-element.24.stat_ref, bf16[1024,256]{1,0:T(8,128)(2,1)S(1)} %get-tuple-element.25.srows_ref, ...), custom_call_target="tpu_custom_call" | custom-call | flops 536870912 | bytes 8388608 | tf_op jit(solution)/shard_map/pallas_call | solution.py:344
  65.0 3.1 %all-to-all-done.3.recv_ref = bf16[8,8,128]{2,1,0:T(8,128)(2,1)S(1)} async-done(((bf16[8,8,128]{2,1,0:T(8,128)(2,1)}), bf16[8,8,128]{2,1,0:T(8,128)(2,1)S(1)}, u32[]{:S(2)}, u32[]{:S(2)}) %all-to-all-start.3) | async-done | bytes 16416 | tf_op jit(solution)/shard_map/all_to_all | solution.py:297
  68.0 0.4 shard_map.72
  68.4 12.3 %all_to_all.43.recv_ref = bf16[32,8,128]{2,1,0:T(8,128)(2,1)S(1)} all-to-all(bf16[32,8,128]{2,1,0:T(8,128)(2,1)S(1)} %shard_map.72), channel_id=1, replica_groups=mesh['z'=8,'x'=4,'c'=2,'y'=4] {'x','y','c'}, dimensions={0} | all-to-all | bytes 131072 | tf_op jit(solution)/shard_map/all_to_all | solution.py:297
  80.7 0.7 shard_map.73
  81.4 9.1 %all_to_all.44.recv_ref = bf16[8,8,128]{2,1,0:T(8,128)(2,1)S(1)} all-to-all(bf16[8,8,128]{2,1,0:T(8,128)(2,1)S(1)} %shard_map.73), channel_id=1, replica_groups=mesh['z'=8,'x'=4,'c'=2,'y'=4] {'z'}, dimensions={0} | all-to-all | bytes 32768 | tf_op jit(solution)/shard_map/all_to_all | solution.py:297
  90.5 0.7 shard_map.74
  91.2 13.3 %all_to_all.45.recv_ref = bf16[32,24,128]{2,1,0:T(8,128)(2,1)S(1)} all-to-all(bf16[32,24,128]{2,1,0:T(8,128)(2,1)S(1)} %get-tuple-element.28), channel_id=1, replica_groups=mesh['z'=8,'x'=4,'c'=2,'y'=4] {'x','y','c'}, dimensions={0} | all-to-all | bytes 393216 | tf_op jit(solution)/shard_map/all_to_all | solution.py:297
  104.4 1.6 %shard_map.75 = (bf16[8,264,128]{2,1,0:T(8,128)(2,1)}, f32[2,8,128]{2,1,0:T(8,128)S(1)}) custom-call(bf16[32,24,128]{2,1,0:T(8,128)(2,1)S(1)} %all_to_all.45.recv_ref, f32[3,8,128]{2,1,0:T(8,128)S(1)} %get-tuple-element.24.stat_ref, f32[8,128]{1,0:T(8,128)S(1)} %get-tuple-element.29.col_ref, bf16[1024,1024]{1,0:T(8,128)(2,1)S(1)} %get-tuple-element.23.et_ref, ...), custom_call_target="tpu_custom_call" | custom-call | tf_op jit(solution)/shard_map/pallas_call | solution.py:371
  106.1 3.5 %all-to-all-start.7 = ((bf16[8,264,128]{2,1,0:T(8,128)(2,1)}), bf16[8,264,128]{2,1,0:T(8,128)(2,1)S(1)}, u32[]{:S(2)}, u32[]{:S(2)}) async-start(bf16[8,264,128]{2,1,0:T(8,128)(2,1)} %get-tuple-element.31), calls=%async_computation.7 | async-start | bytes 1081344 | tf_op jit(solution)/shard_map/all_to_all | solution.py:297
  109.6 4.4 %shard_map.77.a_ref = bf16[128,256]{1,0:T(8,128)(2,1)S(1)} custom-call(bf16[32,24,128]{2,1,0:T(8,128)(2,1)S(1)} %all_to_all.45.recv_ref, f32[2,8,128]{2,1,0:T(8,128)S(1)} %get-tuple-element.33.scale_ref, f32[3,8,128]{2,1,0:T(8,128)S(1)} %get-tuple-element.24.stat_ref, f32[8,128]{1,0:T(8,128)S(1)} %get-tuple-element.26.refs_0_.norm_ref, ...), custom_call_target="tpu_custom_call" | custom-call | flops 2147483648 | bytes 4194304 | tf_op jit(solution)/shard_map/pallas_call | solution.py:380
  114.0 1.0 collective-permute-start.6
  115.0 1.1 collective-permute-start.5
  116.1 1.4 %collective-permute-done.6.d_ref = bf16[128,256]{1,0:T(8,128)(2,1)S(1)} collective-permute-done((bf16[128,256]{1,0:T(8,128)(2,1)S(1)}, bf16[128,256]{1,0:T(8,128)(2,1)S(1)}, u32[]{:S(2)}, u32[]{:S(2)}) %collective-permute-start.6) | collective-permute-done | bytes 65568 | tf_op jit(solution)/shard_map/ppermute | solution.py:301
  117.5 2.3 %collective-permute-done.5.c_ref = bf16[128,256]{1,0:T(8,128)(2,1)S(1)} collective-permute-done((bf16[128,256]{1,0:T(8,128)(2,1)S(1)}, bf16[128,256]{1,0:T(8,128)(2,1)S(1)}, u32[]{:S(2)}, u32[]{:S(2)}) %collective-permute-start.5) | collective-permute-done | bytes 65568 | tf_op jit(solution)/shard_map/ppermute | solution.py:301
  119.8 1.5 %collective-permute-done.4.b_ref = bf16[128,256]{1,0:T(8,128)(2,1)S(1)} collective-permute-done((bf16[128,256]{1,0:T(8,128)(2,1)S(1)}, bf16[128,256]{1,0:T(8,128)(2,1)S(1)}, u32[]{:S(2)}, u32[]{:S(2)}) %collective-permute-start.4) | collective-permute-done | bytes 65568 | tf_op jit(solution)/shard_map/ppermute | solution.py:301
  121.3 1.2 shard_map.78
  122.4 5.5 %all-to-all-done.7.recv_ref = bf16[8,264,128]{2,1,0:T(8,128)(2,1)S(1)} async-done(((bf16[8,264,128]{2,1,0:T(8,128)(2,1)}), bf16[8,264,128]{2,1,0:T(8,128)(2,1)S(1)}, u32[]{:S(2)}, u32[]{:S(2)}) %all-to-all-start.7) | async-done | bytes 540704 | tf_op jit(solution)/shard_map/all_to_all | solution.py:297
  127.9 0.7 shard_map.76
  (13 shorter events, 0.1 us)
Async XLA Ops:
  4.3 60.7 %copy-start.2 = (bf16[2,128,256]{2,1,0:T(8,128)(2,1)}, bf16[2,128,256]{2,1,0:T(8,128)(2,1)S(1)}, u32[]{:S(2)}) copy-start(bf16[2,128,256]{2,1,0:T(8,128)(2,1)S(1)} %get-tuple-element.20.rows_hbm) | copy-start | bytes 393220
  4.3 4.3 %collective-permute-start = (bf16[2,128,256]{2,1,0:T(8,128)(2,1)S(1)}, bf16[2,128,256]{2,1,0:T(8,128)(2,1)S(1)}, u32[]{:S(2)}, u32[]{:S(2)}) collective-permute-start(bf16[2,128,256]{2,1,0:T(8,128)(2,1)S(1)} %get-tuple-element.20.rows_hbm), channel_id=1, source_target_pairs={{0,4},{4,0},{1,5},{5,1},{2,6},{6,2},{3,7},{7,3},{8,12},{12,8},{9,1... | collective-permute-start | bytes 393224 | tf_op jit(solution)/shard_map/ppermute | solution.py:301
  8.6 19.5 %collective-permute-start.3 = (bf16[2,2,128,256]{3,2,1,0:T(8,128)(2,1)S(1)}, bf16[2,2,128,256]{3,2,1,0:T(8,128)(2,1)S(1)}, u32[]{:S(2)}, u32[]{:S(2)}) collective-permute-start(bf16[2,2,128,256]{3,2,1,0:T(8,128)(2,1)S(1)} %maximum_select_fusion.a_ref), channel_id=1, source_target_pairs={{0,24},{8,0},{16,8},{24,16},{1,25},{9,1},{17,9},{25,17},{2,26},{10... | collective-permute-start | bytes 786440 | tf_op jit(solution)/shard_map/ppermute | solution.py:301
  9.5 18.6 %collective-permute-start.2 = (bf16[2,2,128,256]{3,2,1,0:T(8,128)(2,1)S(1)}, bf16[2,2,128,256]{3,2,1,0:T(8,128)(2,1)S(1)}, u32[]{:S(2)}, u32[]{:S(2)}) collective-permute-start(bf16[2,2,128,256]{3,2,1,0:T(8,128)(2,1)S(1)} %maximum_select_fusion.a_ref), channel_id=1, source_target_pairs={{0,16},{8,24},{16,0},{24,8},{1,17},{9,25},{17,1},{25,9},{2,18},{10... | collective-permute-start | bytes 786440 | tf_op jit(solution)/shard_map/ppermute | solution.py:301
  10.0 18.1 %collective-permute-start.1 = (bf16[2,2,128,256]{3,2,1,0:T(8,128)(2,1)S(1)}, bf16[2,2,128,256]{3,2,1,0:T(8,128)(2,1)S(1)}, u32[]{:S(2)}, u32[]{:S(2)}) collective-permute-start(bf16[2,2,128,256]{3,2,1,0:T(8,128)(2,1)S(1)} %maximum_select_fusion.a_ref), channel_id=1, source_target_pairs={{0,8},{8,16},{16,24},{24,0},{1,9},{9,17},{17,25},{25,1},{2,10},{10... | collective-permute-start | bytes 786440 | tf_op jit(solution)/shard_map/ppermute | solution.py:301
  58.1 9.9 %all-to-all-start.3 = ((bf16[8,8,128]{2,1,0:T(8,128)(2,1)}), bf16[8,8,128]{2,1,0:T(8,128)(2,1)S(1)}, u32[]{:S(2)}, u32[]{:S(2)}) async-start(bf16[8,8,128]{2,1,0:T(8,128)(2,1)} %shard_map.70), calls=%async_computation.3 | async-start | bytes 32768 | tf_op jit(solution)/shard_map/all_to_all | solution.py:297
  68.0 22.4 %copy-start.1 = (bf16[1024,1024]{1,0:T(8,128)(2,1)S(1)}, bf16[1024,1024]{1,0:T(8,128)(2,1)}, u32[]{:S(2)}) copy-start(bf16[1024,1024]{1,0:T(8,128)(2,1)} %get-tuple-element.27.w_ref) | copy-start | bytes 6291460
  68.0 36.4 %copy-start = (f32[1024,1024]{1,0:T(8,128)S(1)}, f32[1024,1024]{1,0:T(8,128)}, u32[]{:S(2)}) copy-start(f32[1024,1024]{1,0:T(8,128)} %get-tuple-element.30.prob_ref) | copy-start | bytes 12582916
  106.1 21.8 %all-to-all-start.7 = ((bf16[8,264,128]{2,1,0:T(8,128)(2,1)}), bf16[8,264,128]{2,1,0:T(8,128)(2,1)S(1)}, u32[]{:S(2)}, u32[]{:S(2)}) async-start(bf16[8,264,128]{2,1,0:T(8,128)(2,1)} %get-tuple-element.31), calls=%async_computation.7 | async-start | bytes 1081344 | tf_op jit(solution)/shard_map/all_to_all | solution.py:297
  109.6 11.6 %copy-start.3 = (s32[1,256]{1,0:T(1,128)S(1)}, s32[1,256]{1,0:T(1,128)}, u32[]{:S(2)}) copy-start(s32[1,256]{1,0:T(1,128)} %mask_ref.1) | copy-start | bytes 3076
  114.0 3.5 %collective-permute-start.6 = (bf16[128,256]{1,0:T(8,128)(2,1)S(1)}, bf16[128,256]{1,0:T(8,128)(2,1)S(1)}, u32[]{:S(2)}, u32[]{:S(2)}) collective-permute-start(bf16[128,256]{1,0:T(8,128)(2,1)S(1)} %shard_map.77.a_ref), channel_id=1, source_target_pairs={{0,3},{1,0},{2,1},{3,2},{4,7},{5,4},{6,5},{7,6},{8,11},{9,8},{10,9... | collective-permute-start | bytes 196616 | tf_op jit(solution)/shard_map/ppermute | solution.py:301
  115.0 4.8 %collective-permute-start.5 = (bf16[128,256]{1,0:T(8,128)(2,1)S(1)}, bf16[128,256]{1,0:T(8,128)(2,1)S(1)}, u32[]{:S(2)}, u32[]{:S(2)}) collective-permute-start(bf16[128,256]{1,0:T(8,128)(2,1)S(1)} %shard_map.77.a_ref), channel_id=1, source_target_pairs={{0,2},{1,3},{2,0},{3,1},{4,6},{5,7},{6,4},{7,5},{8,10},{9,11},{10,... | collective-permute-start | bytes 196616 | tf_op jit(solution)/shard_map/ppermute | solution.py:301
  116.1 5.2 %collective-permute-start.4 = (bf16[128,256]{1,0:T(8,128)(2,1)S(1)}, bf16[128,256]{1,0:T(8,128)(2,1)S(1)}, u32[]{:S(2)}, u32[]{:S(2)}) collective-permute-start(bf16[128,256]{1,0:T(8,128)(2,1)S(1)} %shard_map.77.a_ref), channel_id=1, source_target_pairs={{0,1},{1,2},{2,3},{3,0},{4,5},{5,6},{6,7},{7,4},{8,9},{9,10},{10,1... | collective-permute-start | bytes 196616 | tf_op jit(solution)/shard_map/ppermute | solution.py:301

commit v7 on v6

--- a/solution.py
+++ b/solution.py
@@ -108,7 +108,8 @@
     ref[...] = jnp.broadcast_to(tile[None].astype(ref.dtype), ref.shape)
 
 
-def expo_kernel(recv_ref, a_ref, b_ref, c_ref, d_ref, mine_ref, et_ref, srows_ref, stat_ref, pay_ref, peak_ref, live_ref):
+def expo_kernel(recv_ref, *refs):
+    pieces, (mine_ref, et_ref, srows_ref, stat_ref, pay_ref, trows_ref) = refs[:8], refs[8:]
     peaks, counts = [], []
     for x in range(4):
         for core in range(2):
@@ -122,21 +123,24 @@
     stat_ref[0] = live
     stat_ref[1] = live / count
     stat_ref[2] = jnp.concatenate(peaks, axis=0)
-    for x in range(4):
-        peak_ref[x : x + 1, :] = jnp.concatenate(peaks[2 * x : 2 * x + 2], axis=1)
-        live_ref[x : x + 1, :] = jnp.concatenate([live[2 * x : 2 * x + 1], live[2 * x + 1 : 2 * x + 2]], axis=1)
-    total = jnp.zeros((16, 1024), f32)
-    for k, piece in enumerate((a_ref, b_ref, c_ref, d_ref)):
+    peak = jnp.concatenate(peaks, axis=1)
+    live_rows = jnp.broadcast_to(to_lanes(live), (16, 1024)).astype(bf16)
+    here = lax.axis_index("c")
+    for k in range(4):
         x = (lax.axis_index("x") + 4 - k) & 3
-        start = pl.multiple_of(x * 256, 256)
-        rows = jnp.concatenate([piece[0, 0], piece[1, 0]], axis=0)
-        logits = dot(mine_ref[...], rows, NT)
-        block = jnp.exp(logits * TEACHER_INV - peak_ref[pl.ds(x, 1), :]).astype(bf16)
-        et_ref[:, pl.ds(start, 256)] = block
-        total += dot(jnp.broadcast_to(live_ref[pl.ds(x, 1), :], (16, 256)).astype(bf16), block, NT)
-        for core in range(2):
-            srows_ref[pl.ds(pl.multiple_of(start + core * 128, 128), 128), :] = piece[core, 1]
-    spread(to_tile(total[0:1]), pay_ref)
+        for core, piece in ((here, pieces[2 * k]), (1 - here, pieces[2 * k + 1])):
+            at = pl.ds(pl.multiple_of(x * 256 + core * 128, 128), 128)
+            trows_ref[at, :] = piece[0]
+            srows_ref[at, :] = piece[1]
+    sums = [jnp.zeros((16, 512), f32)] * 2
+    for r in range(4):
+        at = slice(256 * r, 256 * (r + 1))
+        for j in range(2):
+            logits = dot(mine_ref[512 * j : 512 * (j + 1), :], trows_ref[at, :], NT)
+            block = jnp.exp(logits * TEACHER_INV - peak[:, at]).astype(bf16)
+            et_ref[512 * j : 512 * (j + 1), at] = block
+            sums[j] += dot(live_rows[:, at], block, NT)
+    spread(to_tile(jnp.concatenate(sums, axis=1)[0:1]), pay_ref)
 
 
 def col_kernel(recv_ref, et_ref, *refs):
@@ -306,7 +310,6 @@
 
 
 def local(teacher_feats, student_feats, prototypes, patch_mask):
-    c = lax.axis_index("c")
     own, peak_pay, mine = pl.pallas_call(
         head_kernel,
         out_shape=[
@@ -326,16 +329,15 @@
         compiler_params=pltpu.CompilerParams(vmem_limit_bytes=32 << 20),
     )(*(in_hbm(v) for v in (patch_mask, teacher_feats, student_feats, prototypes)))
 
-    other = shift(own, "c", 2, 1)
-    pair = jnp.where(c == 0, jnp.stack([own, other]), jnp.stack([other, own]))
-    parts = [pair] + [shift(pair, "x", 4, k) for k in (1, 2, 3)]
-
+    parts = [own] + [shift(own, "x", 4, k) for k in (1, 2, 3)]
     peak_recv = a2a(peak_pay, PLANE)
+    peak_recv, *parts = lax.optimization_barrier((peak_recv, *parts))
+    pieces = [v for part in parts for v in (part, shift(part, "c", 2, 1))]
 
     et, srows, stat, pay = call(
         expo_kernel,
         [((1024, 1024), bf16), ((1024, 256), bf16), ((3, 8, 128), f32), ((8, 8, 128), bf16)],
-        peak_recv, *parts, mine, limit=16, scratch=[pltpu.VMEM((8, 256), f32)] * 2,
+        peak_recv, *pieces, mine, limit=16, scratch=[pltpu.VMEM((1024, 256), bf16)],
     )
 
     recv = a2a(pay, "z")

time: 129 us -> 127 us (0.984)
  blocking collectives: 78.7 us -> 76.4 us
    all_to_all x6, blocking collectives: 78.7 us -> 76.4 us  [a2a(): return lax.all_to_all(v, axes, 0, 0, tiled=True)]
    ppermute x7 -> x10, starting transfers between devices: 7.38 us -> 7.72 us  [shift(): return lax.ppermute(v, axis, [(i, (i + k) % n) for i in range(n)])]
    ppermute x7 -> x10, waiting for transfers between devices: 6.15 us -> 6.39 us  [shift(): return lax.ppermute(v, axis, [(i, (i + k) % n) for i in range(n)])]
  transfers between devices with their start and end apart: 9 -> 12, of which waited for: 6 -> 9; matrix products, arithmetic and copies ran while one was open for 0% -> 0% of each run, Pallas kernels for 7% -> 7%
where the time goes in v7:
time: 127 us
  blocking collectives  76.4 us (60%)
  Pallas kernels  20.1 us (16%)
  waiting for transfers between devices  15 us (12%)
  starting transfers between devices  14.6 us (11%)
    all_to_all x6, blocking collectives, a2a(): return lax.all_to_all(v, axes, 0, 0, tiled=True)  76.4 us
    all_to_all x2, waiting for transfers between devices, a2a(): return lax.all_to_all(v, axes, 0, 0, tiled=True)  8.57 us
    ppermute x10, starting transfers between devices, shift(): return lax.ppermute(v, axis, [(i, (i + k) % n) for i in range(n)])  7.72 us
    pallas_call x8, Pallas kernels, call(): pl.pallas_call(kernel, out_shape=out, in_specs=[VM] * len(args), out_spec...  6.98 us
    all_to_all x2, starting transfers between devices, a2a(): return lax.all_to_all(v, axes, 0, 0, tiled=True)  6.88 us
    ppermute x10, waiting for transfers between devices, shift(): return lax.ppermute(v, axis, [(i, (i + k) % n) for i in range(n)])  6.39 us
    pallas_call x1, Pallas kernels, local(): pl.pallas_call(own_kernel, out_shape=jax.ShapeDtypeStruct((LIVE, 256), bf...  4.36 us
    pallas_call x1, Pallas kernels, local(): pl.pallas_call(head_kernel, out_shape=[jax.ShapeDtypeStruct((2, LIVE, 256...  3.65 us
  transfers between devices with their start and end apart: 12, of which 9 were waited for; matrix products, arithmetic and copies ran while one was open for 0% of the time, Pallas kernels for 7%

profile of v7, /device:TPU:1, one launch (start us, length us, event | category | flops | bytes accessed | tf_op | source)
XLA Modules:
  0.0 126.8 jit_solution(16247010268745291446)
XLA Ops:
  0.6 3.7 %shard_map.67 = (bf16[2,128,256]{2,1,0:T(8,128)(2,1)S(1)}, bf16[32,8,128]{2,1,0:T(8,128)(2,1)S(1)}, bf16[1024,256]{1,0:T(8,128)(2,1)S(1)}) custom-call(s32[1,256]{1,0:T(1,128)} %mask_ref.1, bf16[1,256,256]{2,1,0:T(8,128)(2,1)} %teach_hbm.1, bf16[1,256,256]{2,1,0:T(8,128)(2,1)} %student_hbm.1, bf16[8192,256]{1,0:T(8,128)(2,1)} %proto_hbm.3), custom_call_target="tpu_custom_call" | custom-call | tf_op jit(solution)/shard_map/pallas_call | solution.py:313
  4.3 3.4 %collective-permute-start.2 = (bf16[2,128,256]{2,1,0:T(8,128)(2,1)S(1)}, bf16[2,128,256]{2,1,0:T(8,128)(2,1)S(1)}, u32[]{:S(2)}, u32[]{:S(2)}) collective-permute-start(bf16[2,128,256]{2,1,0:T(8,128)(2,1)S(1)} %get-tuple-element.27.refs_0_.rows_hbm), channel_id=1, source_target_pairs={{0,24},{8,0},{16,8},{24,16},{1,25},{9,1},{17,9},{25,17},{2,26},{10... | collective-permute-start | bytes 393224 | tf_op jit(solution)/shard_map/ppermute | solution.py:305
  7.7 0.5 collective-permute-start.1
  8.2 0.6 collective-permute-start
  8.8 15.1 %all_to_all.40.recv_ref = bf16[32,8,128]{2,1,0:T(8,128)(2,1)S(1)} all-to-all(bf16[32,8,128]{2,1,0:T(8,128)(2,1)S(1)} %get-tuple-element.24), channel_id=1, replica_groups=mesh['z'=8,'x'=4,'c'=2,'y'=4] {'x','y','c'}, dimensions={0} | all-to-all | bytes 131072 | tf_op jit(solution)/shard_map/all_to_all | solution.py:301
  23.9 0.5 collective-permute-start.3
  24.5 0.4 collective-permute-start.5
  26.3 1.7 %shard_map.68 = (bf16[1024,1024]{1,0:T(8,128)(2,1)S(1)}, bf16[1024,256]{1,0:T(8,128)(2,1)S(1)}, f32[3,8,128]{2,1,0:T(8,128)S(1)}, bf16[8,8,128]{2,1,0:T(8,128)(2,1)S(1)}) custom-call(bf16[32,8,128]{2,1,0:T(8,128)(2,1)S(1)} %all_to_all.40.recv_ref, bf16[2,128,256]{2,1,0:T(8,128)(2,1)S(1)} %get-tuple-element.27.refs_0_.rows_hbm, ...), custom_call_target="tpu_custom_call" | custom-call | tf_op jit(solution)/shard_map/pallas_call | solution.py:285
  27.9 14.6 %all_to_all.41.recv_ref = bf16[8,8,128]{2,1,0:T(8,128)(2,1)S(1)} all-to-all(bf16[8,8,128]{2,1,0:T(8,128)(2,1)S(1)} %get-tuple-element.32), channel_id=1, replica_groups=mesh['z'=8,'x'=4,'c'=2,'y'=4] {'z'}, dimensions={0} | all-to-all | bytes 32768 | tf_op jit(solution)/shard_map/all_to_all | solution.py:301
  42.5 0.4 shard_map.69
  43.0 12.1 %all_to_all.42.recv_ref = bf16[32,8,128]{2,1,0:T(8,128)(2,1)S(1)} all-to-all(bf16[32,8,128]{2,1,0:T(8,128)(2,1)S(1)} %shard_map.69), channel_id=1, replica_groups=mesh['z'=8,'x'=4,'c'=2,'y'=4] {'x','y','c'}, dimensions={0} | all-to-all | bytes 131072 | tf_op jit(solution)/shard_map/all_to_all | solution.py:301
  55.0 1.3 %shard_map.70 = bf16[8,8,128]{2,1,0:T(8,128)(2,1)} custom-call(bf16[32,8,128]{2,1,0:T(8,128)(2,1)S(1)} %all_to_all.42.recv_ref, f32[3,8,128]{2,1,0:T(8,128)S(1)} %get-tuple-element.34.stat_ref, bf16[1024,1024]{1,0:T(8,128)(2,1)S(1)} %get-tuple-element.33.et_ref), custom_call_target="tpu_custom_call" | custom-call | tf_op jit(solution)/shard_map/pallas_call | solution.py:285
  56.3 3.3 %all-to-all-start.3 = ((bf16[8,8,128]{2,1,0:T(8,128)(2,1)}), bf16[8,8,128]{2,1,0:T(8,128)(2,1)S(1)}, u32[]{:S(2)}, u32[]{:S(2)}) async-start(bf16[8,8,128]{2,1,0:T(8,128)(2,1)} %shard_map.70), calls=%async_computation.3 | async-start | bytes 32768 | tf_op jit(solution)/shard_map/all_to_all | solution.py:301
  59.7 3.5 %shard_map.71 = (f32[1024,1024]{1,0:T(8,128)}, bf16[1024,1024]{1,0:T(8,128)(2,1)}, f32[8,128]{1,0:T(8,128)S(1)}) custom-call(bf16[32,8,128]{2,1,0:T(8,128)(2,1)S(1)} %all_to_all.40.recv_ref, f32[3,8,128]{2,1,0:T(8,128)S(1)} %get-tuple-element.34.stat_ref, bf16[1024,256]{1,0:T(8,128)(2,1)S(1)} %get-tuple-element.35.srows_ref, ...), custom_call_target="tpu_custom_call" | custom-call | flops 536870912 | bytes 8388608 | tf_op jit(solution)/shard_map/pallas_call | solution.py:346
  63.1 3.1 %all-to-all-done.3.recv_ref = bf16[8,8,128]{2,1,0:T(8,128)(2,1)S(1)} async-done(((bf16[8,8,128]{2,1,0:T(8,128)(2,1)}), bf16[8,8,128]{2,1,0:T(8,128)(2,1)S(1)}, u32[]{:S(2)}, u32[]{:S(2)}) %all-to-all-start.3) | async-done | bytes 16416 | tf_op jit(solution)/shard_map/all_to_all | solution.py:301
  66.2 0.4 shard_map.72
  66.6 12.3 %all_to_all.43.recv_ref = bf16[32,8,128]{2,1,0:T(8,128)(2,1)S(1)} all-to-all(bf16[32,8,128]{2,1,0:T(8,128)(2,1)S(1)} %shard_map.72), channel_id=1, replica_groups=mesh['z'=8,'x'=4,'c'=2,'y'=4] {'x','y','c'}, dimensions={0} | all-to-all | bytes 131072 | tf_op jit(solution)/shard_map/all_to_all | solution.py:301
  78.9 0.7 shard_map.73
  79.6 9.1 %all_to_all.44.recv_ref = bf16[8,8,128]{2,1,0:T(8,128)(2,1)S(1)} all-to-all(bf16[8,8,128]{2,1,0:T(8,128)(2,1)S(1)} %shard_map.73), channel_id=1, replica_groups=mesh['z'=8,'x'=4,'c'=2,'y'=4] {'z'}, dimensions={0} | all-to-all | bytes 32768 | tf_op jit(solution)/shard_map/all_to_all | solution.py:301
  88.7 0.7 shard_map.74
  89.3 13.3 %all_to_all.45.recv_ref = bf16[32,24,128]{2,1,0:T(8,128)(2,1)S(1)} all-to-all(bf16[32,24,128]{2,1,0:T(8,128)(2,1)S(1)} %get-tuple-element.38), channel_id=1, replica_groups=mesh['z'=8,'x'=4,'c'=2,'y'=4] {'x','y','c'}, dimensions={0} | all-to-all | bytes 393216 | tf_op jit(solution)/shard_map/all_to_all | solution.py:301
  102.6 1.6 %shard_map.75 = (bf16[8,264,128]{2,1,0:T(8,128)(2,1)}, f32[2,8,128]{2,1,0:T(8,128)S(1)}) custom-call(bf16[32,24,128]{2,1,0:T(8,128)(2,1)S(1)} %all_to_all.45.recv_ref, f32[3,8,128]{2,1,0:T(8,128)S(1)} %get-tuple-element.34.stat_ref, f32[8,128]{1,0:T(8,128)S(1)} %get-tuple-element.39.col_ref, bf16[1024,1024]{1,0:T(8,128)(2,1)S(1)} %get-tuple-element.33.et_ref, ...), custom_call_target="tpu_custom_call" | custom-call | tf_op jit(solution)/shard_map/pallas_call | solution.py:373
  104.2 3.5 %all-to-all-start.7 = ((bf16[8,264,128]{2,1,0:T(8,128)(2,1)}), bf16[8,264,128]{2,1,0:T(8,128)(2,1)S(1)}, u32[]{:S(2)}, u32[]{:S(2)}) async-start(bf16[8,264,128]{2,1,0:T(8,128)(2,1)} %get-tuple-element.41), calls=%async_computation.7 | async-start | bytes 1081344 | tf_op jit(solution)/shard_map/all_to_all | solution.py:301
  107.8 4.4 %shard_map.77.a_ref = bf16[128,256]{1,0:T(8,128)(2,1)S(1)} custom-call(bf16[32,24,128]{2,1,0:T(8,128)(2,1)S(1)} %all_to_all.45.recv_ref, f32[2,8,128]{2,1,0:T(8,128)S(1)} %get-tuple-element.43.scale_ref, f32[3,8,128]{2,1,0:T(8,128)S(1)} %get-tuple-element.34.stat_ref, f32[8,128]{1,0:T(8,128)S(1)} %get-tuple-element.36.refs_0_.norm_ref, ...), custom_call_target="tpu_custom_call" | custom-call | flops 2147483648 | bytes 4194304 | tf_op jit(solution)/shard_map/pallas_call | solution.py:382
  112.2 1.0 collective-permute-start.9
  113.2 1.1 collective-permute-start.8
  114.3 1.4 %collective-permute-done.9.d_ref = bf16[128,256]{1,0:T(8,128)(2,1)S(1)} collective-permute-done((bf16[128,256]{1,0:T(8,128)(2,1)S(1)}, bf16[128,256]{1,0:T(8,128)(2,1)S(1)}, u32[]{:S(2)}, u32[]{:S(2)}) %collective-permute-start.9) | collective-permute-done | bytes 65568 | tf_op jit(solution)/shard_map/ppermute | solution.py:305
  115.7 2.3 %collective-permute-done.8.c_ref = bf16[128,256]{1,0:T(8,128)(2,1)S(1)} collective-permute-done((bf16[128,256]{1,0:T(8,128)(2,1)S(1)}, bf16[128,256]{1,0:T(8,128)(2,1)S(1)}, u32[]{:S(2)}, u32[]{:S(2)}) %collective-permute-start.8) | collective-permute-done | bytes 65568 | tf_op jit(solution)/shard_map/ppermute | solution.py:305
  118.0 1.5 %collective-permute-done.7.b_ref = bf16[128,256]{1,0:T(8,128)(2,1)S(1)} collective-permute-done((bf16[128,256]{1,0:T(8,128)(2,1)S(1)}, bf16[128,256]{1,0:T(8,128)(2,1)S(1)}, u32[]{:S(2)}, u32[]{:S(2)}) %collective-permute-start.7) | collective-permute-done | bytes 65568 | tf_op jit(solution)/shard_map/ppermute | solution.py:305
  119.4 1.2 shard_map.78
  120.6 5.5 %all-to-all-done.7.recv_ref = bf16[8,264,128]{2,1,0:T(8,128)(2,1)S(1)} async-done(((bf16[8,264,128]{2,1,0:T(8,128)(2,1)}), bf16[8,264,128]{2,1,0:T(8,128)(2,1)S(1)}, u32[]{:S(2)}, u32[]{:S(2)}) %all-to-all-start.7) | async-done | bytes 540704 | tf_op jit(solution)/shard_map/all_to_all | solution.py:301
  126.1 0.7 shard_map.76
  (18 shorter events, 1.5 us)
Async XLA Ops:
  4.3 58.8 %copy-start.2 = (bf16[2,128,256]{2,1,0:T(8,128)(2,1)}, bf16[2,128,256]{2,1,0:T(8,128)(2,1)S(1)}, u32[]{:S(2)}) copy-start(bf16[2,128,256]{2,1,0:T(8,128)(2,1)S(1)} %get-tuple-element.27.refs_0_.rows_hbm) | copy-start | bytes 393220
  4.3 19.6 %collective-permute-start.2 = (bf16[2,128,256]{2,1,0:T(8,128)(2,1)S(1)}, bf16[2,128,256]{2,1,0:T(8,128)(2,1)S(1)}, u32[]{:S(2)}, u32[]{:S(2)}) collective-permute-start(bf16[2,128,256]{2,1,0:T(8,128)(2,1)S(1)} %get-tuple-element.27.refs_0_.rows_hbm), channel_id=1, source_target_pairs={{0,24},{8,0},{16,8},{24,16},{1,25},{9,1},{17,9},{25,17},{2,26},{10... | collective-permute-start | bytes 393224 | tf_op jit(solution)/shard_map/ppermute | solution.py:305
  7.7 16.2 %collective-permute-start.1 = (bf16[2,128,256]{2,1,0:T(8,128)(2,1)S(1)}, bf16[2,128,256]{2,1,0:T(8,128)(2,1)S(1)}, u32[]{:S(2)}, u32[]{:S(2)}) collective-permute-start(bf16[2,128,256]{2,1,0:T(8,128)(2,1)S(1)} %get-tuple-element.27.refs_0_.rows_hbm), channel_id=1, source_target_pairs={{0,16},{8,24},{16,0},{24,8},{1,17},{9,25},{17,1},{25,9},{2,18},{10... | collective-permute-start | bytes 393224 | tf_op jit(solution)/shard_map/ppermute | solution.py:305
  8.2 15.7 %collective-permute-start = (bf16[2,128,256]{2,1,0:T(8,128)(2,1)S(1)}, bf16[2,128,256]{2,1,0:T(8,128)(2,1)S(1)}, u32[]{:S(2)}, u32[]{:S(2)}) collective-permute-start(bf16[2,128,256]{2,1,0:T(8,128)(2,1)S(1)} %get-tuple-element.27.refs_0_.rows_hbm), channel_id=1, source_target_pairs={{0,8},{8,16},{16,24},{24,0},{1,9},{9,17},{17,25},{25,1},{2,10},{10... | collective-permute-start | bytes 393224 | tf_op jit(solution)/shard_map/ppermute | solution.py:305
  23.9 1.5 %collective-permute-start.3 = (bf16[2,128,256]{2,1,0:T(8,128)(2,1)S(1)}, bf16[2,128,256]{2,1,0:T(8,128)(2,1)S(1)}, u32[]{:S(2)}, u32[]{:S(2)}) collective-permute-start(bf16[2,128,256]{2,1,0:T(8,128)(2,1)S(1)} %get-tuple-element.27.refs_0_.rows_hbm), channel_id=1, source_target_pairs={{0,4},{4,0},{1,5},{5,1},{2,6},{6,2},{3,7},{7,3},{8,12},{12,8},{9,1... | collective-permute-start | bytes 393224 | tf_op jit(solution)/shard_map/ppermute | solution.py:305
  24.4 1.3 %collective-permute-start.4 = (bf16[2,128,256]{2,1,0:T(8,128)(2,1)S(1)}, bf16[2,128,256]{2,1,0:T(8,128)(2,1)S(1)}, u32[]{:S(2)}, u32[]{:S(2)}) collective-permute-start(bf16[2,128,256]{2,1,0:T(8,128)(2,1)S(1)} %collective-permute-done.refs_2_), channel_id=1, source_target_pairs={{0,4},{4,0},{1,5},{5,1},{2,6},{6,2},{3,7},{7,3},{8,12},{12,8},{9,1... | collective-permute-start | bytes 393224 | tf_op jit(solution)/shard_map/ppermute | solution.py:305
  24.5 1.4 %collective-permute-start.5 = (bf16[2,128,256]{2,1,0:T(8,128)(2,1)S(1)}, bf16[2,128,256]{2,1,0:T(8,128)(2,1)S(1)}, u32[]{:S(2)}, u32[]{:S(2)}) collective-permute-start(bf16[2,128,256]{2,1,0:T(8,128)(2,1)S(1)} %collective-permute-done.1.refs_4_), channel_id=1, source_target_pairs={{0,4},{4,0},{1,5},{5,1},{2,6},{6,2},{3,7},{7,3},{8,12},{12,8},{9,1... | collective-permute-start | bytes 393224 | tf_op jit(solution)/shard_map/ppermute | solution.py:305
  24.9 1.3 %collective-permute-start.6 = (bf16[2,128,256]{2,1,0:T(8,128)(2,1)S(1)}, bf16[2,128,256]{2,1,0:T(8,128)(2,1)S(1)}, u32[]{:S(2)}, u32[]{:S(2)}) collective-permute-start(bf16[2,128,256]{2,1,0:T(8,128)(2,1)S(1)} %collective-permute-done.2.refs_6_), channel_id=1, source_target_pairs={{0,4},{4,0},{1,5},{5,1},{2,6},{6,2},{3,7},{7,3},{8,12},{12,8},{9,1... | collective-permute-start | bytes 393224 | tf_op jit(solution)/shard_map/ppermute | solution.py:305
  56.3 9.9 %all-to-all-start.3 = ((bf16[8,8,128]{2,1,0:T(8,128)(2,1)}), bf16[8,8,128]{2,1,0:T(8,128)(2,1)S(1)}, u32[]{:S(2)}, u32[]{:S(2)}) async-start(bf16[8,8,128]{2,1,0:T(8,128)(2,1)} %shard_map.70), calls=%async_computation.3 | async-start | bytes 32768 | tf_op jit(solution)/shard_map/all_to_all | solution.py:301
  66.2 22.4 %copy-start.1 = (bf16[1024,1024]{1,0:T(8,128)(2,1)S(1)}, bf16[1024,1024]{1,0:T(8,128)(2,1)}, u32[]{:S(2)}) copy-start(bf16[1024,1024]{1,0:T(8,128)(2,1)} %get-tuple-element.37.w_ref) | copy-start | bytes 6291460
  66.2 36.4 %copy-start = (f32[1024,1024]{1,0:T(8,128)S(1)}, f32[1024,1024]{1,0:T(8,128)}, u32[]{:S(2)}) copy-start(f32[1024,1024]{1,0:T(8,128)} %get-tuple-element.40.prob_ref) | copy-start | bytes 12582916
  104.2 21.8 %all-to-all-start.7 = ((bf16[8,264,128]{2,1,0:T(8,128)(2,1)}), bf16[8,264,128]{2,1,0:T(8,128)(2,1)S(1)}, u32[]{:S(2)}, u32[]{:S(2)}) async-start(bf16[8,264,128]{2,1,0:T(8,128)(2,1)} %get-tuple-element.41), calls=%async_computation.7 | async-start | bytes 1081344 | tf_op jit(solution)/shard_map/all_to_all | solution.py:301
  107.8 11.6 %copy-start.3 = (s32[1,256]{1,0:T(1,128)S(1)}, s32[1,256]{1,0:T(1,128)}, u32[]{:S(2)}) copy-start(s32[1,256]{1,0:T(1,128)} %mask_ref.1) | copy-start | bytes 3076
  112.2 3.5 %collective-permute-start.9 = (bf16[128,256]{1,0:T(8,128)(2,1)S(1)}, bf16[128,256]{1,0:T(8,128)(2,1)S(1)}, u32[]{:S(2)}, u32[]{:S(2)}) collective-permute-start(bf16[128,256]{1,0:T(8,128)(2,1)S(1)} %shard_map.77.a_ref), channel_id=1, source_target_pairs={{0,3},{1,0},{2,1},{3,2},{4,7},{5,4},{6,5},{7,6},{8,11},{9,8},{10,9... | collective-permute-start | bytes 196616 | tf_op jit(solution)/shard_map/ppermute | solution.py:305
  113.2 4.8 %collective-permute-start.8 = (bf16[128,256]{1,0:T(8,128)(2,1)S(1)}, bf16[128,256]{1,0:T(8,128)(2,1)S(1)}, u32[]{:S(2)}, u32[]{:S(2)}) collective-permute-start(bf16[128,256]{1,0:T(8,128)(2,1)S(1)} %shard_map.77.a_ref), channel_id=1, source_target_pairs={{0,2},{1,3},{2,0},{3,1},{4,6},{5,7},{6,4},{7,5},{8,10},{9,11},{10,... | collective-permute-start | bytes 196616 | tf_op jit(solution)/shard_map/ppermute | solution.py:305
  114.3 5.2 %collective-permute-start.7 = (bf16[128,256]{1,0:T(8,128)(2,1)S(1)}, bf16[128,256]{1,0:T(8,128)(2,1)S(1)}, u32[]{:S(2)}, u32[]{:S(2)}) collective-permute-start(bf16[128,256]{1,0:T(8,128)(2,1)S(1)} %shard_map.77.a_ref), channel_id=1, source_target_pairs={{0,1},{1,2},{2,3},{3,0},{4,5},{5,6},{6,7},{7,4},{8,9},{9,10},{10,1... | collective-permute-start | bytes 196616 | tf_op jit(solution)/shard_map/ppermute | solution.py:305

commit v8 on v7

--- a/solution.py
+++ b/solution.py
@@ -29,6 +29,18 @@
 
 def to_tile(v):
     return jnp.concatenate([v[:, 128 * i : 128 * (i + 1)] for i in range(8)], axis=0)
+
+
+def halves(tile):
+    even, odd = (jnp.concatenate([tile[i : i + 1] for i in range(start, 8, 2)], axis=1) for start in (0, 1))
+    first = lax.axis_index("c") == 0
+    return jnp.where(first, even, odd), jnp.where(first, odd, even)
+
+
+def join(own, other):
+    first = lax.axis_index("c") == 0
+    even, odd = jnp.where(first, own, other), jnp.where(first, other, own)
+    return jnp.concatenate([v[:, 128 * x : 128 * (x + 1)] for x in range(4) for v in (even, odd)], axis=0)
 
 
 def thirds(v):
@@ -108,8 +120,26 @@
     ref[...] = jnp.broadcast_to(tile[None].astype(ref.dtype), ref.shape)
 
 
-def expo_kernel(recv_ref, *refs):
-    pieces, (mine_ref, et_ref, srows_ref, stat_ref, pay_ref, trows_ref) = refs[:8], refs[8:]
+def order_kernel(recv_ref, a_ref, b_ref, c_ref, d_ref, teach_ref, student_ref):
+    for k, piece in enumerate((a_ref, b_ref, c_ref, d_ref)):
+        x = (lax.axis_index("x") + 4 - k) & 3
+        teach_ref[x] = piece[0]
+        student_ref[x] = piece[1]
+
+
+def expo_half(rows_ref, mine_ref, et_ref, peak, live, sums):
+    for r in range(2):
+        at = slice(256 * r, 256 * (r + 1))
+        rows = rows_ref[2 * r : 2 * r + 2].reshape(256, 256)
+        weights = jnp.broadcast_to(live[:, at], (16, 256)).astype(bf16)
+        for j in range(2):
+            logits = dot(mine_ref[512 * j : 512 * (j + 1), :], rows, NT)
+            block = jnp.exp(logits * TEACHER_INV - peak[:, at]).astype(bf16)
+            et_ref[512 * j : 512 * (j + 1), at] = block
+            sums[j] += dot(weights, block, NT)
+
+
+def expo_own_kernel(recv_ref, rows_ref, mine_ref, et_ref, stat_ref, sum_ref):
     peaks, counts = [], []
     for x in range(4):
         for core in range(2):
@@ -117,68 +147,69 @@
             tops = [v[0:1] + v[1:2] + v[2:3] for v in got]
             peaks.append(jnp.maximum(jnp.maximum(tops[0], tops[1]), jnp.maximum(tops[2], tops[3])))
             counts.append(got[0][3:4])
+    peak = jnp.concatenate(peaks, axis=0)
     count = jnp.concatenate(counts, axis=0)
     slot = lax.broadcasted_iota(jnp.int32, (8, 128), 1).astype(f32)
     live = jnp.where(slot < count, 1.0, 0.0)
     stat_ref[0] = live
     stat_ref[1] = live / count
-    stat_ref[2] = jnp.concatenate(peaks, axis=0)
-    peak = jnp.concatenate(peaks, axis=1)
-    live_rows = jnp.broadcast_to(to_lanes(live), (16, 1024)).astype(bf16)
-    here = lax.axis_index("c")
-    for k in range(4):
-        x = (lax.axis_index("x") + 4 - k) & 3
-        for core, piece in ((here, pieces[2 * k]), (1 - here, pieces[2 * k + 1])):
-            at = pl.ds(pl.multiple_of(x * 256 + core * 128, 128), 128)
-            trows_ref[at, :] = piece[0]
-            srows_ref[at, :] = piece[1]
+    stat_ref[2] = peak
     sums = [jnp.zeros((16, 512), f32)] * 2
-    for r in range(4):
-        at = slice(256 * r, 256 * (r + 1))
-        for j in range(2):
-            logits = dot(mine_ref[512 * j : 512 * (j + 1), :], trows_ref[at, :], NT)
-            block = jnp.exp(logits * TEACHER_INV - peak[:, at]).astype(bf16)
-            et_ref[512 * j : 512 * (j + 1), at] = block
-            sums[j] += dot(live_rows[:, at], block, NT)
+    expo_half(rows_ref, mine_ref, et_ref, halves(peak)[0], halves(live)[0], sums)
+    sum_ref[...] = jnp.concatenate(sums, axis=1)
+
+
+def expo_other_kernel(stat_ref, sum_ref, rows_ref, mine_ref, et_ref, pay_ref):
+    sums = [sum_ref[:, 0:512], sum_ref[:, 512:1024]]
+    expo_half(rows_ref, mine_ref, et_ref, halves(stat_ref[2])[1], halves(stat_ref[0])[1], sums)
     spread(to_tile(jnp.concatenate(sums, axis=1)[0:1]), pay_ref)
 
 
-def col_kernel(recv_ref, et_ref, *refs):
+def over_columns(lhs, own_ref, other_ref):
+    parts = [jnp.sum(dot(lhs, ref[...], NN), axis=0, keepdims=True) for ref in (own_ref, other_ref)]
+    return join(*parts)
+
+
+def col_kernel(recv_ref, own_ref, other_ref, *refs):
     col = 1.0 / jnp.sum(recv_ref[...].astype(f32), axis=0)
-    out = jnp.sum(dot(split3(to_lanes(col)), et_ref[...], NN), axis=0, keepdims=True)
-    spread(to_tile(out), refs[-1])
-
-
-def last_col_kernel(recv_ref, et_ref, w_ref, pay_ref, col_ref):
+    spread(over_columns(split3(to_lanes(col)), own_ref, other_ref), refs[-1])
+
+
+def last_col_kernel(recv_ref, own_ref, other_ref, w_ref, pay_ref, col_ref):
     col = 1.0 / jnp.sum(recv_ref[...].astype(f32), axis=0)
     col_ref[...] = col
     lhs = split3(to_lanes(col))
-    out = to_tile(jnp.sum(dot(lhs, et_ref[...], NN), axis=0, keepdims=True))
-    entropy = to_tile(jnp.sum(dot(lhs, w_ref[...], NN), axis=0, keepdims=True))
-    spread(jnp.concatenate([out, entropy, col], axis=0), pay_ref)
-
-
-def row_kernel(recv_ref, stat_ref, et_ref, pay_ref):
+    out = over_columns(lhs, own_ref, other_ref)
+    entropy = jnp.sum(dot(lhs, w_ref[...], NN), axis=0, keepdims=True)
+    spread(jnp.concatenate([out, join(entropy[:, :512], entropy[:, 512:]), col], axis=0), pay_ref)
+
+
+def row_kernel(recv_ref, stat_ref, own_ref, other_ref, pay_ref):
     row = stat_ref[0] / jnp.sum(recv_ref[...].astype(f32), axis=0)
-    out = jnp.sum(dot(split3(to_lanes(row)), et_ref[...], NT), axis=0, keepdims=True)
-    spread(to_tile(out), pay_ref)
-
-
-def student_prob_kernel(recv_ref, stat_ref, srows_ref, mine_ref, et_ref, prob_hbm, w_hbm, norm_ref, prob_ref, w_ref, sems):
+    parts = [dot(split3(v), ref[...], NT) for v, ref in zip(halves(row), (own_ref, other_ref))]
+    spread(to_tile(jnp.sum(parts[0] + parts[1], axis=0, keepdims=True)), pay_ref)
+
+
+def student_prob_kernel(
+    recv_ref, stat_ref, sown_ref, sother_ref, mine_ref, own_ref, other_ref, prob_hbm, w_hbm, norm_ref, prob_ref, w_ref, sems
+):
     for image in range(8):
         got = [recv_ref[(image // 2 * 4 + y) * 2 + image % 2].astype(f32) for y in range(4)]
         parts = [v[4:5] + v[5:6] + v[6:7] for v in got]
         top = jnp.maximum(jnp.maximum(parts[0], parts[1]), jnp.maximum(parts[2], parts[3]))
         total = sum(jnp.exp(v - top) for v in parts)
         norm_ref[image : image + 1, :] = top + jnp.log(total)
-    norm = to_lanes(norm_ref[...])
-    coef = to_lanes(stat_ref[1]) * GRAD_FACTOR
+    norm = jnp.concatenate(halves(norm_ref[...]), axis=1)
+    coef = jnp.concatenate(halves(stat_ref[1]), axis=1) * GRAD_FACTOR
     copies = []
     for r in range(4):
         at = slice(256 * r, 256 * (r + 1))
-        log_prob = dot(mine_ref[...], srows_ref[at, :], NT) * STUDENT_INV - norm[:, at]
+        rows_ref, et_ref = ((sown_ref, own_ref), (sother_ref, other_ref))[r // 2]
+        rows = rows_ref[2 * (r % 2) : 2 * (r % 2) + 2].reshape(256, 256)
+        log_prob = dot(mine_ref[...], rows, NT) * STUDENT_INV - norm[:, at]
         prob_ref[:, at] = jnp.exp(log_prob) * coef[:, at]
-        w_ref[:, at] = (et_ref[:, at].astype(f32) * log_prob).astype(bf16)
+        here = slice(256 * (r % 2), 256 * (r % 2) + 256)
+        w_ref[:, at] = (et_ref[:, here].astype(f32) * log_prob).astype(bf16)
         if r % 2:
             at = (pl.ds(0, 1024), pl.ds(256 * (r - 1), 512))
             copies.append(pltpu.make_async_copy(prob_ref.at[at], prob_hbm.at[at], sems.at[r - 1]))
@@ -189,7 +220,9 @@
         copy.wait()
 
 
-def grad_kernel(recv_ref, stat_ref, col_ref, et_ref, prob_ref, srows_ref, pout_hbm, scale_ref, pout_ref, sems):
+def grad_kernel(
+    recv_ref, stat_ref, col_ref, own_ref, other_ref, prob_ref, sown_ref, sother_ref, pout_hbm, scale_ref, pout_ref, sems
+):
     sums = jnp.sum(recv_ref[...].astype(f32), axis=0)
     entropy = sums[8:16]
     row = stat_ref[0] / sums[0:8]
@@ -203,14 +236,16 @@
     coef = weight * GRAD_FACTOR
     scale_ref[0] = coef
     scale_ref[1] = coef * row
-    scale_rows = to_lanes(coef * row)
+    scale_rows = jnp.concatenate(halves(coef * row), axis=1)
+    sown, sother = sown_ref[...].reshape(512, 256), sother_ref[...].reshape(512, 256)
     copies = []
     for j in range(4):
         at = slice(256 * j, 256 * (j + 1))
         col = jnp.concatenate([jnp.broadcast_to(col_ref[i : i + 1, :], (128, 128)).T for i in (2 * j, 2 * j + 1)], axis=0)
         col = jnp.concatenate([col] * 8, axis=1)
-        grad = (prob_ref[at, :] - et_ref[at, :].astype(f32) * col * scale_rows).astype(bf16)
-        part = dot(grad, srows_ref[...], NN).astype(bf16)
+        teach = jnp.concatenate([own_ref[at, :], other_ref[at, :]], axis=1).astype(f32)
+        grad = (prob_ref[at, :] - teach * col * scale_rows).astype(bf16)
+        part = (dot(grad[:, :512], sown, NN) + dot(grad[:, 512:], sother, NN)).astype(bf16)
         for i in (0, 1):
             pout_ref[2 * j + i, 0:128, :] = part[128 * i : 128 * (i + 1), 0:128]
             pout_ref[2 * j + i, 128:256, :] = part[128 * i : 128 * (i + 1), 128:256]
@@ -331,17 +366,20 @@
 
     parts = [own] + [shift(own, "x", 4, k) for k in (1, 2, 3)]
     peak_recv = a2a(peak_pay, PLANE)
-    peak_recv, *parts = lax.optimization_barrier((peak_recv, *parts))
-    pieces = [v for part in parts for v in (part, shift(part, "c", 2, 1))]
-
-    et, srows, stat, pay = call(
-        expo_kernel,
-        [((1024, 1024), bf16), ((1024, 256), bf16), ((3, 8, 128), f32), ((8, 8, 128), bf16)],
-        peak_recv, *pieces, mine, limit=16, scratch=[pltpu.VMEM((1024, 256), bf16)],
+    teach_own, student_own = call(order_kernel, [((4, LIVE, 256), bf16)] * 2, peak_recv, *parts)
+    teach_other, student_other = shift(teach_own, "c", 2, 1), shift(student_own, "c", 2, 1)
+    et_own, stat, sums = call(
+        expo_own_kernel,
+        [((1024, 512), bf16), ((3, 8, 128), f32), ((16, 1024), f32)],
+        peak_recv, teach_own, mine, limit=16, cost=1 << 28,
     )
+    et_other, pay = call(
+        expo_other_kernel, [((1024, 512), bf16), ((8, 8, 128), bf16)], stat, sums, teach_other, mine, limit=16
+    )
+    et = (et_own, et_other)
 
     recv = a2a(pay, "z")
-    (pay,) = call(col_kernel, [((32, 8, 128), bf16)], recv, et)
+    (pay,) = call(col_kernel, [((32, 8, 128), bf16)], recv, *et)
     recv = a2a(pay, PLANE)
     prob, w, norm = pl.pallas_call(
         student_prob_kernel,
@@ -350,7 +388,7 @@
             pltpu.HBM((1024, 1024), bf16),
             jax.ShapeDtypeStruct((8, 128), f32),
         ],
-        in_specs=[VM] * 5,
+        in_specs=[VM] * 7,
         out_specs=[pl.BlockSpec(memory_space=pltpu.HBM)] * 2 + [VM],
         scratch_shapes=[
             pltpu.VMEM((1024, 1024), f32),
@@ -359,25 +397,25 @@
         ],
         compiler_params=pltpu.CompilerParams(vmem_limit_bytes=24 << 20),
         cost_estimate=pl.CostEstimate(flops=1 << 29, bytes_accessed=8 << 20, transcendentals=1 << 20),
-    )(peak_recv, stat, srows, mine, et)
-    (pay,) = call(row_kernel, [((8, 8, 128), bf16)], recv, stat, et)
+    )(peak_recv, stat, student_own, student_other, mine, *et)
+    (pay,) = call(row_kernel, [((8, 8, 128), bf16)], recv, stat, *et)
     for _ in range(BALANCING_PASSES - 2):
         recv = a2a(pay, "z")
-        (pay,) = call(col_kernel, [((32, 8, 128), bf16)], recv, et, norm)
+        (pay,) = call(col_kernel, [((32, 8, 128), bf16)], recv, *et, norm)
         recv = a2a(pay, PLANE)
-        (pay,) = call(row_kernel, [((8, 8, 128), bf16)], recv, stat, et)
+        (pay,) = call(row_kernel, [((8, 8, 128), bf16)], recv, stat, *et)
     recv = a2a(pay, "z")
-    pay, col = call(last_col_kernel, [((32, 24, 128), bf16), ((8, 128), f32)], recv, et, w)
+    pay, col = call(last_col_kernel, [((32, 24, 128), bf16), ((8, 128), f32)], recv, *et, w)
     recv = a2a(pay, PLANE)
 
     proto_part, scale = pl.pallas_call(
         grad_kernel,
         out_shape=[pltpu.HBM((8, 264, 128), bf16), jax.ShapeDtypeStruct((2, 8, 128), f32)],
-        in_specs=[VM] * 6,
+        in_specs=[VM] * 8,
         out_specs=[pl.BlockSpec(memory_space=pltpu.HBM), VM],
         scratch_shapes=[pltpu.VMEM((8, 264, 128), bf16), pltpu.SemaphoreType.DMA((2,))],
         compiler_params=pltpu.CompilerParams(vmem_limit_bytes=24 << 20),
-    )(recv, stat, col, et, prob, srows)
+    )(recv, stat, col, *et, prob, student_own, student_other)
     proto_recv = a2a(proto_part, "z")
     student_rows = pl.pallas_call(
         own_kernel,

time: 127 us -> 126 us (level)
    ppermute x10 -> x8, waiting for transfers between devices: 6.39 us -> 5.37 us  [shift(): return lax.ppermute(v, axis, [(i, (i + k) % n) for i in range(n)])]
    ppermute x10 -> x8, starting transfers between devices: 7.72 us -> 7.2 us  [shift(): return lax.ppermute(v, axis, [(i, (i + k) % n) for i in range(n)])]
    pallas_call x8 -> x10, Pallas kernels: 6.98 us -> 7.04 us  [call(): pl.pallas_call(kernel, out_shape=out, in_specs=[VM] * len(args), out_spec...]
  transfers between devices with their start and end apart: 12 -> 10, of which waited for: 9 -> 6; matrix products, arithmetic and copies ran while one was open for 0% -> 0% of each run, Pallas kernels for 7% -> 10%
where the time goes in v8:
time: 126 us
  blocking collectives  76.6 us (61%)
  Pallas kernels  20.2 us (16%)
  starting transfers between devices  14.1 us (11%)
  waiting for transfers between devices  13.9 us (11%)
    all_to_all x6, blocking collectives, a2a(): return lax.all_to_all(v, axes, 0, 0, tiled=True)  76.6 us
    all_to_all x2, waiting for transfers between devices, a2a(): return lax.all_to_all(v, axes, 0, 0, tiled=True)  8.56 us
    ppermute x8, starting transfers between devices, shift(): return lax.ppermute(v, axis, [(i, (i + k) % n) for i in range(n)])  7.2 us
    pallas_call x10, Pallas kernels, call(): pl.pallas_call(kernel, out_shape=out, in_specs=[VM] * len(args), out_spec...  7.04 us
    all_to_all x2, starting transfers between devices, a2a(): return lax.all_to_all(v, axes, 0, 0, tiled=True)  6.88 us
    ppermute x8, waiting for transfers between devices, shift(): return lax.ppermute(v, axis, [(i, (i + k) % n) for i in range(n)])  5.37 us
    pallas_call x1, Pallas kernels, local(): pl.pallas_call(own_kernel, out_shape=jax.ShapeDtypeStruct((LIVE, 256), bf...  4.36 us
    pallas_call x1, Pallas kernels, local(): pl.pallas_call(head_kernel, out_shape=[jax.ShapeDtypeStruct((2, LIVE, 256...  3.65 us
  transfers between devices with their start and end apart: 10, of which 6 were waited for; matrix products, arithmetic and copies ran while one was open for 0% of the time, Pallas kernels for 10%

profile of v8, /device:TPU:1, one launch (start us, length us, event | category | flops | bytes accessed | tf_op | source)
XLA Modules:
  0.0 125.6 jit_solution(2305608713690573272)
XLA Ops:
  0.6 3.7 %shard_map.67 = (bf16[2,128,256]{2,1,0:T(8,128)(2,1)S(1)}, bf16[32,8,128]{2,1,0:T(8,128)(2,1)S(1)}, bf16[1024,256]{1,0:T(8,128)(2,1)S(1)}) custom-call(s32[1,256]{1,0:T(1,128)} %mask_ref.1, bf16[1,256,256]{2,1,0:T(8,128)(2,1)} %teach_hbm.1, bf16[1,256,256]{2,1,0:T(8,128)(2,1)} %student_hbm.1, bf16[8192,256]{1,0:T(8,128)(2,1)} %proto_hbm.3), custom_call_target="tpu_custom_call" | custom-call | tf_op jit(solution)/shard_map/pallas_call | solution.py:348
  4.3 3.4 %collective-permute-start.2 = (bf16[2,128,256]{2,1,0:T(8,128)(2,1)S(1)}, bf16[2,128,256]{2,1,0:T(8,128)(2,1)S(1)}, u32[]{:S(2)}, u32[]{:S(2)}) collective-permute-start(bf16[2,128,256]{2,1,0:T(8,128)(2,1)S(1)} %get-tuple-element.23.a_ref.rows_hbm), channel_id=1, source_target_pairs={{0,24},{8,0},{16,8},{24,16},{1,25},{9,1},{17,9},{25,17},{2,26},{10... | collective-permute-start | bytes 393224 | tf_op jit(solution)/shard_map/ppermute | solution.py:340
  7.7 0.5 collective-permute-start.1
  8.2 0.6 collective-permute-start
  8.8 15.1 %all_to_all.40.recv_ref = bf16[32,8,128]{2,1,0:T(8,128)(2,1)S(1)} all-to-all(bf16[32,8,128]{2,1,0:T(8,128)(2,1)S(1)} %get-tuple-element.22), channel_id=1, replica_groups=mesh['z'=8,'x'=4,'c'=2,'y'=4] {'x','y','c'}, dimensions={0} | all-to-all | bytes 131072 | tf_op jit(solution)/shard_map/all_to_all | solution.py:336
  24.0 0.5 collective-permute-start.3
  24.6 0.8 shard_map.69
  25.6 0.8 shard_map.70
  26.5 14.6 %all_to_all.41.recv_ref = bf16[8,8,128]{2,1,0:T(8,128)(2,1)S(1)} all-to-all(bf16[8,8,128]{2,1,0:T(8,128)(2,1)S(1)} %get-tuple-element.28), channel_id=1, replica_groups=mesh['z'=8,'x'=4,'c'=2,'y'=4] {'z'}, dimensions={0} | all-to-all | bytes 32768 | tf_op jit(solution)/shard_map/all_to_all | solution.py:336
  41.1 0.4 shard_map.71
  41.5 12.3 %all_to_all.42.recv_ref = bf16[32,8,128]{2,1,0:T(8,128)(2,1)S(1)} all-to-all(bf16[32,8,128]{2,1,0:T(8,128)(2,1)S(1)} %shard_map.71), channel_id=1, replica_groups=mesh['z'=8,'x'=4,'c'=2,'y'=4] {'x','y','c'}, dimensions={0} | all-to-all | bytes 131072 | tf_op jit(solution)/shard_map/all_to_all | solution.py:336
  53.7 1.3 %shard_map.72 = bf16[8,8,128]{2,1,0:T(8,128)(2,1)} custom-call(bf16[32,8,128]{2,1,0:T(8,128)(2,1)S(1)} %all_to_all.42.recv_ref, f32[3,8,128]{2,1,0:T(8,128)S(1)} %get-tuple-element.26.stat_ref, bf16[1024,512]{1,0:T(8,128)(2,1)S(1)} %get-tuple-element.29.own_ref, bf16[1024,512]{1,0:T(8,128)(2,1)S(1)} %get-tuple-element.30.other_ref), custom_call_target="tpu_custom_call" | custom-call | tf_op jit(solution)/shard_map/pallas_call | solution.py:320
  55.0 3.3 %all-to-all-start.3 = ((bf16[8,8,128]{2,1,0:T(8,128)(2,1)}), bf16[8,8,128]{2,1,0:T(8,128)(2,1)S(1)}, u32[]{:S(2)}, u32[]{:S(2)}) async-start(bf16[8,8,128]{2,1,0:T(8,128)(2,1)} %shard_map.72), calls=%async_computation.3 | async-start | bytes 32768 | tf_op jit(solution)/shard_map/all_to_all | solution.py:336
  58.4 3.5 %shard_map.73 = (f32[1024,1024]{1,0:T(8,128)}, bf16[1024,1024]{1,0:T(8,128)(2,1)}, f32[8,128]{1,0:T(8,128)S(1)}) custom-call(bf16[32,8,128]{2,1,0:T(8,128)(2,1)S(1)} %all_to_all.40.recv_ref, f32[3,8,128]{2,1,0:T(8,128)S(1)} %get-tuple-element.26.stat_ref, bf16[4,128,256]{2,1,0:T(8,128)(2,1)S(1)} %get-tuple-element.31.sown_ref, ...), custom_call_target="tpu_custom_call" | custom-call | flops 536870912 | bytes 8388608 | tf_op jit(solution)/shard_map/pallas_call | solution.py:384
  61.9 3.1 %all-to-all-done.3.recv_ref = bf16[8,8,128]{2,1,0:T(8,128)(2,1)S(1)} async-done(((bf16[8,8,128]{2,1,0:T(8,128)(2,1)}), bf16[8,8,128]{2,1,0:T(8,128)(2,1)S(1)}, u32[]{:S(2)}, u32[]{:S(2)}) %all-to-all-start.3) | async-done | bytes 16416 | tf_op jit(solution)/shard_map/all_to_all | solution.py:336
  64.9 0.4 shard_map.74
  65.3 12.3 %all_to_all.43.recv_ref = bf16[32,8,128]{2,1,0:T(8,128)(2,1)S(1)} all-to-all(bf16[32,8,128]{2,1,0:T(8,128)(2,1)S(1)} %shard_map.74), channel_id=1, replica_groups=mesh['z'=8,'x'=4,'c'=2,'y'=4] {'x','y','c'}, dimensions={0} | all-to-all | bytes 131072 | tf_op jit(solution)/shard_map/all_to_all | solution.py:336
  77.6 0.7 shard_map.75
  78.3 9.1 %all_to_all.44.recv_ref = bf16[8,8,128]{2,1,0:T(8,128)(2,1)S(1)} all-to-all(bf16[8,8,128]{2,1,0:T(8,128)(2,1)S(1)} %shard_map.75), channel_id=1, replica_groups=mesh['z'=8,'x'=4,'c'=2,'y'=4] {'z'}, dimensions={0} | all-to-all | bytes 32768 | tf_op jit(solution)/shard_map/all_to_all | solution.py:336
  87.4 0.7 shard_map.76
  88.0 13.3 %all_to_all.45.recv_ref = bf16[32,24,128]{2,1,0:T(8,128)(2,1)S(1)} all-to-all(bf16[32,24,128]{2,1,0:T(8,128)(2,1)S(1)} %get-tuple-element.34), channel_id=1, replica_groups=mesh['z'=8,'x'=4,'c'=2,'y'=4] {'x','y','c'}, dimensions={0} | all-to-all | bytes 393216 | tf_op jit(solution)/shard_map/all_to_all | solution.py:336
  101.3 1.7 %shard_map.77 = (bf16[8,264,128]{2,1,0:T(8,128)(2,1)}, f32[2,8,128]{2,1,0:T(8,128)S(1)}) custom-call(bf16[32,24,128]{2,1,0:T(8,128)(2,1)S(1)} %all_to_all.45.recv_ref, f32[3,8,128]{2,1,0:T(8,128)S(1)} %get-tuple-element.26.stat_ref, f32[8,128]{1,0:T(8,128)S(1)} %get-tuple-element.35.col_ref, bf16[1024,512]{1,0:T(8,128)(2,1)S(1)} %get-tuple-element.29.own_ref, ...), custom_call_target="tpu_custom_call" | custom-call | tf_op jit(solution)/shard_map/pallas_call | solution.py:411
  103.0 3.5 %all-to-all-start.7 = ((bf16[8,264,128]{2,1,0:T(8,128)(2,1)}), bf16[8,264,128]{2,1,0:T(8,128)(2,1)S(1)}, u32[]{:S(2)}, u32[]{:S(2)}) async-start(bf16[8,264,128]{2,1,0:T(8,128)(2,1)} %get-tuple-element.37), calls=%async_computation.7 | async-start | bytes 1081344 | tf_op jit(solution)/shard_map/all_to_all | solution.py:336
  106.5 4.4 %shard_map.79.a_ref = bf16[128,256]{1,0:T(8,128)(2,1)S(1)} custom-call(bf16[32,24,128]{2,1,0:T(8,128)(2,1)S(1)} %all_to_all.45.recv_ref, f32[2,8,128]{2,1,0:T(8,128)S(1)} %get-tuple-element.39.scale_ref, f32[3,8,128]{2,1,0:T(8,128)S(1)} %get-tuple-element.26.stat_ref, f32[8,128]{1,0:T(8,128)S(1)} %get-tuple-element.32.refs_0_.norm_ref, ...), custom_call_target="tpu_custom_call" | custom-call | flops 2147483648 | bytes 4194304 | tf_op jit(solution)/shard_map/pallas_call | solution.py:420
  110.9 1.0 collective-permute-start.7
  111.9 1.1 collective-permute-start.6
  113.0 1.4 %collective-permute-done.7.d_ref = bf16[128,256]{1,0:T(8,128)(2,1)S(1)} collective-permute-done((bf16[128,256]{1,0:T(8,128)(2,1)S(1)}, bf16[128,256]{1,0:T(8,128)(2,1)S(1)}, u32[]{:S(2)}, u32[]{:S(2)}) %collective-permute-start.7) | collective-permute-done | bytes 65568 | tf_op jit(solution)/shard_map/ppermute | solution.py:340
  114.4 2.3 %collective-permute-done.6.c_ref = bf16[128,256]{1,0:T(8,128)(2,1)S(1)} collective-permute-done((bf16[128,256]{1,0:T(8,128)(2,1)S(1)}, bf16[128,256]{1,0:T(8,128)(2,1)S(1)}, u32[]{:S(2)}, u32[]{:S(2)}) %collective-permute-start.6) | collective-permute-done | bytes 65568 | tf_op jit(solution)/shard_map/ppermute | solution.py:340
  116.7 1.5 %collective-permute-done.5.b_ref = bf16[128,256]{1,0:T(8,128)(2,1)S(1)} collective-permute-done((bf16[128,256]{1,0:T(8,128)(2,1)S(1)}, bf16[128,256]{1,0:T(8,128)(2,1)S(1)}, u32[]{:S(2)}, u32[]{:S(2)}) %collective-permute-start.5) | collective-permute-done | bytes 65568 | tf_op jit(solution)/shard_map/ppermute | solution.py:340
  118.2 1.2 shard_map.80
  119.3 5.5 %all-to-all-done.7.recv_ref = bf16[8,264,128]{2,1,0:T(8,128)(2,1)S(1)} async-done(((bf16[8,264,128]{2,1,0:T(8,128)(2,1)}), bf16[8,264,128]{2,1,0:T(8,128)(2,1)S(1)}, u32[]{:S(2)}, u32[]{:S(2)}) %all-to-all-start.7) | async-done | bytes 540704 | tf_op jit(solution)/shard_map/all_to_all | solution.py:336
  124.8 0.7 shard_map.78
  (16 shorter events, 0.4 us)
Async XLA Ops:
  4.3 57.6 %copy-start.2 = (bf16[2,128,256]{2,1,0:T(8,128)(2,1)}, bf16[2,128,256]{2,1,0:T(8,128)(2,1)S(1)}, u32[]{:S(2)}) copy-start(bf16[2,128,256]{2,1,0:T(8,128)(2,1)S(1)} %get-tuple-element.23.a_ref.rows_hbm) | copy-start | bytes 393220
  4.3 19.6 %collective-permute-start.2 = (bf16[2,128,256]{2,1,0:T(8,128)(2,1)S(1)}, bf16[2,128,256]{2,1,0:T(8,128)(2,1)S(1)}, u32[]{:S(2)}, u32[]{:S(2)}) collective-permute-start(bf16[2,128,256]{2,1,0:T(8,128)(2,1)S(1)} %get-tuple-element.23.a_ref.rows_hbm), channel_id=1, source_target_pairs={{0,24},{8,0},{16,8},{24,16},{1,25},{9,1},{17,9},{25,17},{2,26},{10... | collective-permute-start | bytes 393224 | tf_op jit(solution)/shard_map/ppermute | solution.py:340
  7.7 16.2 %collective-permute-start.1 = (bf16[2,128,256]{2,1,0:T(8,128)(2,1)S(1)}, bf16[2,128,256]{2,1,0:T(8,128)(2,1)S(1)}, u32[]{:S(2)}, u32[]{:S(2)}) collective-permute-start(bf16[2,128,256]{2,1,0:T(8,128)(2,1)S(1)} %get-tuple-element.23.a_ref.rows_hbm), channel_id=1, source_target_pairs={{0,16},{8,24},{16,0},{24,8},{1,17},{9,25},{17,1},{25,9},{2,18},{10... | collective-permute-start | bytes 393224 | tf_op jit(solution)/shard_map/ppermute | solution.py:340
  8.2 15.7 %collective-permute-start = (bf16[2,128,256]{2,1,0:T(8,128)(2,1)S(1)}, bf16[2,128,256]{2,1,0:T(8,128)(2,1)S(1)}, u32[]{:S(2)}, u32[]{:S(2)}) collective-permute-start(bf16[2,128,256]{2,1,0:T(8,128)(2,1)S(1)} %get-tuple-element.23.a_ref.rows_hbm), channel_id=1, source_target_pairs={{0,8},{8,16},{16,24},{24,0},{1,9},{9,17},{17,25},{25,1},{2,10},{10... | collective-permute-start | bytes 393224 | tf_op jit(solution)/shard_map/ppermute | solution.py:340
  24.0 1.6 %collective-permute-start.3 = (bf16[4,128,256]{2,1,0:T(8,128)(2,1)S(1)}, bf16[4,128,256]{2,1,0:T(8,128)(2,1)S(1)}, u32[]{:S(2)}, u32[]{:S(2)}) collective-permute-start(bf16[4,128,256]{2,1,0:T(8,128)(2,1)S(1)} %get-tuple-element.24.rows_ref), channel_id=1, source_target_pairs={{0,4},{4,0},{1,5},{5,1},{2,6},{6,2},{3,7},{7,3},{8,12},{12,8},{9,1... | collective-permute-start | bytes 786440 | tf_op jit(solution)/shard_map/ppermute | solution.py:340
  24.5 33.9 %collective-permute-start.4 = (bf16[4,128,256]{2,1,0:T(8,128)(2,1)S(1)}, bf16[4,128,256]{2,1,0:T(8,128)(2,1)S(1)}, u32[]{:S(2)}, u32[]{:S(2)}) collective-permute-start(bf16[4,128,256]{2,1,0:T(8,128)(2,1)S(1)} %get-tuple-element.31.sown_ref), channel_id=1, source_target_pairs={{0,4},{4,0},{1,5},{5,1},{2,6},{6,2},{3,7},{7,3},{8,12},{12,8},{9,1... | collective-permute-start | bytes 786440 | tf_op jit(solution)/shard_map/ppermute | solution.py:340
  55.0 9.9 %all-to-all-start.3 = ((bf16[8,8,128]{2,1,0:T(8,128)(2,1)}), bf16[8,8,128]{2,1,0:T(8,128)(2,1)S(1)}, u32[]{:S(2)}, u32[]{:S(2)}) async-start(bf16[8,8,128]{2,1,0:T(8,128)(2,1)} %shard_map.72), calls=%async_computation.3 | async-start | bytes 32768 | tf_op jit(solution)/shard_map/all_to_all | solution.py:336
  64.9 22.4 %copy-start.1 = (bf16[1024,1024]{1,0:T(8,128)(2,1)S(1)}, bf16[1024,1024]{1,0:T(8,128)(2,1)}, u32[]{:S(2)}) copy-start(bf16[1024,1024]{1,0:T(8,128)(2,1)} %get-tuple-element.33.w_ref) | copy-start | bytes 6291460
  64.9 36.4 %copy-start = (f32[1024,1024]{1,0:T(8,128)S(1)}, f32[1024,1024]{1,0:T(8,128)}, u32[]{:S(2)}) copy-start(f32[1024,1024]{1,0:T(8,128)} %get-tuple-element.36.prob_ref) | copy-start | bytes 12582916
  103.0 21.8 %all-to-all-start.7 = ((bf16[8,264,128]{2,1,0:T(8,128)(2,1)}), bf16[8,264,128]{2,1,0:T(8,128)(2,1)S(1)}, u32[]{:S(2)}, u32[]{:S(2)}) async-start(bf16[8,264,128]{2,1,0:T(8,128)(2,1)} %get-tuple-element.37), calls=%async_computation.7 | async-start | bytes 1081344 | tf_op jit(solution)/shard_map/all_to_all | solution.py:336
  106.5 11.6 %copy-start.3 = (s32[1,256]{1,0:T(1,128)S(1)}, s32[1,256]{1,0:T(1,128)}, u32[]{:S(2)}) copy-start(s32[1,256]{1,0:T(1,128)} %mask_ref.1) | copy-start | bytes 3076
  110.9 3.5 %collective-permute-start.7 = (bf16[128,256]{1,0:T(8,128)(2,1)S(1)}, bf16[128,256]{1,0:T(8,128)(2,1)S(1)}, u32[]{:S(2)}, u32[]{:S(2)}) collective-permute-start(bf16[128,256]{1,0:T(8,128)(2,1)S(1)} %shard_map.79.a_ref), channel_id=1, source_target_pairs={{0,3},{1,0},{2,1},{3,2},{4,7},{5,4},{6,5},{7,6},{8,11},{9,8},{10,9... | collective-permute-start | bytes 196616 | tf_op jit(solution)/shard_map/ppermute | solution.py:340
  111.9 4.8 %collective-permute-start.6 = (bf16[128,256]{1,0:T(8,128)(2,1)S(1)}, bf16[128,256]{1,0:T(8,128)(2,1)S(1)}, u32[]{:S(2)}, u32[]{:S(2)}) collective-permute-start(bf16[128,256]{1,0:T(8,128)(2,1)S(1)} %shard_map.79.a_ref), channel_id=1, source_target_pairs={{0,2},{1,3},{2,0},{3,1},{4,6},{5,7},{6,4},{7,5},{8,10},{9,11},{10,... | collective-permute-start | bytes 196616 | tf_op jit(solution)/shard_map/ppermute | solution.py:340
  113.0 5.2 %collective-permute-start.5 = (bf16[128,256]{1,0:T(8,128)(2,1)S(1)}, bf16[128,256]{1,0:T(8,128)(2,1)S(1)}, u32[]{:S(2)}, u32[]{:S(2)}) collective-permute-start(bf16[128,256]{1,0:T(8,128)(2,1)S(1)} %shard_map.79.a_ref), channel_id=1, source_target_pairs={{0,1},{1,2},{2,3},{3,0},{4,5},{5,6},{6,7},{7,4},{8,9},{9,10},{10,1... | collective-permute-start | bytes 196616 | tf_op jit(solution)/shard_map/ppermute | solution.py:340

commit v9 on v8

--- a/solution.py
+++ b/solution.py
@@ -191,7 +191,7 @@
 
 
 def student_prob_kernel(
-    recv_ref, stat_ref, sown_ref, sother_ref, mine_ref, own_ref, other_ref, prob_hbm, w_hbm, norm_ref, prob_ref, w_ref, sems
+    recv_ref, stat_ref, sown_ref, sother_ref, mine_ref, own_ref, other_ref, prob_ref, w_ref, norm_ref
 ):
     for image in range(8):
         got = [recv_ref[(image // 2 * 4 + y) * 2 + image % 2].astype(f32) for y in range(4)]
@@ -201,7 +201,6 @@
         norm_ref[image : image + 1, :] = top + jnp.log(total)
     norm = jnp.concatenate(halves(norm_ref[...]), axis=1)
     coef = jnp.concatenate(halves(stat_ref[1]), axis=1) * GRAD_FACTOR
-    copies = []
     for r in range(4):
         at = slice(256 * r, 256 * (r + 1))
         rows_ref, et_ref = ((sown_ref, own_ref), (sother_ref, other_ref))[r // 2]
@@ -210,14 +209,6 @@
         prob_ref[:, at] = jnp.exp(log_prob) * coef[:, at]
         here = slice(256 * (r % 2), 256 * (r % 2) + 256)
         w_ref[:, at] = (et_ref[:, here].astype(f32) * log_prob).astype(bf16)
-        if r % 2:
-            at = (pl.ds(0, 1024), pl.ds(256 * (r - 1), 512))
-            copies.append(pltpu.make_async_copy(prob_ref.at[at], prob_hbm.at[at], sems.at[r - 1]))
-            copies.append(pltpu.make_async_copy(w_ref.at[at], w_hbm.at[at], sems.at[r]))
-            copies[-2].start()
-            copies[-1].start()
-    for copy in copies:
-        copy.wait()
 
 
 def grad_kernel(
@@ -381,27 +372,16 @@
     recv = a2a(pay, "z")
     (pay,) = call(col_kernel, [((32, 8, 128), bf16)], recv, *et)
     recv = a2a(pay, PLANE)
-    prob, w, norm = pl.pallas_call(
-        student_prob_kernel,
-        out_shape=[
-            pltpu.HBM((1024, 1024), f32),
-            pltpu.HBM((1024, 1024), bf16),
-            jax.ShapeDtypeStruct((8, 128), f32),
-        ],
-        in_specs=[VM] * 7,
-        out_specs=[pl.BlockSpec(memory_space=pltpu.HBM)] * 2 + [VM],
-        scratch_shapes=[
-            pltpu.VMEM((1024, 1024), f32),
-            pltpu.VMEM((1024, 1024), bf16),
-            pltpu.SemaphoreType.DMA((4,)),
-        ],
-        compiler_params=pltpu.CompilerParams(vmem_limit_bytes=24 << 20),
-        cost_estimate=pl.CostEstimate(flops=1 << 29, bytes_accessed=8 << 20, transcendentals=1 << 20),
-    )(peak_recv, stat, student_own, student_other, mine, *et)
+    recv, stat2 = lax.optimization_barrier((recv, stat))
+    prob, w, norm = call(
+        student_prob_kernel, [((1024, 1024), f32), ((1024, 1024), bf16), ((8, 128), f32)],
+        peak_recv, stat2, student_own, student_other, mine, *et, limit=24,
+    )
     (pay,) = call(row_kernel, [((8, 8, 128), bf16)], recv, stat, *et)
+    pay, prob, w, norm = lax.optimization_barrier((pay, prob, w, norm))
     for _ in range(BALANCING_PASSES - 2):
         recv = a2a(pay, "z")
-        (pay,) = call(col_kernel, [((32, 8, 128), bf16)], recv, *et, norm)
+        (pay,) = call(col_kernel, [((32, 8, 128), bf16)], recv, *et)
         recv = a2a(pay, PLANE)
         (pay,) = call(row_kernel, [((8, 8, 128), bf16)], recv, stat, *et)
     recv = a2a(pay, "z")

time: 126 us -> 125 us (level)
  blocking collectives: 76.6 us -> 84.9 us
  starting transfers between devices: 14.1 us -> 10.8 us
  Pallas kernels: 20.2 us -> 17.2 us
  waiting for transfers between devices: 13.9 us -> 10.9 us
    all_to_all x6 -> x7, blocking collectives: 76.6 us -> 84.9 us  [a2a(): return lax.all_to_all(v, axes, 0, 0, tiled=True)]
    pallas_call x1 -> x0, Pallas kernels: 3.47 us -> none  [local(): pl.pallas_call(student_prob_kernel, out_shape=[pltpu.HBM((1024, 1024), f3...]
    all_to_all x2 -> x1, starting transfers between devices: 6.88 us -> 3.55 us  [a2a(): return lax.all_to_all(v, axes, 0, 0, tiled=True)]
    all_to_all x2 -> x1, waiting for transfers between devices: 8.56 us -> 5.5 us  [a2a(): return lax.all_to_all(v, axes, 0, 0, tiled=True)]
    pallas_call x10 -> x11, Pallas kernels: 7.04 us -> 7.67 us  [call(): pl.pallas_call(kernel, out_shape=out, in_specs=[VM] * len(args), out_spec...]
  transfers between devices with their start and end apart: 10 -> 9, of which waited for: 6 -> 5; matrix products, arithmetic and copies ran while one was open for 0% -> 0% of each run, Pallas kernels for 10% -> 7%
where the time goes in v9:
time: 125 us
  blocking collectives  84.9 us (68%)
  Pallas kernels  17.2 us (14%)
  waiting for transfers between devices  10.9 us (9%)
  starting transfers between devices  10.8 us (9%)
    all_to_all x7, blocking collectives, a2a(): return lax.all_to_all(v, axes, 0, 0, tiled=True)  84.9 us
    pallas_call x11, Pallas kernels, call(): pl.pallas_call(kernel, out_shape=out, in_specs=[VM] * len(args), out_spec...  7.67 us
    ppermute x8, starting transfers between devices, shift(): return lax.ppermute(v, axis, [(i, (i + k) % n) for i in range(n)])  7.21 us
    all_to_all x1, waiting for transfers between devices, a2a(): return lax.all_to_all(v, axes, 0, 0, tiled=True)  5.5 us
    ppermute x8, waiting for transfers between devices, shift(): return lax.ppermute(v, axis, [(i, (i + k) % n) for i in range(n)])  5.36 us
    pallas_call x1, Pallas kernels, local(): pl.pallas_call(own_kernel, out_shape=jax.ShapeDtypeStruct((LIVE, 256), bf...  4.35 us
    pallas_call x1, Pallas kernels, local(): pl.pallas_call(head_kernel, out_shape=[jax.ShapeDtypeStruct((2, LIVE, 256...  3.65 us
    all_to_all x1, starting transfers between devices, a2a(): return lax.all_to_all(v, axes, 0, 0, tiled=True)  3.55 us
  transfers between devices with their start and end apart: 9, of which 5 were waited for; matrix products, arithmetic and copies ran while one was open for 0% of the time, Pallas kernels for 7%

profile of v9, /device:TPU:1, one launch (start us, length us, event | category | flops | bytes accessed | tf_op | source)
XLA Modules:
  0.0 124.6 jit_solution(4589090480305015397)
XLA Ops:
  0.6 3.7 %shard_map.67 = (bf16[2,128,256]{2,1,0:T(8,128)(2,1)S(1)}, bf16[32,8,128]{2,1,0:T(8,128)(2,1)S(1)}, bf16[1024,256]{1,0:T(8,128)(2,1)S(1)}) custom-call(s32[1,256]{1,0:T(1,128)} %mask_ref.1, bf16[1,256,256]{2,1,0:T(8,128)(2,1)} %teach_hbm.1, bf16[1,256,256]{2,1,0:T(8,128)(2,1)} %student_hbm.1, bf16[8192,256]{1,0:T(8,128)(2,1)} %proto_hbm.3), custom_call_target="tpu_custom_call" | custom-call | tf_op jit(solution)/shard_map/pallas_call | solution.py:339
  4.3 3.4 %collective-permute-start.2 = (bf16[2,128,256]{2,1,0:T(8,128)(2,1)S(1)}, bf16[2,128,256]{2,1,0:T(8,128)(2,1)S(1)}, u32[]{:S(2)}, u32[]{:S(2)}) collective-permute-start(bf16[2,128,256]{2,1,0:T(8,128)(2,1)S(1)} %get-tuple-element.29.a_ref.rows_hbm), channel_id=1, source_target_pairs={{0,24},{8,0},{16,8},{24,16},{1,25},{9,1},{17,9},{25,17},{2,26},{10... | collective-permute-start | bytes 393224 | tf_op jit(solution)/shard_map/ppermute | solution.py:331
  7.7 0.5 collective-permute-start.1
  8.2 0.6 collective-permute-start
  8.8 15.1 %all_to_all.40.recv_ref = bf16[32,8,128]{2,1,0:T(8,128)(2,1)S(1)} all-to-all(bf16[32,8,128]{2,1,0:T(8,128)(2,1)S(1)} %get-tuple-element.28), channel_id=1, replica_groups=mesh['z'=8,'x'=4,'c'=2,'y'=4] {'x','y','c'}, dimensions={0} | all-to-all | bytes 131072 | tf_op jit(solution)/shard_map/all_to_all | solution.py:327
  24.0 0.5 collective-permute-start.3
  24.6 0.8 shard_map.69
  25.4 0.2 collective-permute-done.3.rows_ref
  25.6 0.8 shard_map.70
  26.5 14.6 %all_to_all.41.recv_ref = bf16[8,8,128]{2,1,0:T(8,128)(2,1)S(1)} all-to-all(bf16[8,8,128]{2,1,0:T(8,128)(2,1)S(1)} %get-tuple-element.34), channel_id=1, replica_groups=mesh['z'=8,'x'=4,'c'=2,'y'=4] {'z'}, dimensions={0} | all-to-all | bytes 32768 | tf_op jit(solution)/shard_map/all_to_all | solution.py:327
  41.1 0.4 shard_map.71
  41.5 12.3 %all_to_all.42.recv_ref = bf16[32,8,128]{2,1,0:T(8,128)(2,1)S(1)} all-to-all(bf16[32,8,128]{2,1,0:T(8,128)(2,1)S(1)} %shard_map.71), channel_id=1, replica_groups=mesh['z'=8,'x'=4,'c'=2,'y'=4] {'x','y','c'}, dimensions={0} | all-to-all | bytes 131072 | tf_op jit(solution)/shard_map/all_to_all | solution.py:327
  53.7 0.7 shard_map.72
  54.4 1.2 shard_map.73
  55.7 9.0 %all_to_all.43.recv_ref = bf16[8,8,128]{2,1,0:T(8,128)(2,1)S(1)} all-to-all(bf16[8,8,128]{2,1,0:T(8,128)(2,1)S(1)} %shard_map.72), channel_id=1, replica_groups=mesh['z'=8,'x'=4,'c'=2,'y'=4] {'z'}, dimensions={0} | all-to-all | bytes 32768 | tf_op jit(solution)/shard_map/all_to_all | solution.py:327
  64.7 0.4 shard_map.74
  65.1 12.0 %all_to_all.44.recv_ref = bf16[32,8,128]{2,1,0:T(8,128)(2,1)S(1)} all-to-all(bf16[32,8,128]{2,1,0:T(8,128)(2,1)S(1)} %shard_map.74), channel_id=1, replica_groups=mesh['z'=8,'x'=4,'c'=2,'y'=4] {'x','y','c'}, dimensions={0} | all-to-all | bytes 131072 | tf_op jit(solution)/shard_map/all_to_all | solution.py:327
  77.1 0.7 shard_map.75
  77.8 9.0 %all_to_all.45.recv_ref = bf16[8,8,128]{2,1,0:T(8,128)(2,1)S(1)} all-to-all(bf16[8,8,128]{2,1,0:T(8,128)(2,1)S(1)} %shard_map.75), channel_id=1, replica_groups=mesh['z'=8,'x'=4,'c'=2,'y'=4] {'z'}, dimensions={0} | all-to-all | bytes 32768 | tf_op jit(solution)/shard_map/all_to_all | solution.py:327
  86.7 0.7 shard_map.76
  87.4 13.0 %all_to_all.46.recv_ref = bf16[32,24,128]{2,1,0:T(8,128)(2,1)S(1)} all-to-all(bf16[32,24,128]{2,1,0:T(8,128)(2,1)S(1)} %get-tuple-element.45), channel_id=1, replica_groups=mesh['z'=8,'x'=4,'c'=2,'y'=4] {'x','y','c'}, dimensions={0} | all-to-all | bytes 393216 | tf_op jit(solution)/shard_map/all_to_all | solution.py:327
  100.4 1.6 %shard_map.77 = (bf16[8,264,128]{2,1,0:T(8,128)(2,1)}, f32[2,8,128]{2,1,0:T(8,128)S(1)}) custom-call(bf16[32,24,128]{2,1,0:T(8,128)(2,1)S(1)} %all_to_all.46.recv_ref, f32[3,8,128]{2,1,0:T(8,128)S(1)} %get-tuple-element.38.stat_ref, f32[8,128]{1,0:T(8,128)S(1)} %get-tuple-element.46.col_ref, bf16[1024,512]{1,0:T(8,128)(2,1)S(1)} %get-tuple-element.35.own_ref, ...), custom_call_target="tpu_custom_call" | custom-call | tf_op jit(solution)/shard_map/pallas_call | solution.py:391
  102.0 3.5 %all-to-all-start.7 = ((bf16[8,264,128]{2,1,0:T(8,128)(2,1)}), bf16[8,264,128]{2,1,0:T(8,128)(2,1)S(1)}, u32[]{:S(2)}, u32[]{:S(2)}) async-start(bf16[8,264,128]{2,1,0:T(8,128)(2,1)} %get-tuple-element.48), calls=%async_computation.7 | async-start | bytes 1081344 | tf_op jit(solution)/shard_map/all_to_all | solution.py:327
  105.6 4.4 %shard_map.79.a_ref = bf16[128,256]{1,0:T(8,128)(2,1)S(1)} custom-call(bf16[32,24,128]{2,1,0:T(8,128)(2,1)S(1)} %all_to_all.46.recv_ref, f32[2,8,128]{2,1,0:T(8,128)S(1)} %get-tuple-element.50.scale_ref, f32[3,8,128]{2,1,0:T(8,128)S(1)} %get-tuple-element.38.stat_ref, f32[8,128]{1,0:T(8,128)S(1)} %get-tuple-element.51.norm_ref, ...), custom_call_target="tpu_custom_call" | custom-call | flops 2147483648 | bytes 4194304 | tf_op jit(solution)/shard_map/pallas_call | solution.py:400
  109.9 1.0 collective-permute-start.7
  110.9 1.1 collective-permute-start.6
  112.0 1.4 %collective-permute-done.7.d_ref = bf16[128,256]{1,0:T(8,128)(2,1)S(1)} collective-permute-done((bf16[128,256]{1,0:T(8,128)(2,1)S(1)}, bf16[128,256]{1,0:T(8,128)(2,1)S(1)}, u32[]{:S(2)}, u32[]{:S(2)}) %collective-permute-start.7) | collective-permute-done | bytes 65568 | tf_op jit(solution)/shard_map/ppermute | solution.py:331
  113.4 2.3 %collective-permute-done.6.c_ref = bf16[128,256]{1,0:T(8,128)(2,1)S(1)} collective-permute-done((bf16[128,256]{1,0:T(8,128)(2,1)S(1)}, bf16[128,256]{1,0:T(8,128)(2,1)S(1)}, u32[]{:S(2)}, u32[]{:S(2)}) %collective-permute-start.6) | collective-permute-done | bytes 65568 | tf_op jit(solution)/shard_map/ppermute | solution.py:331
  115.7 1.5 %collective-permute-done.5.b_ref = bf16[128,256]{1,0:T(8,128)(2,1)S(1)} collective-permute-done((bf16[128,256]{1,0:T(8,128)(2,1)S(1)}, bf16[128,256]{1,0:T(8,128)(2,1)S(1)}, u32[]{:S(2)}, u32[]{:S(2)}) %collective-permute-start.5) | collective-permute-done | bytes 65568 | tf_op jit(solution)/shard_map/ppermute | solution.py:331
  117.2 1.2 shard_map.80
  118.3 5.5 %all-to-all-done.7.recv_ref = bf16[8,264,128]{2,1,0:T(8,128)(2,1)S(1)} async-done(((bf16[8,264,128]{2,1,0:T(8,128)(2,1)}), bf16[8,264,128]{2,1,0:T(8,128)(2,1)S(1)}, u32[]{:S(2)}, u32[]{:S(2)}) %all-to-all-start.7) | async-done | bytes 540704 | tf_op jit(solution)/shard_map/all_to_all | solution.py:327
  123.8 0.7 shard_map.78
  (11 shorter events, 0.2 us)
Async XLA Ops:
  4.3 51.4 %copy-start = (bf16[2,128,256]{2,1,0:T(8,128)(2,1)}, bf16[2,128,256]{2,1,0:T(8,128)(2,1)S(1)}, u32[]{:S(2)}) copy-start(bf16[2,128,256]{2,1,0:T(8,128)(2,1)S(1)} %get-tuple-element.29.a_ref.rows_hbm) | copy-start | bytes 393220
  4.3 19.6 %collective-permute-start.2 = (bf16[2,128,256]{2,1,0:T(8,128)(2,1)S(1)}, bf16[2,128,256]{2,1,0:T(8,128)(2,1)S(1)}, u32[]{:S(2)}, u32[]{:S(2)}) collective-permute-start(bf16[2,128,256]{2,1,0:T(8,128)(2,1)S(1)} %get-tuple-element.29.a_ref.rows_hbm), channel_id=1, source_target_pairs={{0,24},{8,0},{16,8},{24,16},{1,25},{9,1},{17,9},{25,17},{2,26},{10... | collective-permute-start | bytes 393224 | tf_op jit(solution)/shard_map/ppermute | solution.py:331
  7.7 16.2 %collective-permute-start.1 = (bf16[2,128,256]{2,1,0:T(8,128)(2,1)S(1)}, bf16[2,128,256]{2,1,0:T(8,128)(2,1)S(1)}, u32[]{:S(2)}, u32[]{:S(2)}) collective-permute-start(bf16[2,128,256]{2,1,0:T(8,128)(2,1)S(1)} %get-tuple-element.29.a_ref.rows_hbm), channel_id=1, source_target_pairs={{0,16},{8,24},{16,0},{24,8},{1,17},{9,25},{17,1},{25,9},{2,18},{10... | collective-permute-start | bytes 393224 | tf_op jit(solution)/shard_map/ppermute | solution.py:331
  8.2 15.7 %collective-permute-start = (bf16[2,128,256]{2,1,0:T(8,128)(2,1)S(1)}, bf16[2,128,256]{2,1,0:T(8,128)(2,1)S(1)}, u32[]{:S(2)}, u32[]{:S(2)}) collective-permute-start(bf16[2,128,256]{2,1,0:T(8,128)(2,1)S(1)} %get-tuple-element.29.a_ref.rows_hbm), channel_id=1, source_target_pairs={{0,8},{8,16},{16,24},{24,0},{1,9},{9,17},{17,25},{25,1},{2,10},{10... | collective-permute-start | bytes 393224 | tf_op jit(solution)/shard_map/ppermute | solution.py:331
  24.0 1.6 %collective-permute-start.3 = (bf16[4,128,256]{2,1,0:T(8,128)(2,1)S(1)}, bf16[4,128,256]{2,1,0:T(8,128)(2,1)S(1)}, u32[]{:S(2)}, u32[]{:S(2)}) collective-permute-start(bf16[4,128,256]{2,1,0:T(8,128)(2,1)S(1)} %get-tuple-element.30.rows_ref), channel_id=1, source_target_pairs={{0,4},{4,0},{1,5},{5,1},{2,6},{6,2},{3,7},{7,3},{8,12},{12,8},{9,1... | collective-permute-start | bytes 786440 | tf_op jit(solution)/shard_map/ppermute | solution.py:331
  24.5 30.0 %collective-permute-start.4 = (bf16[4,128,256]{2,1,0:T(8,128)(2,1)S(1)}, bf16[4,128,256]{2,1,0:T(8,128)(2,1)S(1)}, u32[]{:S(2)}, u32[]{:S(2)}) collective-permute-start(bf16[4,128,256]{2,1,0:T(8,128)(2,1)S(1)} %get-tuple-element.39.sown_ref), channel_id=1, source_target_pairs={{0,4},{4,0},{1,5},{5,1},{2,6},{6,2},{3,7},{7,3},{8,12},{12,8},{9,1... | collective-permute-start | bytes 786440 | tf_op jit(solution)/shard_map/ppermute | solution.py:331
  102.0 21.8 %all-to-all-start.7 = ((bf16[8,264,128]{2,1,0:T(8,128)(2,1)}), bf16[8,264,128]{2,1,0:T(8,128)(2,1)S(1)}, u32[]{:S(2)}, u32[]{:S(2)}) async-start(bf16[8,264,128]{2,1,0:T(8,128)(2,1)} %get-tuple-element.48), calls=%async_computation.7 | async-start | bytes 1081344 | tf_op jit(solution)/shard_map/all_to_all | solution.py:327
  105.5 11.6 %copy-start.1 = (s32[1,256]{1,0:T(1,128)S(1)}, s32[1,256]{1,0:T(1,128)}, u32[]{:S(2)}) copy-start(s32[1,256]{1,0:T(1,128)} %mask_ref.1) | copy-start | bytes 3076
  109.9 3.5 %collective-permute-start.7 = (bf16[128,256]{1,0:T(8,128)(2,1)S(1)}, bf16[128,256]{1,0:T(8,128)(2,1)S(1)}, u32[]{:S(2)}, u32[]{:S(2)}) collective-permute-start(bf16[128,256]{1,0:T(8,128)(2,1)S(1)} %shard_map.79.a_ref), channel_id=1, source_target_pairs={{0,3},{1,0},{2,1},{3,2},{4,7},{5,4},{6,5},{7,6},{8,11},{9,8},{10,9... | collective-permute-start | bytes 196616 | tf_op jit(solution)/shard_map/ppermute | solution.py:331
  110.9 4.8 %collective-permute-start.6 = (bf16[128,256]{1,0:T(8,128)(2,1)S(1)}, bf16[128,256]{1,0:T(8,128)(2,1)S(1)}, u32[]{:S(2)}, u32[]{:S(2)}) collective-permute-start(bf16[128,256]{1,0:T(8,128)(2,1)S(1)} %shard_map.79.a_ref), channel_id=1, source_target_pairs={{0,2},{1,3},{2,0},{3,1},{4,6},{5,7},{6,4},{7,5},{8,10},{9,11},{10,... | collective-permute-start | bytes 196616 | tf_op jit(solution)/shard_map/ppermute | solution.py:331
  112.0 5.1 %collective-permute-start.5 = (bf16[128,256]{1,0:T(8,128)(2,1)S(1)}, bf16[128,256]{1,0:T(8,128)(2,1)S(1)}, u32[]{:S(2)}, u32[]{:S(2)}) collective-permute-start(bf16[128,256]{1,0:T(8,128)(2,1)S(1)} %shard_map.79.a_ref), channel_id=1, source_target_pairs={{0,1},{1,2},{2,3},{3,0},{4,5},{5,6},{6,7},{7,4},{8,9},{9,10},{10,1... | collective-permute-start | bytes 196616 | tf_op jit(solution)/shard_map/ppermute | solution.py:331

commit v10 on v9

--- a/solution.py
+++ b/solution.py
@@ -32,15 +32,23 @@
 
 
 def halves(tile):
-    even, odd = (jnp.concatenate([tile[i : i + 1] for i in range(start, 8, 2)], axis=1) for start in (0, 1))
+    left = lax.broadcasted_iota(jnp.int32, (1, 128), 1) < 64
+    turned = pltpu.roll(tile, 64, 1)
+    low = [jnp.where(left, tile[i : i + 1], turned[i + 1 : i + 2]) for i in range(0, 8, 2)]
+    high = [jnp.where(left, turned[i : i + 1], tile[i + 1 : i + 2]) for i in range(0, 8, 2)]
+    low, high = jnp.concatenate(low, axis=1), jnp.concatenate(high, axis=1)
     first = lax.axis_index("c") == 0
-    return jnp.where(first, even, odd), jnp.where(first, odd, even)
+    return jnp.where(first, low, high), jnp.where(first, high, low)
 
 
 def join(own, other):
     first = lax.axis_index("c") == 0
-    even, odd = jnp.where(first, own, other), jnp.where(first, other, own)
-    return jnp.concatenate([v[:, 128 * x : 128 * (x + 1)] for x in range(4) for v in (even, odd)], axis=0)
+    low, high = jnp.where(first, own, other), jnp.where(first, other, own)
+    low, high = (jnp.concatenate([v[:, 128 * i : 128 * (i + 1)] for i in range(4)], axis=0) for v in (low, high))
+    left = lax.broadcasted_iota(jnp.int32, (4, 128), 1) < 64
+    even = jnp.where(left, low, pltpu.roll(high, 64, 1))
+    odd = jnp.where(left, pltpu.roll(low, 64, 1), high)
+    return jnp.concatenate([v[i : i + 1] for i in range(4) for v in (even, odd)], axis=0)
 
 
 def thirds(v):
@@ -113,24 +121,33 @@
         + [jnp.zeros((1, LIVE), f32)],
         axis=0,
     )
-    out_ref[...] = jnp.broadcast_to(tile[None].astype(bf16), out_ref.shape)
+    out_ref[:, :, 64:72, :] = jnp.broadcast_to(tile[None, None].astype(bf16), (16, 2, 8, 128))
+    for core in range(2):
+        at = pl.ds(pl.multiple_of(core * 64 + lax.axis_index("y") * 16, 16), 16)
+        for i in range(2):
+            block = own_ref[i, at, :]
+            block = jnp.concatenate([block[:, :128], block[:, 128:]], axis=0)
+            out_ref[:, core, 32 * i : 32 * i + 32, :] = jnp.broadcast_to(block[None], (16, 32, 128))
 
 
 def spread(tile, ref):
     ref[...] = jnp.broadcast_to(tile[None].astype(ref.dtype), ref.shape)
 
 
-def order_kernel(recv_ref, a_ref, b_ref, c_ref, d_ref, teach_ref, student_ref):
-    for k, piece in enumerate((a_ref, b_ref, c_ref, d_ref)):
-        x = (lax.axis_index("x") + 4 - k) & 3
-        teach_ref[x] = piece[0]
-        student_ref[x] = piece[1]
+def order_kernel(recv_ref, teach_ref, student_ref):
+    for image in range(8):
+        for y in range(4):
+            at = slice(64 * image + 16 * y, 64 * image + 16 * y + 16)
+            source = (image // 2 * 4 + y) * 2 + image % 2
+            for i, ref in enumerate((teach_ref, student_ref)):
+                ref[at, 0:128] = recv_ref[source, 32 * i : 32 * i + 16, :]
+                ref[at, 128:256] = recv_ref[source, 32 * i + 16 : 32 * i + 32, :]
 
 
 def expo_half(rows_ref, mine_ref, et_ref, peak, live, sums):
     for r in range(2):
         at = slice(256 * r, 256 * (r + 1))
-        rows = rows_ref[2 * r : 2 * r + 2].reshape(256, 256)
+        rows = rows_ref[at, :]
         weights = jnp.broadcast_to(live[:, at], (16, 256)).astype(bf16)
         for j in range(2):
             logits = dot(mine_ref[512 * j : 512 * (j + 1), :], rows, NT)
@@ -143,7 +160,7 @@
     peaks, counts = [], []
     for x in range(4):
         for core in range(2):
-            got = [recv_ref[(x * 4 + y) * 2 + core].astype(f32) for y in range(4)]
+            got = [recv_ref[(x * 4 + y) * 2 + core, 64:72, :].astype(f32) for y in range(4)]
             tops = [v[0:1] + v[1:2] + v[2:3] for v in got]
             peaks.append(jnp.maximum(jnp.maximum(tops[0], tops[1]), jnp.maximum(tops[2], tops[3])))
             counts.append(got[0][3:4])
@@ -194,7 +211,7 @@
     recv_ref, stat_ref, sown_ref, sother_ref, mine_ref, own_ref, other_ref, prob_ref, w_ref, norm_ref
 ):
     for image in range(8):
-        got = [recv_ref[(image // 2 * 4 + y) * 2 + image % 2].astype(f32) for y in range(4)]
+        got = [recv_ref[(image // 2 * 4 + y) * 2 + image % 2, 64:72, :].astype(f32) for y in range(4)]
         parts = [v[4:5] + v[5:6] + v[6:7] for v in got]
         top = jnp.maximum(jnp.maximum(parts[0], parts[1]), jnp.maximum(parts[2], parts[3]))
         total = sum(jnp.exp(v - top) for v in parts)
@@ -204,7 +221,7 @@
     for r in range(4):
         at = slice(256 * r, 256 * (r + 1))
         rows_ref, et_ref = ((sown_ref, own_ref), (sother_ref, other_ref))[r // 2]
-        rows = rows_ref[2 * (r % 2) : 2 * (r % 2) + 2].reshape(256, 256)
+        rows = rows_ref[256 * (r % 2) : 256 * (r % 2) + 256, :]
         log_prob = dot(mine_ref[...], rows, NT) * STUDENT_INV - norm[:, at]
         prob_ref[:, at] = jnp.exp(log_prob) * coef[:, at]
         here = slice(256 * (r % 2), 256 * (r % 2) + 256)
@@ -228,7 +245,7 @@
     scale_ref[0] = coef
     scale_ref[1] = coef * row
     scale_rows = jnp.concatenate(halves(coef * row), axis=1)
-    sown, sother = sown_ref[...].reshape(512, 256), sother_ref[...].reshape(512, 256)
+    sown, sother = sown_ref[...], sother_ref[...]
     copies = []
     for j in range(4):
         at = slice(256 * j, 256 * (j + 1))
@@ -340,7 +357,7 @@
         head_kernel,
         out_shape=[
             jax.ShapeDtypeStruct((2, LIVE, 256), bf16),
-            jax.ShapeDtypeStruct((32, 8, 128), bf16),
+            jax.ShapeDtypeStruct((16, 2, 72, 128), bf16),
             jax.ShapeDtypeStruct((1024, 256), bf16),
         ],
         in_specs=[HBM] * 4,
@@ -355,9 +372,8 @@
         compiler_params=pltpu.CompilerParams(vmem_limit_bytes=32 << 20),
     )(*(in_hbm(v) for v in (patch_mask, teacher_feats, student_feats, prototypes)))
 
-    parts = [own] + [shift(own, "x", 4, k) for k in (1, 2, 3)]
-    peak_recv = a2a(peak_pay, PLANE)
-    teach_own, student_own = call(order_kernel, [((4, LIVE, 256), bf16)] * 2, peak_recv, *parts)
+    peak_recv = a2a(peak_pay.reshape(32, 72, 128), PLANE)
+    teach_own, student_own = call(order_kernel, [((512, 256), bf16)] * 2, peak_recv)
     teach_other, student_other = shift(teach_own, "c", 2, 1), shift(student_own, "c", 2, 1)
     et_own, stat, sums = call(
         expo_own_kernel,

time: 125 us -> 125 us (level)
  blocking collectives: 84.9 us -> 90.5 us
  starting transfers between devices: 10.8 us -> 6.42 us
  waiting for transfers between devices: 10.9 us -> 9.21 us
    all_to_all x7, blocking collectives: 84.9 us -> 90.5 us  [a2a(): return lax.all_to_all(v, axes, 0, 0, tiled=True)]
    ppermute x8 -> x5, starting transfers between devices: 7.21 us -> 2.69 us  [shift(): return lax.ppermute(v, axis, [(i, (i + k) % n) for i in range(n)])]
    all_to_all x1, waiting for transfers between devices: 5.5 us -> 3.92 us  [a2a(): return lax.all_to_all(v, axes, 0, 0, tiled=True)]
    ppermute x8 -> x5, waiting for transfers between devices: 5.36 us -> 5.29 us  [shift(): return lax.ppermute(v, axis, [(i, (i + k) % n) for i in range(n)])]
  transfers between devices with their start and end apart: 9 -> 6, of which waited for: 5 -> 5; matrix products, arithmetic and copies ran while one was open for 0% -> 0% of each run, Pallas kernels for 7% -> 7%
where the time goes in v10:
time: 125 us
  blocking collectives  90.5 us (72%)
  Pallas kernels  17.8 us (14%)
  waiting for transfers between devices  9.21 us (7%)
  starting transfers between devices  6.42 us (5%)
    all_to_all x7, blocking collectives, a2a(): return lax.all_to_all(v, axes, 0, 0, tiled=True)  90.5 us
    pallas_call x11, Pallas kernels, call(): pl.pallas_call(kernel, out_shape=out, in_specs=[VM] * len(args), out_spec...  8.1 us
    ppermute x5, waiting for transfers between devices, shift(): return lax.ppermute(v, axis, [(i, (i + k) % n) for i in range(n)])  5.29 us
    pallas_call x1, Pallas kernels, local(): pl.pallas_call(own_kernel, out_shape=jax.ShapeDtypeStruct((LIVE, 256), bf...  4.36 us
    all_to_all x1, waiting for transfers between devices, a2a(): return lax.all_to_all(v, axes, 0, 0, tiled=True)  3.92 us
    all_to_all x1, starting transfers between devices, a2a(): return lax.all_to_all(v, axes, 0, 0, tiled=True)  3.73 us
    pallas_call x1, Pallas kernels, local(): pl.pallas_call(head_kernel, out_shape=[jax.ShapeDtypeStruct((2, LIVE, 256...  3.66 us
    ppermute x5, starting transfers between devices, shift(): return lax.ppermute(v, axis, [(i, (i + k) % n) for i in range(n)])  2.69 us
  transfers between devices with their start and end apart: 6, of which 5 were waited for; matrix products, arithmetic and copies ran while one was open for 0% of the time, Pallas kernels for 7%

profile of v10, /device:TPU:1, one launch (start us, length us, event | category | flops | bytes accessed | tf_op | source)
XLA Modules:
  0.0 124.7 jit_solution(7930961485443868407)
XLA Ops:
  0.6 3.7 %shard_map.67 = (bf16[2,128,256]{2,1,0:T(8,128)(2,1)S(1)}, bf16[16,2,72,128]{3,2,1,0:T(8,128)(2,1)S(1)}, bf16[1024,256]{1,0:T(8,128)(2,1)S(1)}) custom-call(s32[1,256]{1,0:T(1,128)} %mask_ref.1, bf16[1,256,256]{2,1,0:T(8,128)(2,1)} %teach_hbm.1, bf16[1,256,256]{2,1,0:T(8,128)(2,1)} %student_hbm.1, bf16[8192,256]{1,0:T(8,128)(2,1)} %proto_hbm.3), custom_call_target="tpu_custom_call" | custom-call | tf_op jit(solution)/shard_map/pallas_call | solution.py:356
  4.3 0.0 copy-start.1
  4.3 20.7 %all_to_all.40.recv_ref = bf16[32,72,128]{2,1,0:T(8,128)(2,1)S(1)} all-to-all(bf16[32,72,128]{2,1,0:T(8,128)(2,1)S(1)} %bitcast.5), channel_id=1, replica_groups=mesh['z'=8,'x'=4,'c'=2,'y'=4] {'x','y','c'}, dimensions={0} | all-to-all | bytes 1179648 | tf_op jit(solution)/shard_map/all_to_all | solution.py:344
  25.0 0.1 shard_map.68
  25.1 0.1 collective-permute-start
  25.2 0.5 collective-permute-start.1
  25.7 0.9 shard_map.69
  26.6 0.1 collective-permute-done.rows_ref
  26.7 0.8 shard_map.70
  27.5 14.7 %all_to_all.41.recv_ref = bf16[8,8,128]{2,1,0:T(8,128)(2,1)S(1)} all-to-all(bf16[8,8,128]{2,1,0:T(8,128)(2,1)S(1)} %get-tuple-element.33), channel_id=1, replica_groups=mesh['z'=8,'x'=4,'c'=2,'y'=4] {'z'}, dimensions={0} | all-to-all | bytes 32768 | tf_op jit(solution)/shard_map/all_to_all | solution.py:344
  42.2 0.5 shard_map.71
  42.7 12.2 %all_to_all.42.recv_ref = bf16[32,8,128]{2,1,0:T(8,128)(2,1)S(1)} all-to-all(bf16[32,8,128]{2,1,0:T(8,128)(2,1)S(1)} %shard_map.71), channel_id=1, replica_groups=mesh['z'=8,'x'=4,'c'=2,'y'=4] {'x','y','c'}, dimensions={0} | all-to-all | bytes 131072 | tf_op jit(solution)/shard_map/all_to_all | solution.py:344
  54.9 0.7 shard_map.72
  55.6 1.2 shard_map.73
  56.9 9.0 %all_to_all.43.recv_ref = bf16[8,8,128]{2,1,0:T(8,128)(2,1)S(1)} all-to-all(bf16[8,8,128]{2,1,0:T(8,128)(2,1)S(1)} %shard_map.72), channel_id=1, replica_groups=mesh['z'=8,'x'=4,'c'=2,'y'=4] {'z'}, dimensions={0} | all-to-all | bytes 32768 | tf_op jit(solution)/shard_map/all_to_all | solution.py:344
  65.9 0.5 shard_map.74
  66.4 12.0 %all_to_all.44.recv_ref = bf16[32,8,128]{2,1,0:T(8,128)(2,1)S(1)} all-to-all(bf16[32,8,128]{2,1,0:T(8,128)(2,1)S(1)} %shard_map.74), channel_id=1, replica_groups=mesh['z'=8,'x'=4,'c'=2,'y'=4] {'x','y','c'}, dimensions={0} | all-to-all | bytes 131072 | tf_op jit(solution)/shard_map/all_to_all | solution.py:344
  78.4 0.7 shard_map.75
  79.1 9.0 %all_to_all.45.recv_ref = bf16[8,8,128]{2,1,0:T(8,128)(2,1)S(1)} all-to-all(bf16[8,8,128]{2,1,0:T(8,128)(2,1)S(1)} %shard_map.75), channel_id=1, replica_groups=mesh['z'=8,'x'=4,'c'=2,'y'=4] {'z'}, dimensions={0} | all-to-all | bytes 32768 | tf_op jit(solution)/shard_map/all_to_all | solution.py:344
  88.1 0.8 shard_map.76
  88.8 13.0 %all_to_all.46.recv_ref = bf16[32,24,128]{2,1,0:T(8,128)(2,1)S(1)} all-to-all(bf16[32,24,128]{2,1,0:T(8,128)(2,1)S(1)} %get-tuple-element.44), channel_id=1, replica_groups=mesh['z'=8,'x'=4,'c'=2,'y'=4] {'x','y','c'}, dimensions={0} | all-to-all | bytes 393216 | tf_op jit(solution)/shard_map/all_to_all | solution.py:344
  101.8 1.7 %shard_map.77 = (bf16[8,264,128]{2,1,0:T(8,128)(2,1)}, f32[2,8,128]{2,1,0:T(8,128)S(1)}) custom-call(bf16[32,24,128]{2,1,0:T(8,128)(2,1)S(1)} %all_to_all.46.recv_ref, f32[3,8,128]{2,1,0:T(8,128)S(1)} %get-tuple-element.37.stat_ref, f32[8,128]{1,0:T(8,128)S(1)} %get-tuple-element.45.col_ref, bf16[1024,512]{1,0:T(8,128)(2,1)S(1)} %get-tuple-element.34.own_ref, ...), custom_call_target="tpu_custom_call" | custom-call | tf_op jit(solution)/shard_map/pallas_call | solution.py:407
  103.5 3.7 %all-to-all-start.7 = ((bf16[8,264,128]{2,1,0:T(8,128)(2,1)}), bf16[8,264,128]{2,1,0:T(8,128)(2,1)S(1)}, u32[]{:S(2)}, u32[]{:S(2)}) async-start(bf16[8,264,128]{2,1,0:T(8,128)(2,1)} %get-tuple-element.47), calls=%async_computation.7 | async-start | bytes 1081344 | tf_op jit(solution)/shard_map/all_to_all | solution.py:344
  107.2 4.4 %shard_map.79.a_ref = bf16[128,256]{1,0:T(8,128)(2,1)S(1)} custom-call(bf16[32,24,128]{2,1,0:T(8,128)(2,1)S(1)} %all_to_all.46.recv_ref, f32[2,8,128]{2,1,0:T(8,128)S(1)} %get-tuple-element.49.scale_ref, f32[3,8,128]{2,1,0:T(8,128)S(1)} %get-tuple-element.37.stat_ref, f32[8,128]{1,0:T(8,128)S(1)} %get-tuple-element.50.norm_ref, ...), custom_call_target="tpu_custom_call" | custom-call | flops 2147483648 | bytes 4194304 | tf_op jit(solution)/shard_map/pallas_call | solution.py:416
  111.6 1.0 collective-permute-start.4
  112.6 1.1 collective-permute-start.3
  113.7 1.4 %collective-permute-done.4.d_ref = bf16[128,256]{1,0:T(8,128)(2,1)S(1)} collective-permute-done((bf16[128,256]{1,0:T(8,128)(2,1)S(1)}, bf16[128,256]{1,0:T(8,128)(2,1)S(1)}, u32[]{:S(2)}, u32[]{:S(2)}) %collective-permute-start.4) | collective-permute-done | bytes 65568 | tf_op jit(solution)/shard_map/ppermute | solution.py:348
  115.1 2.4 %collective-permute-done.3.c_ref = bf16[128,256]{1,0:T(8,128)(2,1)S(1)} collective-permute-done((bf16[128,256]{1,0:T(8,128)(2,1)S(1)}, bf16[128,256]{1,0:T(8,128)(2,1)S(1)}, u32[]{:S(2)}, u32[]{:S(2)}) %collective-permute-start.3) | collective-permute-done | bytes 65568 | tf_op jit(solution)/shard_map/ppermute | solution.py:348
  117.5 1.3 %collective-permute-done.2.b_ref = bf16[128,256]{1,0:T(8,128)(2,1)S(1)} collective-permute-done((bf16[128,256]{1,0:T(8,128)(2,1)S(1)}, bf16[128,256]{1,0:T(8,128)(2,1)S(1)}, u32[]{:S(2)}, u32[]{:S(2)}) %collective-permute-start.2) | collective-permute-done | bytes 65568 | tf_op jit(solution)/shard_map/ppermute | solution.py:348
  118.9 1.2 shard_map.80
  120.0 3.9 %all-to-all-done.7.recv_ref = bf16[8,264,128]{2,1,0:T(8,128)(2,1)S(1)} async-done(((bf16[8,264,128]{2,1,0:T(8,128)(2,1)}), bf16[8,264,128]{2,1,0:T(8,128)(2,1)S(1)}, u32[]{:S(2)}, u32[]{:S(2)}) %all-to-all-start.7) | async-done | bytes 540704 | tf_op jit(solution)/shard_map/all_to_all | solution.py:344
  123.9 0.7 shard_map.78
  (5 shorter events, 0.0 us)
Async XLA Ops:
  4.3 51.3 %copy-start.1 = (bf16[2,128,256]{2,1,0:T(8,128)(2,1)}, bf16[2,128,256]{2,1,0:T(8,128)(2,1)S(1)}, u32[]{:S(2)}) copy-start(bf16[2,128,256]{2,1,0:T(8,128)(2,1)S(1)} %get-tuple-element.51.rows_hbm) | copy-start | bytes 393220
  25.1 1.6 %collective-permute-start = (bf16[512,256]{1,0:T(8,128)(2,1)S(1)}, bf16[512,256]{1,0:T(8,128)(2,1)S(1)}, u32[]{:S(2)}, u32[]{:S(2)}) collective-permute-start(bf16[512,256]{1,0:T(8,128)(2,1)S(1)} %get-tuple-element.29.rows_ref), channel_id=1, source_target_pairs={{0,4},{4,0},{1,5},{5,1},{2,6},{6,2},{3,7},{7,3},{8,12},{12,8},{9,1... | collective-permute-start | bytes 786440 | tf_op jit(solution)/shard_map/ppermute | solution.py:348
  25.2 30.5 %collective-permute-start.1 = (bf16[512,256]{1,0:T(8,128)(2,1)S(1)}, bf16[512,256]{1,0:T(8,128)(2,1)S(1)}, u32[]{:S(2)}, u32[]{:S(2)}) collective-permute-start(bf16[512,256]{1,0:T(8,128)(2,1)S(1)} %get-tuple-element.38.sown_ref), channel_id=1, source_target_pairs={{0,4},{4,0},{1,5},{5,1},{2,6},{6,2},{3,7},{7,3},{8,12},{12,8},{9,1... | collective-permute-start | bytes 786440 | tf_op jit(solution)/shard_map/ppermute | solution.py:348
  103.5 20.5 %all-to-all-start.7 = ((bf16[8,264,128]{2,1,0:T(8,128)(2,1)}), bf16[8,264,128]{2,1,0:T(8,128)(2,1)S(1)}, u32[]{:S(2)}, u32[]{:S(2)}) async-start(bf16[8,264,128]{2,1,0:T(8,128)(2,1)} %get-tuple-element.47), calls=%async_computation.7 | async-start | bytes 1081344 | tf_op jit(solution)/shard_map/all_to_all | solution.py:344
  107.2 11.6 %copy-start = (s32[1,256]{1,0:T(1,128)S(1)}, s32[1,256]{1,0:T(1,128)}, u32[]{:S(2)}) copy-start(s32[1,256]{1,0:T(1,128)} %mask_ref.1) | copy-start | bytes 3076
  111.6 3.5 %collective-permute-start.4 = (bf16[128,256]{1,0:T(8,128)(2,1)S(1)}, bf16[128,256]{1,0:T(8,128)(2,1)S(1)}, u32[]{:S(2)}, u32[]{:S(2)}) collective-permute-start(bf16[128,256]{1,0:T(8,128)(2,1)S(1)} %shard_map.79.a_ref), channel_id=1, source_target_pairs={{0,3},{1,0},{2,1},{3,2},{4,7},{5,4},{6,5},{7,6},{8,11},{9,8},{10,9... | collective-permute-start | bytes 196616 | tf_op jit(solution)/shard_map/ppermute | solution.py:348
  112.6 4.9 %collective-permute-start.3 = (bf16[128,256]{1,0:T(8,128)(2,1)S(1)}, bf16[128,256]{1,0:T(8,128)(2,1)S(1)}, u32[]{:S(2)}, u32[]{:S(2)}) collective-permute-start(bf16[128,256]{1,0:T(8,128)(2,1)S(1)} %shard_map.79.a_ref), channel_id=1, source_target_pairs={{0,2},{1,3},{2,0},{3,1},{4,6},{5,7},{6,4},{7,5},{8,10},{9,11},{10,... | collective-permute-start | bytes 196616 | tf_op jit(solution)/shard_map/ppermute | solution.py:348
  113.7 5.2 %collective-permute-start.2 = (bf16[128,256]{1,0:T(8,128)(2,1)S(1)}, bf16[128,256]{1,0:T(8,128)(2,1)S(1)}, u32[]{:S(2)}, u32[]{:S(2)}) collective-permute-start(bf16[128,256]{1,0:T(8,128)(2,1)S(1)} %shard_map.79.a_ref), channel_id=1, source_target_pairs={{0,1},{1,2},{2,3},{3,0},{4,5},{5,6},{6,7},{7,4},{8,9},{9,10},{10,1... | collective-permute-start | bytes 196616 | tf_op jit(solution)/shard_map/ppermute | solution.py:348

commit v11 on v9

--- a/solution.py
+++ b/solution.py
@@ -10,6 +10,9 @@
 TEACHER_INV = 1.0 / 0.07
 STUDENT_INV = 1.0 / 0.1
 IMAGES = 64
+LOG2E = 1.4426950408889634
+TEACHER_LOG2 = TEACHER_INV * LOG2E
+STUDENT_LOG2 = STUDENT_INV * LOG2E
 GRAD_FACTOR = LOSS_SCALE / (IMAGES * 0.1)
 LIVE = 128
 NT = (((1,), (1,)), ((), ()))
@@ -68,13 +71,12 @@
 def head_kernel(
     mask_hbm, teach_hbm, student_hbm, proto_hbm, own_ref, out_ref, mine_ref, mask_ref, teach_ref, student_ref, proto_ref, sems
 ):
-    chunks = 2
-    tall = proto_ref.shape[0] // chunks
+    starts, sizes = (0, 3072), (3072, 5120)
     small = ((mask_hbm, mask_ref), (teach_hbm, teach_ref), (student_hbm, student_ref))
-    first = [pltpu.make_async_copy(src, dst, sems.at[chunks + i]) for i, (src, dst) in enumerate(small)]
+    first = [pltpu.make_async_copy(src, dst, sems.at[2 + i]) for i, (src, dst) in enumerate(small)]
     copies = [
-        pltpu.make_async_copy(proto_hbm.at[pl.ds(i * tall, tall)], proto_ref.at[pl.ds(i * tall, tall)], sems.at[i])
-        for i in range(chunks)
+        pltpu.make_async_copy(proto_hbm.at[pl.ds(at, size)], proto_ref.at[pl.ds(at, size)], sems.at[i])
+        for i, (at, size) in enumerate(zip(starts, sizes))
     ]
     for copy in first + copies:
         copy.start()
@@ -89,27 +91,27 @@
     rows = own_ref[...].reshape(2 * LIVE, 256)
     peak = top = total = None
     for i in range(0, 8192, 512):
-        if i % tall == 0:
-            copies[i // tall].wait()
+        if i in starts:
+            copies[starts.index(i)].wait()
         if i % 1024 == 0:
             at = pl.multiple_of(i + image * 128, 128)
             mine_ref[i // 8 : i // 8 + 128, :] = proto_ref[pl.ds(at, 128), :]
         low = dot(proto_ref[i : i + 256, :], rows, NT)
         high = dot(proto_ref[i + 256 : i + 512, :], rows, NT)
         teach = jnp.max(jnp.maximum(low[:, :LIVE], high[:, :LIVE]), axis=0, keepdims=True)
-        student = jnp.concatenate([low[:, LIVE:], high[:, LIVE:]], axis=0) * STUDENT_INV
-        now = jnp.max(student, axis=0, keepdims=True)
-        part = jnp.sum(jnp.exp(student - now), axis=0, keepdims=True)
+        student = jnp.concatenate([low[:, LIVE:], high[:, LIVE:]], axis=0)
+        now = jnp.max(student, axis=0, keepdims=True) * STUDENT_LOG2
+        part = jnp.sum(jnp.exp2(student * STUDENT_LOG2 - now), axis=0, keepdims=True)
         if peak is None:
             peak, top, total = teach, now, part
         else:
             peak, both = jnp.maximum(peak, teach), jnp.maximum(top, now)
-            total = total * jnp.exp(top - both) + part * jnp.exp(now - both)
+            total = total * jnp.exp2(top - both) + part * jnp.exp2(now - both)
             top = both
     tile = jnp.concatenate(
         thirds(peak * TEACHER_INV)
         + [jnp.broadcast_to(count, (1, LIVE))]
-        + thirds(top + jnp.log(total))
+        + thirds(top / LOG2E + jnp.log(total))
         + [jnp.zeros((1, LIVE), f32)],
         axis=0,
     )
@@ -134,7 +136,7 @@
         weights = jnp.broadcast_to(live[:, at], (16, 256)).astype(bf16)
         for j in range(2):
             logits = dot(mine_ref[512 * j : 512 * (j + 1), :], rows, NT)
-            block = jnp.exp(logits * TEACHER_INV - peak[:, at]).astype(bf16)
+            block = jnp.exp2(logits * TEACHER_LOG2 - peak[:, at]).astype(bf16)
             et_ref[512 * j : 512 * (j + 1), at] = block
             sums[j] += dot(weights, block, NT)
 
@@ -155,13 +157,13 @@
     stat_ref[1] = live / count
     stat_ref[2] = peak
     sums = [jnp.zeros((16, 512), f32)] * 2
-    expo_half(rows_ref, mine_ref, et_ref, halves(peak)[0], halves(live)[0], sums)
+    expo_half(rows_ref, mine_ref, et_ref, halves(peak * LOG2E)[0], halves(live)[0], sums)
     sum_ref[...] = jnp.concatenate(sums, axis=1)
 
 
 def expo_other_kernel(stat_ref, sum_ref, rows_ref, mine_ref, et_ref, pay_ref):
     sums = [sum_ref[:, 0:512], sum_ref[:, 512:1024]]
-    expo_half(rows_ref, mine_ref, et_ref, halves(stat_ref[2])[1], halves(stat_ref[0])[1], sums)
+    expo_half(rows_ref, mine_ref, et_ref, halves(stat_ref[2] * LOG2E)[1], halves(stat_ref[0])[1], sums)
     spread(to_tile(jnp.concatenate(sums, axis=1)[0:1]), pay_ref)
 
 
@@ -205,10 +207,11 @@
         at = slice(256 * r, 256 * (r + 1))
         rows_ref, et_ref = ((sown_ref, own_ref), (sother_ref, other_ref))[r // 2]
         rows = rows_ref[2 * (r % 2) : 2 * (r % 2) + 2].reshape(256, 256)
-        log_prob = dot(mine_ref[...], rows, NT) * STUDENT_INV - norm[:, at]
-        prob_ref[:, at] = jnp.exp(log_prob) * coef[:, at]
         here = slice(256 * (r % 2), 256 * (r % 2) + 256)
-        w_ref[:, at] = (et_ref[:, here].astype(f32) * log_prob).astype(bf16)
+        for j in (slice(0, 512), slice(512, 1024)):
+            log_prob = dot(mine_ref[j, :], rows, NT) * STUDENT_INV - norm[:, at]
+            prob_ref[j, at] = jnp.exp(log_prob) * coef[:, at]
+            w_ref[j, at] = (et_ref[j, here].astype(f32) * log_prob).astype(bf16)
 
 
 def grad_kernel(
@@ -268,8 +271,8 @@
     for copy in [rows_copy] + copies:
         copy.start()
     y = lax.axis_index("y")
-    peak = column(stat_ref[2, own_image(), :], 1024)
-    norm = column(norm_ref[own_image(), :], 1024)
+    peak = column(stat_ref[2, own_image(), :] * LOG2E, 1024)
+    norm = column(norm_ref[own_image(), :] * LOG2E, 1024)
     coef = column(scale_ref[0, own_image(), :], 1024)
     scale = column(scale_ref[1, own_image(), :], 1024)
     cols = [recv_ref[(x * 4 + y) * 2 + c].astype(f32)[16:24] for x in range(4) for c in range(2)]
@@ -282,8 +285,8 @@
         col = jnp.concatenate([v[i : i + 1, :] for v in cols], axis=1)
         block = proto_ref[1024 * i : 1024 * (i + 1), :]
         logits = dot(rows, block, NT)
-        teach = jnp.exp(logits[0:LIVE] * TEACHER_INV - peak).astype(bf16).astype(f32)
-        prob = jnp.exp(logits[LIVE:] * STUDENT_INV - norm)
+        teach = jnp.exp2(logits[0:LIVE] * TEACHER_LOG2 - peak).astype(bf16).astype(f32)
+        prob = jnp.exp2(logits[LIVE:] * STUDENT_LOG2 - norm)
         grad = (prob * coef - teach * (col * scale)).astype(bf16)
         total += dot(grad, block, NN)
     out_ref[...] = total.astype(bf16)

time: 125 us -> 125 us (level)
  transfers between devices with their start and end apart: 9 -> 9, of which waited for: 5 -> 5; matrix products, arithmetic and copies ran while one was open for 0% -> 0% of each run, Pallas kernels for 7% -> 6%
where the time goes in v11:
time: 125 us
  blocking collectives  84.9 us (68%)
  Pallas kernels  17.1 us (14%)
  waiting for transfers between devices  11 us (9%)
  starting transfers between devices  10.8 us (9%)
    all_to_all x7, blocking collectives, a2a(): return lax.all_to_all(v, axes, 0, 0, tiled=True)  84.9 us
    pallas_call x11, Pallas kernels, call(): pl.pallas_call(kernel, out_shape=out, in_specs=[VM] * len(args), out_spec...  7.67 us
    ppermute x8, starting transfers between devices, shift(): return lax.ppermute(v, axis, [(i, (i + k) % n) for i in range(n)])  7.21 us
    all_to_all x1, waiting for transfers between devices, a2a(): return lax.all_to_all(v, axes, 0, 0, tiled=True)  5.65 us
    ppermute x8, waiting for transfers between devices, shift(): return lax.ppermute(v, axis, [(i, (i + k) % n) for i in range(n)])  5.39 us
    pallas_call x1, Pallas kernels, local(): pl.pallas_call(own_kernel, out_shape=jax.ShapeDtypeStruct((LIVE, 256), bf...  4.18 us
    pallas_call x1, Pallas kernels, local(): pl.pallas_call(head_kernel, out_shape=[jax.ShapeDtypeStruct((2, LIVE, 256...  3.69 us
    all_to_all x1, starting transfers between devices, a2a(): return lax.all_to_all(v, axes, 0, 0, tiled=True)  3.55 us
  transfers between devices with their start and end apart: 9, of which 5 were waited for; matrix products, arithmetic and copies ran while one was open for 0% of the time, Pallas kernels for 6%

profile of v11, /device:TPU:1, one launch (start us, length us, event | category | flops | bytes accessed | tf_op | source)
XLA Modules:
  0.0 124.6 jit_solution(7152293295481914225)
XLA Ops:
  0.6 3.7 %shard_map.67 = (bf16[2,128,256]{2,1,0:T(8,128)(2,1)S(1)}, bf16[32,8,128]{2,1,0:T(8,128)(2,1)S(1)}, bf16[1024,256]{1,0:T(8,128)(2,1)S(1)}) custom-call(s32[1,256]{1,0:T(1,128)} %mask_ref.1, bf16[1,256,256]{2,1,0:T(8,128)(2,1)} %teach_hbm.1, bf16[1,256,256]{2,1,0:T(8,128)(2,1)} %student_hbm.1, bf16[8192,256]{1,0:T(8,128)(2,1)} %proto_hbm.3), custom_call_target="tpu_custom_call" | custom-call | tf_op jit(solution)/shard_map/pallas_call | solution.py:342
  4.3 3.4 %collective-permute-start.2 = (bf16[2,128,256]{2,1,0:T(8,128)(2,1)S(1)}, bf16[2,128,256]{2,1,0:T(8,128)(2,1)S(1)}, u32[]{:S(2)}, u32[]{:S(2)}) collective-permute-start(bf16[2,128,256]{2,1,0:T(8,128)(2,1)S(1)} %get-tuple-element.29.a_ref.rows_hbm), channel_id=1, source_target_pairs={{0,24},{8,0},{16,8},{24,16},{1,25},{9,1},{17,9},{25,17},{2,26},{10... | collective-permute-start | bytes 393224 | tf_op jit(solution)/shard_map/ppermute | solution.py:334
  7.7 0.5 collective-permute-start.1
  8.2 0.6 collective-permute-start
  8.9 15.1 %all_to_all.40.recv_ref = bf16[32,8,128]{2,1,0:T(8,128)(2,1)S(1)} all-to-all(bf16[32,8,128]{2,1,0:T(8,128)(2,1)S(1)} %get-tuple-element.28), channel_id=1, replica_groups=mesh['z'=8,'x'=4,'c'=2,'y'=4] {'x','y','c'}, dimensions={0} | all-to-all | bytes 131072 | tf_op jit(solution)/shard_map/all_to_all | solution.py:330
  24.0 0.5 collective-permute-start.3
  24.6 0.8 shard_map.69
  25.4 0.2 collective-permute-done.3.rows_ref
  25.6 0.8 shard_map.70
  26.5 14.6 %all_to_all.41.recv_ref = bf16[8,8,128]{2,1,0:T(8,128)(2,1)S(1)} all-to-all(bf16[8,8,128]{2,1,0:T(8,128)(2,1)S(1)} %get-tuple-element.34), channel_id=1, replica_groups=mesh['z'=8,'x'=4,'c'=2,'y'=4] {'z'}, dimensions={0} | all-to-all | bytes 32768 | tf_op jit(solution)/shard_map/all_to_all | solution.py:330
  41.1 0.4 shard_map.71
  41.5 12.3 %all_to_all.42.recv_ref = bf16[32,8,128]{2,1,0:T(8,128)(2,1)S(1)} all-to-all(bf16[32,8,128]{2,1,0:T(8,128)(2,1)S(1)} %shard_map.71), channel_id=1, replica_groups=mesh['z'=8,'x'=4,'c'=2,'y'=4] {'x','y','c'}, dimensions={0} | all-to-all | bytes 131072 | tf_op jit(solution)/shard_map/all_to_all | solution.py:330
  53.8 0.7 shard_map.72
  54.5 1.2 shard_map.73
  55.7 9.0 %all_to_all.43.recv_ref = bf16[8,8,128]{2,1,0:T(8,128)(2,1)S(1)} all-to-all(bf16[8,8,128]{2,1,0:T(8,128)(2,1)S(1)} %shard_map.72), channel_id=1, replica_groups=mesh['z'=8,'x'=4,'c'=2,'y'=4] {'z'}, dimensions={0} | all-to-all | bytes 32768 | tf_op jit(solution)/shard_map/all_to_all | solution.py:330
  64.7 0.4 shard_map.74
  65.1 12.0 %all_to_all.44.recv_ref = bf16[32,8,128]{2,1,0:T(8,128)(2,1)S(1)} all-to-all(bf16[32,8,128]{2,1,0:T(8,128)(2,1)S(1)} %shard_map.74), channel_id=1, replica_groups=mesh['z'=8,'x'=4,'c'=2,'y'=4] {'x','y','c'}, dimensions={0} | all-to-all | bytes 131072 | tf_op jit(solution)/shard_map/all_to_all | solution.py:330
  77.1 0.7 shard_map.75
  77.8 9.0 %all_to_all.45.recv_ref = bf16[8,8,128]{2,1,0:T(8,128)(2,1)S(1)} all-to-all(bf16[8,8,128]{2,1,0:T(8,128)(2,1)S(1)} %shard_map.75), channel_id=1, replica_groups=mesh['z'=8,'x'=4,'c'=2,'y'=4] {'z'}, dimensions={0} | all-to-all | bytes 32768 | tf_op jit(solution)/shard_map/all_to_all | solution.py:330
  86.8 0.7 shard_map.76
  87.5 13.0 %all_to_all.46.recv_ref = bf16[32,24,128]{2,1,0:T(8,128)(2,1)S(1)} all-to-all(bf16[32,24,128]{2,1,0:T(8,128)(2,1)S(1)} %get-tuple-element.45), channel_id=1, replica_groups=mesh['z'=8,'x'=4,'c'=2,'y'=4] {'x','y','c'}, dimensions={0} | all-to-all | bytes 393216 | tf_op jit(solution)/shard_map/all_to_all | solution.py:330
  100.5 1.6 %shard_map.77 = (bf16[8,264,128]{2,1,0:T(8,128)(2,1)}, f32[2,8,128]{2,1,0:T(8,128)S(1)}) custom-call(bf16[32,24,128]{2,1,0:T(8,128)(2,1)S(1)} %all_to_all.46.recv_ref, f32[3,8,128]{2,1,0:T(8,128)S(1)} %get-tuple-element.38.stat_ref, f32[8,128]{1,0:T(8,128)S(1)} %get-tuple-element.46.col_ref, bf16[1024,512]{1,0:T(8,128)(2,1)S(1)} %get-tuple-element.35.own_ref, ...), custom_call_target="tpu_custom_call" | custom-call | tf_op jit(solution)/shard_map/pallas_call | solution.py:394
  102.0 3.5 %all-to-all-start.7 = ((bf16[8,264,128]{2,1,0:T(8,128)(2,1)}), bf16[8,264,128]{2,1,0:T(8,128)(2,1)S(1)}, u32[]{:S(2)}, u32[]{:S(2)}) async-start(bf16[8,264,128]{2,1,0:T(8,128)(2,1)} %get-tuple-element.48), calls=%async_computation.7 | async-start | bytes 1081344 | tf_op jit(solution)/shard_map/all_to_all | solution.py:330
  105.6 4.2 %shard_map.79.a_ref = bf16[128,256]{1,0:T(8,128)(2,1)S(1)} custom-call(bf16[32,24,128]{2,1,0:T(8,128)(2,1)S(1)} %all_to_all.46.recv_ref, f32[2,8,128]{2,1,0:T(8,128)S(1)} %get-tuple-element.50.scale_ref, f32[3,8,128]{2,1,0:T(8,128)S(1)} %get-tuple-element.38.stat_ref, f32[8,128]{1,0:T(8,128)S(1)} %get-tuple-element.51.norm_ref, ...), custom_call_target="tpu_custom_call" | custom-call | flops 2147483648 | bytes 4194304 | tf_op jit(solution)/shard_map/pallas_call | solution.py:403
  109.8 1.0 collective-permute-start.7
  110.8 1.1 collective-permute-start.6
  111.9 1.4 %collective-permute-done.7.d_ref = bf16[128,256]{1,0:T(8,128)(2,1)S(1)} collective-permute-done((bf16[128,256]{1,0:T(8,128)(2,1)S(1)}, bf16[128,256]{1,0:T(8,128)(2,1)S(1)}, u32[]{:S(2)}, u32[]{:S(2)}) %collective-permute-start.7) | collective-permute-done | bytes 65568 | tf_op jit(solution)/shard_map/ppermute | solution.py:334
  113.3 2.3 %collective-permute-done.6.c_ref = bf16[128,256]{1,0:T(8,128)(2,1)S(1)} collective-permute-done((bf16[128,256]{1,0:T(8,128)(2,1)S(1)}, bf16[128,256]{1,0:T(8,128)(2,1)S(1)}, u32[]{:S(2)}, u32[]{:S(2)}) %collective-permute-start.6) | collective-permute-done | bytes 65568 | tf_op jit(solution)/shard_map/ppermute | solution.py:334
  115.6 1.5 %collective-permute-done.5.b_ref = bf16[128,256]{1,0:T(8,128)(2,1)S(1)} collective-permute-done((bf16[128,256]{1,0:T(8,128)(2,1)S(1)}, bf16[128,256]{1,0:T(8,128)(2,1)S(1)}, u32[]{:S(2)}, u32[]{:S(2)}) %collective-permute-start.5) | collective-permute-done | bytes 65568 | tf_op jit(solution)/shard_map/ppermute | solution.py:334
  117.1 1.2 shard_map.80
  118.2 5.7 %all-to-all-done.7.recv_ref = bf16[8,264,128]{2,1,0:T(8,128)(2,1)S(1)} async-done(((bf16[8,264,128]{2,1,0:T(8,128)(2,1)}), bf16[8,264,128]{2,1,0:T(8,128)(2,1)S(1)}, u32[]{:S(2)}, u32[]{:S(2)}) %all-to-all-start.7) | async-done | bytes 540704 | tf_op jit(solution)/shard_map/all_to_all | solution.py:330
  123.9 0.7 shard_map.78
  (11 shorter events, 0.2 us)
Async XLA Ops:
  4.3 51.4 %copy-start = (bf16[2,128,256]{2,1,0:T(8,128)(2,1)}, bf16[2,128,256]{2,1,0:T(8,128)(2,1)S(1)}, u32[]{:S(2)}) copy-start(bf16[2,128,256]{2,1,0:T(8,128)(2,1)S(1)} %get-tuple-element.29.a_ref.rows_hbm) | copy-start | bytes 393220
  4.3 19.6 %collective-permute-start.2 = (bf16[2,128,256]{2,1,0:T(8,128)(2,1)S(1)}, bf16[2,128,256]{2,1,0:T(8,128)(2,1)S(1)}, u32[]{:S(2)}, u32[]{:S(2)}) collective-permute-start(bf16[2,128,256]{2,1,0:T(8,128)(2,1)S(1)} %get-tuple-element.29.a_ref.rows_hbm), channel_id=1, source_target_pairs={{0,24},{8,0},{16,8},{24,16},{1,25},{9,1},{17,9},{25,17},{2,26},{10... | collective-permute-start | bytes 393224 | tf_op jit(solution)/shard_map/ppermute | solution.py:334
  7.7 16.2 %collective-permute-start.1 = (bf16[2,128,256]{2,1,0:T(8,128)(2,1)S(1)}, bf16[2,128,256]{2,1,0:T(8,128)(2,1)S(1)}, u32[]{:S(2)}, u32[]{:S(2)}) collective-permute-start(bf16[2,128,256]{2,1,0:T(8,128)(2,1)S(1)} %get-tuple-element.29.a_ref.rows_hbm), channel_id=1, source_target_pairs={{0,16},{8,24},{16,0},{24,8},{1,17},{9,25},{17,1},{25,9},{2,18},{10... | collective-permute-start | bytes 393224 | tf_op jit(solution)/shard_map/ppermute | solution.py:334
  8.2 15.7 %collective-permute-start = (bf16[2,128,256]{2,1,0:T(8,128)(2,1)S(1)}, bf16[2,128,256]{2,1,0:T(8,128)(2,1)S(1)}, u32[]{:S(2)}, u32[]{:S(2)}) collective-permute-start(bf16[2,128,256]{2,1,0:T(8,128)(2,1)S(1)} %get-tuple-element.29.a_ref.rows_hbm), channel_id=1, source_target_pairs={{0,8},{8,16},{16,24},{24,0},{1,9},{9,17},{17,25},{25,1},{2,10},{10... | collective-permute-start | bytes 393224 | tf_op jit(solution)/shard_map/ppermute | solution.py:334
  24.0 1.6 %collective-permute-start.3 = (bf16[4,128,256]{2,1,0:T(8,128)(2,1)S(1)}, bf16[4,128,256]{2,1,0:T(8,128)(2,1)S(1)}, u32[]{:S(2)}, u32[]{:S(2)}) collective-permute-start(bf16[4,128,256]{2,1,0:T(8,128)(2,1)S(1)} %get-tuple-element.30.rows_ref), channel_id=1, source_target_pairs={{0,4},{4,0},{1,5},{5,1},{2,6},{6,2},{3,7},{7,3},{8,12},{12,8},{9,1... | collective-permute-start | bytes 786440 | tf_op jit(solution)/shard_map/ppermute | solution.py:334
  24.5 30.0 %collective-permute-start.4 = (bf16[4,128,256]{2,1,0:T(8,128)(2,1)S(1)}, bf16[4,128,256]{2,1,0:T(8,128)(2,1)S(1)}, u32[]{:S(2)}, u32[]{:S(2)}) collective-permute-start(bf16[4,128,256]{2,1,0:T(8,128)(2,1)S(1)} %get-tuple-element.39.sown_ref), channel_id=1, source_target_pairs={{0,4},{4,0},{1,5},{5,1},{2,6},{6,2},{3,7},{7,3},{8,12},{12,8},{9,1... | collective-permute-start | bytes 786440 | tf_op jit(solution)/shard_map/ppermute | solution.py:334
  102.0 21.8 %all-to-all-start.7 = ((bf16[8,264,128]{2,1,0:T(8,128)(2,1)}), bf16[8,264,128]{2,1,0:T(8,128)(2,1)S(1)}, u32[]{:S(2)}, u32[]{:S(2)}) async-start(bf16[8,264,128]{2,1,0:T(8,128)(2,1)} %get-tuple-element.48), calls=%async_computation.7 | async-start | bytes 1081344 | tf_op jit(solution)/shard_map/all_to_all | solution.py:330
  105.6 11.5 %copy-start.1 = (s32[1,256]{1,0:T(1,128)S(1)}, s32[1,256]{1,0:T(1,128)}, u32[]{:S(2)}) copy-start(s32[1,256]{1,0:T(1,128)} %mask_ref.1) | copy-start | bytes 3076
  109.8 3.5 %collective-permute-start.7 = (bf16[128,256]{1,0:T(8,128)(2,1)S(1)}, bf16[128,256]{1,0:T(8,128)(2,1)S(1)}, u32[]{:S(2)}, u32[]{:S(2)}) collective-permute-start(bf16[128,256]{1,0:T(8,128)(2,1)S(1)} %shard_map.79.a_ref), channel_id=1, source_target_pairs={{0,3},{1,0},{2,1},{3,2},{4,7},{5,4},{6,5},{7,6},{8,11},{9,8},{10,9... | collective-permute-start | bytes 196616 | tf_op jit(solution)/shard_map/ppermute | solution.py:334
  110.8 4.8 %collective-permute-start.6 = (bf16[128,256]{1,0:T(8,128)(2,1)S(1)}, bf16[128,256]{1,0:T(8,128)(2,1)S(1)}, u32[]{:S(2)}, u32[]{:S(2)}) collective-permute-start(bf16[128,256]{1,0:T(8,128)(2,1)S(1)} %shard_map.79.a_ref), channel_id=1, source_target_pairs={{0,2},{1,3},{2,0},{3,1},{4,6},{5,7},{6,4},{7,5},{8,10},{9,11},{10,... | collective-permute-start | bytes 196616 | tf_op jit(solution)/shard_map/ppermute | solution.py:334
  111.9 5.2 %collective-permute-start.5 = (bf16[128,256]{1,0:T(8,128)(2,1)S(1)}, bf16[128,256]{1,0:T(8,128)(2,1)S(1)}, u32[]{:S(2)}, u32[]{:S(2)}) collective-permute-start(bf16[128,256]{1,0:T(8,128)(2,1)S(1)} %shard_map.79.a_ref), channel_id=1, source_target_pairs={{0,1},{1,2},{2,3},{3,0},{4,5},{5,6},{6,7},{7,4},{8,9},{9,10},{10,1... | collective-permute-start | bytes 196616 | tf_op jit(solution)/shard_map/ppermute | solution.py:334

commit v12 on v9

--- a/solution.py
+++ b/solution.py
@@ -230,21 +230,20 @@
     scale_rows = jnp.concatenate(halves(coef * row), axis=1)
     sown, sother = sown_ref[...].reshape(512, 256), sother_ref[...].reshape(512, 256)
     copies = []
-    for j in range(4):
-        at = slice(256 * j, 256 * (j + 1))
-        col = jnp.concatenate([jnp.broadcast_to(col_ref[i : i + 1, :], (128, 128)).T for i in (2 * j, 2 * j + 1)], axis=0)
-        col = jnp.concatenate([col] * 8, axis=1)
+    for j in range(2):
+        at = slice(512 * j, 512 * (j + 1))
+        col = [jnp.broadcast_to(col_ref[i : i + 1, :], (128, 128)).T for i in range(4 * j, 4 * j + 4)]
+        col = jnp.concatenate([jnp.concatenate(col, axis=0)] * 8, axis=1)
         teach = jnp.concatenate([own_ref[at, :], other_ref[at, :]], axis=1).astype(f32)
         grad = (prob_ref[at, :] - teach * col * scale_rows).astype(bf16)
         part = (dot(grad[:, :512], sown, NN) + dot(grad[:, 512:], sother, NN)).astype(bf16)
-        for i in (0, 1):
-            pout_ref[2 * j + i, 0:128, :] = part[128 * i : 128 * (i + 1), 0:128]
-            pout_ref[2 * j + i, 128:256, :] = part[128 * i : 128 * (i + 1), 128:256]
-            pout_ref[2 * j + i, 256:264, :] = tail
-        if j % 2:
-            at = pl.ds(2 * j - 2, 4)
-            copies.append(pltpu.make_async_copy(pout_ref.at[at], pout_hbm.at[at], sems.at[j // 2]))
-            copies[-1].start()
+        for i in range(4):
+            pout_ref[4 * j + i, 0:128, :] = part[128 * i : 128 * (i + 1), 0:128]
+            pout_ref[4 * j + i, 128:256, :] = part[128 * i : 128 * (i + 1), 128:256]
+            pout_ref[4 * j + i, 256:264, :] = tail
+        at = pl.ds(4 * j, 4)
+        copies.append(pltpu.make_async_copy(pout_ref.at[at], pout_hbm.at[at], sems.at[j]))
+        copies[-1].start()
     for copy in copies:
         copy.wait()
 

time: 125 us -> 125 us (level)
  no operation moved by 1% of the time
where the time goes in v12:
time: 125 us
  blocking collectives  84.9 us (68%)
  Pallas kernels  17.3 us (14%)
  waiting for transfers between devices  10.9 us (9%)
  starting transfers between devices  10.8 us (9%)
    all_to_all x7, blocking collectives, a2a(): return lax.all_to_all(v, axes, 0, 0, tiled=True)  84.9 us
    pallas_call x11, Pallas kernels, call(): pl.pallas_call(kernel, out_shape=out, in_specs=[VM] * len(args), out_spec...  7.67 us
    ppermute x8, starting transfers between devices, shift(): return lax.ppermute(v, axis, [(i, (i + k) % n) for i in range(n)])  7.2 us
    all_to_all x1, waiting for transfers between devices, a2a(): return lax.all_to_all(v, axes, 0, 0, tiled=True)  5.49 us
    ppermute x8, waiting for transfers between devices, shift(): return lax.ppermute(v, axis, [(i, (i + k) % n) for i in range(n)])  5.37 us
    pallas_call x1, Pallas kernels, local(): pl.pallas_call(own_kernel, out_shape=jax.ShapeDtypeStruct((LIVE, 256), bf...  4.36 us
    pallas_call x1, Pallas kernels, local(): pl.pallas_call(head_kernel, out_shape=[jax.ShapeDtypeStruct((2, LIVE, 256...  3.65 us
    all_to_all x1, starting transfers between devices, a2a(): return lax.all_to_all(v, axes, 0, 0, tiled=True)  3.55 us
  transfers between devices with their start and end apart: 9, of which 5 were waited for; matrix products, arithmetic and copies ran while one was open for 0% of the time, Pallas kernels for 7%

profile of v12, /device:TPU:1, one launch (start us, length us, event | category | flops | bytes accessed | tf_op | source)
XLA Modules:
  0.0 124.7 jit_solution(16767679002817516296)
XLA Ops:
  0.6 3.7 %shard_map.67 = (bf16[2,128,256]{2,1,0:T(8,128)(2,1)S(1)}, bf16[32,8,128]{2,1,0:T(8,128)(2,1)S(1)}, bf16[1024,256]{1,0:T(8,128)(2,1)S(1)}) custom-call(s32[1,256]{1,0:T(1,128)} %mask_ref.1, bf16[1,256,256]{2,1,0:T(8,128)(2,1)} %teach_hbm.1, bf16[1,256,256]{2,1,0:T(8,128)(2,1)} %student_hbm.1, bf16[8192,256]{1,0:T(8,128)(2,1)} %proto_hbm.3), custom_call_target="tpu_custom_call" | custom-call | tf_op jit(solution)/shard_map/pallas_call | solution.py:338
  4.3 3.4 %collective-permute-start.2 = (bf16[2,128,256]{2,1,0:T(8,128)(2,1)S(1)}, bf16[2,128,256]{2,1,0:T(8,128)(2,1)S(1)}, u32[]{:S(2)}, u32[]{:S(2)}) collective-permute-start(bf16[2,128,256]{2,1,0:T(8,128)(2,1)S(1)} %get-tuple-element.29.a_ref.rows_hbm), channel_id=1, source_target_pairs={{0,24},{8,0},{16,8},{24,16},{1,25},{9,1},{17,9},{25,17},{2,26},{10... | collective-permute-start | bytes 393224 | tf_op jit(solution)/shard_map/ppermute | solution.py:330
  7.7 0.5 collective-permute-start.1
  8.2 0.6 collective-permute-start
  8.8 15.1 %all_to_all.40.recv_ref = bf16[32,8,128]{2,1,0:T(8,128)(2,1)S(1)} all-to-all(bf16[32,8,128]{2,1,0:T(8,128)(2,1)S(1)} %get-tuple-element.28), channel_id=1, replica_groups=mesh['z'=8,'x'=4,'c'=2,'y'=4] {'x','y','c'}, dimensions={0} | all-to-all | bytes 131072 | tf_op jit(solution)/shard_map/all_to_all | solution.py:326
  24.0 0.5 collective-permute-start.3
  24.6 0.8 shard_map.69
  25.4 0.2 collective-permute-done.3.rows_ref
  25.6 0.8 shard_map.70
  26.5 14.6 %all_to_all.41.recv_ref = bf16[8,8,128]{2,1,0:T(8,128)(2,1)S(1)} all-to-all(bf16[8,8,128]{2,1,0:T(8,128)(2,1)S(1)} %get-tuple-element.34), channel_id=1, replica_groups=mesh['z'=8,'x'=4,'c'=2,'y'=4] {'z'}, dimensions={0} | all-to-all | bytes 32768 | tf_op jit(solution)/shard_map/all_to_all | solution.py:326
  41.1 0.4 shard_map.71
  41.5 12.3 %all_to_all.42.recv_ref = bf16[32,8,128]{2,1,0:T(8,128)(2,1)S(1)} all-to-all(bf16[32,8,128]{2,1,0:T(8,128)(2,1)S(1)} %shard_map.71), channel_id=1, replica_groups=mesh['z'=8,'x'=4,'c'=2,'y'=4] {'x','y','c'}, dimensions={0} | all-to-all | bytes 131072 | tf_op jit(solution)/shard_map/all_to_all | solution.py:326
  53.7 0.7 shard_map.72
  54.4 1.2 shard_map.73
  55.7 9.0 %all_to_all.43.recv_ref = bf16[8,8,128]{2,1,0:T(8,128)(2,1)S(1)} all-to-all(bf16[8,8,128]{2,1,0:T(8,128)(2,1)S(1)} %shard_map.72), channel_id=1, replica_groups=mesh['z'=8,'x'=4,'c'=2,'y'=4] {'z'}, dimensions={0} | all-to-all | bytes 32768 | tf_op jit(solution)/shard_map/all_to_all | solution.py:326
  64.7 0.4 shard_map.74
  65.1 12.0 %all_to_all.44.recv_ref = bf16[32,8,128]{2,1,0:T(8,128)(2,1)S(1)} all-to-all(bf16[32,8,128]{2,1,0:T(8,128)(2,1)S(1)} %shard_map.74), channel_id=1, replica_groups=mesh['z'=8,'x'=4,'c'=2,'y'=4] {'x','y','c'}, dimensions={0} | all-to-all | bytes 131072 | tf_op jit(solution)/shard_map/all_to_all | solution.py:326
  77.1 0.7 shard_map.75
  77.8 9.0 %all_to_all.45.recv_ref = bf16[8,8,128]{2,1,0:T(8,128)(2,1)S(1)} all-to-all(bf16[8,8,128]{2,1,0:T(8,128)(2,1)S(1)} %shard_map.75), channel_id=1, replica_groups=mesh['z'=8,'x'=4,'c'=2,'y'=4] {'z'}, dimensions={0} | all-to-all | bytes 32768 | tf_op jit(solution)/shard_map/all_to_all | solution.py:326
  86.7 0.7 shard_map.76
  87.4 13.0 %all_to_all.46.recv_ref = bf16[32,24,128]{2,1,0:T(8,128)(2,1)S(1)} all-to-all(bf16[32,24,128]{2,1,0:T(8,128)(2,1)S(1)} %get-tuple-element.45), channel_id=1, replica_groups=mesh['z'=8,'x'=4,'c'=2,'y'=4] {'x','y','c'}, dimensions={0} | all-to-all | bytes 393216 | tf_op jit(solution)/shard_map/all_to_all | solution.py:326
  100.4 1.7 %shard_map.77 = (bf16[8,264,128]{2,1,0:T(8,128)(2,1)}, f32[2,8,128]{2,1,0:T(8,128)S(1)}) custom-call(bf16[32,24,128]{2,1,0:T(8,128)(2,1)S(1)} %all_to_all.46.recv_ref, f32[3,8,128]{2,1,0:T(8,128)S(1)} %get-tuple-element.38.stat_ref, f32[8,128]{1,0:T(8,128)S(1)} %get-tuple-element.46.col_ref, bf16[1024,512]{1,0:T(8,128)(2,1)S(1)} %get-tuple-element.35.own_ref, ...), custom_call_target="tpu_custom_call" | custom-call | tf_op jit(solution)/shard_map/pallas_call | solution.py:390
  102.1 3.5 %all-to-all-start.7 = ((bf16[8,264,128]{2,1,0:T(8,128)(2,1)}), bf16[8,264,128]{2,1,0:T(8,128)(2,1)S(1)}, u32[]{:S(2)}, u32[]{:S(2)}) async-start(bf16[8,264,128]{2,1,0:T(8,128)(2,1)} %get-tuple-element.48), calls=%async_computation.7 | async-start | bytes 1081344 | tf_op jit(solution)/shard_map/all_to_all | solution.py:326
  105.7 4.4 %shard_map.79.a_ref = bf16[128,256]{1,0:T(8,128)(2,1)S(1)} custom-call(bf16[32,24,128]{2,1,0:T(8,128)(2,1)S(1)} %all_to_all.46.recv_ref, f32[2,8,128]{2,1,0:T(8,128)S(1)} %get-tuple-element.50.scale_ref, f32[3,8,128]{2,1,0:T(8,128)S(1)} %get-tuple-element.38.stat_ref, f32[8,128]{1,0:T(8,128)S(1)} %get-tuple-element.51.norm_ref, ...), custom_call_target="tpu_custom_call" | custom-call | flops 2147483648 | bytes 4194304 | tf_op jit(solution)/shard_map/pallas_call | solution.py:399
  110.0 1.0 collective-permute-start.7
  111.0 1.1 collective-permute-start.6
  112.1 1.4 %collective-permute-done.7.d_ref = bf16[128,256]{1,0:T(8,128)(2,1)S(1)} collective-permute-done((bf16[128,256]{1,0:T(8,128)(2,1)S(1)}, bf16[128,256]{1,0:T(8,128)(2,1)S(1)}, u32[]{:S(2)}, u32[]{:S(2)}) %collective-permute-start.7) | collective-permute-done | bytes 65568 | tf_op jit(solution)/shard_map/ppermute | solution.py:330
  113.5 2.3 %collective-permute-done.6.c_ref = bf16[128,256]{1,0:T(8,128)(2,1)S(1)} collective-permute-done((bf16[128,256]{1,0:T(8,128)(2,1)S(1)}, bf16[128,256]{1,0:T(8,128)(2,1)S(1)}, u32[]{:S(2)}, u32[]{:S(2)}) %collective-permute-start.6) | collective-permute-done | bytes 65568 | tf_op jit(solution)/shard_map/ppermute | solution.py:330
  115.8 1.5 %collective-permute-done.5.b_ref = bf16[128,256]{1,0:T(8,128)(2,1)S(1)} collective-permute-done((bf16[128,256]{1,0:T(8,128)(2,1)S(1)}, bf16[128,256]{1,0:T(8,128)(2,1)S(1)}, u32[]{:S(2)}, u32[]{:S(2)}) %collective-permute-start.5) | collective-permute-done | bytes 65568 | tf_op jit(solution)/shard_map/ppermute | solution.py:330
  117.3 1.2 shard_map.80
  118.4 5.5 %all-to-all-done.7.recv_ref = bf16[8,264,128]{2,1,0:T(8,128)(2,1)S(1)} async-done(((bf16[8,264,128]{2,1,0:T(8,128)(2,1)}), bf16[8,264,128]{2,1,0:T(8,128)(2,1)S(1)}, u32[]{:S(2)}, u32[]{:S(2)}) %all-to-all-start.7) | async-done | bytes 540704 | tf_op jit(solution)/shard_map/all_to_all | solution.py:326
  123.9 0.7 shard_map.78
  (11 shorter events, 0.2 us)
Async XLA Ops:
  4.3 51.4 %copy-start = (bf16[2,128,256]{2,1,0:T(8,128)(2,1)}, bf16[2,128,256]{2,1,0:T(8,128)(2,1)S(1)}, u32[]{:S(2)}) copy-start(bf16[2,128,256]{2,1,0:T(8,128)(2,1)S(1)} %get-tuple-element.29.a_ref.rows_hbm) | copy-start | bytes 393220
  4.3 19.6 %collective-permute-start.2 = (bf16[2,128,256]{2,1,0:T(8,128)(2,1)S(1)}, bf16[2,128,256]{2,1,0:T(8,128)(2,1)S(1)}, u32[]{:S(2)}, u32[]{:S(2)}) collective-permute-start(bf16[2,128,256]{2,1,0:T(8,128)(2,1)S(1)} %get-tuple-element.29.a_ref.rows_hbm), channel_id=1, source_target_pairs={{0,24},{8,0},{16,8},{24,16},{1,25},{9,1},{17,9},{25,17},{2,26},{10... | collective-permute-start | bytes 393224 | tf_op jit(solution)/shard_map/ppermute | solution.py:330
  7.7 16.2 %collective-permute-start.1 = (bf16[2,128,256]{2,1,0:T(8,128)(2,1)S(1)}, bf16[2,128,256]{2,1,0:T(8,128)(2,1)S(1)}, u32[]{:S(2)}, u32[]{:S(2)}) collective-permute-start(bf16[2,128,256]{2,1,0:T(8,128)(2,1)S(1)} %get-tuple-element.29.a_ref.rows_hbm), channel_id=1, source_target_pairs={{0,16},{8,24},{16,0},{24,8},{1,17},{9,25},{17,1},{25,9},{2,18},{10... | collective-permute-start | bytes 393224 | tf_op jit(solution)/shard_map/ppermute | solution.py:330
  8.2 15.7 %collective-permute-start = (bf16[2,128,256]{2,1,0:T(8,128)(2,1)S(1)}, bf16[2,128,256]{2,1,0:T(8,128)(2,1)S(1)}, u32[]{:S(2)}, u32[]{:S(2)}) collective-permute-start(bf16[2,128,256]{2,1,0:T(8,128)(2,1)S(1)} %get-tuple-element.29.a_ref.rows_hbm), channel_id=1, source_target_pairs={{0,8},{8,16},{16,24},{24,0},{1,9},{9,17},{17,25},{25,1},{2,10},{10... | collective-permute-start | bytes 393224 | tf_op jit(solution)/shard_map/ppermute | solution.py:330
  24.0 1.6 %collective-permute-start.3 = (bf16[4,128,256]{2,1,0:T(8,128)(2,1)S(1)}, bf16[4,128,256]{2,1,0:T(8,128)(2,1)S(1)}, u32[]{:S(2)}, u32[]{:S(2)}) collective-permute-start(bf16[4,128,256]{2,1,0:T(8,128)(2,1)S(1)} %get-tuple-element.30.rows_ref), channel_id=1, source_target_pairs={{0,4},{4,0},{1,5},{5,1},{2,6},{6,2},{3,7},{7,3},{8,12},{12,8},{9,1... | collective-permute-start | bytes 786440 | tf_op jit(solution)/shard_map/ppermute | solution.py:330
  24.5 30.0 %collective-permute-start.4 = (bf16[4,128,256]{2,1,0:T(8,128)(2,1)S(1)}, bf16[4,128,256]{2,1,0:T(8,128)(2,1)S(1)}, u32[]{:S(2)}, u32[]{:S(2)}) collective-permute-start(bf16[4,128,256]{2,1,0:T(8,128)(2,1)S(1)} %get-tuple-element.39.sown_ref), channel_id=1, source_target_pairs={{0,4},{4,0},{1,5},{5,1},{2,6},{6,2},{3,7},{7,3},{8,12},{12,8},{9,1... | collective-permute-start | bytes 786440 | tf_op jit(solution)/shard_map/ppermute | solution.py:330
  102.1 21.8 %all-to-all-start.7 = ((bf16[8,264,128]{2,1,0:T(8,128)(2,1)}), bf16[8,264,128]{2,1,0:T(8,128)(2,1)S(1)}, u32[]{:S(2)}, u32[]{:S(2)}) async-start(bf16[8,264,128]{2,1,0:T(8,128)(2,1)} %get-tuple-element.48), calls=%async_computation.7 | async-start | bytes 1081344 | tf_op jit(solution)/shard_map/all_to_all | solution.py:326
  105.6 11.6 %copy-start.1 = (s32[1,256]{1,0:T(1,128)S(1)}, s32[1,256]{1,0:T(1,128)}, u32[]{:S(2)}) copy-start(s32[1,256]{1,0:T(1,128)} %mask_ref.1) | copy-start | bytes 3076
  110.0 3.5 %collective-permute-start.7 = (bf16[128,256]{1,0:T(8,128)(2,1)S(1)}, bf16[128,256]{1,0:T(8,128)(2,1)S(1)}, u32[]{:S(2)}, u32[]{:S(2)}) collective-permute-start(bf16[128,256]{1,0:T(8,128)(2,1)S(1)} %shard_map.79.a_ref), channel_id=1, source_target_pairs={{0,3},{1,0},{2,1},{3,2},{4,7},{5,4},{6,5},{7,6},{8,11},{9,8},{10,9... | collective-permute-start | bytes 196616 | tf_op jit(solution)/shard_map/ppermute | solution.py:330
  111.0 4.8 %collective-permute-start.6 = (bf16[128,256]{1,0:T(8,128)(2,1)S(1)}, bf16[128,256]{1,0:T(8,128)(2,1)S(1)}, u32[]{:S(2)}, u32[]{:S(2)}) collective-permute-start(bf16[128,256]{1,0:T(8,128)(2,1)S(1)} %shard_map.79.a_ref), channel_id=1, source_target_pairs={{0,2},{1,3},{2,0},{3,1},{4,6},{5,7},{6,4},{7,5},{8,10},{9,11},{10,... | collective-permute-start | bytes 196616 | tf_op jit(solution)/shard_map/ppermute | solution.py:330
  112.1 5.2 %collective-permute-start.5 = (bf16[128,256]{1,0:T(8,128)(2,1)S(1)}, bf16[128,256]{1,0:T(8,128)(2,1)S(1)}, u32[]{:S(2)}, u32[]{:S(2)}) collective-permute-start(bf16[128,256]{1,0:T(8,128)(2,1)S(1)} %shard_map.79.a_ref), channel_id=1, source_target_pairs={{0,1},{1,2},{2,3},{3,0},{4,5},{5,6},{6,7},{7,4},{8,9},{9,10},{10,1... | collective-permute-start | bytes 196616 | tf_op jit(solution)/shard_map/ppermute | solution.py:330
